TPU v7x, 32 devices: a whole 2x2x4 slice. The times are simulated.
32 devices in a mesh: dp: 16 (over z, x, core), shard: 2 (over y).
Axes of the slice: x: 2, y: 2, z: 4, core: 2. Of those that a mesh axis runs over, the one named last changes fastest.
Arguments:
- group_grads: bfloat16 [16, 1024, 1024], P('dp', 'shard'), may hold values from -2 to 2
- moment: float32 [1024, 1024], P('shard'), may hold values from -6 to 6
- second: float32 [1024, 1024], P(None, 'shard'), may hold values from 0.5 to 4
- stat_left: float32 [1024, 1024], P('shard'), may hold values from -200 to 2000, as said below
- stat_right: float32 [1024, 1024], P('shard'), may hold values from -200 to 2000, as said below
- basis_left: float32 [1024, 1024], P('shard'), as said below
- basis_right: float32 [1024, 1024], P('shard'), as said below
Outputs:
- update: bfloat16 [1024, 1024], P('shard')
- second_new: float32 [1024, 1024], P(None, 'shard')
- left_new: float32 [1024, 1024], P('shard')
- right_new: float32 [1024, 1024], P('shard')
Inputs may be any that keep to these rules, and one draw needn't show every extreme that they name: `stat_left`: each statistic is symmetric. `stat_right`: each statistic is symmetric. `basis_left`: diagonal entries near 0.9 sqrt(1024), off-diagonal entries of order one. `basis_right`: diagonal entries near 0.9 sqrt(1024), off-diagonal entries of order one.
All inputs are finite; a program needn't handle non-finite values.
Results may differ from a plain program's by a relative error of at most 0.0049.
The roundings to bfloat16 on the way count: a program that leaves them out, or rounds other values in their place, can miss the bound.
Values may be sent and summed in bfloat16 or wider, within the bound.
No kernel may reach another device: no remote copies, remote signals or barrier semaphores. Data moves between devices by JAX's collectives and lax.ppermute only.
A program may use at most 128 MiB of HBM per device.

v0:
```python
import jax
import jax.numpy as jnp
from jax import lax
from jax.sharding import PartitionSpec as P

NS_ITERS = 2


BETA_ONE = 0.9
BETA_TWO = 0.9
BETA_STAT = 0.95
EPSILON = 1e-08
NORM_EPS = 1e-06


def contract_rows(left_mat, right_mat):
    return lax.dot_general(
        left_mat, right_mat, (((0,), (0,)), ((), ())), preferred_element_type=jnp.float32
    )


def contract_cols(left_mat, right_mat):
    return lax.dot_general(
        left_mat, right_mat, (((1,), (1,)), ((), ())), preferred_element_type=jnp.float32
    )


def body(group_grads, moment, second, stat_left, stat_right, basis_left, basis_right):
    position = lax.axis_index("shard")
    row_count = moment.shape[0]
    block_width = moment.shape[1]
    local_sum = group_grads[0].astype(jnp.float32)
    summed = lax.psum(local_sum, "dp")
    grad_rows = summed.astype(jnp.bfloat16)
    gradient = lax.all_gather(grad_rows, "shard", axis=0, tiled=True)
    moment_half = (BETA_ONE * moment + (1.0 - BETA_ONE) * grad_rows.astype(jnp.float32)).astype(
        jnp.bfloat16
    )
    left_stat = BETA_STAT * stat_left + (1.0 - BETA_STAT) * contract_cols(grad_rows, gradient)
    grad_cols = lax.dynamic_slice_in_dim(gradient, position * row_count, row_count, 1)
    right_stat = BETA_STAT * stat_right + (1.0 - BETA_STAT) * contract_rows(grad_cols, gradient)
    left_rot, right_rot = (
        lax.all_gather(basis_left.astype(jnp.bfloat16), "shard", axis=0, tiled=True),
        lax.all_gather(basis_right.astype(jnp.bfloat16), "shard", axis=0, tiled=True),
    )
    grad_turned = jnp.dot(grad_rows, right_rot, preferred_element_type=jnp.float32).astype(
        jnp.bfloat16
    )
    moment_turned = jnp.dot(moment_half, right_rot, preferred_element_type=jnp.float32).astype(
        jnp.bfloat16
    )
    grad_block, moment_block = (
        lax.all_to_all(grad_turned, "shard", split_axis=1, concat_axis=0, tiled=True),
        lax.all_to_all(moment_turned, "shard", split_axis=1, concat_axis=0, tiled=True),
    )
    grad_rot = contract_rows(left_rot, grad_block) / block_width
    moment_rot = contract_rows(left_rot, moment_block) / block_width
    second_new = BETA_TWO * second + (1.0 - BETA_TWO) * grad_rot * grad_rot
    scaled = (moment_rot / (jnp.sqrt(second_new) + EPSILON)).astype(jnp.bfloat16)
    turned_back = jnp.dot(left_rot, scaled, preferred_element_type=jnp.float32).astype(jnp.bfloat16)
    back_rows = lax.all_to_all(turned_back, "shard", split_axis=0, concat_axis=1, tiled=True)
    update = (contract_cols(back_rows, right_rot) / block_width).astype(jnp.bfloat16)
    left_product = jnp.dot(
        left_stat.astype(jnp.bfloat16), left_rot, preferred_element_type=jnp.float32
    )
    right_product = jnp.dot(
        right_stat.astype(jnp.bfloat16), right_rot, preferred_element_type=jnp.float32
    )
    left_sq, right_sq = lax.psum(
        (
            jnp.sum(left_product * left_product, axis=0),
            jnp.sum(right_product * right_product, axis=0),
        ),
        "shard",
    )
    left_start = left_product / jnp.sqrt(left_sq / block_width + NORM_EPS)
    right_start = right_product / jnp.sqrt(right_sq / block_width + NORM_EPS)
    left_current = left_start.astype(jnp.bfloat16)
    right_current = right_start.astype(jnp.bfloat16)
    left_result = left_start
    right_result = right_start
    for iteration in range(NS_ITERS):
        left_full, right_full = (
            lax.all_gather(left_current, "shard", axis=0, tiled=True),
            lax.all_gather(right_current, "shard", axis=0, tiled=True),
        )
        left_gram = (contract_cols(left_current, left_full) / block_width).astype(jnp.bfloat16)
        right_gram = (contract_cols(right_current, right_full) / block_width).astype(jnp.bfloat16)
        left_result = 1.5 * left_current.astype(jnp.float32) - 0.5 * jnp.dot(
            left_gram, left_full, preferred_element_type=jnp.float32
        )
        right_result = 1.5 * right_current.astype(jnp.float32) - 0.5 * jnp.dot(
            right_gram, right_full, preferred_element_type=jnp.float32
        )
        if iteration + 1 < NS_ITERS:
            left_current = left_result.astype(jnp.bfloat16)
            right_current = right_result.astype(jnp.bfloat16)
    return (update, second_new, left_result, right_result)


def solution(mesh):
    return jax.shard_map(
        body,
        mesh=mesh,
        in_specs=(
            P("dp", "shard", None),
            P("shard", None),
            P(None, "shard"),
            P("shard", None),
            P("shard", None),
            P("shard", None),
            P("shard", None),
        ),
        out_specs=(P("shard", None), P(None, "shard"), P("shard", None), P("shard", None)),
        check_vma=False,
    )
```

profile of v0, /device:TPU:0, one launch (start us, length us, event | category | flops | bytes accessed | tf_op | source)
XLA Modules:
  0.0 339.9 jit_solution(2151220700834970638)
XLA Ops:
  7.2 0.0 copy-start.4
  7.2 0.0 all-gather.10.cloned.1.call-start
  7.2 2.8 convert_element_type.88
  10.0 0.0 all-gather.10.cloned.1.call-update
  10.0 0.0 all-gather.12.cloned.1.call-start
  10.1 0.0 copy-done.4
  10.1 0.2 bitcast_convert_fusion
  10.4 77.3 %all-reduce.2 = bf16[512,1024]{1,0:T(8,128)(2,1)} all-reduce(f32[512,1024]{1,0:T(8,128)S(1)} %bitcast_convert_fusion), channel_id=1, replica_groups=mesh['dp'=16,'shard'=2] {'dp'}, use_global_device_ids=true, to_apply=%region_0.0 | all-reduce | flops 524288 | bytes 3145728 | tf_op jit(solution)/shard_map/psum | solution.py:33
  87.6 0.0 all-gather.12.cloned.1.call-update
  87.7 0.0 copy-start
  87.7 0.0 all-gather.8.cloned.1.call-start
  87.7 2.8 convert_element_type.86
  90.5 0.0 all-gather.8.cloned.1.call-update
  90.6 0.0 all-gather.14.cloned.1.call-start
  90.6 0.0 all-gather.10.cloned.1.call-done
  90.6 27.4 %all-gather.12.cloned.1.call-done = bf16[1024,1024]{1,0:T(8,128)(2,1)} async-done(((bf16[512,1024]{1,0:T(8,128)(2,1)}), bf16[1024,1024]{1,0:T(8,128)(2,1)}) %all-gather.12.cloned.1.call-update) | async-done | bytes 2097168 | tf_op jit(solution)/shard_map/all_gather | solution.py:35
  118.0 0.0 copy-done
  118.0 5.3 %multiply_reduce_fusion.1 = (f32[1024]{0:T(1024)S(1)}, f32[512,1024]{1,0:T(8,128)S(1)}) fusion(bf16[1024,1024]{1,0:T(8,128)(2,1)} %all-gather.10.cloned.1.call-done, f32[512,1024]{1,0:T(8,128)} %param.10, bf16[512,1024]{1,0:T(8,128)(2,1)S(1)} %copy-done, bf16[1024,1024]{1,0:T(8,128)(2,1)} %all-gather.12.cloned.1.call-done), kind=kOutput, calls=%fused_computation.15 | convolution fusion | flops 2150628352 | bytes 9441280 | tf_op jit(solution)/shard_map/dot_general | solution.py:63
  123.4 29.9 %all-gather.8.cloned.1.call-done = bf16[1024,1024]{1,0:T(8,128)(2,1)} async-done(((bf16[512,1024]{1,0:T(8,128)(2,1)}), bf16[1024,1024]{1,0:T(8,128)(2,1)}) %all-gather.8.cloned.1.call-update) | async-done | bytes 2097168 | tf_op jit(solution)/shard_map/all_gather | solution.py:44
  153.3 6.9 %multiply_reduce_fusion = (f32[1024]{0:T(1024)S(1)}, f32[512,1024]{1,0:T(8,128)}) fusion(bf16[1024,1024]{1,0:T(8,128)(2,1)} %all-gather.8.cloned.1.call-done, f32[512,1024]{1,0:T(8,128)} %param.11, bf16[1024,1024]{1,0:T(8,128)(2,1)} %all-gather.12.cloned.1.call-done, s32[]{:T(128)S(6)} %select_n.3), kind=kOutput, calls=%fused_computation.8 | convolution fusion | flops 2150628352 | bytes 9441284 | tf_op jit(solution)/shard_map/dot_general | solution.py:66
  160.2 5.0 %all-reduce = (f32[1024]{0:T(1024)S(1)}, f32[1024]{0:T(1024)S(1)}) all-reduce(f32[1024]{0:T(1024)S(1)} %get-tuple-element.14, f32[1024]{0:T(1024)S(1)} %get-tuple-element.16), channel_id=1, replica_groups=mesh['dp'=16,'shard'=2] {'shard'}, use_global_device_ids=true, to_apply=%region_2.0 | all-reduce | flops 2048 | bytes 16384 | tf_op jit(solution)/shard_map/psum | solution.py:69
  165.2 1.2 divide_convert_fusion.1
  166.4 0.0 all-gather.14.cloned.1.call-update
  166.5 0.0 all-gather.18.cloned.1.call-start
  166.5 0.0 copy-start.2
  166.5 2.9 divide_convert_fusion
  169.5 0.0 all-gather.18.cloned.1.call-update
  169.5 0.0 all-gather.16.cloned.1.call-start
  169.5 30.2 %all-gather.14.cloned.1.call-done = bf16[1024,1024]{1,0:T(8,128)(2,1)} async-done(((bf16[512,1024]{1,0:T(8,128)(2,1)}), bf16[1024,1024]{1,0:T(8,128)(2,1)}) %all-gather.14.cloned.1.call-update) | async-done | bytes 2097168 | tf_op jit(solution)/shard_map/all_gather | solution.py:84
  199.7 0.0 copy-done.2
  199.7 5.7 %subtract_convert_fusion.1 = bf16[512,1024]{1,0:T(8,128)(2,1)} fusion(bf16[512,1024]{1,0:T(8,128)(2,1)S(1)} %copy-done.2, bf16[1024,1024]{1,0:T(8,128)(2,1)} %all-gather.14.cloned.1.call-done), kind=kOutput, calls=%fused_computation.12 | convolution fusion | flops 2151153664 | bytes 4194304 | tf_op jit(solution)/shard_map/dot_general | solution.py:89
  205.4 0.0 all-gather.16.cloned.1.call-update
  205.4 2.8 convolution_convert_fusion.1
  208.3 0.0 copy-start.3
  208.3 1.0 copy.25
  209.3 4.6 %all-to-all-start.1 = ((bf16[512,2,512]{2,0,1:T(8,128)(2,1)}), bf16[512,2,512]{2,0,1:T(8,128)(2,1)}, u32[]{:S(2)}, u32[]{:S(2)}) async-start(bf16[512,2,512]{2,0,1:T(8,128)(2,1)} %bitcast.58), calls=%async_computation.1 | async-start | bytes 2097152 | tf_op jit(solution)/shard_map/all_to_all | solution.py:53
  213.9 0.0 copy-done.3
  213.9 1.8 copy.14
  215.7 3.5 %convolution_convert_fusion.2 = bf16[512,1024]{1,0:T(8,128)(2,1)S(1)} fusion(bf16[1024,1024]{1,0:T(8,128)(2,1)} %all-gather.8.cloned.1.call-done, bf16[512,1024]{1,0:T(8,128)(2,1)S(1)} %copy-done, f32[512,1024]{1,0:T(8,128)} %param.8), kind=kOutput, calls=%fused_computation.21 | convolution fusion | flops 1076887552 | bytes 6291456 | tf_op jit(solution)/shard_map/dot_general | solution.py:49
  219.2 1.1 copy.26
  220.3 19.6 %all-to-all-done.1 = bf16[512,2,512]{2,0,1:T(8,128)(2,1)} async-done(((bf16[512,2,512]{2,0,1:T(8,128)(2,1)}), bf16[512,2,512]{2,0,1:T(8,128)(2,1)}, u32[]{:S(2)}, u32[]{:S(2)}) %all-to-all-start.1) | async-done | bytes 1048608 | tf_op jit(solution)/shard_map/all_to_all | solution.py:53
  239.8 4.4 %all-to-all-start = ((bf16[512,2,512]{2,0,1:T(8,128)(2,1)}), bf16[512,2,512]{2,0,1:T(8,128)(2,1)}, u32[]{:S(2)}, u32[]{:S(2)}) async-start(bf16[512,2,512]{2,0,1:T(8,128)(2,1)} %bitcast.59), calls=%async_computation | async-start | bytes 2097152 | tf_op jit(solution)/shard_map/all_to_all | solution.py:54
  244.3 0.2 all-gather.20.cloned.1.call-start
  244.5 0.0 copy-start.1
  244.5 4.0 %bitcast_add_fusion = f32[1024,512]{0,1:T(8,128)S(1)} fusion(f32[1024,512]{0,1:T(8,128)} %copy.14, bf16[1024,512]{1,0:T(8,128)(2,1)} %bitcast.5, bf16[1024,1024]{1,0:T(8,128)(2,1)} %all-gather.10.cloned.1.call-done), kind=kOutput, calls=%fused_computation | convolution fusion | flops 1076363264 | bytes 7340032 | tf_op jit(solution)/shard_map/dot_general | solution.py:17
  248.5 0.0 all-gather.18.cloned.1.call-done
  248.5 0.0 copy-done.1
  248.5 5.6 %subtract_convert_fusion = bf16[512,1024]{1,0:T(8,128)(2,1)} fusion(bf16[512,1024]{1,0:T(8,128)(2,1)S(1)} %copy-done.1, bf16[1024,1024]{1,0:T(8,128)(2,1)} %all-gather.18.cloned.1.call-done), kind=kOutput, calls=%fused_computation.5 | convolution fusion | flops 2151153664 | bytes 4194304 | tf_op jit(solution)/shard_map/dot_general | solution.py:92
  254.1 0.0 all-gather.20.cloned.1.call-update
  254.1 3.3 all-to-all-done
  257.4 5.1 %convolution_convert_fusion = bf16[512,1024]{1,0:T(8,128)(2,1)S(1)} fusion(bf16[1024,1024]{1,0:T(8,128)(2,1)} %all-gather.10.cloned.1.call-done, f32[1024,512]{0,1:T(8,128)S(1)} %bitcast_add_fusion, bf16[1024,512]{1,0:T(8,128)(2,1)} %bitcast.2), kind=kOutput, calls=%fused_computation.19 | convolution fusion | flops 2150105088 | bytes 6291456 | tf_op jit(solution)/shard_map/dot_general | solution.py:60
  262.5 1.1 copy.24
  263.5 3.6 %all-to-all-start.2 = ((bf16[2,512,512]{1,2,0:T(8,128)(2,1)}), bf16[2,512,512]{1,2,0:T(8,128)(2,1)S(1)}, u32[]{:S(2)}, u32[]{:S(2)}) async-start(bf16[2,512,512]{1,2,0:T(8,128)(2,1)} %bitcast.57), calls=%async_computation.2 | async-start | bytes 2097152 | tf_op jit(solution)/shard_map/all_to_all | solution.py:61
  267.1 1.8 copy.17
  268.9 22.7 %all-to-all-done.2 = bf16[2,512,512]{1,2,0:T(8,128)(2,1)S(1)} async-done(((bf16[2,512,512]{1,2,0:T(8,128)(2,1)}), bf16[2,512,512]{1,2,0:T(8,128)(2,1)S(1)}, u32[]{:S(2)}, u32[]{:S(2)}) %all-to-all-start.2) | async-done | bytes 1048608 | tf_op jit(solution)/shard_map/all_to_all | solution.py:61
  291.7 0.0 copy-start.5
  291.7 4.0 %multiply_convert_fusion.4 = bf16[512,1024]{1,0:T(8,128)(2,1)} fusion(bf16[512,1024]{0,1:T(8,128)(2,1)S(1)} %bitcast.60, bf16[1024,1024]{1,0:T(8,128)(2,1)} %all-gather.8.cloned.1.call-done), kind=kOutput, calls=%fused_computation.17 | convolution fusion | flops 1074790400 | bytes 4194304 | tf_op jit(solution)/shard_map/dot_general | solution.py:23
  295.6 0.0 copy-start.6
  295.6 0.0 all-gather.16.cloned.1.call-done
  295.6 0.0 copy-done.5
  295.6 6.0 %multiply_subtract_fusion.1 = f32[512,1024]{1,0:T(8,128)} fusion(bf16[512,1024]{1,0:T(8,128)(2,1)S(1)} %copy-done.5, bf16[1024,1024]{1,0:T(8,128)(2,1)} %all-gather.16.cloned.1.call-done), kind=kOutput, calls=%fused_computation.10 | convolution fusion | flops 2150629376 | bytes 5242880 | tf_op jit(solution)/shard_map/dot_general | solution.py:89
  301.6 25.5 %all-gather.20.cloned.1.call-done = bf16[1024,1024]{1,0:T(8,128)(2,1)} async-done(((bf16[512,1024]{1,0:T(8,128)(2,1)}), bf16[1024,1024]{1,0:T(8,128)(2,1)}) %all-gather.20.cloned.1.call-update) | async-done | bytes 2097168 | tf_op jit(solution)/shard_map/all_gather | solution.py:85
  327.1 0.0 copy-done.6
  327.1 5.9 %multiply_subtract_fusion = f32[512,1024]{1,0:T(8,128)} fusion(bf16[512,1024]{1,0:T(8,128)(2,1)S(1)} %copy-done.6, bf16[1024,1024]{1,0:T(8,128)(2,1)} %all-gather.20.cloned.1.call-done), kind=kOutput, calls=%fused_computation.3 | convolution fusion | flops 2150629376 | bytes 5242880 | tf_op jit(solution)/shard_map/dot_general | solution.py:92
  (2 shorter events, 0.0 us)
Async XLA Ops:
  7.2 2.9 copy-start.4
  7.2 83.5 %all-gather.10.cloned.1.call-start = ((), (), s32[]{:S(2)}) async-start(), calls=%async_computation.4 | async-start | bytes 3145728 | tf_op jit(solution)/shard_map/all_gather | solution.py:43
  10.0 108.0 %all-gather.12.cloned.1.call-start = ((), (), s32[]{:S(2)}) async-start(), calls=%async_computation.5 | async-start | bytes 3145728 | tf_op jit(solution)/shard_map/all_gather | solution.py:35
  87.7 30.4 %copy-start = (bf16[512,1024]{1,0:T(8,128)(2,1)S(1)}, bf16[512,1024]{1,0:T(8,128)(2,1)}, u32[]{:S(2)}) copy-start(bf16[512,1024]{1,0:T(8,128)(2,1)} %all-reduce.2) | copy-start | bytes 3145732
  87.7 65.6 %all-gather.8.cloned.1.call-start = ((), (), s32[]{:S(2)}) async-start(), calls=%async_computation.3 | async-start | bytes 3145728 | tf_op jit(solution)/shard_map/all_gather | solution.py:44
  90.6 109.2 %all-gather.14.cloned.1.call-start = ((), (), s32[]{:S(2)}) async-start(), calls=%async_computation.6 | async-start | bytes 3145728 | tf_op jit(solution)/shard_map/all_gather | solution.py:84
  166.5 82.0 %all-gather.18.cloned.1.call-start = ((), (), s32[]{:S(2)}) async-start(), calls=%async_computation.8 | async-start | bytes 3145728 | tf_op jit(solution)/shard_map/all_gather | solution.py:85
  166.5 33.2 %copy-start.2 = (bf16[512,1024]{1,0:T(8,128)(2,1)S(1)}, bf16[512,1024]{1,0:T(8,128)(2,1)}, u32[]{:S(2)}) copy-start(bf16[512,1024]{1,0:T(8,128)(2,1)} %divide_convert_fusion.1) | copy-start | bytes 3145732
  169.5 126.2 %all-gather.16.cloned.1.call-start = ((), (), s32[]{:S(2)}) async-start(), calls=%async_computation.7 | async-start | bytes 3145728 | tf_op jit(solution)/shard_map/all_gather | solution.py:84
  208.3 5.6 %copy-start.3 = (f32[1024,512]{1,0:T(8,128)S(1)}, f32[1024,512]{1,0:T(8,128)}, u32[]{:S(2)}) copy-start(f32[1024,512]{1,0:T(8,128)} %param.9) | copy-start | bytes 6291460
  209.3 30.5 %all-to-all-start.1 = ((bf16[512,2,512]{2,0,1:T(8,128)(2,1)}), bf16[512,2,512]{2,0,1:T(8,128)(2,1)}, u32[]{:S(2)}, u32[]{:S(2)}) async-start(bf16[512,2,512]{2,0,1:T(8,128)(2,1)} %bitcast.58), calls=%async_computation.1 | async-start | bytes 2097152 | tf_op jit(solution)/shard_map/all_to_all | solution.py:53
  239.8 17.6 %all-to-all-start = ((bf16[512,2,512]{2,0,1:T(8,128)(2,1)}), bf16[512,2,512]{2,0,1:T(8,128)(2,1)}, u32[]{:S(2)}, u32[]{:S(2)}) async-start(bf16[512,2,512]{2,0,1:T(8,128)(2,1)} %bitcast.59), calls=%async_computation | async-start | bytes 2097152 | tf_op jit(solution)/shard_map/all_to_all | solution.py:54
  244.3 82.9 %all-gather.20.cloned.1.call-start = ((), (), s32[]{:S(2)}) async-start(), calls=%async_computation.9 | async-start | bytes 3145728 | tf_op jit(solution)/shard_map/all_gather | solution.py:85
  244.5 4.0 %copy-start.1 = (bf16[512,1024]{1,0:T(8,128)(2,1)S(1)}, bf16[512,1024]{1,0:T(8,128)(2,1)}, u32[]{:S(2)}) copy-start(bf16[512,1024]{1,0:T(8,128)(2,1)} %divide_convert_fusion) | copy-start | bytes 3145732
  263.5 28.1 %all-to-all-start.2 = ((bf16[2,512,512]{1,2,0:T(8,128)(2,1)}), bf16[2,512,512]{1,2,0:T(8,128)(2,1)S(1)}, u32[]{:S(2)}, u32[]{:S(2)}) async-start(bf16[2,512,512]{1,2,0:T(8,128)(2,1)} %bitcast.57), calls=%async_computation.2 | async-start | bytes 2097152 | tf_op jit(solution)/shard_map/all_to_all | solution.py:61
  291.7 4.0 %copy-start.5 = (bf16[512,1024]{1,0:T(8,128)(2,1)S(1)}, bf16[512,1024]{1,0:T(8,128)(2,1)}, u32[]{:S(2)}) copy-start(bf16[512,1024]{1,0:T(8,128)(2,1)} %subtract_convert_fusion.1) | copy-start | bytes 3145732
  295.6 31.5 %copy-start.6 = (bf16[512,1024]{1,0:T(8,128)(2,1)S(1)}, bf16[512,1024]{1,0:T(8,128)(2,1)}, u32[]{:S(2)}) copy-start(bf16[512,1024]{1,0:T(8,128)(2,1)} %subtract_convert_fusion) | copy-start | bytes 3145732
Sparse Core Ops, SparseCore 0:
  10.2 35.8 all-gather.9
  87.8 30.1 all-gather.11
  120.1 33.1 all-gather.7
  166.6 33.1 all-gather.13
  201.7 44.3 all-gather.17
  247.5 44.0 all-gather.15
  293.7 33.3 all-gather.19
where the time goes:
time: 340 us
  waiting for transfers between devices  159 us (47%)
  blocking collectives  82.3 us (24%)
  matrix products  54.7 us (16%)
  between operations  14.3 us (4%)
  starting transfers between devices  13 us (4%)
  other arithmetic  10 us (3%)
  local copies, waits for them, and re-layouts  6.81 us (2%)
    psum x1, blocking collectives, body(): summed = lax.psum(local_sum, 'dp')  77.3 us
    all_gather x2, waiting for transfers between devices, body(): lax.all_gather(left_current, 'shard', axis=0, tiled=True)  30.2 us
    all_gather x1, waiting for transfers between devices, body(): lax.all_gather(basis_right.astype(jnp.bfloat16), 'shard', axis=0, tiled=T...  29.9 us
    all_gather x1, waiting for transfers between devices, body(): gradient = lax.all_gather(grad_rows, 'shard', axis=0, tiled=True)  27.4 us
    all_gather x2, waiting for transfers between devices, body(): lax.all_gather(right_current, 'shard', axis=0, tiled=True)  25.5 us
    all_to_all x1, waiting for transfers between devices, body(): lax.all_to_all(turned_back, 'shard', split_axis=0, concat_axis=1, tiled=T...  22.7 us
    all_to_all x1, waiting for transfers between devices, body(): lax.all_to_all(grad_turned, 'shard', split_axis=1, concat_axis=0, tiled=T...  19.6 us
    dot_general x2, matrix products, body(): jnp.dot(left_gram, left_full, preferred_element_type=jnp.float32)  11.7 us
  transfers between devices with their start and end apart: 10, of which 7 were waited for; matrix products, arithmetic and copies ran while one was open for 16% of the time, Pallas kernels for 0%

commit v1 on v0

v1 whole, which is shorter than its diff:
```python
import functools

import jax
import jax.numpy as jnp
from jax import lax
from jax.experimental import pallas as pl
from jax.experimental.pallas import tpu as pltpu
from jax.sharding import PartitionSpec as P

NS_ITERS = 2


BETA_ONE = 0.9
BETA_TWO = 0.9
BETA_STAT = 0.95
EPSILON = 1e-08
NORM_EPS = 1e-06
HALF = jnp.bfloat16
FULL = jnp.float32
VMEM = pl.BlockSpec(memory_space=pltpu.VMEM)
ANY = pl.BlockSpec(memory_space=pl.ANY)
SMEM = pl.BlockSpec(memory_space=pltpu.SMEM)


def matmul(left_mat, right_mat, left_dim=1, right_dim=0):
    return lax.dot_general(
        left_mat,
        right_mat,
        (((left_dim,), (right_dim,)), ((), ())),
        preferred_element_type=FULL,
    )


def shaped(shape, dtype):
    return jax.ShapeDtypeStruct(shape, dtype)


def tile(index, size):
    return pl.ds(pl.multiple_of(index * size, size), size)


def call(kernel, outs, operands, specs, scratch=(), flops=0, moved=0):
    return pl.pallas_call(
        kernel,
        out_shape=outs,
        in_specs=specs,
        out_specs=[VMEM] * len(outs),
        scratch_shapes=list(scratch),
        compiler_params=pltpu.CompilerParams(vmem_limit_bytes=50 * 2**20),
        cost_estimate=pl.CostEstimate(flops=flops, bytes_accessed=moved, transcendentals=0),
    )(*operands)


def state_parts_kernel(where, left, right, stat_left, stat_right, bases, stats):
    half = left.shape[0] // 2
    rows = left.shape[0]
    near = tile(where[0], rows)
    mine = tile(where[1], half)
    bases[:half] = left[mine].astype(HALF)
    bases[half:] = right[mine].astype(HALF)
    stats[:, :rows] = stat_left[mine, near]
    stats[:, rows:] = stat_right[mine, near]


def first_sum_kernel(where, group, came, kept, sent):
    size = kept.shape[0]
    core, x = where[1], where[2]
    kept[...] = group[0, tile(core * 2 + x, size)].astype(FULL) + came[tile(x, size)].astype(FULL)
    sent[...] = group[0, tile(core * 2 + 1 - x, size)].astype(FULL) + came[
        tile(1 - x, size)
    ].astype(FULL)


def second_sum_kernel(where, kept, came, own, *sent):
    size = own.shape[0]
    z = where[3]
    own[...] = kept[tile(z, size)] + came[tile(z, size)]
    for k, out in enumerate(sent):
        there = tile(z ^ (k + 1), size)
        out[...] = kept[there] + came[there]


def third_sum_kernel(own, one, two, three, out):
    out[...] = ((own[...] + one[...]) + (two[...] + three[...])).astype(HALF)


def joined_kernel(where, *refs):
    out = refs[-1]
    z = where[3]
    size = refs[0].shape[0]
    for k, part in enumerate(refs[:-1]):
        out[tile(z ^ k, size)] = part[...]


def place_basis(where, out, own, mine, theirs, begin, natural):
    rows = own.shape[0]
    half = rows // 2
    position, core = where[0], where[1]
    first = position if natural else 0
    out[tile(first, rows)] = own[...].astype(HALF)
    other = (1 - first) * 2
    out[tile(other + core, half)] = mine[begin : begin + half]
    out[tile(other + 1 - core, half)] = theirs[begin : begin + half]


def place_stat(where, out, own, mine, theirs, begin, natural):
    rows = own.shape[0]
    half = rows // 2
    position, core = where[0], where[1]
    first = position if natural else 0
    here, there = tile(first, rows), tile(1 - first, rows)
    out[here, here] = own[:, tile(position, rows)]
    cross = own[:, tile(1 - position, rows)]
    out[here, there] = cross
    out[there, here] = cross.T
    other = (1 - first) * 2
    out[tile(other + core, half), there] = mine[:, begin : begin + rows]
    out[tile(other + 1 - core, half), there] = theirs[:, begin : begin + rows]


def left_state_kernel(where, basis, bmine, btheirs, stat, smine, stheirs, rot, turned, full):
    place_basis(where, rot, basis, bmine, btheirs, 0, False)
    place_stat(where, full, stat, smine, stheirs, 0, False)
    turned[...] = rot[...].T


def right_state_kernel(where, basis, bmine, btheirs, stat, smine, stheirs, rot, near, full):
    rows = basis.shape[0]
    place_basis(where, rot, basis, bmine, btheirs, rows // 2, True)
    place_stat(where, full, stat, smine, stheirs, rows, True)
    near[:, :rows] = rot[:, tile(where[0], rows)]
    near[:, rows:] = rot[:, tile(1 - where[0], rows)]


def moment_kernel(where, moment, near, *refs):
    parts, (gradient, ours, others, sem) = refs[:-4], refs[-4:]
    core, x = where[1], where[2]
    size = parts[0].shape[0]
    rows = moment.shape[0]
    copies = []
    for place, part in enumerate(parts):
        block = (
            (place // 4) * 4 + (core ^ (place % 4 // 2)) * 2 + (x ^ (place % 2))
        )
        copies.append(
            pltpu.make_async_copy(part, gradient.at[tile(block, size)], sem.at[place])
        )
    for copy in copies:
        copy.start()
    for copy in copies:
        copy.wait()
    step = rows // 2

    @pl.loop(0, 2)
    def _(i):
        here = tile(i, step)
        half = (
            BETA_ONE * moment[here] + (1.0 - BETA_ONE) * gradient[here].astype(FULL)
        ).astype(HALF)
        ours[here] = matmul(half, near[:, :rows]).astype(HALF)
        others[here] = matmul(half, near[:, rows:]).astype(HALF)


def adam_kernel(gradient, near, rot, turned, mine, came, second, new, kept, sent, block, scaled):
    width = gradient.shape[0]
    rows = mine.shape[0]
    step = width // 4

    @pl.loop(0, 4)
    def _(i):
        here = tile(i, step)
        block[here] = matmul(gradient[here], near[:, :rows]).astype(HALF)

    @pl.loop(0, 4)
    def _(i):
        here = tile(i, step)
        grad_rot = matmul(turned[here], block[...]) * (1.0 / width)
        moment_rot = (
            matmul(turned[here, :rows], mine[...]) + matmul(turned[here, rows:], came[...])
        ) * (1.0 / width)
        value = BETA_TWO * second[here] + (1.0 - BETA_TWO) * grad_rot * grad_rot
        new[here] = value
        scaled[here] = (moment_rot / (jnp.sqrt(value) + EPSILON)).astype(HALF)

    @pl.loop(0, rows // step)
    def _(i):
        here = tile(i, step)
        kept[here] = matmul(rot[here], scaled[...]).astype(HALF)
        sent[here] = matmul(rot[tile(i + rows // step, step)], scaled[...]).astype(HALF)


def update_kernel(mine, came, near, out):
    rows, width = out.shape
    step = rows // 2

    @pl.loop(0, 2)
    def _(i):
        here = tile(i, step)
        total = matmul(mine[here], near[:, :rows], 1, 1) + matmul(
            came[here], near[:, rows:], 1, 1
        )
        out[here] = (total * (1.0 / width)).astype(HALF)


def refresh_kernel(natural, where, gradient, rot, stat, out, stat_in, turned, half, product, sem):
    width = gradient.shape[0]
    rows = out.shape[0]
    steps = 4
    step = width // steps
    copies = [
        pltpu.make_async_copy(stat.at[tile(i, step)], stat_in.at[tile(i, step)], sem.at[i])
        for i in range(steps)
    ]
    for copy in copies:
        copy.start()
    if natural:

        @pl.loop(0, steps)
        def _(i):
            turned[:, tile(i, step)] = gradient[tile(i, step)].T

        source, dim = turned, 0
    else:
        source, dim = gradient, 1
    for copy in copies:
        copy.wait()

    @pl.loop(0, steps)
    def _(i):
        here = tile(i, step)
        grads = matmul(source[here], gradient[...], 1, dim)
        half[here] = (BETA_STAT * stat_in[here] + (1.0 - BETA_STAT) * grads).astype(HALF)

    def power(i, total):
        here = tile(i, step)
        value = matmul(half[here], rot[...])
        product[here] = value
        return total + jnp.sum(value * value, axis=0, keepdims=True)

    total = lax.fori_loop(0, steps, power, jnp.zeros((1, width), FULL))
    scale = lax.rsqrt(total * (1.0 / width) + NORM_EPS)

    @pl.loop(0, steps)
    def _(i):
        here = tile(i, step)
        half[here] = (product[here] * scale).astype(HALF)

    def improved(current, here):
        gram = (matmul(current[here], current[...], 1, 1) * (1.0 / width)).astype(HALF)
        return 1.5 * current[here].astype(FULL) - 0.5 * matmul(gram, current[...])

    current, following = half, turned
    for _ in range(NS_ITERS - 1):

        @pl.loop(0, steps)
        def _(i):
            here = tile(i, step)
            following[here] = improved(current, here).astype(HALF)

        current, following = following, current

    first = where[0] * (rows // step) if natural else 0

    @pl.loop(0, rows // step)
    def _(i):
        out[tile(i, step)] = improved(current, tile(first + i, step))


def fast_body(group_grads, moment, second, stat_left, stat_right, basis_left, basis_right):
    position = lax.axis_index("shard")
    member = lax.axis_index("dp")
    rows, width = moment.shape
    half = rows // 2
    quarter = rows // 4
    chunk = rows // 16
    core, x, z = member & 1, (member >> 1) & 1, member >> 2
    where = jnp.stack([position, core, x, z]).astype(jnp.int32)
    unit = 2 * width**3

    def dp_swap(value, distance):
        return lax.ppermute(value, "dp", [(i, i ^ distance) for i in range(16)])

    def shard_swap(value):
        return lax.ppermute(value, "shard", [(0, 1), (1, 0)])

    def cross_swap(value):
        pairs = [(i, i ^ 5) for i in range(32)]
        return lax.ppermute(value, ("dp", "shard"), pairs)

    bases_sent, stats_sent = call(
        state_parts_kernel,
        [shaped((rows, width), HALF), shaped((half, width), FULL)],
        (where, basis_left, basis_right, stat_left, stat_right),
        [SMEM] + [VMEM] * 4,
        moved=2**23,
    )
    bases_mine = shard_swap(bases_sent)
    stats_mine = shard_swap(stats_sent)

    raw = lax.dynamic_slice_in_dim(group_grads[0], (1 - core) * half, half, 0)
    came = dp_swap(raw, 1)
    kept, sent = call(
        first_sum_kernel,
        [shaped((quarter, width), FULL)] * 2,
        (where, group_grads, came),
        [SMEM, VMEM, VMEM],
        moved=2**21,
    )
    came = dp_swap(sent, 2)
    own, *sent = call(
        second_sum_kernel,
        [shaped((chunk, width), FULL)] * 4,
        (where, kept, came),
        [SMEM, VMEM, VMEM],
        moved=2**20,
    )
    pieces = [dp_swap(value, 4 * (k + 1)) for k, value in enumerate(sent)]
    (piece,) = call(
        third_sum_kernel, [shaped((chunk, width), HALF)], (own, *pieces), [VMEM] * 4, moved=2**19
    )
    pieces = [piece] + [dp_swap(piece, 4 * k) for k in (1, 2, 3)]
    (part,) = call(
        joined_kernel, [shaped((quarter, width), HALF)], (where, *pieces), [SMEM] + [VMEM] * 4,
        moved=2**19,
    )
    parts = [part, dp_swap(part, 2), shard_swap(part), cross_swap(part)]
    swapped = [dp_swap(value, 1) for value in parts]

    bases_theirs = dp_swap(bases_mine, 1)
    stats_theirs = dp_swap(stats_mine, 1)
    bases = (bases_mine, bases_theirs)
    stats = (stats_mine, stats_theirs)
    state_outs = [
        shaped((width, width), HALF),
        shaped((width, width), HALF),
        shaped((width, width), FULL),
    ]
    left_rot, left_turned, left_stat = call(
        left_state_kernel,
        state_outs,
        (where, basis_left, *bases, stat_left, *stats),
        [SMEM] + [VMEM] * 6,
        moved=2**24,
    )
    right_rot, right_near, right_stat = call(
        right_state_kernel,
        state_outs,
        (where, basis_right, *bases, stat_right, *stats),
        [SMEM] + [VMEM] * 6,
        moved=2**24,
    )

    ordered = [parts[0], parts[1], swapped[0], swapped[1], parts[2], parts[3], swapped[2], swapped[3]]
    gradient, moment_mine, moment_sent = call(
        moment_kernel,
        [shaped((width, width), HALF)] + [shaped((rows, rows), HALF)] * 2,
        (where, moment, right_near, *ordered),
        [SMEM, VMEM, VMEM] + [ANY] * 8,
        [pltpu.SemaphoreType.DMA((8,))],
        flops=unit // 2,
        moved=2**23,
    )
    moment_came = shard_swap(moment_sent)

    def refreshed(natural, rot, stat):
        (out,) = call(
            functools.partial(refresh_kernel, natural),
            [shaped((rows, width), FULL)],
            (where, gradient, rot, stat),
            [SMEM, VMEM, VMEM, ANY],
            [
                pltpu.VMEM((width, width), FULL),
                pltpu.VMEM((width, width), HALF),
                pltpu.VMEM((width, width), HALF),
                pltpu.VMEM((width, width), FULL),
                pltpu.SemaphoreType.DMA((4,)),
            ],
            flops=5 * unit,
            moved=2**23,
        )
        return out

    left_new = refreshed(False, left_rot, left_stat)
    second_new, back_mine, back_sent = call(
        adam_kernel,
        [shaped((width, rows), FULL)] + [shaped((rows, rows), HALF)] * 2,
        (gradient, right_near, left_rot, left_turned, moment_mine, moment_came, second),
        [VMEM] * 7,
        [pltpu.VMEM((width, rows), HALF)] * 2,
        flops=2 * unit,
        moved=2**23,
    )
    back_came = shard_swap(back_sent)
    right_new = refreshed(True, right_rot, right_stat)
    (update,) = call(
        update_kernel,
        [shaped((rows, width), HALF)],
        (back_mine, back_came, right_near),
        [VMEM] * 3,
        flops=unit // 2,
        moved=2**22,
    )
    return (update, second_new, left_new, right_new)


def make_plain_body(n_dp, n_shard):
    def swap(value, axis, distance):
        size = n_dp if axis == "dp" else n_shard
        return lax.ppermute(value, axis, [(i, i ^ distance) for i in range(size)])

    dp_bits = []
    bit = 1
    while bit < n_dp:
        dp_bits.append(bit)
        bit *= 2

    def ordered(first_is_low, own, other, dim):
        return jnp.where(
            first_is_low,
            jnp.concatenate([own, other], dim),
            jnp.concatenate([other, own], dim),
        )

    def body(group_grads, moment, second, stat_left, stat_right, basis_left, basis_right):
        position = lax.axis_index("shard")
        member = lax.axis_index("dp")
        rows, width = moment.shape
        core = member & 1
        half = rows // 2

        def near_columns(value):
            blocks = [
                lax.dynamic_slice_in_dim(value, (position ^ k) * rows, rows, 1)
                for k in range(n_shard)
            ]
            return jnp.concatenate(blocks, 1)

        def fetch(value, distance):
            size = value.shape[0] // 2
            part = lax.dynamic_slice_in_dim(value, core * size, size, 0)
            part = swap(part, "shard", distance)
            other = swap(part, "dp", 1)
            return ordered(core == 0, part, other, 0)

        left_own = basis_left.astype(jnp.bfloat16)
        right_own = basis_right.astype(jnp.bfloat16)
        left_rot = jnp.concatenate([left_own] + [fetch(left_own, k) for k in range(1, n_shard)], 0)
        right_rot = jnp.concatenate(
            [right_own] + [fetch(right_own, k) for k in range(1, n_shard)], 0
        )

        def whole_stat(stat):
            own = near_columns(stat)
            blocks = [own[:, b * rows : (b + 1) * rows] for b in range(n_shard)]
            bands = [own]
            for k in range(1, n_shard):
                others = [b for b in range(n_shard) if b != k]
                sent = jnp.concatenate([blocks[b] for b in others], 1).astype(jnp.bfloat16)
                came = fetch(sent, k).astype(jnp.float32)
                band = [None] * n_shard
                band[0] = blocks[k].T
                for place, b in enumerate(others):
                    band[k ^ b] = came[:, place * rows : (place + 1) * rows]
                bands.append(jnp.concatenate(band, 1))
            return jnp.concatenate(bands, 0)

        stat_left_full = whole_stat(stat_left)
        stat_right_full = whole_stat(stat_right)

        part = group_grads[0]
        for bit in dp_bits:
            size = part.shape[0] // 2
            high = (member & bit) // bit
            kept = lax.dynamic_slice_in_dim(part, high * size, size, 0)
            sent = lax.dynamic_slice_in_dim(part, (1 - high) * size, size, 0)
            part = kept.astype(jnp.float32) + swap(sent, "dp", bit).astype(jnp.float32)
        chunk = part.astype(jnp.bfloat16)[None]
        chunk = jnp.concatenate([chunk] + [swap(chunk, "shard", k) for k in range(1, n_shard)], 0)
        for bit in reversed(dp_bits):
            chunk = ordered((member & bit) == 0, chunk, swap(chunk, "dp", bit), 1)
        gradient = near_columns(chunk.reshape(width, width))

        grad_rows = gradient[:rows].astype(jnp.float32)
        moment_half = (
            BETA_ONE * near_columns(moment) + (1.0 - BETA_ONE) * grad_rows
        ).astype(jnp.bfloat16)
        near_rot = near_columns(right_rot)
        moment_turned = matmul(moment_half, near_rot).astype(jnp.bfloat16)
        moment_block = jnp.concatenate(
            [moment_turned[:, :rows]]
            + [
                swap(moment_turned[:, k * rows : (k + 1) * rows], "shard", k)
                for k in range(1, n_shard)
            ],
            0,
        )
        grad_block = matmul(gradient, near_rot[:, :rows]).astype(jnp.bfloat16)
        grad_rot = matmul(left_rot, grad_block, 0) / width
        moment_rot = matmul(left_rot, moment_block, 0) / width
        second_new = BETA_TWO * second + (1.0 - BETA_TWO) * grad_rot * grad_rot
        scaled = (moment_rot / (jnp.sqrt(second_new) + EPSILON)).astype(jnp.bfloat16)
        turned_back = matmul(left_rot, scaled).astype(jnp.bfloat16)
        back_rows = jnp.concatenate(
            [turned_back[:rows]]
            + [
                swap(turned_back[k * rows : (k + 1) * rows], "shard", k)
                for k in range(1, n_shard)
            ],
            1,
        )
        update = (near_columns(matmul(back_rows, near_rot, 1, 1)) / width).astype(jnp.bfloat16)

        def refreshed(stat, product_of_grads, rot):
            stat_new = BETA_STAT * stat + (1.0 - BETA_STAT) * product_of_grads
            product = matmul(stat_new.astype(jnp.bfloat16), rot)
            start = product / jnp.sqrt(jnp.sum(product * product, axis=0) / width + NORM_EPS)
            current = start.astype(jnp.bfloat16)
            for iteration in range(NS_ITERS):
                kept = width if iteration + 1 < NS_ITERS else rows
                gram = (matmul(current[:kept], current, 1, 1) / width).astype(jnp.bfloat16)
                result = 1.5 * current[:kept].astype(jnp.float32) - 0.5 * matmul(gram, current)
                current = result.astype(jnp.bfloat16)
            return result

        left_new = refreshed(stat_left_full, matmul(gradient, gradient, 1, 1), left_rot)
        right_new = refreshed(stat_right_full, matmul(gradient, gradient, 0, 0), right_rot)
        return (update, second_new, left_new, right_new)

    return body


def solution(mesh):
    n_dp, n_shard = mesh.shape["dp"], mesh.shape["shard"]
    body = fast_body if (n_dp, n_shard) == (16, 2) else make_plain_body(n_dp, n_shard)
    return jax.shard_map(
        body,
        mesh=mesh,
        in_specs=(
            P("dp", "shard", None),
            P("shard", None),
            P(None, "shard"),
            P("shard", None),
            P("shard", None),
            P("shard", None),
            P("shard", None),
        ),
        out_specs=(P("shard", None), P(None, "shard"), P("shard", None), P("shard", None)),
        check_vma=False,
    )
```

time: 340 us -> 166 us (0.49)
  waiting for transfers between devices: 159 us -> 67.6 us
  blocking collectives: 82.3 us -> 0 us
  Pallas kernels: 0 us -> 75.7 us
  matrix products: 54.7 us -> 0 us
  between operations: 14.3 us -> 0.78 us
  other arithmetic: 10 us -> 0.08 us
  starting transfers between devices: 13 us -> 21 us
  local copies, waits for them, and re-layouts: 6.81 us -> 1.02 us
    all_gather x7 -> x0, waiting for transfers between devices: 113 us -> none  [the longest x2 30.2 us: body(): lax.all_gather(left_current, 'shard', axis=0, tiled=True)]
    psum x2 -> x0, blocking collectives: 82.3 us -> none  [the longest x1 77.3 us: body(): summed = lax.psum(local_sum, 'dp')]
    pallas_call x0 -> x12, Pallas kernels: none -> 75.7 us  [call(): pl.pallas_call(kernel, out_shape=outs, in_specs=specs, out_specs=[VMEM] *...]
    ppermute x0 -> x21, waiting for transfers between devices: none -> 67.6 us  [the longest x5 46.9 us: shard_swap(): return lax.ppermute(value, 'shard', [(0, 1), (1, 0)])]
    dot_general x11 -> x0, matrix products: 54.7 us -> none  [the longest x2 11.7 us: body(): jnp.dot(left_gram, left_full, preferred_element_type=jnp.float32)]
    all_to_all x3 -> x0, waiting for transfers between devices: 45.6 us -> none  [the longest x1 22.7 us: body(): lax.all_to_all(turned_back, 'shard', split_axis=0, concat_axis=1, tiled=T...]
    ppermute x0 -> x21, starting transfers between devices: none -> 21 us  [the longest x15 13.9 us: dp_swap(): return lax.ppermute(value, 'dp', [(i, i ^ distance) for i in range(16)])]
    all_to_all x3 -> x0, starting transfers between devices: 12.5 us -> none  [the longest x1 4.55 us: body(): lax.all_to_all(grad_turned, 'shard', split_axis=1, concat_axis=0, tiled=T...]
  transfers between devices with their start and end apart: 10 -> 21, of which waited for: 7 -> 9; matrix products, arithmetic and copies ran while one was open for 16% -> 0% of each run, Pallas kernels for 0% -> 32%
where the time goes in v1:
time: 166 us
  Pallas kernels  75.7 us (46%)
  waiting for transfers between devices  67.6 us (41%)
  starting transfers between devices  21 us (13%)
    pallas_call x12, Pallas kernels, call(): pl.pallas_call(kernel, out_shape=outs, in_specs=specs, out_specs=[VMEM] *...  75.7 us
    ppermute x5, waiting for transfers between devices, shard_swap(): return lax.ppermute(value, 'shard', [(0, 1), (1, 0)])  46.9 us
    ppermute x15, waiting for transfers between devices, dp_swap(): return lax.ppermute(value, 'dp', [(i, i ^ distance) for i in range(16)])  20.7 us
    ppermute x15, starting transfers between devices, dp_swap(): return lax.ppermute(value, 'dp', [(i, i ^ distance) for i in range(16)])  13.9 us
    ppermute x5, starting transfers between devices, shard_swap(): return lax.ppermute(value, 'shard', [(0, 1), (1, 0)])  6.62 us
  transfers between devices with their start and end apart: 21, of which 9 were waited for; matrix products, arithmetic and copies ran while one was open for 0% of the time, Pallas kernels for 32%

profile of v1, /device:TPU:0, one launch (start us, length us, event | category | flops | bytes accessed | tf_op | source)
XLA Modules:
  0.0 166.2 jit_solution(13274336888619398344)
XLA Ops:
  0.6 0.1 pad_add_fusion.where
  0.7 0.0 copy-start.1
  0.7 5.0 %shard_map.102 = (bf16[512,1024]{1,0:T(8,128)(2,1)}, f32[256,1024]{1,0:T(8,128)}) custom-call(s32[4]{0:T(128)S(1)} %pad_add_fusion.where, f32[512,1024]{1,0:T(8,128)} %basis.3, f32[512,1024]{1,0:T(8,128)} %basis.2, f32[512,1024]{1,0:T(8,128)} %stat.3, f32[512,1024]{1,0:T(8,128)} %stat.2), custom_call_target="tpu_custom_call" | custom-call | bytes 8388608 | tf_op jit(solution)/shard_map/pallas_call | solution.py:43
  5.8 3.0 %collective-permute-start = (bf16[512,1024]{1,0:T(8,128)(2,1)}, bf16[512,1024]{1,0:T(8,128)(2,1)S(1)}, u32[]{:S(2)}, u32[]{:S(2)}) collective-permute-start(bf16[512,1024]{1,0:T(8,128)(2,1)} %get-tuple-element.24), channel_id=1, source_target_pairs={{0,1},{1,0},{2,3},{3,2},{4,5},{5,4},{6,7},{7,6},{8,9},{9,8},{10,11... | collective-permute-start | bytes 3145736 | tf_op jit(solution)/shard_map/ppermute | solution.py:284
  8.7 0.0 collective-permute-start.2
  8.8 0.0 copy-done.1
  8.8 0.1 collective-permute-start.4
  8.9 24.0 %collective-permute-done.bmine = bf16[512,1024]{1,0:T(8,128)(2,1)S(1)} collective-permute-done((bf16[512,1024]{1,0:T(8,128)(2,1)}, bf16[512,1024]{1,0:T(8,128)(2,1)S(1)}, u32[]{:S(2)}, u32[]{:S(2)}) %collective-permute-start) | collective-permute-done | bytes 1048608 | tf_op jit(solution)/shard_map/ppermute | solution.py:284
  32.9 0.0 collective-permute-start.1
  32.9 0.0 collective-permute-done.4.came
  32.9 0.7 shard_map.104
  33.6 2.1 %collective-permute-start.5 = (f32[128,1024]{1,0:T(8,128)S(1)}, f32[128,1024]{1,0:T(8,128)S(1)}, u32[]{:S(2)}, u32[]{:S(2)}) collective-permute-start(f32[128,1024]{1,0:T(8,128)S(1)} %get-tuple-element.28), channel_id=1, source_target_pairs={{0,4},{2,6},{4,0},{6,2},{8,12},{10,14},{12,8},{14,10},{16,20},{18,... | collective-permute-start | bytes 1572872 | tf_op jit(solution)/shard_map/ppermute | solution.py:281
  35.7 18.9 %collective-permute-done.2.smine = f32[256,1024]{1,0:T(8,128)S(1)} collective-permute-done((f32[256,1024]{1,0:T(8,128)}, f32[256,1024]{1,0:T(8,128)S(1)}, u32[]{:S(2)}, u32[]{:S(2)}) %collective-permute-start.2) | collective-permute-done | bytes 1048608 | tf_op jit(solution)/shard_map/ppermute | solution.py:284
  54.6 0.0 collective-permute-start.3
  54.6 0.0 collective-permute-done.5.came
  54.6 0.6 shard_map.105
  55.2 1.9 %collective-permute-start.6 = (f32[32,1024]{1,0:T(8,128)S(1)}, f32[32,1024]{1,0:T(8,128)S(1)}, u32[]{:S(2)}, u32[]{:S(2)}) collective-permute-start(f32[32,1024]{1,0:T(8,128)S(1)} %get-tuple-element.30), channel_id=1, source_target_pairs={{0,8},{2,10},{4,12},{6,14},{8,0},{10,2},{12,4},{14,6},{16,24},{18,... | collective-permute-start | bytes 393224 | tf_op jit(solution)/shard_map/ppermute | solution.py:281
  57.0 2.6 %collective-permute-start.7 = (f32[32,1024]{1,0:T(8,128)S(1)}, f32[32,1024]{1,0:T(8,128)S(1)}, u32[]{:S(2)}, u32[]{:S(2)}) collective-permute-start(f32[32,1024]{1,0:T(8,128)S(1)} %get-tuple-element.31), channel_id=1, source_target_pairs={{0,16},{2,18},{4,20},{6,22},{8,24},{10,26},{12,28},{14,30},{16,0},... | collective-permute-start | bytes 393224 | tf_op jit(solution)/shard_map/ppermute | solution.py:281
  59.6 0.0 collective-permute-start.8
  59.6 3.8 %collective-permute-done.6.one = f32[32,1024]{1,0:T(8,128)S(1)} collective-permute-done((f32[32,1024]{1,0:T(8,128)S(1)}, f32[32,1024]{1,0:T(8,128)S(1)}, u32[]{:S(2)}, u32[]{:S(2)}) %collective-permute-start.6) | collective-permute-done | bytes 131104 | tf_op jit(solution)/shard_map/ppermute | solution.py:281
  63.5 6.5 %collective-permute-done.7.two = f32[32,1024]{1,0:T(8,128)S(1)} collective-permute-done((f32[32,1024]{1,0:T(8,128)S(1)}, f32[32,1024]{1,0:T(8,128)S(1)}, u32[]{:S(2)}, u32[]{:S(2)}) %collective-permute-start.7) | collective-permute-done | bytes 131104 | tf_op jit(solution)/shard_map/ppermute | solution.py:281
  69.9 0.0 collective-permute-done.8.three
  70.0 3.7 %collective-permute-start.10 = (bf16[32,1024]{1,0:T(8,128)(2,1)S(1)}, bf16[32,1024]{1,0:T(8,128)(2,1)S(1)}, u32[]{:S(2)}, u32[]{:S(2)}) collective-permute-start(bf16[32,1024]{1,0:T(8,128)(2,1)S(1)} %shard_map.106.refs_0_), channel_id=1, source_target_pairs={{0,16},{2,18},{4,20},{6,22},{8,24},{10,26},{12,28},{14,30},{16,0},... | collective-permute-start | bytes 196616 | tf_op jit(solution)/shard_map/ppermute | solution.py:281
  73.7 1.4 collective-permute-start.11
  75.1 0.0 collective-permute-start.9
  75.1 3.1 %collective-permute-done.10.refs_2_ = bf16[32,1024]{1,0:T(8,128)(2,1)S(1)} collective-permute-done((bf16[32,1024]{1,0:T(8,128)(2,1)S(1)}, bf16[32,1024]{1,0:T(8,128)(2,1)S(1)}, u32[]{:S(2)}, u32[]{:S(2)}) %collective-permute-start.10) | collective-permute-done | bytes 65568 | tf_op jit(solution)/shard_map/ppermute | solution.py:281
  78.2 1.7 %collective-permute-done.11.refs_3_ = bf16[32,1024]{1,0:T(8,128)(2,1)S(1)} collective-permute-done((bf16[32,1024]{1,0:T(8,128)(2,1)S(1)}, bf16[32,1024]{1,0:T(8,128)(2,1)S(1)}, u32[]{:S(2)}, u32[]{:S(2)}) %collective-permute-start.11) | collective-permute-done | bytes 65568 | tf_op jit(solution)/shard_map/ppermute | solution.py:281
  79.9 0.2 collective-permute-done.9.refs_1_
  80.0 0.6 shard_map.107.refs_0_
  80.6 1.6 collective-permute-start.12
  82.2 1.5 collective-permute-start.15
  83.7 0.5 collective-permute-start.16
  84.2 5.4 %collective-permute-done.12.refs_1_ = bf16[128,1024]{1,0:T(8,128)(2,1)S(1)} collective-permute-done((bf16[128,1024]{1,0:T(8,128)(2,1)S(1)}, bf16[128,1024]{1,0:T(8,128)(2,1)S(1)}, u32[]{:S(2)}, u32[]{:S(2)}) %collective-permute-start.12) | collective-permute-done | bytes 262176 | tf_op jit(solution)/shard_map/ppermute | solution.py:281
  89.6 0.0 collective-permute-start.13
  89.6 4.0 %collective-permute-done.15.refs_4_ = bf16[128,1024]{1,0:T(8,128)(2,1)S(1)} collective-permute-done((bf16[128,1024]{1,0:T(8,128)(2,1)S(1)}, bf16[128,1024]{1,0:T(8,128)(2,1)S(1)}, u32[]{:S(2)}, u32[]{:S(2)}) %collective-permute-start.15) | collective-permute-done | bytes 262176 | tf_op jit(solution)/shard_map/ppermute | solution.py:284
  93.6 0.0 collective-permute-start.14
  93.6 0.0 collective-permute-done.16.refs_5_
  93.6 0.5 collective-permute-start.17
  94.1 0.0 collective-permute-done.1.btheirs
  94.1 0.1 collective-permute-start.18
  94.2 0.0 collective-permute-done.3.stheirs
  94.2 0.0 copy-start.4
  94.2 1.0 copy-done.4
  95.2 6.3 %shard_map.103 = (bf16[1024,1024]{1,0:T(8,128)(2,1)}, bf16[1024,1024]{1,0:T(8,128)(2,1)}, f32[1024,1024]{1,0:T(8,128)}) custom-call(s32[4]{0:T(128)S(1)} %pad_add_fusion.where, f32[512,1024]{1,0:T(8,128)} %basis.2, bf16[512,1024]{1,0:T(8,128)(2,1)S(1)} %collective-permute-done.bmine, bf16[512,1024]{1,0:T(8,128)(2,1)S(1)} %collective-permute-done.1.btheirs, ...), custom_call_target="tpu_custom_call" | custom-call | bytes 16777216 | tf_op jit(solution)/shard_map/pallas_call | solution.py:43
  101.5 0.0 collective-permute-done.13.refs_2_
  101.5 0.0 collective-permute-done.14.refs_3_
  101.5 0.0 collective-permute-done.17.refs_6_
  101.5 0.0 collective-permute-done.18.refs_7_
  101.5 4.7 %shard_map.108 = (bf16[1024,1024]{1,0:T(8,128)(2,1)}, bf16[512,512]{1,0:T(8,128)(2,1)S(1)}, bf16[512,512]{1,0:T(8,128)(2,1)S(1)}) custom-call(s32[4]{0:T(128)S(1)} %pad_add_fusion.where, f32[512,1024]{1,0:T(8,128)} %moment.1, bf16[1024,1024]{1,0:T(8,128)(2,1)} %get-tuple-element.26.near, bf16[128,1024]{1,0:T(8,128)(2,1)S(1)} %shard_map.107.refs_0_, ...), custom_call_target="tpu_custom_call" | custom-call | flops 1073741824 | bytes 8388608 | tf_op jit(solution)/shard_map/pallas_call | solution.py:43
  106.2 0.0 copy-start.2
  106.2 1.6 collective-permute-start.19
  107.8 6.3 %shard_map.109 = (bf16[1024,1024]{1,0:T(8,128)(2,1)}, bf16[1024,1024]{1,0:T(8,128)(2,1)}, f32[1024,1024]{1,0:T(8,128)}) custom-call(s32[4]{0:T(128)S(1)} %pad_add_fusion.where, f32[512,1024]{1,0:T(8,128)} %basis.3, bf16[512,1024]{1,0:T(8,128)(2,1)S(1)} %collective-permute-done.bmine, bf16[512,1024]{1,0:T(8,128)(2,1)S(1)} %collective-permute-done.1.btheirs, ...), custom_call_target="tpu_custom_call" | custom-call | bytes 16777216 | tf_op jit(solution)/shard_map/pallas_call | solution.py:43
  114.1 0.0 copy-done.2
  114.1 19.0 %shard_map.112 = f32[512,1024]{1,0:T(8,128)} custom-call(s32[4]{0:T(128)S(1)} %pad_add_fusion.where, bf16[1024,1024]{1,0:T(8,128)(2,1)S(1)} %copy-done.2, bf16[1024,1024]{1,0:T(8,128)(2,1)} %get-tuple-element.34.rot, f32[1024,1024]{1,0:T(8,128)} %get-tuple-element.41.stat), custom_call_target="tpu_custom_call" | custom-call | flops 10737418240 | bytes 8388608 | tf_op jit(solution)/shard_map/pallas_call | solution.py:43
  133.2 0.0 collective-permute-done.19.came
  133.2 0.0 copy-start.3
  133.2 10.9 %shard_map.110 = (f32[1024,512]{1,0:T(8,128)}, bf16[512,512]{1,0:T(8,128)(2,1)S(1)}, bf16[512,512]{1,0:T(8,128)(2,1)S(1)}) custom-call(bf16[1024,1024]{1,0:T(8,128)(2,1)} %get-tuple-element.33.gradient, bf16[1024,1024]{1,0:T(8,128)(2,1)} %get-tuple-element.26.near, bf16[1024,1024]{1,0:T(8,128)(2,1)} %get-tuple-element.34.rot, ...), custom_call_target="tpu_custom_call" | custom-call | flops 4294967296 | bytes 8388608 | tf_op jit(solution)/shard_map/pallas_call | solution.py:43
  144.1 0.5 collective-permute-start.20
  144.6 0.0 copy-done.3
  144.6 0.0 copy-start
  144.6 19.1 %shard_map.113 = f32[512,1024]{1,0:T(8,128)} custom-call(s32[4]{0:T(128)S(1)} %pad_add_fusion.where, bf16[1024,1024]{1,0:T(8,128)(2,1)S(1)} %copy-done.3, bf16[1024,1024]{1,0:T(8,128)(2,1)} %get-tuple-element.42.rot, f32[1024,1024]{1,0:T(8,128)} %get-tuple-element.43.stat), custom_call_target="tpu_custom_call" | custom-call | flops 10737418240 | bytes 8388608 | tf_op jit(solution)/shard_map/pallas_call | solution.py:43
  163.7 0.0 collective-permute-done.20.came
  163.8 0.0 copy-done
  163.8 2.5 %shard_map.111 = bf16[512,1024]{1,0:T(8,128)(2,1)} custom-call(bf16[512,512]{1,0:T(8,128)(2,1)S(1)} %get-tuple-element.38.mine, bf16[512,512]{1,0:T(8,128)(2,1)S(1)} %collective-permute-done.20.came, bf16[1024,1024]{1,0:T(8,128)(2,1)S(1)} %copy-done), custom_call_target="tpu_custom_call" | custom-call | flops 1073741824 | bytes 4194304 | tf_op jit(solution)/shard_map/pallas_call | solution.py:43
  (2 shorter events, 0.1 us)
Async XLA Ops:
  0.7 8.1 %copy-start.1 = (bf16[1,512,1024]{2,1,0:T(8,128)(2,1)S(1)}, bf16[1,512,1024]{2,1,0:T(8,128)(2,1)}, u32[]{:S(2)}) copy-start(bf16[1,512,1024]{2,1,0:T(8,128)(2,1)} %group.1) | copy-start | bytes 3145732
  5.8 27.2 %collective-permute-start = (bf16[512,1024]{1,0:T(8,128)(2,1)}, bf16[512,1024]{1,0:T(8,128)(2,1)S(1)}, u32[]{:S(2)}, u32[]{:S(2)}) collective-permute-start(bf16[512,1024]{1,0:T(8,128)(2,1)} %get-tuple-element.24), channel_id=1, source_target_pairs={{0,1},{1,0},{2,3},{3,2},{4,5},{5,4},{6,7},{7,6},{8,9},{9,8},{10,11... | collective-permute-start | bytes 3145736 | tf_op jit(solution)/shard_map/ppermute | solution.py:284
  8.7 45.8 %collective-permute-start.2 = (f32[256,1024]{1,0:T(8,128)}, f32[256,1024]{1,0:T(8,128)S(1)}, u32[]{:S(2)}, u32[]{:S(2)}) collective-permute-start(f32[256,1024]{1,0:T(8,128)} %get-tuple-element.25), channel_id=1, source_target_pairs={{0,1},{1,0},{2,3},{3,2},{4,5},{5,4},{6,7},{7,6},{8,9},{9,8},{10,11... | collective-permute-start | bytes 3145736 | tf_op jit(solution)/shard_map/ppermute | solution.py:284
  8.8 24.1 %collective-permute-start.4 = (bf16[256,1024]{1,0:T(8,128)(2,1)S(1)}, bf16[256,1024]{1,0:T(8,128)(2,1)S(1)}, u32[]{:S(2)}, u32[]{:S(2)}) collective-permute-start(bf16[256,1024]{1,0:T(8,128)(2,1)S(1)} %dynamic-slice_bitcast_fusion), channel_id=1, source_target_pairs={{0,2},{2,0},{4,6},{6,4},{8,10},{10,8},{12,14},{14,12},{16,18},{18,... | collective-permute-start | bytes 1572872 | tf_op jit(solution)/shard_map/ppermute | solution.py:281
  32.9 61.2 %collective-permute-start.1 = (bf16[512,1024]{1,0:T(8,128)(2,1)S(1)}, bf16[512,1024]{1,0:T(8,128)(2,1)S(1)}, u32[]{:S(2)}, u32[]{:S(2)}) collective-permute-start(bf16[512,1024]{1,0:T(8,128)(2,1)S(1)} %collective-permute-done.bmine), channel_id=1, source_target_pairs={{0,2},{2,0},{4,6},{6,4},{8,10},{10,8},{12,14},{14,12},{16,18},{18,... | collective-permute-start | bytes 3145736 | tf_op jit(solution)/shard_map/ppermute | solution.py:281
  33.6 21.0 %collective-permute-start.5 = (f32[128,1024]{1,0:T(8,128)S(1)}, f32[128,1024]{1,0:T(8,128)S(1)}, u32[]{:S(2)}, u32[]{:S(2)}) collective-permute-start(f32[128,1024]{1,0:T(8,128)S(1)} %get-tuple-element.28), channel_id=1, source_target_pairs={{0,4},{2,6},{4,0},{6,2},{8,12},{10,14},{12,8},{14,10},{16,20},{18,... | collective-permute-start | bytes 1572872 | tf_op jit(solution)/shard_map/ppermute | solution.py:281
  54.6 39.6 %collective-permute-start.3 = (f32[256,1024]{1,0:T(8,128)S(1)}, f32[256,1024]{1,0:T(8,128)S(1)}, u32[]{:S(2)}, u32[]{:S(2)}) collective-permute-start(f32[256,1024]{1,0:T(8,128)S(1)} %collective-permute-done.2.smine), channel_id=1, source_target_pairs={{0,2},{2,0},{4,6},{6,4},{8,10},{10,8},{12,14},{14,12},{16,18},{18,... | collective-permute-start | bytes 3145736 | tf_op jit(solution)/shard_map/ppermute | solution.py:281
  55.2 8.3 %collective-permute-start.6 = (f32[32,1024]{1,0:T(8,128)S(1)}, f32[32,1024]{1,0:T(8,128)S(1)}, u32[]{:S(2)}, u32[]{:S(2)}) collective-permute-start(f32[32,1024]{1,0:T(8,128)S(1)} %get-tuple-element.30), channel_id=1, source_target_pairs={{0,8},{2,10},{4,12},{6,14},{8,0},{10,2},{12,4},{14,6},{16,24},{18,... | collective-permute-start | bytes 393224 | tf_op jit(solution)/shard_map/ppermute | solution.py:281
  57.0 12.9 %collective-permute-start.7 = (f32[32,1024]{1,0:T(8,128)S(1)}, f32[32,1024]{1,0:T(8,128)S(1)}, u32[]{:S(2)}, u32[]{:S(2)}) collective-permute-start(f32[32,1024]{1,0:T(8,128)S(1)} %get-tuple-element.31), channel_id=1, source_target_pairs={{0,16},{2,18},{4,20},{6,22},{8,24},{10,26},{12,28},{14,30},{16,0},... | collective-permute-start | bytes 393224 | tf_op jit(solution)/shard_map/ppermute | solution.py:281
  59.6 10.3 %collective-permute-start.8 = (f32[32,1024]{1,0:T(8,128)S(1)}, f32[32,1024]{1,0:T(8,128)S(1)}, u32[]{:S(2)}, u32[]{:S(2)}) collective-permute-start(f32[32,1024]{1,0:T(8,128)S(1)} %get-tuple-element.32), channel_id=1, source_target_pairs={{0,24},{2,26},{4,28},{6,30},{8,16},{10,18},{12,20},{14,22},{16,8},... | collective-permute-start | bytes 393224 | tf_op jit(solution)/shard_map/ppermute | solution.py:281
  70.0 8.2 %collective-permute-start.10 = (bf16[32,1024]{1,0:T(8,128)(2,1)S(1)}, bf16[32,1024]{1,0:T(8,128)(2,1)S(1)}, u32[]{:S(2)}, u32[]{:S(2)}) collective-permute-start(bf16[32,1024]{1,0:T(8,128)(2,1)S(1)} %shard_map.106.refs_0_), channel_id=1, source_target_pairs={{0,16},{2,18},{4,20},{6,22},{8,24},{10,26},{12,28},{14,30},{16,0},... | collective-permute-start | bytes 196616 | tf_op jit(solution)/shard_map/ppermute | solution.py:281
  73.7 6.2 %collective-permute-start.11 = (bf16[32,1024]{1,0:T(8,128)(2,1)S(1)}, bf16[32,1024]{1,0:T(8,128)(2,1)S(1)}, u32[]{:S(2)}, u32[]{:S(2)}) collective-permute-start(bf16[32,1024]{1,0:T(8,128)(2,1)S(1)} %shard_map.106.refs_0_), channel_id=1, source_target_pairs={{0,24},{2,26},{4,28},{6,30},{8,16},{10,18},{12,20},{14,22},{16,8},... | collective-permute-start | bytes 196616 | tf_op jit(solution)/shard_map/ppermute | solution.py:281
  75.1 5.0 %collective-permute-start.9 = (bf16[32,1024]{1,0:T(8,128)(2,1)S(1)}, bf16[32,1024]{1,0:T(8,128)(2,1)S(1)}, u32[]{:S(2)}, u32[]{:S(2)}) collective-permute-start(bf16[32,1024]{1,0:T(8,128)(2,1)S(1)} %shard_map.106.refs_0_), channel_id=1, source_target_pairs={{0,8},{2,10},{4,12},{6,14},{8,0},{10,2},{12,4},{14,6},{16,24},{18,... | collective-permute-start | bytes 196616 | tf_op jit(solution)/shard_map/ppermute | solution.py:281
  80.6 9.0 %collective-permute-start.12 = (bf16[128,1024]{1,0:T(8,128)(2,1)S(1)}, bf16[128,1024]{1,0:T(8,128)(2,1)S(1)}, u32[]{:S(2)}, u32[]{:S(2)}) collective-permute-start(bf16[128,1024]{1,0:T(8,128)(2,1)S(1)} %shard_map.107.refs_0_), channel_id=1, source_target_pairs={{0,4},{2,6},{4,0},{6,2},{8,12},{10,14},{12,8},{14,10},{16,20},{18,... | collective-permute-start | bytes 786440 | tf_op jit(solution)/shard_map/ppermute | solution.py:281
  82.2 11.5 %collective-permute-start.15 = (bf16[128,1024]{1,0:T(8,128)(2,1)S(1)}, bf16[128,1024]{1,0:T(8,128)(2,1)S(1)}, u32[]{:S(2)}, u32[]{:S(2)}) collective-permute-start(bf16[128,1024]{1,0:T(8,128)(2,1)S(1)} %shard_map.107.refs_0_), channel_id=1, source_target_pairs={{0,1},{1,0},{2,3},{3,2},{4,5},{5,4},{6,7},{7,6},{8,9},{9,8},{10,11... | collective-permute-start | bytes 786440 | tf_op jit(solution)/shard_map/ppermute | solution.py:284
  83.7 9.9 %collective-permute-start.16 = (bf16[128,1024]{1,0:T(8,128)(2,1)S(1)}, bf16[128,1024]{1,0:T(8,128)(2,1)S(1)}, u32[]{:S(2)}, u32[]{:S(2)}) collective-permute-start(bf16[128,1024]{1,0:T(8,128)(2,1)S(1)} %shard_map.107.refs_0_), channel_id=1, source_target_pairs={{0,5},{1,4},{2,7},{3,6},{4,1},{5,0},{6,3},{7,2},{8,13},{9,12},{10,... | collective-permute-start | bytes 786440 | tf_op jit(solution)/shard_map/ppermute | solution.py:288
  89.6 11.9 %collective-permute-start.13 = (bf16[128,1024]{1,0:T(8,128)(2,1)S(1)}, bf16[128,1024]{1,0:T(8,128)(2,1)S(1)}, u32[]{:S(2)}, u32[]{:S(2)}) collective-permute-start(bf16[128,1024]{1,0:T(8,128)(2,1)S(1)} %shard_map.107.refs_0_), channel_id=1, source_target_pairs={{0,2},{2,0},{4,6},{6,4},{8,10},{10,8},{12,14},{14,12},{16,18},{18,... | collective-permute-start | bytes 786440 | tf_op jit(solution)/shard_map/ppermute | solution.py:281
  93.6 7.9 %collective-permute-start.14 = (bf16[128,1024]{1,0:T(8,128)(2,1)S(1)}, bf16[128,1024]{1,0:T(8,128)(2,1)S(1)}, u32[]{:S(2)}, u32[]{:S(2)}) collective-permute-start(bf16[128,1024]{1,0:T(8,128)(2,1)S(1)} %collective-permute-done.12.refs_1_), channel_id=1, source_target_pairs={{0,2},{2,0},{4,6},{6,4},{8,10},{10,8},{12,14},{14,12},{16,18},{18,... | collective-permute-start | bytes 786440 | tf_op jit(solution)/shard_map/ppermute | solution.py:281
  93.6 7.9 %collective-permute-start.17 = (bf16[128,1024]{1,0:T(8,128)(2,1)S(1)}, bf16[128,1024]{1,0:T(8,128)(2,1)S(1)}, u32[]{:S(2)}, u32[]{:S(2)}) collective-permute-start(bf16[128,1024]{1,0:T(8,128)(2,1)S(1)} %collective-permute-done.15.refs_4_), channel_id=1, source_target_pairs={{0,2},{2,0},{4,6},{6,4},{8,10},{10,8},{12,14},{14,12},{16,18},{18,... | collective-permute-start | bytes 786440 | tf_op jit(solution)/shard_map/ppermute | solution.py:281
  94.1 7.4 %collective-permute-start.18 = (bf16[128,1024]{1,0:T(8,128)(2,1)S(1)}, bf16[128,1024]{1,0:T(8,128)(2,1)S(1)}, u32[]{:S(2)}, u32[]{:S(2)}) collective-permute-start(bf16[128,1024]{1,0:T(8,128)(2,1)S(1)} %collective-permute-done.16.refs_5_), channel_id=1, source_target_pairs={{0,2},{2,0},{4,6},{6,4},{8,10},{10,8},{12,14},{14,12},{16,18},{18,... | collective-permute-start | bytes 786440 | tf_op jit(solution)/shard_map/ppermute | solution.py:281
  94.2 1.0 copy-start.4
  106.2 7.9 %copy-start.2 = (bf16[1024,1024]{1,0:T(8,128)(2,1)S(1)}, bf16[1024,1024]{1,0:T(8,128)(2,1)}, u32[]{:S(2)}) copy-start(bf16[1024,1024]{1,0:T(8,128)(2,1)} %get-tuple-element.33.gradient) | copy-start | bytes 6291460
  106.2 26.9 %collective-permute-start.19 = (bf16[512,512]{1,0:T(8,128)(2,1)S(1)}, bf16[512,512]{1,0:T(8,128)(2,1)S(1)}, u32[]{:S(2)}, u32[]{:S(2)}) collective-permute-start(bf16[512,512]{1,0:T(8,128)(2,1)S(1)} %get-tuple-element.37), channel_id=1, source_target_pairs={{0,1},{1,0},{2,3},{3,2},{4,5},{5,4},{6,7},{7,6},{8,9},{9,8},{10,11... | collective-permute-start | bytes 1572872 | tf_op jit(solution)/shard_map/ppermute | solution.py:284
  133.2 11.5 %copy-start.3 = (bf16[1024,1024]{1,0:T(8,128)(2,1)S(1)}, bf16[1024,1024]{1,0:T(8,128)(2,1)}, u32[]{:S(2)}) copy-start(bf16[1024,1024]{1,0:T(8,128)(2,1)} %get-tuple-element.33.gradient) | copy-start | bytes 6291460
  144.1 19.6 %collective-permute-start.20 = (bf16[512,512]{1,0:T(8,128)(2,1)S(1)}, bf16[512,512]{1,0:T(8,128)(2,1)S(1)}, u32[]{:S(2)}, u32[]{:S(2)}) collective-permute-start(bf16[512,512]{1,0:T(8,128)(2,1)S(1)} %get-tuple-element.39), channel_id=1, source_target_pairs={{0,1},{1,0},{2,3},{3,2},{4,5},{5,4},{6,7},{7,6},{8,9},{9,8},{10,11... | collective-permute-start | bytes 1572872 | tf_op jit(solution)/shard_map/ppermute | solution.py:284
  144.6 19.1 %copy-start = (bf16[1024,1024]{1,0:T(8,128)(2,1)S(1)}, bf16[1024,1024]{1,0:T(8,128)(2,1)}, u32[]{:S(2)}) copy-start(bf16[1024,1024]{1,0:T(8,128)(2,1)} %get-tuple-element.26.near) | copy-start | bytes 6291460

commit v2 on v1

--- a/solution.py
+++ b/solution.py
@@ -39,27 +39,25 @@
     return pl.ds(pl.multiple_of(index * size, size), size)
 
 
-def call(kernel, outs, operands, specs, scratch=(), flops=0, moved=0):
+def call(kernel, outs, operands, specs, scratch=(), flops=0, moved=0, limit=24):
     return pl.pallas_call(
         kernel,
         out_shape=outs,
         in_specs=specs,
         out_specs=[VMEM] * len(outs),
         scratch_shapes=list(scratch),
-        compiler_params=pltpu.CompilerParams(vmem_limit_bytes=50 * 2**20),
+        compiler_params=pltpu.CompilerParams(vmem_limit_bytes=limit * 2**20),
         cost_estimate=pl.CostEstimate(flops=flops, bytes_accessed=moved, transcendentals=0),
     )(*operands)
 
 
 def state_parts_kernel(where, left, right, stat_left, stat_right, bases, stats):
-    half = left.shape[0] // 2
-    rows = left.shape[0]
-    near = tile(where[0], rows)
-    mine = tile(where[1], half)
-    bases[:half] = left[mine].astype(HALF)
-    bases[half:] = right[mine].astype(HALF)
-    stats[:, :rows] = stat_left[mine, near]
-    stats[:, rows:] = stat_right[mine, near]
+    half = left.shape[0]
+    rows = stat_left.shape[1]
+    bases[:half] = left[...].astype(HALF)
+    bases[half:] = right[...].astype(HALF)
+    stats[:, :rows] = stat_left[...]
+    stats[:, rows:] = stat_right[...]
 
 
 def first_sum_kernel(where, group, came, kept, sent):
@@ -149,121 +147,89 @@
         copy.start()
     for copy in copies:
         copy.wait()
+    half = (
+        BETA_ONE * moment[...] + (1.0 - BETA_ONE) * gradient[:rows].astype(FULL)
+    ).astype(HALF)
     step = rows // 2
-
-    @pl.loop(0, 2)
-    def _(i):
-        here = tile(i, step)
-        half = (
-            BETA_ONE * moment[here] + (1.0 - BETA_ONE) * gradient[here].astype(FULL)
-        ).astype(HALF)
-        ours[here] = matmul(half, near[:, :rows]).astype(HALF)
-        others[here] = matmul(half, near[:, rows:]).astype(HALF)
+    for i in range(2):
+        here = slice(i * step, (i + 1) * step)
+        others[:, here] = matmul(half, near[:, rows + i * step : rows + (i + 1) * step]).astype(HALF)
+        ours[:, here] = matmul(half, near[:, here]).astype(HALF)
 
 
 def adam_kernel(gradient, near, rot, turned, mine, came, second, new, kept, sent, block, scaled):
     width = gradient.shape[0]
     rows = mine.shape[0]
-    step = width // 4
-
-    @pl.loop(0, 4)
-    def _(i):
-        here = tile(i, step)
-        block[here] = matmul(gradient[here], near[:, :rows]).astype(HALF)
-
-    @pl.loop(0, 4)
-    def _(i):
-        here = tile(i, step)
-        grad_rot = matmul(turned[here], block[...]) * (1.0 / width)
+    step = rows // 2
+    columns = [slice(i * step, (i + 1) * step) for i in range(2)]
+    for here in columns:
+        block[:, here] = matmul(gradient[...], near[:, here]).astype(HALF)
+    for here in columns:
+        grad_rot = matmul(turned[...], block[:, here]) * (1.0 / width)
         moment_rot = (
-            matmul(turned[here, :rows], mine[...]) + matmul(turned[here, rows:], came[...])
+            matmul(turned[:, :rows], mine[:, here]) + matmul(turned[:, rows:], came[:, here])
         ) * (1.0 / width)
-        value = BETA_TWO * second[here] + (1.0 - BETA_TWO) * grad_rot * grad_rot
-        new[here] = value
-        scaled[here] = (moment_rot / (jnp.sqrt(value) + EPSILON)).astype(HALF)
-
-    @pl.loop(0, rows // step)
-    def _(i):
-        here = tile(i, step)
-        kept[here] = matmul(rot[here], scaled[...]).astype(HALF)
-        sent[here] = matmul(rot[tile(i + rows // step, step)], scaled[...]).astype(HALF)
+        value = BETA_TWO * second[:, here] + (1.0 - BETA_TWO) * grad_rot * grad_rot
+        new[:, here] = value
+        scaled[:, here] = (moment_rot / (jnp.sqrt(value) + EPSILON)).astype(HALF)
+    for here in columns:
+        sent[:, here] = matmul(rot[rows:], scaled[:, here]).astype(HALF)
+        kept[:, here] = matmul(rot[:rows], scaled[:, here]).astype(HALF)
 
 
 def update_kernel(mine, came, near, out):
     rows, width = out.shape
-    step = rows // 2
-
-    @pl.loop(0, 2)
-    def _(i):
-        here = tile(i, step)
-        total = matmul(mine[here], near[:, :rows], 1, 1) + matmul(
-            came[here], near[:, rows:], 1, 1
-        )
-        out[here] = (total * (1.0 / width)).astype(HALF)
-
-
-def refresh_kernel(natural, where, gradient, rot, stat, out, stat_in, turned, half, product, sem):
+    step = width // 4
+    for here in [slice(i * step, (i + 1) * step) for i in range(4)]:
+        total = matmul(mine[...], near[here, :rows], 1, 1) + matmul(
+            came[...], near[here, rows:], 1, 1
+        )
+        out[:, here] = (total * (1.0 / width)).astype(HALF)
+
+
+def refresh_kernel(natural, where, gradient, rot, stat, out, stat_in, turned, half, gram, sem):
     width = gradient.shape[0]
     rows = out.shape[0]
-    steps = 4
-    step = width // steps
+    step = width // 4
+    columns = [slice(i * step, (i + 1) * step) for i in range(4)]
     copies = [
-        pltpu.make_async_copy(stat.at[tile(i, step)], stat_in.at[tile(i, step)], sem.at[i])
-        for i in range(steps)
+        pltpu.make_async_copy(stat.at[:, here], stat_in.at[:, here], sem.at[i])
+        for i, here in enumerate(columns)
     ]
     for copy in copies:
         copy.start()
     if natural:
-
-        @pl.loop(0, steps)
-        def _(i):
-            turned[:, tile(i, step)] = gradient[tile(i, step)].T
-
-        source, dim = turned, 0
-    else:
-        source, dim = gradient, 1
-    for copy in copies:
+        for here in columns:
+            turned[:, here] = gradient[here].T
+    for here, copy in zip(columns, copies):
+        if natural:
+            grads = matmul(turned[...], gradient[:, here])
+        else:
+            grads = matmul(gradient[...], gradient[here], 1, 1)
         copy.wait()
-
-    @pl.loop(0, steps)
-    def _(i):
-        here = tile(i, step)
-        grads = matmul(source[here], gradient[...], 1, dim)
-        half[here] = (BETA_STAT * stat_in[here] + (1.0 - BETA_STAT) * grads).astype(HALF)
-
-    def power(i, total):
-        here = tile(i, step)
-        value = matmul(half[here], rot[...])
-        product[here] = value
-        return total + jnp.sum(value * value, axis=0, keepdims=True)
-
-    total = lax.fori_loop(0, steps, power, jnp.zeros((1, width), FULL))
-    scale = lax.rsqrt(total * (1.0 / width) + NORM_EPS)
-
-    @pl.loop(0, steps)
-    def _(i):
-        here = tile(i, step)
-        half[here] = (product[here] * scale).astype(HALF)
-
-    def improved(current, here):
-        gram = (matmul(current[here], current[...], 1, 1) * (1.0 / width)).astype(HALF)
-        return 1.5 * current[here].astype(FULL) - 0.5 * matmul(gram, current[...])
-
-    current, following = half, turned
+        half[:, here] = (BETA_STAT * stat_in[:, here] + (1.0 - BETA_STAT) * grads).astype(HALF)
+    for here in columns:
+        product = matmul(half[...], rot[:, here])
+        square = jnp.sum(product * product, axis=0, keepdims=True) * (1.0 / width)
+        turned[:, here] = (product * lax.rsqrt(square + NORM_EPS)).astype(HALF)
+
+    def improved(current, kept, result, dtype):
+        size = result.shape[0]
+        for here in columns:
+            gram[:size, here] = (
+                matmul(current[kept], current[here], 1, 1) * (1.0 / width)
+            ).astype(HALF)
+        for here in columns:
+            result[:, here] = (
+                1.5 * current[kept, here].astype(FULL)
+                - 0.5 * matmul(gram[:size], current[:, here])
+            ).astype(dtype)
+
+    current, following = turned, half
     for _ in range(NS_ITERS - 1):
-
-        @pl.loop(0, steps)
-        def _(i):
-            here = tile(i, step)
-            following[here] = improved(current, here).astype(HALF)
-
+        improved(current, slice(0, width), following, HALF)
         current, following = following, current
-
-    first = where[0] * (rows // step) if natural else 0
-
-    @pl.loop(0, rows // step)
-    def _(i):
-        out[tile(i, step)] = improved(current, tile(first + i, step))
+    improved(current, tile(where[0], rows) if natural else slice(0, rows), out, FULL)
 
 
 def fast_body(group_grads, moment, second, stat_left, stat_right, basis_left, basis_right):
@@ -287,13 +253,22 @@
         pairs = [(i, i ^ 5) for i in range(32)]
         return lax.ppermute(value, ("dp", "shard"), pairs)
 
-    bases_sent, stats_sent = call(
+    bases_sent, stats_sent = pl.pallas_call(
         state_parts_kernel,
-        [shaped((rows, width), HALF), shaped((half, width), FULL)],
-        (where, basis_left, basis_right, stat_left, stat_right),
-        [SMEM] + [VMEM] * 4,
-        moved=2**23,
-    )
+        out_shape=[shaped((rows, width), HALF), shaped((half, width), FULL)],
+        grid_spec=pltpu.PrefetchScalarGridSpec(
+            num_scalar_prefetch=1,
+            grid=(1,),
+            in_specs=[pl.BlockSpec((half, width), lambda i, where: (where[1], 0))] * 2
+            + [pl.BlockSpec((half, rows), lambda i, where: (where[1], where[0]))] * 2,
+            out_specs=[
+                pl.BlockSpec((rows, width), lambda i, where: (0, 0)),
+                pl.BlockSpec((half, width), lambda i, where: (0, 0)),
+            ],
+        ),
+        compiler_params=pltpu.CompilerParams(vmem_limit_bytes=56 * 2**20),
+        cost_estimate=pl.CostEstimate(flops=0, bytes_accessed=2**22, transcendentals=0),
+    )(where, basis_left, basis_right, stat_left, stat_right)
     bases_mine = shard_swap(bases_sent)
     stats_mine = shard_swap(stats_sent)
 
@@ -323,6 +298,7 @@
         joined_kernel, [shaped((quarter, width), HALF)], (where, *pieces), [SMEM] + [VMEM] * 4,
         moved=2**19,
     )
+    part, bases_mine, stats_mine = lax.optimization_barrier((part, bases_mine, stats_mine))
     parts = [part, dp_swap(part, 2), shard_swap(part), cross_swap(part)]
     swapped = [dp_swap(value, 1) for value in parts]
 
@@ -372,7 +348,7 @@
                 pltpu.VMEM((width, width), FULL),
                 pltpu.VMEM((width, width), HALF),
                 pltpu.VMEM((width, width), HALF),
-                pltpu.VMEM((width, width), FULL),
+                pltpu.VMEM((width, width), HALF),
                 pltpu.SemaphoreType.DMA((4,)),
             ],
             flops=5 * unit,

time: 166 us -> 123 us (0.74)
  waiting for transfers between devices: 67.6 us -> 45.6 us
  Pallas kernels: 75.7 us -> 53.9 us
    ppermute x5, waiting for transfers between devices: 46.9 us -> 13.3 us  [shard_swap(): return lax.ppermute(value, 'shard', [(0, 1), (1, 0)])]
    pallas_call x12 -> x11, Pallas kernels: 75.7 us -> 49.7 us  [call(): pl.pallas_call(kernel, out_shape=outs, in_specs=specs, out_specs=[VMEM] *...]
    ppermute x15, waiting for transfers between devices: 20.7 us -> 32.3 us  [dp_swap(): return lax.ppermute(value, 'dp', [(i, i ^ distance) for i in range(16)])]
    pallas_call x0 -> x1, Pallas kernels: none -> 4.19 us  [fast_body(): pl.pallas_call(state_parts_kernel, out_shape=[shaped((rows, width), HALF)...]
  transfers between devices with their start and end apart: 21 -> 21, of which waited for: 9 -> 10; matrix products, arithmetic and copies ran while one was open for 0% -> 0% of each run, Pallas kernels for 32% -> 36%
where the time goes in v2:
time: 123 us
  Pallas kernels  53.9 us (44%)
  waiting for transfers between devices  45.6 us (37%)
  starting transfers between devices  20.7 us (17%)
    pallas_call x11, Pallas kernels, call(): pl.pallas_call(kernel, out_shape=outs, in_specs=specs, out_specs=[VMEM] *...  49.7 us
    ppermute x15, waiting for transfers between devices, dp_swap(): return lax.ppermute(value, 'dp', [(i, i ^ distance) for i in range(16)])  32.3 us
    ppermute x15, starting transfers between devices, dp_swap(): return lax.ppermute(value, 'dp', [(i, i ^ distance) for i in range(16)])  14.3 us
    ppermute x5, waiting for transfers between devices, shard_swap(): return lax.ppermute(value, 'shard', [(0, 1), (1, 0)])  13.3 us
    ppermute x5, starting transfers between devices, shard_swap(): return lax.ppermute(value, 'shard', [(0, 1), (1, 0)])  6.18 us
    pallas_call x1, Pallas kernels, fast_body(): pl.pallas_call(state_parts_kernel, out_shape=[shaped((rows, width), HALF)...  4.19 us
  transfers between devices with their start and end apart: 21, of which 10 were waited for; matrix products, arithmetic and copies ran while one was open for 0% of the time, Pallas kernels for 36%

profile of v2, /device:TPU:0, one launch (start us, length us, event | category | flops | bytes accessed | tf_op | source)
XLA Modules:
  0.0 122.7 jit_solution(8658047568180856139)
XLA Ops:
  0.6 1.1 dynamic-slice_bitcast_fusion
  1.7 0.5 collective-permute-start
  2.2 0.6 pad_add_fusion.where
  2.8 4.2 %shard_map.106 = (bf16[512,1024]{1,0:T(8,128)(2,1)}, f32[256,1024]{1,0:T(8,128)}) custom-call(s32[4]{0:T(128)} %pad_add_fusion.where, f32[512,1024]{1,0:T(8,128)} %basis.3, f32[512,1024]{1,0:T(8,128)} %basis.2, f32[512,1024]{1,0:T(8,128)} %stat.3, f32[512,1024]{1,0:T(8,128)} %stat.2), custom_call_target="tpu_custom_call" | custom-call | bytes 4194304 | tf_op jit(solution)/shard_map/pallas_call | solution.py:256
  7.0 2.5 %collective-permute-start.8 = (bf16[512,1024]{1,0:T(8,128)(2,1)}, bf16[512,1024]{1,0:T(8,128)(2,1)S(1)}, u32[]{:S(2)}, u32[]{:S(2)}) collective-permute-start(bf16[512,1024]{1,0:T(8,128)(2,1)} %get-tuple-element.33), channel_id=1, source_target_pairs={{0,1},{1,0},{2,3},{3,2},{4,5},{5,4},{6,7},{7,6},{8,9},{9,8},{10,11... | collective-permute-start | bytes 3145736 | tf_op jit(solution)/shard_map/ppermute | solution.py:250
  9.6 0.0 collective-permute-start.9
  9.6 0.0 collective-permute-done.came
  9.6 0.0 copy-done.4
  9.6 0.0 copy-done.6
  9.6 0.7 shard_map.102
  10.3 2.0 %collective-permute-start.1 = (f32[128,1024]{1,0:T(8,128)S(1)}, f32[128,1024]{1,0:T(8,128)S(1)}, u32[]{:S(2)}, u32[]{:S(2)}) collective-permute-start(f32[128,1024]{1,0:T(8,128)S(1)} %get-tuple-element.28), channel_id=1, source_target_pairs={{0,4},{2,6},{4,0},{6,2},{8,12},{10,14},{12,8},{14,10},{16,20},{18,... | collective-permute-start | bytes 1572872 | tf_op jit(solution)/shard_map/ppermute | solution.py:247
  12.3 12.1 %collective-permute-done.1.came = f32[128,1024]{1,0:T(8,128)S(1)} collective-permute-done((f32[128,1024]{1,0:T(8,128)S(1)}, f32[128,1024]{1,0:T(8,128)S(1)}, u32[]{:S(2)}, u32[]{:S(2)}) %collective-permute-start.1) | collective-permute-done | bytes 524320 | tf_op jit(solution)/shard_map/ppermute | solution.py:247
  24.4 0.6 shard_map.103
  25.0 1.8 %collective-permute-start.2 = (f32[32,1024]{1,0:T(8,128)S(1)}, f32[32,1024]{1,0:T(8,128)S(1)}, u32[]{:S(2)}, u32[]{:S(2)}) collective-permute-start(f32[32,1024]{1,0:T(8,128)S(1)} %get-tuple-element.30), channel_id=1, source_target_pairs={{0,8},{2,10},{4,12},{6,14},{8,0},{10,2},{12,4},{14,6},{16,24},{18,... | collective-permute-start | bytes 393224 | tf_op jit(solution)/shard_map/ppermute | solution.py:247
  26.8 2.6 %collective-permute-start.3 = (f32[32,1024]{1,0:T(8,128)S(1)}, f32[32,1024]{1,0:T(8,128)S(1)}, u32[]{:S(2)}, u32[]{:S(2)}) collective-permute-start(f32[32,1024]{1,0:T(8,128)S(1)} %get-tuple-element.31), channel_id=1, source_target_pairs={{0,16},{2,18},{4,20},{6,22},{8,24},{10,26},{12,28},{14,30},{16,0},... | collective-permute-start | bytes 393224 | tf_op jit(solution)/shard_map/ppermute | solution.py:247
  29.4 0.0 collective-permute-start.4
  29.4 2.0 %collective-permute-done.2.one = f32[32,1024]{1,0:T(8,128)S(1)} collective-permute-done((f32[32,1024]{1,0:T(8,128)S(1)}, f32[32,1024]{1,0:T(8,128)S(1)}, u32[]{:S(2)}, u32[]{:S(2)}) %collective-permute-start.2) | collective-permute-done | bytes 131104 | tf_op jit(solution)/shard_map/ppermute | solution.py:247
  31.4 7.5 %collective-permute-done.3.two = f32[32,1024]{1,0:T(8,128)S(1)} collective-permute-done((f32[32,1024]{1,0:T(8,128)S(1)}, f32[32,1024]{1,0:T(8,128)S(1)}, u32[]{:S(2)}, u32[]{:S(2)}) %collective-permute-start.3) | collective-permute-done | bytes 131104 | tf_op jit(solution)/shard_map/ppermute | solution.py:247
  39.0 0.0 collective-permute-done.4.three
  39.0 2.0 %collective-permute-start.5 = (bf16[32,1024]{1,0:T(8,128)(2,1)S(1)}, bf16[32,1024]{1,0:T(8,128)(2,1)S(1)}, u32[]{:S(2)}, u32[]{:S(2)}) collective-permute-start(bf16[32,1024]{1,0:T(8,128)(2,1)S(1)} %shard_map.104.refs_0_), channel_id=1, source_target_pairs={{0,8},{2,10},{4,12},{6,14},{8,0},{10,2},{12,4},{14,6},{16,24},{18,... | collective-permute-start | bytes 196616 | tf_op jit(solution)/shard_map/ppermute | solution.py:247
  41.0 1.1 collective-permute-start.6
  42.1 1.4 %collective-permute-start.7 = (bf16[32,1024]{1,0:T(8,128)(2,1)S(1)}, bf16[32,1024]{1,0:T(8,128)(2,1)S(1)}, u32[]{:S(2)}, u32[]{:S(2)}) collective-permute-start(bf16[32,1024]{1,0:T(8,128)(2,1)S(1)} %shard_map.104.refs_0_), channel_id=1, source_target_pairs={{0,24},{2,26},{4,28},{6,30},{8,16},{10,18},{12,20},{14,22},{16,8},... | collective-permute-start | bytes 196616 | tf_op jit(solution)/shard_map/ppermute | solution.py:247
  43.5 0.3 collective-permute-done.5.refs_1_
  43.8 3.3 %collective-permute-done.6.refs_2_ = bf16[32,1024]{1,0:T(8,128)(2,1)S(1)} collective-permute-done((bf16[32,1024]{1,0:T(8,128)(2,1)S(1)}, bf16[32,1024]{1,0:T(8,128)(2,1)S(1)}, u32[]{:S(2)}, u32[]{:S(2)}) %collective-permute-start.6) | collective-permute-done | bytes 65568 | tf_op jit(solution)/shard_map/ppermute | solution.py:247
  47.1 1.2 collective-permute-done.7.refs_3_
  48.3 0.6 shard_map.105.refs_0_
  48.9 0.0 copy-start.5
  48.9 0.0 collective-permute-done.8.bmine
  48.9 7.2 %collective-permute-done.9.smine = f32[256,1024]{1,0:T(8,128)S(1)} collective-permute-done((f32[256,1024]{1,0:T(8,128)}, f32[256,1024]{1,0:T(8,128)S(1)}, u32[]{:S(2)}, u32[]{:S(2)}) %collective-permute-start.9) | collective-permute-done | bytes 1048608 | tf_op jit(solution)/shard_map/ppermute | solution.py:250
  56.0 0.0 collective-permute-start.10
  56.0 0.5 collective-permute-start.11
  56.6 1.7 %collective-permute-start.12 = (bf16[128,1024]{1,0:T(8,128)(2,1)S(1)}, bf16[128,1024]{1,0:T(8,128)(2,1)S(1)}, u32[]{:S(2)}, u32[]{:S(2)}) collective-permute-start(bf16[128,1024]{1,0:T(8,128)(2,1)S(1)} %shard_map.105.refs_0_), channel_id=1, source_target_pairs={{0,4},{2,6},{4,0},{6,2},{8,12},{10,14},{12,8},{14,10},{16,20},{18,... | collective-permute-start | bytes 786440 | tf_op jit(solution)/shard_map/ppermute | solution.py:247
  58.3 1.5 %collective-permute-start.15 = (bf16[128,1024]{1,0:T(8,128)(2,1)S(1)}, bf16[128,1024]{1,0:T(8,128)(2,1)S(1)}, u32[]{:S(2)}, u32[]{:S(2)}) collective-permute-start(bf16[128,1024]{1,0:T(8,128)(2,1)S(1)} %shard_map.105.refs_0_), channel_id=1, source_target_pairs={{0,1},{1,0},{2,3},{3,2},{4,5},{5,4},{6,7},{7,6},{8,9},{9,8},{10,11... | collective-permute-start | bytes 786440 | tf_op jit(solution)/shard_map/ppermute | solution.py:250
  59.8 0.3 collective-permute-start.16
  60.0 5.7 %collective-permute-done.12.refs_1_ = bf16[128,1024]{1,0:T(8,128)(2,1)S(1)} collective-permute-done((bf16[128,1024]{1,0:T(8,128)(2,1)S(1)}, bf16[128,1024]{1,0:T(8,128)(2,1)S(1)}, u32[]{:S(2)}, u32[]{:S(2)}) %collective-permute-start.12) | collective-permute-done | bytes 262176 | tf_op jit(solution)/shard_map/ppermute | solution.py:247
  65.7 0.0 collective-permute-start.13
  65.7 6.1 %collective-permute-done.15.refs_4_ = bf16[128,1024]{1,0:T(8,128)(2,1)S(1)} collective-permute-done((bf16[128,1024]{1,0:T(8,128)(2,1)S(1)}, bf16[128,1024]{1,0:T(8,128)(2,1)S(1)}, u32[]{:S(2)}, u32[]{:S(2)}) %collective-permute-start.15) | collective-permute-done | bytes 262176 | tf_op jit(solution)/shard_map/ppermute | solution.py:250
  71.8 0.0 collective-permute-start.14
  71.8 0.0 collective-permute-done.16.refs_5_
  71.8 0.5 collective-permute-start.17
  72.3 0.0 collective-permute-done.10.btheirs
  72.3 0.1 collective-permute-start.18
  72.4 0.0 collective-permute-done.11.stheirs
  72.4 0.0 copy-done.1
  72.4 0.0 copy-done
  72.4 1.4 %shard_map.107 = (bf16[1024,1024]{1,0:T(8,128)(2,1)S(1)}, bf16[1024,1024]{1,0:T(8,128)(2,1)S(1)}, f32[1024,1024]{1,0:T(8,128)S(1)}) custom-call(s32[4]{0:T(128)S(1)} %copy-done.6, f32[512,1024]{1,0:T(8,128)S(1)} %copy-done, bf16[512,1024]{1,0:T(8,128)(2,1)S(1)} %collective-permute-done.8.bmine, bf16[512,1024]{1,0:T(8,128)(2,1)S(1)} %collective-permute-done.10.btheirs, ...), custom_call_target="tpu_custom_call" | custom-call | bytes 16777216 | tf_op jit(solution)/shard_map/pallas_call | solution.py:43
  73.8 0.0 collective-permute-done.13.refs_2_
  73.8 0.0 collective-permute-done.14.refs_3_
  73.9 0.0 collective-permute-done.17.refs_6_
  73.9 0.2 collective-permute-done.18.refs_7_
  74.1 0.0 copy-done.5
  74.1 2.1 %shard_map.108 = (bf16[1024,1024]{1,0:T(8,128)(2,1)S(1)}, bf16[512,512]{1,0:T(8,128)(2,1)S(1)}, bf16[512,512]{1,0:T(8,128)(2,1)S(1)}) custom-call(s32[4]{0:T(128)S(1)} %copy-done.6, f32[512,1024]{1,0:T(8,128)S(1)} %copy-done.5, bf16[1024,1024]{1,0:T(8,128)(2,1)S(1)} %get-tuple-element.37.near, bf16[128,1024]{1,0:T(8,128)(2,1)S(1)} %shard_map.105.refs_0_, ...), custom_call_target="tpu_custom_call" | custom-call | flops 1073741824 | bytes 8388608 | tf_op jit(solution)/shard_map/pallas_call | solution.py:43
  76.2 1.6 %collective-permute-start.19 = (bf16[512,512]{1,0:T(8,128)(2,1)S(1)}, bf16[512,512]{1,0:T(8,128)(2,1)S(1)}, u32[]{:S(2)}, u32[]{:S(2)}) collective-permute-start(bf16[512,512]{1,0:T(8,128)(2,1)S(1)} %get-tuple-element.43), channel_id=1, source_target_pairs={{0,1},{1,0},{2,3},{3,2},{4,5},{5,4},{6,7},{7,6},{8,9},{9,8},{10,11... | collective-permute-start | bytes 1572872 | tf_op jit(solution)/shard_map/ppermute | solution.py:250
  77.8 0.0 copy-done.2
  77.8 0.0 copy-done.3
  77.8 1.7 %shard_map.109 = (bf16[1024,1024]{1,0:T(8,128)(2,1)S(1)}, bf16[1024,1024]{1,0:T(8,128)(2,1)S(1)}, f32[1024,1024]{1,0:T(8,128)S(1)}) custom-call(s32[4]{0:T(128)S(1)} %copy-done.6, f32[512,1024]{1,0:T(8,128)S(1)} %copy-done.2, bf16[512,1024]{1,0:T(8,128)(2,1)S(1)} %collective-permute-done.8.bmine, bf16[512,1024]{1,0:T(8,128)(2,1)S(1)} %collective-permute-done.10.btheirs, ...), custom_call_target="tpu_custom_call" | custom-call | bytes 16777216 | tf_op jit(solution)/shard_map/pallas_call | solution.py:43
  79.5 0.0 copy-start.7
  79.5 17.5 %shard_map.112 = f32[512,1024]{1,0:T(8,128)} custom-call(s32[4]{0:T(128)S(1)} %copy-done.6, bf16[1024,1024]{1,0:T(8,128)(2,1)S(1)} %get-tuple-element.39.gradient, bf16[1024,1024]{1,0:T(8,128)(2,1)S(1)} %get-tuple-element.40.rot, f32[1024,1024]{1,0:T(8,128)S(1)} %get-tuple-element.47.stat), custom_call_target="tpu_custom_call" | custom-call | flops 10737418240 | bytes 8388608 | tf_op jit(solution)/shard_map/pallas_call | solution.py:43
  97.0 0.0 collective-permute-done.19.came
  97.0 5.1 %shard_map.110 = (f32[1024,512]{1,0:T(8,128)}, bf16[512,512]{1,0:T(8,128)(2,1)S(1)}, bf16[512,512]{1,0:T(8,128)(2,1)S(1)}) custom-call(bf16[1024,1024]{1,0:T(8,128)(2,1)S(1)} %get-tuple-element.39.gradient, bf16[1024,1024]{1,0:T(8,128)(2,1)S(1)} %get-tuple-element.37.near, bf16[1024,1024]{1,0:T(8,128)(2,1)S(1)} %get-tuple-element.40.rot, ...), custom_call_target="tpu_custom_call" | custom-call | flops 4294967296 | bytes 8388608 | tf_op jit(solution)/shard_map/pallas_call | solution.py:43
  102.1 0.5 collective-permute-start.20
  102.6 17.8 %shard_map.113 = f32[512,1024]{1,0:T(8,128)} custom-call(s32[4]{0:T(128)S(1)} %copy-done.6, bf16[1024,1024]{1,0:T(8,128)(2,1)S(1)} %get-tuple-element.39.gradient, bf16[1024,1024]{1,0:T(8,128)(2,1)S(1)} %get-tuple-element.48.rot, f32[1024,1024]{1,0:T(8,128)S(1)} %get-tuple-element.49.stat), custom_call_target="tpu_custom_call" | custom-call | flops 10737418240 | bytes 8388608 | tf_op jit(solution)/shard_map/pallas_call | solution.py:43
  120.4 0.0 collective-permute-done.20.came
  120.4 2.3 %shard_map.111 = bf16[512,1024]{1,0:T(8,128)(2,1)} custom-call(bf16[512,512]{1,0:T(8,128)(2,1)S(1)} %get-tuple-element.44.mine, bf16[512,512]{1,0:T(8,128)(2,1)S(1)} %collective-permute-done.20.came, bf16[1024,1024]{1,0:T(8,128)(2,1)S(1)} %get-tuple-element.37.near), custom_call_target="tpu_custom_call" | custom-call | flops 1073741824 | bytes 4194304 | tf_op jit(solution)/shard_map/pallas_call | solution.py:43
  (8 shorter events, 0.0 us)
Async XLA Ops:
  1.7 7.9 %collective-permute-start = (bf16[256,1024]{1,0:T(8,128)(2,1)S(1)}, bf16[256,1024]{1,0:T(8,128)(2,1)S(1)}, u32[]{:S(2)}, u32[]{:S(2)}) collective-permute-start(bf16[256,1024]{1,0:T(8,128)(2,1)S(1)} %dynamic-slice_bitcast_fusion), channel_id=1, source_target_pairs={{0,2},{2,0},{4,6},{6,4},{8,10},{10,8},{12,14},{14,12},{16,18},{18,... | collective-permute-start | bytes 1572872 | tf_op jit(solution)/shard_map/ppermute | solution.py:247
  2.8 6.8 %copy-start.4 = (bf16[1,512,1024]{2,1,0:T(8,128)(2,1)S(1)}, bf16[1,512,1024]{2,1,0:T(8,128)(2,1)}, u32[]{:S(2)}) copy-start(bf16[1,512,1024]{2,1,0:T(8,128)(2,1)} %group.1) | copy-start | bytes 3145732
  2.8 6.8 %copy-start.6 = (s32[4]{0:T(128)S(1)}, s32[4]{0:T(128)}, u32[]{:S(2)}) copy-start(s32[4]{0:T(128)} %pad_add_fusion.where) | copy-start | bytes 52
  2.8 69.6 %copy-start.1 = (f32[512,1024]{1,0:T(8,128)S(1)}, f32[512,1024]{1,0:T(8,128)}, u32[]{:S(2)}) copy-start(f32[512,1024]{1,0:T(8,128)} %stat.2) | copy-start | bytes 6291460
  7.0 65.4 %copy-start = (f32[512,1024]{1,0:T(8,128)S(1)}, f32[512,1024]{1,0:T(8,128)}, u32[]{:S(2)}) copy-start(f32[512,1024]{1,0:T(8,128)} %basis.2) | copy-start | bytes 6291460
  7.0 41.9 %collective-permute-start.8 = (bf16[512,1024]{1,0:T(8,128)(2,1)}, bf16[512,1024]{1,0:T(8,128)(2,1)S(1)}, u32[]{:S(2)}, u32[]{:S(2)}) collective-permute-start(bf16[512,1024]{1,0:T(8,128)(2,1)} %get-tuple-element.33), channel_id=1, source_target_pairs={{0,1},{1,0},{2,3},{3,2},{4,5},{5,4},{6,7},{7,6},{8,9},{9,8},{10,11... | collective-permute-start | bytes 3145736 | tf_op jit(solution)/shard_map/ppermute | solution.py:250
  9.6 46.5 %collective-permute-start.9 = (f32[256,1024]{1,0:T(8,128)}, f32[256,1024]{1,0:T(8,128)S(1)}, u32[]{:S(2)}, u32[]{:S(2)}) collective-permute-start(f32[256,1024]{1,0:T(8,128)} %get-tuple-element.34), channel_id=1, source_target_pairs={{0,1},{1,0},{2,3},{3,2},{4,5},{5,4},{6,7},{7,6},{8,9},{9,8},{10,11... | collective-permute-start | bytes 3145736 | tf_op jit(solution)/shard_map/ppermute | solution.py:250
  10.3 14.1 %collective-permute-start.1 = (f32[128,1024]{1,0:T(8,128)S(1)}, f32[128,1024]{1,0:T(8,128)S(1)}, u32[]{:S(2)}, u32[]{:S(2)}) collective-permute-start(f32[128,1024]{1,0:T(8,128)S(1)} %get-tuple-element.28), channel_id=1, source_target_pairs={{0,4},{2,6},{4,0},{6,2},{8,12},{10,14},{12,8},{14,10},{16,20},{18,... | collective-permute-start | bytes 1572872 | tf_op jit(solution)/shard_map/ppermute | solution.py:247
  25.0 6.4 %collective-permute-start.2 = (f32[32,1024]{1,0:T(8,128)S(1)}, f32[32,1024]{1,0:T(8,128)S(1)}, u32[]{:S(2)}, u32[]{:S(2)}) collective-permute-start(f32[32,1024]{1,0:T(8,128)S(1)} %get-tuple-element.30), channel_id=1, source_target_pairs={{0,8},{2,10},{4,12},{6,14},{8,0},{10,2},{12,4},{14,6},{16,24},{18,... | collective-permute-start | bytes 393224 | tf_op jit(solution)/shard_map/ppermute | solution.py:247
  26.8 12.2 %collective-permute-start.3 = (f32[32,1024]{1,0:T(8,128)S(1)}, f32[32,1024]{1,0:T(8,128)S(1)}, u32[]{:S(2)}, u32[]{:S(2)}) collective-permute-start(f32[32,1024]{1,0:T(8,128)S(1)} %get-tuple-element.31), channel_id=1, source_target_pairs={{0,16},{2,18},{4,20},{6,22},{8,24},{10,26},{12,28},{14,30},{16,0},... | collective-permute-start | bytes 393224 | tf_op jit(solution)/shard_map/ppermute | solution.py:247
  29.4 9.6 %collective-permute-start.4 = (f32[32,1024]{1,0:T(8,128)S(1)}, f32[32,1024]{1,0:T(8,128)S(1)}, u32[]{:S(2)}, u32[]{:S(2)}) collective-permute-start(f32[32,1024]{1,0:T(8,128)S(1)} %get-tuple-element.32), channel_id=1, source_target_pairs={{0,24},{2,26},{4,28},{6,30},{8,16},{10,18},{12,20},{14,22},{16,8},... | collective-permute-start | bytes 393224 | tf_op jit(solution)/shard_map/ppermute | solution.py:247
  39.0 4.8 %collective-permute-start.5 = (bf16[32,1024]{1,0:T(8,128)(2,1)S(1)}, bf16[32,1024]{1,0:T(8,128)(2,1)S(1)}, u32[]{:S(2)}, u32[]{:S(2)}) collective-permute-start(bf16[32,1024]{1,0:T(8,128)(2,1)S(1)} %shard_map.104.refs_0_), channel_id=1, source_target_pairs={{0,8},{2,10},{4,12},{6,14},{8,0},{10,2},{12,4},{14,6},{16,24},{18,... | collective-permute-start | bytes 196616 | tf_op jit(solution)/shard_map/ppermute | solution.py:247
  41.0 6.1 %collective-permute-start.6 = (bf16[32,1024]{1,0:T(8,128)(2,1)S(1)}, bf16[32,1024]{1,0:T(8,128)(2,1)S(1)}, u32[]{:S(2)}, u32[]{:S(2)}) collective-permute-start(bf16[32,1024]{1,0:T(8,128)(2,1)S(1)} %shard_map.104.refs_0_), channel_id=1, source_target_pairs={{0,16},{2,18},{4,20},{6,22},{8,24},{10,26},{12,28},{14,30},{16,0},... | collective-permute-start | bytes 196616 | tf_op jit(solution)/shard_map/ppermute | solution.py:247
  42.1 6.2 %collective-permute-start.7 = (bf16[32,1024]{1,0:T(8,128)(2,1)S(1)}, bf16[32,1024]{1,0:T(8,128)(2,1)S(1)}, u32[]{:S(2)}, u32[]{:S(2)}) collective-permute-start(bf16[32,1024]{1,0:T(8,128)(2,1)S(1)} %shard_map.104.refs_0_), channel_id=1, source_target_pairs={{0,24},{2,26},{4,28},{6,30},{8,16},{10,18},{12,20},{14,22},{16,8},... | collective-permute-start | bytes 196616 | tf_op jit(solution)/shard_map/ppermute | solution.py:247
  48.9 25.3 %copy-start.5 = (f32[512,1024]{1,0:T(8,128)S(1)}, f32[512,1024]{1,0:T(8,128)}, u32[]{:S(2)}) copy-start(f32[512,1024]{1,0:T(8,128)} %moment.1) | copy-start | bytes 6291460
  56.0 16.3 %collective-permute-start.10 = (bf16[512,1024]{1,0:T(8,128)(2,1)S(1)}, bf16[512,1024]{1,0:T(8,128)(2,1)S(1)}, u32[]{:S(2)}, u32[]{:S(2)}) collective-permute-start(bf16[512,1024]{1,0:T(8,128)(2,1)S(1)} %collective-permute-done.8.bmine), channel_id=1, source_target_pairs={{0,2},{2,0},{4,6},{6,4},{8,10},{10,8},{12,14},{14,12},{16,18},{18,... | collective-permute-start | bytes 3145736 | tf_op jit(solution)/shard_map/ppermute | solution.py:247
  56.0 16.4 %collective-permute-start.11 = (f32[256,1024]{1,0:T(8,128)S(1)}, f32[256,1024]{1,0:T(8,128)S(1)}, u32[]{:S(2)}, u32[]{:S(2)}) collective-permute-start(f32[256,1024]{1,0:T(8,128)S(1)} %collective-permute-done.9.smine), channel_id=1, source_target_pairs={{0,2},{2,0},{4,6},{6,4},{8,10},{10,8},{12,14},{14,12},{16,18},{18,... | collective-permute-start | bytes 3145736 | tf_op jit(solution)/shard_map/ppermute | solution.py:247
  56.6 9.2 %collective-permute-start.12 = (bf16[128,1024]{1,0:T(8,128)(2,1)S(1)}, bf16[128,1024]{1,0:T(8,128)(2,1)S(1)}, u32[]{:S(2)}, u32[]{:S(2)}) collective-permute-start(bf16[128,1024]{1,0:T(8,128)(2,1)S(1)} %shard_map.105.refs_0_), channel_id=1, source_target_pairs={{0,4},{2,6},{4,0},{6,2},{8,12},{10,14},{12,8},{14,10},{16,20},{18,... | collective-permute-start | bytes 786440 | tf_op jit(solution)/shard_map/ppermute | solution.py:247
  58.3 13.6 %collective-permute-start.15 = (bf16[128,1024]{1,0:T(8,128)(2,1)S(1)}, bf16[128,1024]{1,0:T(8,128)(2,1)S(1)}, u32[]{:S(2)}, u32[]{:S(2)}) collective-permute-start(bf16[128,1024]{1,0:T(8,128)(2,1)S(1)} %shard_map.105.refs_0_), channel_id=1, source_target_pairs={{0,1},{1,0},{2,3},{3,2},{4,5},{5,4},{6,7},{7,6},{8,9},{9,8},{10,11... | collective-permute-start | bytes 786440 | tf_op jit(solution)/shard_map/ppermute | solution.py:250
  59.8 12.0 %collective-permute-start.16 = (bf16[128,1024]{1,0:T(8,128)(2,1)S(1)}, bf16[128,1024]{1,0:T(8,128)(2,1)S(1)}, u32[]{:S(2)}, u32[]{:S(2)}) collective-permute-start(bf16[128,1024]{1,0:T(8,128)(2,1)S(1)} %shard_map.105.refs_0_), channel_id=1, source_target_pairs={{0,5},{1,4},{2,7},{3,6},{4,1},{5,0},{6,3},{7,2},{8,13},{9,12},{10,... | collective-permute-start | bytes 786440 | tf_op jit(solution)/shard_map/ppermute | solution.py:254
  65.7 8.1 %collective-permute-start.13 = (bf16[128,1024]{1,0:T(8,128)(2,1)S(1)}, bf16[128,1024]{1,0:T(8,128)(2,1)S(1)}, u32[]{:S(2)}, u32[]{:S(2)}) collective-permute-start(bf16[128,1024]{1,0:T(8,128)(2,1)S(1)} %shard_map.105.refs_0_), channel_id=1, source_target_pairs={{0,2},{2,0},{4,6},{6,4},{8,10},{10,8},{12,14},{14,12},{16,18},{18,... | collective-permute-start | bytes 786440 | tf_op jit(solution)/shard_map/ppermute | solution.py:247
  71.8 2.0 %collective-permute-start.14 = (bf16[128,1024]{1,0:T(8,128)(2,1)S(1)}, bf16[128,1024]{1,0:T(8,128)(2,1)S(1)}, u32[]{:S(2)}, u32[]{:S(2)}) collective-permute-start(bf16[128,1024]{1,0:T(8,128)(2,1)S(1)} %collective-permute-done.12.refs_1_), channel_id=1, source_target_pairs={{0,2},{2,0},{4,6},{6,4},{8,10},{10,8},{12,14},{14,12},{16,18},{18,... | collective-permute-start | bytes 786440 | tf_op jit(solution)/shard_map/ppermute | solution.py:247
  71.8 2.0 %collective-permute-start.17 = (bf16[128,1024]{1,0:T(8,128)(2,1)S(1)}, bf16[128,1024]{1,0:T(8,128)(2,1)S(1)}, u32[]{:S(2)}, u32[]{:S(2)}) collective-permute-start(bf16[128,1024]{1,0:T(8,128)(2,1)S(1)} %collective-permute-done.15.refs_4_), channel_id=1, source_target_pairs={{0,2},{2,0},{4,6},{6,4},{8,10},{10,8},{12,14},{14,12},{16,18},{18,... | collective-permute-start | bytes 786440 | tf_op jit(solution)/shard_map/ppermute | solution.py:247
  72.3 1.8 %collective-permute-start.18 = (bf16[128,1024]{1,0:T(8,128)(2,1)S(1)}, bf16[128,1024]{1,0:T(8,128)(2,1)S(1)}, u32[]{:S(2)}, u32[]{:S(2)}) collective-permute-start(bf16[128,1024]{1,0:T(8,128)(2,1)S(1)} %collective-permute-done.16.refs_5_), channel_id=1, source_target_pairs={{0,2},{2,0},{4,6},{6,4},{8,10},{10,8},{12,14},{14,12},{16,18},{18,... | collective-permute-start | bytes 786440 | tf_op jit(solution)/shard_map/ppermute | solution.py:247
  74.1 3.7 %copy-start.2 = (f32[512,1024]{1,0:T(8,128)S(1)}, f32[512,1024]{1,0:T(8,128)}, u32[]{:S(2)}) copy-start(f32[512,1024]{1,0:T(8,128)} %basis.3) | copy-start | bytes 6291460
  74.1 3.7 %copy-start.3 = (f32[512,1024]{1,0:T(8,128)S(1)}, f32[512,1024]{1,0:T(8,128)}, u32[]{:S(2)}) copy-start(f32[512,1024]{1,0:T(8,128)} %stat.3) | copy-start | bytes 6291460
  76.2 20.8 %collective-permute-start.19 = (bf16[512,512]{1,0:T(8,128)(2,1)S(1)}, bf16[512,512]{1,0:T(8,128)(2,1)S(1)}, u32[]{:S(2)}, u32[]{:S(2)}) collective-permute-start(bf16[512,512]{1,0:T(8,128)(2,1)S(1)} %get-tuple-element.43), channel_id=1, source_target_pairs={{0,1},{1,0},{2,3},{3,2},{4,5},{5,4},{6,7},{7,6},{8,9},{9,8},{10,11... | collective-permute-start | bytes 1572872 | tf_op jit(solution)/shard_map/ppermute | solution.py:250
  79.5 17.5 %copy-start.7 = (f32[1024,512]{1,0:T(8,128)S(1)}, f32[1024,512]{1,0:T(8,128)}, u32[]{:S(2)}) copy-start(f32[1024,512]{1,0:T(8,128)} %second.1) | copy-start | bytes 6291460
  102.1 18.3 %collective-permute-start.20 = (bf16[512,512]{1,0:T(8,128)(2,1)S(1)}, bf16[512,512]{1,0:T(8,128)(2,1)S(1)}, u32[]{:S(2)}, u32[]{:S(2)}) collective-permute-start(bf16[512,512]{1,0:T(8,128)(2,1)S(1)} %get-tuple-element.45), channel_id=1, source_target_pairs={{0,1},{1,0},{2,3},{3,2},{4,5},{5,4},{6,7},{7,6},{8,9},{9,8},{10,11... | collective-permute-start | bytes 1572872 | tf_op jit(solution)/shard_map/ppermute | solution.py:250

commit v3 on v2

--- a/solution.py
+++ b/solution.py
@@ -51,13 +51,27 @@
     )(*operands)
 
 
-def state_parts_kernel(where, left, right, stat_left, stat_right, bases, stats):
-    half = left.shape[0]
-    rows = stat_left.shape[1]
-    bases[:half] = left[...].astype(HALF)
-    bases[half:] = right[...].astype(HALF)
-    stats[:, :rows] = stat_left[...]
-    stats[:, rows:] = stat_right[...]
+TILES = 4
+UPPER = [(i, j) for i in range(TILES) for j in range(i, TILES)]
+
+
+def bases_kernel(where, left, right, out):
+    out[0] = left[...].astype(HALF)
+    out[1] = right[...].astype(HALF)
+
+
+def stats_kernel(where, left, right, out):
+    size = left.shape[0] // TILES
+    count = len(UPPER) // 2
+    for core in range(2):
+
+        @pl.when(where[1] == core)
+        def _():
+            for place, (i, j) in enumerate(UPPER[core * count : (core + 1) * count]):
+                for side, stat in enumerate((left, right)):
+                    out[side, :, place * size : (place + 1) * size] = stat[
+                        i * size : (i + 1) * size, j * size : (j + 1) * size
+                    ]
 
 
 def first_sum_kernel(where, group, came, kept, sent):
@@ -90,20 +104,21 @@
         out[tile(z ^ k, size)] = part[...]
 
 
-def place_basis(where, out, own, mine, theirs, begin, natural):
+def place_basis(where, out, own, mine, theirs, side, natural):
     rows = own.shape[0]
     half = rows // 2
     position, core = where[0], where[1]
     first = position if natural else 0
     out[tile(first, rows)] = own[...].astype(HALF)
     other = (1 - first) * 2
-    out[tile(other + core, half)] = mine[begin : begin + half]
-    out[tile(other + 1 - core, half)] = theirs[begin : begin + half]
-
-
-def place_stat(where, out, own, mine, theirs, begin, natural):
+    out[tile(other + core, half)] = mine[side]
+    out[tile(other + 1 - core, half)] = theirs[side]
+
+
+def place_stat(where, out, own, mine, theirs, side, natural):
     rows = own.shape[0]
-    half = rows // 2
+    size = rows // TILES
+    count = len(UPPER) // 2
     position, core = where[0], where[1]
     first = position if natural else 0
     here, there = tile(first, rows), tile(1 - first, rows)
@@ -111,9 +126,14 @@
     cross = own[:, tile(1 - position, rows)]
     out[here, there] = cross
     out[there, here] = cross.T
-    other = (1 - first) * 2
-    out[tile(other + core, half), there] = mine[:, begin : begin + rows]
-    out[tile(other + 1 - core, half), there] = theirs[:, begin : begin + rows]
+    base = (1 - first) * TILES
+    for place, (i, j) in enumerate(UPPER):
+        from_mine = core == place // count
+        columns = slice(place % count * size, (place % count + 1) * size)
+        value = jnp.where(from_mine, mine[side, :, columns], theirs[side, :, columns])
+        out[tile(base + i, size), tile(base + j, size)] = value
+        if i != j:
+            out[tile(base + j, size), tile(base + i, size)] = value.T
 
 
 def left_state_kernel(where, basis, bmine, btheirs, stat, smine, stheirs, rot, turned, full):
@@ -122,16 +142,17 @@
     turned[...] = rot[...].T
 
 
-def right_state_kernel(where, basis, bmine, btheirs, stat, smine, stheirs, rot, near, full):
+def right_state_kernel(where, basis, bmine, btheirs, stat, smine, stheirs, rot, near, back, full):
     rows = basis.shape[0]
-    place_basis(where, rot, basis, bmine, btheirs, rows // 2, True)
-    place_stat(where, full, stat, smine, stheirs, rows, True)
+    place_basis(where, rot, basis, bmine, btheirs, 1, True)
+    place_stat(where, full, stat, smine, stheirs, 1, True)
     near[:, :rows] = rot[:, tile(where[0], rows)]
     near[:, rows:] = rot[:, tile(1 - where[0], rows)]
+    back[...] = near[...].T
 
 
 def moment_kernel(where, moment, near, *refs):
-    parts, (gradient, ours, others, sem) = refs[:-4], refs[-4:]
+    parts, (gradient, turned, ours, others, sem) = refs[:-5], refs[-5:]
     core, x = where[1], where[2]
     size = parts[0].shape[0]
     rows = moment.shape[0]
@@ -155,6 +176,10 @@
         here = slice(i * step, (i + 1) * step)
         others[:, here] = matmul(half, near[:, rows + i * step : rows + (i + 1) * step]).astype(HALF)
         ours[:, here] = matmul(half, near[:, here]).astype(HALF)
+    step = gradient.shape[0] // 4
+    for i in range(4):
+        here = slice(i * step, (i + 1) * step)
+        turned[:, here] = gradient[here].T
 
 
 def adam_kernel(gradient, near, rot, turned, mine, came, second, new, kept, sent, block, scaled):
@@ -177,59 +202,49 @@
         kept[:, here] = matmul(rot[:rows], scaled[:, here]).astype(HALF)
 
 
-def update_kernel(mine, came, near, out):
+def update_kernel(mine, came, back, out):
     rows, width = out.shape
     step = width // 4
     for here in [slice(i * step, (i + 1) * step) for i in range(4)]:
-        total = matmul(mine[...], near[here, :rows], 1, 1) + matmul(
-            came[...], near[here, rows:], 1, 1
-        )
+        total = matmul(mine[...], back[:rows, here]) + matmul(came[...], back[rows:, here])
         out[:, here] = (total * (1.0 / width)).astype(HALF)
 
 
-def refresh_kernel(natural, where, gradient, rot, stat, out, stat_in, turned, half, gram, sem):
-    width = gradient.shape[0]
+def refresh_kernel(natural, where, one, two, rot, stat, out, half, first, second, turned, gram):
+    width = one.shape[0]
     rows = out.shape[0]
     step = width // 4
     columns = [slice(i * step, (i + 1) * step) for i in range(4)]
-    copies = [
-        pltpu.make_async_copy(stat.at[:, here], stat_in.at[:, here], sem.at[i])
-        for i, here in enumerate(columns)
-    ]
-    for copy in copies:
-        copy.start()
-    if natural:
-        for here in columns:
-            turned[:, here] = gradient[here].T
-    for here, copy in zip(columns, copies):
-        if natural:
-            grads = matmul(turned[...], gradient[:, here])
-        else:
-            grads = matmul(gradient[...], gradient[here], 1, 1)
-        copy.wait()
-        half[:, here] = (BETA_STAT * stat_in[:, here] + (1.0 - BETA_STAT) * grads).astype(HALF)
+    for here in columns:
+        grads = matmul(one[...], two[:, here])
+        half[:, here] = (BETA_STAT * stat[:, here] + (1.0 - BETA_STAT) * grads).astype(HALF)
     for here in columns:
         product = matmul(half[...], rot[:, here])
         square = jnp.sum(product * product, axis=0, keepdims=True) * (1.0 / width)
-        turned[:, here] = (product * lax.rsqrt(square + NORM_EPS)).astype(HALF)
-
-    def improved(current, kept, result, dtype):
+        start = (product * lax.rsqrt(square + NORM_EPS)).astype(HALF)
+        first[:, here] = start
+        turned[here] = start.T
+
+    def improved(current, kept, result, dtype, again):
         size = result.shape[0]
         for here in columns:
-            gram[:size, here] = (
-                matmul(current[kept], current[here], 1, 1) * (1.0 / width)
-            ).astype(HALF)
+            gram[:size, here] = (matmul(current[kept], turned[:, here]) * (1.0 / width)).astype(
+                HALF
+            )
         for here in columns:
-            result[:, here] = (
+            value = (
                 1.5 * current[kept, here].astype(FULL)
                 - 0.5 * matmul(gram[:size], current[:, here])
             ).astype(dtype)
-
-    current, following = turned, half
+            result[:, here] = value
+            if again:
+                turned[here] = value.T
+
+    current, following = first, second
     for _ in range(NS_ITERS - 1):
-        improved(current, slice(0, width), following, HALF)
+        improved(current, slice(0, width), following, HALF, True)
         current, following = following, current
-    improved(current, tile(where[0], rows) if natural else slice(0, rows), out, FULL)
+    improved(current, tile(where[0], rows) if natural else slice(0, rows), out, FULL, False)
 
 
 def fast_body(group_grads, moment, second, stat_left, stat_right, basis_left, basis_right):
@@ -253,24 +268,20 @@
         pairs = [(i, i ^ 5) for i in range(32)]
         return lax.ppermute(value, ("dp", "shard"), pairs)
 
-    bases_sent, stats_sent = pl.pallas_call(
-        state_parts_kernel,
-        out_shape=[shaped((rows, width), HALF), shaped((half, width), FULL)],
+    step = half // 2
+    (bases_sent,) = pl.pallas_call(
+        bases_kernel,
+        out_shape=[shaped((2, half, width), HALF)],
         grid_spec=pltpu.PrefetchScalarGridSpec(
             num_scalar_prefetch=1,
-            grid=(1,),
-            in_specs=[pl.BlockSpec((half, width), lambda i, where: (where[1], 0))] * 2
-            + [pl.BlockSpec((half, rows), lambda i, where: (where[1], where[0]))] * 2,
-            out_specs=[
-                pl.BlockSpec((rows, width), lambda i, where: (0, 0)),
-                pl.BlockSpec((half, width), lambda i, where: (0, 0)),
-            ],
+            grid=(2,),
+            in_specs=[pl.BlockSpec((step, width), lambda i, where: (where[1] * 2 + i, 0))] * 2,
+            out_specs=[pl.BlockSpec((2, step, width), lambda i, where: (0, i, 0))],
         ),
         compiler_params=pltpu.CompilerParams(vmem_limit_bytes=56 * 2**20),
         cost_estimate=pl.CostEstimate(flops=0, bytes_accessed=2**22, transcendentals=0),
-    )(where, basis_left, basis_right, stat_left, stat_right)
+    )(where, basis_left, basis_right)
     bases_mine = shard_swap(bases_sent)
-    stats_mine = shard_swap(stats_sent)
 
     raw = lax.dynamic_slice_in_dim(group_grads[0], (1 - core) * half, half, 0)
     came = dp_swap(raw, 1)
@@ -289,6 +300,21 @@
         [SMEM, VMEM, VMEM],
         moved=2**20,
     )
+    (stats_sent,) = pl.pallas_call(
+        stats_kernel,
+        out_shape=[shaped((2, quarter, 5 * quarter), FULL)],
+        grid_spec=pltpu.PrefetchScalarGridSpec(
+            num_scalar_prefetch=1,
+            grid=(1,),
+            in_specs=[pl.BlockSpec((rows, rows), lambda i, where: (0, where[0]))] * 2,
+            out_specs=[
+                pl.BlockSpec((2, quarter, 5 * quarter), lambda i, where: (0, 0, 0)),
+            ],
+        ),
+        compiler_params=pltpu.CompilerParams(vmem_limit_bytes=56 * 2**20),
+        cost_estimate=pl.CostEstimate(flops=0, bytes_accessed=2**22, transcendentals=0),
+    )(where, stat_left, stat_right)
+    stats_mine = shard_swap(stats_sent)
     pieces = [dp_swap(value, 4 * (k + 1)) for k, value in enumerate(sent)]
     (piece,) = call(
         third_sum_kernel, [shaped((chunk, width), HALF)], (own, *pieces), [VMEM] * 4, moved=2**19
@@ -318,18 +344,18 @@
         [SMEM] + [VMEM] * 6,
         moved=2**24,
     )
-    right_rot, right_near, right_stat = call(
+    right_rot, right_near, right_back, right_stat = call(
         right_state_kernel,
-        state_outs,
+        state_outs[:1] + state_outs,
         (where, basis_right, *bases, stat_right, *stats),
         [SMEM] + [VMEM] * 6,
         moved=2**24,
     )
 
     ordered = [parts[0], parts[1], swapped[0], swapped[1], parts[2], parts[3], swapped[2], swapped[3]]
-    gradient, moment_mine, moment_sent = call(
+    gradient, gradient_turned, moment_mine, moment_sent = call(
         moment_kernel,
-        [shaped((width, width), HALF)] + [shaped((rows, rows), HALF)] * 2,
+        [shaped((width, width), HALF)] * 2 + [shaped((rows, rows), HALF)] * 2,
         (where, moment, right_near, *ordered),
         [SMEM, VMEM, VMEM] + [ANY] * 8,
         [pltpu.SemaphoreType.DMA((8,))],
@@ -338,25 +364,19 @@
     )
     moment_came = shard_swap(moment_sent)
 
-    def refreshed(natural, rot, stat):
+    def refreshed(natural, one, two, rot, stat):
         (out,) = call(
             functools.partial(refresh_kernel, natural),
             [shaped((rows, width), FULL)],
-            (where, gradient, rot, stat),
-            [SMEM, VMEM, VMEM, ANY],
-            [
-                pltpu.VMEM((width, width), FULL),
-                pltpu.VMEM((width, width), HALF),
-                pltpu.VMEM((width, width), HALF),
-                pltpu.VMEM((width, width), HALF),
-                pltpu.SemaphoreType.DMA((4,)),
-            ],
+            (where, one, two, rot, stat),
+            [SMEM] + [VMEM] * 4,
+            [pltpu.VMEM((width, width), HALF)] * 5,
             flops=5 * unit,
             moved=2**23,
         )
         return out
 
-    left_new = refreshed(False, left_rot, left_stat)
+    left_new = refreshed(False, gradient, gradient_turned, left_rot, left_stat)
     second_new, back_mine, back_sent = call(
         adam_kernel,
         [shaped((width, rows), FULL)] + [shaped((rows, rows), HALF)] * 2,
@@ -367,11 +387,11 @@
         moved=2**23,
     )
     back_came = shard_swap(back_sent)
-    right_new = refreshed(True, right_rot, right_stat)
+    right_new = refreshed(True, gradient_turned, gradient, right_rot, right_stat)
     (update,) = call(
         update_kernel,
         [shaped((rows, width), HALF)],
-        (back_mine, back_came, right_near),
+        (back_mine, back_came, right_back),
         [VMEM] * 3,
         flops=unit // 2,
         moved=2**22,

time: 123 us -> 107 us (0.87)
  waiting for transfers between devices: 45.6 us -> 34.9 us
  Pallas kernels: 53.9 us -> 49 us
    ppermute x5, waiting for transfers between devices: 13.3 us -> 5.96 us  [shard_swap(): return lax.ppermute(value, 'shard', [(0, 1), (1, 0)])]
    pallas_call x11, Pallas kernels: 49.7 us -> 42.6 us  [call(): pl.pallas_call(kernel, out_shape=outs, in_specs=specs, out_specs=[VMEM] *...]
    ppermute x15, waiting for transfers between devices: 32.3 us -> 28.9 us  [dp_swap(): return lax.ppermute(value, 'dp', [(i, i ^ distance) for i in range(16)])]
    pallas_call x1 -> x2, Pallas kernels: 4.19 us -> 6.4 us  [the longest x1 3.23 us: fast_body(): pl.pallas_call(stats_kernel, out_shape=[shaped((2, quarter, 5 * quarter),...]
    ppermute x1, starting transfers between devices: 0.25 us -> 1.49 us  [cross_swap(): return lax.ppermute(value, ('dp', 'shard'), pairs)]
  transfers between devices with their start and end apart: 21 -> 21, of which waited for: 10 -> 8; matrix products, arithmetic and copies ran while one was open for 0% -> 1% of each run, Pallas kernels for 36% -> 37%
where the time goes in v3:
time: 107 us
  Pallas kernels  49 us (46%)
  waiting for transfers between devices  34.9 us (33%)
  starting transfers between devices  20.8 us (19%)
  local copies, waits for them, and re-layouts  1.13 us (1%)
    pallas_call x11, Pallas kernels, call(): pl.pallas_call(kernel, out_shape=outs, in_specs=specs, out_specs=[VMEM] *...  42.6 us
    ppermute x15, waiting for transfers between devices, dp_swap(): return lax.ppermute(value, 'dp', [(i, i ^ distance) for i in range(16)])  28.9 us
    ppermute x15, starting transfers between devices, dp_swap(): return lax.ppermute(value, 'dp', [(i, i ^ distance) for i in range(16)])  13.7 us
    ppermute x5, waiting for transfers between devices, shard_swap(): return lax.ppermute(value, 'shard', [(0, 1), (1, 0)])  5.96 us
    ppermute x5, starting transfers between devices, shard_swap(): return lax.ppermute(value, 'shard', [(0, 1), (1, 0)])  5.64 us
    pallas_call x1, Pallas kernels, fast_body(): pl.pallas_call(stats_kernel, out_shape=[shaped((2, quarter, 5 * quarter),...  3.23 us
    pallas_call x1, Pallas kernels, fast_body(): pl.pallas_call(bases_kernel, out_shape=[shaped((2, half, width), HALF)],...  3.18 us
  transfers between devices with their start and end apart: 21, of which 8 were waited for; matrix products, arithmetic and copies ran while one was open for 1% of the time, Pallas kernels for 37%

profile of v3, /device:TPU:0, one launch (start us, length us, event | category | flops | bytes accessed | tf_op | source)
XLA Modules:
  0.0 107.3 jit_solution(9099834052229711057)
XLA Ops:
  0.6 1.1 %dynamic-slice_bitcast_fusion = bf16[256,1024]{1,0:T(8,128)(2,1)S(1)} fusion(bf16[1,512,1024]{2,1,0:T(8,128)(2,1)} %group.1, s32[]{:T(128)S(6)} %select_n.3), kind=kLoop, calls=%fused_computation | loop fusion | bytes 1048580 | tf_op jit(solution)/shard_map/dynamic_slice | solution.py:286
  1.7 0.5 collective-permute-start
  2.2 0.6 pad_add_fusion.where
  2.8 3.2 %shard_map.106 = bf16[2,256,1024]{2,1,0:T(8,128)(2,1)} custom-call(s32[4]{0:T(128)} %pad_add_fusion.where, f32[512,1024]{1,0:T(8,128)} %basis.3, f32[512,1024]{1,0:T(8,128)} %basis.2), custom_call_target="tpu_custom_call" | custom-call | bytes 4194304 | tf_op jit(solution)/shard_map/pallas_call | solution.py:272
  6.0 2.5 %collective-permute-start.8 = (bf16[2,256,1024]{2,1,0:T(8,128)(2,1)}, bf16[2,256,1024]{2,1,0:T(8,128)(2,1)S(1)}, u32[]{:S(2)}, u32[]{:S(2)}) collective-permute-start(bf16[2,256,1024]{2,1,0:T(8,128)(2,1)} %shard_map.106), channel_id=1, source_target_pairs={{0,1},{1,0},{2,3},{3,2},{4,5},{5,4},{6,7},{7,6},{8,9},{9,8},{10,11... | collective-permute-start | bytes 3145736 | tf_op jit(solution)/shard_map/ppermute | solution.py:265
  8.5 0.0 collective-permute-done.came
  8.5 0.0 copy-done.4
  8.5 0.0 copy-done.6
  8.6 0.7 shard_map.102
  9.2 0.0 copy-start.7
  9.2 1.6 %collective-permute-start.1 = (f32[128,1024]{1,0:T(8,128)S(1)}, f32[128,1024]{1,0:T(8,128)S(1)}, u32[]{:S(2)}, u32[]{:S(2)}) collective-permute-start(f32[128,1024]{1,0:T(8,128)S(1)} %get-tuple-element.28), channel_id=1, source_target_pairs={{0,4},{2,6},{4,0},{6,2},{8,12},{10,14},{12,8},{14,10},{16,20},{18,... | collective-permute-start | bytes 1572872 | tf_op jit(solution)/shard_map/ppermute | solution.py:262
  10.8 3.2 %shard_map.107 = f32[2,128,640]{2,1,0:T(8,128)} custom-call(s32[4]{0:T(128)} %pad_add_fusion.where, f32[512,1024]{1,0:T(8,128)} %stat.3, f32[512,1024]{1,0:T(8,128)} %stat.2), custom_call_target="tpu_custom_call" | custom-call | bytes 4194304 | tf_op jit(solution)/shard_map/pallas_call | solution.py:303
  14.0 0.5 collective-permute-start.9
  14.5 8.8 %collective-permute-done.1.came = f32[128,1024]{1,0:T(8,128)S(1)} collective-permute-done((f32[128,1024]{1,0:T(8,128)S(1)}, f32[128,1024]{1,0:T(8,128)S(1)}, u32[]{:S(2)}, u32[]{:S(2)}) %collective-permute-start.1) | collective-permute-done | bytes 524320 | tf_op jit(solution)/shard_map/ppermute | solution.py:262
  23.3 0.0 copy-done.7
  23.3 0.6 shard_map.103
  23.9 1.6 %collective-permute-start.2 = (f32[32,1024]{1,0:T(8,128)S(1)}, f32[32,1024]{1,0:T(8,128)S(1)}, u32[]{:S(2)}, u32[]{:S(2)}) collective-permute-start(f32[32,1024]{1,0:T(8,128)S(1)} %get-tuple-element.30), channel_id=1, source_target_pairs={{0,8},{2,10},{4,12},{6,14},{8,0},{10,2},{12,4},{14,6},{16,24},{18,... | collective-permute-start | bytes 393224 | tf_op jit(solution)/shard_map/ppermute | solution.py:262
  25.6 2.6 %collective-permute-start.3 = (f32[32,1024]{1,0:T(8,128)S(1)}, f32[32,1024]{1,0:T(8,128)S(1)}, u32[]{:S(2)}, u32[]{:S(2)}) collective-permute-start(f32[32,1024]{1,0:T(8,128)S(1)} %get-tuple-element.31), channel_id=1, source_target_pairs={{0,16},{2,18},{4,20},{6,22},{8,24},{10,26},{12,28},{14,30},{16,0},... | collective-permute-start | bytes 393224 | tf_op jit(solution)/shard_map/ppermute | solution.py:262
  28.2 0.2 collective-permute-start.4
  28.4 2.0 %collective-permute-done.2.one = f32[32,1024]{1,0:T(8,128)S(1)} collective-permute-done((f32[32,1024]{1,0:T(8,128)S(1)}, f32[32,1024]{1,0:T(8,128)S(1)}, u32[]{:S(2)}, u32[]{:S(2)}) %collective-permute-start.2) | collective-permute-done | bytes 131104 | tf_op jit(solution)/shard_map/ppermute | solution.py:262
  30.4 7.6 %collective-permute-done.3.two = f32[32,1024]{1,0:T(8,128)S(1)} collective-permute-done((f32[32,1024]{1,0:T(8,128)S(1)}, f32[32,1024]{1,0:T(8,128)S(1)}, u32[]{:S(2)}, u32[]{:S(2)}) %collective-permute-start.3) | collective-permute-done | bytes 131104 | tf_op jit(solution)/shard_map/ppermute | solution.py:262
  38.0 0.0 collective-permute-done.4.three
  38.1 2.0 %collective-permute-start.5 = (bf16[32,1024]{1,0:T(8,128)(2,1)S(1)}, bf16[32,1024]{1,0:T(8,128)(2,1)S(1)}, u32[]{:S(2)}, u32[]{:S(2)}) collective-permute-start(bf16[32,1024]{1,0:T(8,128)(2,1)S(1)} %shard_map.104.refs_0_), channel_id=1, source_target_pairs={{0,8},{2,10},{4,12},{6,14},{8,0},{10,2},{12,4},{14,6},{16,24},{18,... | collective-permute-start | bytes 196616 | tf_op jit(solution)/shard_map/ppermute | solution.py:262
  40.1 1.1 %collective-permute-start.6 = (bf16[32,1024]{1,0:T(8,128)(2,1)S(1)}, bf16[32,1024]{1,0:T(8,128)(2,1)S(1)}, u32[]{:S(2)}, u32[]{:S(2)}) collective-permute-start(bf16[32,1024]{1,0:T(8,128)(2,1)S(1)} %shard_map.104.refs_0_), channel_id=1, source_target_pairs={{0,16},{2,18},{4,20},{6,22},{8,24},{10,26},{12,28},{14,30},{16,0},... | collective-permute-start | bytes 196616 | tf_op jit(solution)/shard_map/ppermute | solution.py:262
  41.2 1.4 %collective-permute-start.7 = (bf16[32,1024]{1,0:T(8,128)(2,1)S(1)}, bf16[32,1024]{1,0:T(8,128)(2,1)S(1)}, u32[]{:S(2)}, u32[]{:S(2)}) collective-permute-start(bf16[32,1024]{1,0:T(8,128)(2,1)S(1)} %shard_map.104.refs_0_), channel_id=1, source_target_pairs={{0,24},{2,26},{4,28},{6,30},{8,16},{10,18},{12,20},{14,22},{16,8},... | collective-permute-start | bytes 196616 | tf_op jit(solution)/shard_map/ppermute | solution.py:262
  42.6 0.5 collective-permute-done.5.refs_1_
  43.0 3.3 %collective-permute-done.6.refs_2_ = bf16[32,1024]{1,0:T(8,128)(2,1)S(1)} collective-permute-done((bf16[32,1024]{1,0:T(8,128)(2,1)S(1)}, bf16[32,1024]{1,0:T(8,128)(2,1)S(1)}, u32[]{:S(2)}, u32[]{:S(2)}) %collective-permute-start.6) | collective-permute-done | bytes 65568 | tf_op jit(solution)/shard_map/ppermute | solution.py:262
  46.3 1.1 collective-permute-done.7.refs_3_
  47.4 0.6 shard_map.105.refs_0_
  47.9 0.0 copy-start.5
  48.0 0.0 collective-permute-done.9.smine
  48.0 0.0 collective-permute-done.8.bmine
  48.0 0.1 collective-permute-start.10
  48.1 0.5 collective-permute-start.11
  48.5 1.5 %collective-permute-start.12 = (bf16[128,1024]{1,0:T(8,128)(2,1)S(1)}, bf16[128,1024]{1,0:T(8,128)(2,1)S(1)}, u32[]{:S(2)}, u32[]{:S(2)}) collective-permute-start(bf16[128,1024]{1,0:T(8,128)(2,1)S(1)} %shard_map.105.refs_0_), channel_id=1, source_target_pairs={{0,4},{2,6},{4,0},{6,2},{8,12},{10,14},{12,8},{14,10},{16,20},{18,... | collective-permute-start | bytes 786440 | tf_op jit(solution)/shard_map/ppermute | solution.py:262
  50.0 0.5 collective-permute-start.15
  50.5 1.5 %collective-permute-start.16 = (bf16[128,1024]{1,0:T(8,128)(2,1)S(1)}, bf16[128,1024]{1,0:T(8,128)(2,1)S(1)}, u32[]{:S(2)}, u32[]{:S(2)}) collective-permute-start(bf16[128,1024]{1,0:T(8,128)(2,1)S(1)} %shard_map.105.refs_0_), channel_id=1, source_target_pairs={{0,5},{1,4},{2,7},{3,6},{4,1},{5,0},{6,3},{7,2},{8,13},{9,12},{10,... | collective-permute-start | bytes 786440 | tf_op jit(solution)/shard_map/ppermute | solution.py:269
  52.0 5.7 %collective-permute-done.12.refs_1_ = bf16[128,1024]{1,0:T(8,128)(2,1)S(1)} collective-permute-done((bf16[128,1024]{1,0:T(8,128)(2,1)S(1)}, bf16[128,1024]{1,0:T(8,128)(2,1)S(1)}, u32[]{:S(2)}, u32[]{:S(2)}) %collective-permute-start.12) | collective-permute-done | bytes 262176 | tf_op jit(solution)/shard_map/ppermute | solution.py:262
  57.7 0.0 collective-permute-start.13
  57.7 6.0 %collective-permute-done.15.refs_4_ = bf16[128,1024]{1,0:T(8,128)(2,1)S(1)} collective-permute-done((bf16[128,1024]{1,0:T(8,128)(2,1)S(1)}, bf16[128,1024]{1,0:T(8,128)(2,1)S(1)}, u32[]{:S(2)}, u32[]{:S(2)}) %collective-permute-start.15) | collective-permute-done | bytes 262176 | tf_op jit(solution)/shard_map/ppermute | solution.py:265
  63.7 0.0 collective-permute-start.14
  63.7 0.0 collective-permute-done.16.refs_5_
  63.7 0.5 collective-permute-start.17
  64.2 0.0 collective-permute-done.11.stheirs
  64.2 0.1 collective-permute-start.18
  64.3 0.0 collective-permute-done.10.btheirs
  64.3 2.0 %shard_map.108 = (bf16[1024,1024]{1,0:T(8,128)(2,1)S(1)}, bf16[1024,1024]{1,0:T(8,128)(2,1)S(1)}, bf16[1024,1024]{1,0:T(8,128)(2,1)S(1)}, f32[1024,1024]{1,0:T(8,128)S(1)}) custom-call(s32[4]{0:T(128)S(1)} %copy-done.7, f32[512,1024]{1,0:T(8,128)S(1)} %copy-done.2, bf16[2,256,1024]{2,1,0:T(8,128)(2,1)S(1)} %collective-permute-done.8.bmine, ...), custom_call_target="tpu_custom_call" | custom-call | bytes 16777216 | tf_op jit(solution)/shard_map/pallas_call | solution.py:43
  66.3 0.0 collective-permute-done.13.refs_2_
  66.3 0.0 collective-permute-done.14.refs_3_
  66.3 0.0 collective-permute-done.17.refs_6_
  66.3 0.0 collective-permute-done.18.refs_7_
  66.3 0.0 copy-start.1
  66.3 0.0 copy-start.3
  66.3 2.3 %shard_map.109 = (bf16[1024,1024]{1,0:T(8,128)(2,1)S(1)}, bf16[1024,1024]{1,0:T(8,128)(2,1)S(1)}, bf16[512,512]{1,0:T(8,128)(2,1)S(1)}, bf16[512,512]{1,0:T(8,128)(2,1)S(1)}) custom-call(s32[4]{0:T(128)S(1)} %copy-done.7, f32[512,1024]{1,0:T(8,128)S(1)} %copy-done.5, bf16[1024,1024]{1,0:T(8,128)(2,1)S(1)} %get-tuple-element.35.near, ...), custom_call_target="tpu_custom_call" | custom-call | flops 1073741824 | bytes 8388608 | tf_op jit(solution)/shard_map/pallas_call | solution.py:43
  68.6 0.6 collective-permute-start.19
  69.2 1.8 %shard_map.110 = (bf16[1024,1024]{1,0:T(8,128)(2,1)S(1)}, bf16[1024,1024]{1,0:T(8,128)(2,1)S(1)}, f32[1024,1024]{1,0:T(8,128)S(1)}) custom-call(s32[4]{0:T(128)S(1)} %copy-done.7, f32[512,1024]{1,0:T(8,128)S(1)} %copy-done.3, bf16[2,256,1024]{2,1,0:T(8,128)(2,1)S(1)} %collective-permute-done.8.bmine, ...), custom_call_target="tpu_custom_call" | custom-call | bytes 16777216 | tf_op jit(solution)/shard_map/pallas_call | solution.py:43
  71.0 0.0 copy-start.8
  71.0 13.6 %shard_map.113 = f32[512,1024]{1,0:T(8,128)} custom-call(s32[4]{0:T(128)S(1)} %copy-done.7, bf16[1024,1024]{1,0:T(8,128)(2,1)S(1)} %get-tuple-element.37.gradient.one.two, bf16[1024,1024]{1,0:T(8,128)(2,1)S(1)} %get-tuple-element.46.two.one, bf16[1024,1024]{1,0:T(8,128)(2,1)S(1)} %get-tuple-element.38.rot, f32[1024,1024]{1,0:T(8,128)S(1)} %get-tuple-element.47.stat), custom_call_target="tpu_custom_call" | custom-call | flops 10737418240 | bytes 8388608 | tf_op jit(solution)/shard_map/pallas_call | solution.py:43
  84.6 0.0 collective-permute-done.19.came
  84.6 5.1 %shard_map.111 = (f32[1024,512]{1,0:T(8,128)}, bf16[512,512]{1,0:T(8,128)(2,1)S(1)}, bf16[512,512]{1,0:T(8,128)(2,1)S(1)}) custom-call(bf16[1024,1024]{1,0:T(8,128)(2,1)S(1)} %get-tuple-element.37.gradient.one.two, bf16[1024,1024]{1,0:T(8,128)(2,1)S(1)} %get-tuple-element.35.near, bf16[1024,1024]{1,0:T(8,128)(2,1)S(1)} %get-tuple-element.38.rot, ...), custom_call_target="tpu_custom_call" | custom-call | flops 4294967296 | bytes 8388608 | tf_op jit(solution)/shard_map/pallas_call | solution.py:43
  89.7 1.5 %collective-permute-start.20 = (bf16[512,512]{1,0:T(8,128)(2,1)S(1)}, bf16[512,512]{1,0:T(8,128)(2,1)S(1)}, u32[]{:S(2)}, u32[]{:S(2)}) collective-permute-start(bf16[512,512]{1,0:T(8,128)(2,1)S(1)} %get-tuple-element.43), channel_id=1, source_target_pairs={{0,1},{1,0},{2,3},{3,2},{4,5},{5,4},{6,7},{7,6},{8,9},{9,8},{10,11... | collective-permute-start | bytes 1572872 | tf_op jit(solution)/shard_map/ppermute | solution.py:265
  91.2 13.8 %shard_map.114 = f32[512,1024]{1,0:T(8,128)} custom-call(s32[4]{0:T(128)S(1)} %copy-done.7, bf16[1024,1024]{1,0:T(8,128)(2,1)S(1)} %get-tuple-element.46.two.one, bf16[1024,1024]{1,0:T(8,128)(2,1)S(1)} %get-tuple-element.37.gradient.one.two, bf16[1024,1024]{1,0:T(8,128)(2,1)S(1)} %get-tuple-element.48.rot, f32[1024,1024]{1,0:T(8,128)S(1)} %get-tuple-element.49.stat), custom_call_target="tpu_custom_call" | custom-call | flops 10737418240 | bytes 8388608 | tf_op jit(solution)/shard_map/pallas_call | solution.py:43
  105.0 0.0 collective-permute-done.20.came
  105.0 2.2 %shard_map.112 = bf16[512,1024]{1,0:T(8,128)(2,1)} custom-call(bf16[512,512]{1,0:T(8,128)(2,1)S(1)} %get-tuple-element.42.mine, bf16[512,512]{1,0:T(8,128)(2,1)S(1)} %collective-permute-done.20.came, bf16[1024,1024]{1,0:T(8,128)(2,1)S(1)} %get-tuple-element.44.back), custom_call_target="tpu_custom_call" | custom-call | flops 1073741824 | bytes 4194304 | tf_op jit(solution)/shard_map/pallas_call | solution.py:43
  (11 shorter events, 0.0 us)
Async XLA Ops:
  1.7 6.8 %collective-permute-start = (bf16[256,1024]{1,0:T(8,128)(2,1)S(1)}, bf16[256,1024]{1,0:T(8,128)(2,1)S(1)}, u32[]{:S(2)}, u32[]{:S(2)}) collective-permute-start(bf16[256,1024]{1,0:T(8,128)(2,1)S(1)} %dynamic-slice_bitcast_fusion), channel_id=1, source_target_pairs={{0,2},{2,0},{4,6},{6,4},{8,10},{10,8},{12,14},{14,12},{16,18},{18,... | collective-permute-start | bytes 1572872 | tf_op jit(solution)/shard_map/ppermute | solution.py:262
  2.8 5.7 %copy-start.4 = (bf16[1,512,1024]{2,1,0:T(8,128)(2,1)S(1)}, bf16[1,512,1024]{2,1,0:T(8,128)(2,1)}, u32[]{:S(2)}) copy-start(bf16[1,512,1024]{2,1,0:T(8,128)(2,1)} %group.1) | copy-start | bytes 3145732
  2.8 5.7 %copy-start.6 = (s32[4]{0:T(128)S(1)}, s32[4]{0:T(128)}, u32[]{:S(2)}) copy-start(s32[4]{0:T(128)} %pad_add_fusion.where) | copy-start | bytes 52
  6.0 42.0 %collective-permute-start.8 = (bf16[2,256,1024]{2,1,0:T(8,128)(2,1)}, bf16[2,256,1024]{2,1,0:T(8,128)(2,1)S(1)}, u32[]{:S(2)}, u32[]{:S(2)}) collective-permute-start(bf16[2,256,1024]{2,1,0:T(8,128)(2,1)} %shard_map.106), channel_id=1, source_target_pairs={{0,1},{1,0},{2,3},{3,2},{4,5},{5,4},{6,7},{7,6},{8,9},{9,8},{10,11... | collective-permute-start | bytes 3145736 | tf_op jit(solution)/shard_map/ppermute | solution.py:265
  9.2 14.1 %copy-start.7 = (s32[4]{0:T(128)S(1)}, s32[4]{0:T(128)}, u32[]{:S(2)}) copy-start(s32[4]{0:T(128)} %pad_add_fusion.where) | copy-start | bytes 52
  9.2 14.1 %collective-permute-start.1 = (f32[128,1024]{1,0:T(8,128)S(1)}, f32[128,1024]{1,0:T(8,128)S(1)}, u32[]{:S(2)}, u32[]{:S(2)}) collective-permute-start(f32[128,1024]{1,0:T(8,128)S(1)} %get-tuple-element.28), channel_id=1, source_target_pairs={{0,4},{2,6},{4,0},{6,2},{8,12},{10,14},{12,8},{14,10},{16,20},{18,... | collective-permute-start | bytes 1572872 | tf_op jit(solution)/shard_map/ppermute | solution.py:262
  10.8 53.5 %copy-start.2 = (f32[512,1024]{1,0:T(8,128)S(1)}, f32[512,1024]{1,0:T(8,128)}, u32[]{:S(2)}) copy-start(f32[512,1024]{1,0:T(8,128)} %basis.2) | copy-start | bytes 6291460
  14.0 50.3 %copy-start = (f32[512,1024]{1,0:T(8,128)S(1)}, f32[512,1024]{1,0:T(8,128)}, u32[]{:S(2)}) copy-start(f32[512,1024]{1,0:T(8,128)} %stat.2) | copy-start | bytes 6291460
  14.0 33.9 %collective-permute-start.9 = (f32[2,128,640]{2,1,0:T(8,128)}, f32[2,128,640]{2,1,0:T(8,128)S(1)}, u32[]{:S(2)}, u32[]{:S(2)}) collective-permute-start(f32[2,128,640]{2,1,0:T(8,128)} %shard_map.107), channel_id=1, source_target_pairs={{0,1},{1,0},{2,3},{3,2},{4,5},{5,4},{6,7},{7,6},{8,9},{9,8},{10,11... | collective-permute-start | bytes 1966088 | tf_op jit(solution)/shard_map/ppermute | solution.py:265
  23.9 6.5 %collective-permute-start.2 = (f32[32,1024]{1,0:T(8,128)S(1)}, f32[32,1024]{1,0:T(8,128)S(1)}, u32[]{:S(2)}, u32[]{:S(2)}) collective-permute-start(f32[32,1024]{1,0:T(8,128)S(1)} %get-tuple-element.30), channel_id=1, source_target_pairs={{0,8},{2,10},{4,12},{6,14},{8,0},{10,2},{12,4},{14,6},{16,24},{18,... | collective-permute-start | bytes 393224 | tf_op jit(solution)/shard_map/ppermute | solution.py:262
  25.6 12.5 %collective-permute-start.3 = (f32[32,1024]{1,0:T(8,128)S(1)}, f32[32,1024]{1,0:T(8,128)S(1)}, u32[]{:S(2)}, u32[]{:S(2)}) collective-permute-start(f32[32,1024]{1,0:T(8,128)S(1)} %get-tuple-element.31), channel_id=1, source_target_pairs={{0,16},{2,18},{4,20},{6,22},{8,24},{10,26},{12,28},{14,30},{16,0},... | collective-permute-start | bytes 393224 | tf_op jit(solution)/shard_map/ppermute | solution.py:262
  28.2 9.9 %collective-permute-start.4 = (f32[32,1024]{1,0:T(8,128)S(1)}, f32[32,1024]{1,0:T(8,128)S(1)}, u32[]{:S(2)}, u32[]{:S(2)}) collective-permute-start(f32[32,1024]{1,0:T(8,128)S(1)} %get-tuple-element.32), channel_id=1, source_target_pairs={{0,24},{2,26},{4,28},{6,30},{8,16},{10,18},{12,20},{14,22},{16,8},... | collective-permute-start | bytes 393224 | tf_op jit(solution)/shard_map/ppermute | solution.py:262
  38.1 5.0 %collective-permute-start.5 = (bf16[32,1024]{1,0:T(8,128)(2,1)S(1)}, bf16[32,1024]{1,0:T(8,128)(2,1)S(1)}, u32[]{:S(2)}, u32[]{:S(2)}) collective-permute-start(bf16[32,1024]{1,0:T(8,128)(2,1)S(1)} %shard_map.104.refs_0_), channel_id=1, source_target_pairs={{0,8},{2,10},{4,12},{6,14},{8,0},{10,2},{12,4},{14,6},{16,24},{18,... | collective-permute-start | bytes 196616 | tf_op jit(solution)/shard_map/ppermute | solution.py:262
  40.1 6.2 %collective-permute-start.6 = (bf16[32,1024]{1,0:T(8,128)(2,1)S(1)}, bf16[32,1024]{1,0:T(8,128)(2,1)S(1)}, u32[]{:S(2)}, u32[]{:S(2)}) collective-permute-start(bf16[32,1024]{1,0:T(8,128)(2,1)S(1)} %shard_map.104.refs_0_), channel_id=1, source_target_pairs={{0,16},{2,18},{4,20},{6,22},{8,24},{10,26},{12,28},{14,30},{16,0},... | collective-permute-start | bytes 196616 | tf_op jit(solution)/shard_map/ppermute | solution.py:262
  41.2 6.2 %collective-permute-start.7 = (bf16[32,1024]{1,0:T(8,128)(2,1)S(1)}, bf16[32,1024]{1,0:T(8,128)(2,1)S(1)}, u32[]{:S(2)}, u32[]{:S(2)}) collective-permute-start(bf16[32,1024]{1,0:T(8,128)(2,1)S(1)} %shard_map.104.refs_0_), channel_id=1, source_target_pairs={{0,24},{2,26},{4,28},{6,30},{8,16},{10,18},{12,20},{14,22},{16,8},... | collective-permute-start | bytes 196616 | tf_op jit(solution)/shard_map/ppermute | solution.py:262
  47.9 18.4 %copy-start.5 = (f32[512,1024]{1,0:T(8,128)S(1)}, f32[512,1024]{1,0:T(8,128)}, u32[]{:S(2)}) copy-start(f32[512,1024]{1,0:T(8,128)} %moment.1) | copy-start | bytes 6291460
  48.0 16.3 %collective-permute-start.10 = (bf16[2,256,1024]{2,1,0:T(8,128)(2,1)S(1)}, bf16[2,256,1024]{2,1,0:T(8,128)(2,1)S(1)}, u32[]{:S(2)}, u32[]{:S(2)}) collective-permute-start(bf16[2,256,1024]{2,1,0:T(8,128)(2,1)S(1)} %collective-permute-done.8.bmine), channel_id=1, source_target_pairs={{0,2},{2,0},{4,6},{6,4},{8,10},{10,8},{12,14},{14,12},{16,18},{18,... | collective-permute-start | bytes 3145736 | tf_op jit(solution)/shard_map/ppermute | solution.py:262
  48.1 16.1 %collective-permute-start.11 = (f32[2,128,640]{2,1,0:T(8,128)S(1)}, f32[2,128,640]{2,1,0:T(8,128)S(1)}, u32[]{:S(2)}, u32[]{:S(2)}) collective-permute-start(f32[2,128,640]{2,1,0:T(8,128)S(1)} %collective-permute-done.9.smine), channel_id=1, source_target_pairs={{0,2},{2,0},{4,6},{6,4},{8,10},{10,8},{12,14},{14,12},{16,18},{18,... | collective-permute-start | bytes 1966088 | tf_op jit(solution)/shard_map/ppermute | solution.py:262
  48.5 9.2 %collective-permute-start.12 = (bf16[128,1024]{1,0:T(8,128)(2,1)S(1)}, bf16[128,1024]{1,0:T(8,128)(2,1)S(1)}, u32[]{:S(2)}, u32[]{:S(2)}) collective-permute-start(bf16[128,1024]{1,0:T(8,128)(2,1)S(1)} %shard_map.105.refs_0_), channel_id=1, source_target_pairs={{0,4},{2,6},{4,0},{6,2},{8,12},{10,14},{12,8},{14,10},{16,20},{18,... | collective-permute-start | bytes 786440 | tf_op jit(solution)/shard_map/ppermute | solution.py:262
  50.0 13.6 %collective-permute-start.15 = (bf16[128,1024]{1,0:T(8,128)(2,1)S(1)}, bf16[128,1024]{1,0:T(8,128)(2,1)S(1)}, u32[]{:S(2)}, u32[]{:S(2)}) collective-permute-start(bf16[128,1024]{1,0:T(8,128)(2,1)S(1)} %shard_map.105.refs_0_), channel_id=1, source_target_pairs={{0,1},{1,0},{2,3},{3,2},{4,5},{5,4},{6,7},{7,6},{8,9},{9,8},{10,11... | collective-permute-start | bytes 786440 | tf_op jit(solution)/shard_map/ppermute | solution.py:265
  50.5 13.1 %collective-permute-start.16 = (bf16[128,1024]{1,0:T(8,128)(2,1)S(1)}, bf16[128,1024]{1,0:T(8,128)(2,1)S(1)}, u32[]{:S(2)}, u32[]{:S(2)}) collective-permute-start(bf16[128,1024]{1,0:T(8,128)(2,1)S(1)} %shard_map.105.refs_0_), channel_id=1, source_target_pairs={{0,5},{1,4},{2,7},{3,6},{4,1},{5,0},{6,3},{7,2},{8,13},{9,12},{10,... | collective-permute-start | bytes 786440 | tf_op jit(solution)/shard_map/ppermute | solution.py:269
  57.7 8.6 %collective-permute-start.13 = (bf16[128,1024]{1,0:T(8,128)(2,1)S(1)}, bf16[128,1024]{1,0:T(8,128)(2,1)S(1)}, u32[]{:S(2)}, u32[]{:S(2)}) collective-permute-start(bf16[128,1024]{1,0:T(8,128)(2,1)S(1)} %shard_map.105.refs_0_), channel_id=1, source_target_pairs={{0,2},{2,0},{4,6},{6,4},{8,10},{10,8},{12,14},{14,12},{16,18},{18,... | collective-permute-start | bytes 786440 | tf_op jit(solution)/shard_map/ppermute | solution.py:262
  63.7 2.6 %collective-permute-start.14 = (bf16[128,1024]{1,0:T(8,128)(2,1)S(1)}, bf16[128,1024]{1,0:T(8,128)(2,1)S(1)}, u32[]{:S(2)}, u32[]{:S(2)}) collective-permute-start(bf16[128,1024]{1,0:T(8,128)(2,1)S(1)} %collective-permute-done.12.refs_1_), channel_id=1, source_target_pairs={{0,2},{2,0},{4,6},{6,4},{8,10},{10,8},{12,14},{14,12},{16,18},{18,... | collective-permute-start | bytes 786440 | tf_op jit(solution)/shard_map/ppermute | solution.py:262
  63.7 2.6 %collective-permute-start.17 = (bf16[128,1024]{1,0:T(8,128)(2,1)S(1)}, bf16[128,1024]{1,0:T(8,128)(2,1)S(1)}, u32[]{:S(2)}, u32[]{:S(2)}) collective-permute-start(bf16[128,1024]{1,0:T(8,128)(2,1)S(1)} %collective-permute-done.15.refs_4_), channel_id=1, source_target_pairs={{0,2},{2,0},{4,6},{6,4},{8,10},{10,8},{12,14},{14,12},{16,18},{18,... | collective-permute-start | bytes 786440 | tf_op jit(solution)/shard_map/ppermute | solution.py:262
  64.2 2.1 %collective-permute-start.18 = (bf16[128,1024]{1,0:T(8,128)(2,1)S(1)}, bf16[128,1024]{1,0:T(8,128)(2,1)S(1)}, u32[]{:S(2)}, u32[]{:S(2)}) collective-permute-start(bf16[128,1024]{1,0:T(8,128)(2,1)S(1)} %collective-permute-done.16.refs_5_), channel_id=1, source_target_pairs={{0,2},{2,0},{4,6},{6,4},{8,10},{10,8},{12,14},{14,12},{16,18},{18,... | collective-permute-start | bytes 786440 | tf_op jit(solution)/shard_map/ppermute | solution.py:262
  66.3 2.9 %copy-start.1 = (f32[512,1024]{1,0:T(8,128)S(1)}, f32[512,1024]{1,0:T(8,128)}, u32[]{:S(2)}) copy-start(f32[512,1024]{1,0:T(8,128)} %stat.3) | copy-start | bytes 6291460
  66.3 2.9 %copy-start.3 = (f32[512,1024]{1,0:T(8,128)S(1)}, f32[512,1024]{1,0:T(8,128)}, u32[]{:S(2)}) copy-start(f32[512,1024]{1,0:T(8,128)} %basis.3) | copy-start | bytes 6291460
  68.6 15.9 %collective-permute-start.19 = (bf16[512,512]{1,0:T(8,128)(2,1)S(1)}, bf16[512,512]{1,0:T(8,128)(2,1)S(1)}, u32[]{:S(2)}, u32[]{:S(2)}) collective-permute-start(bf16[512,512]{1,0:T(8,128)(2,1)S(1)} %get-tuple-element.41), channel_id=1, source_target_pairs={{0,1},{1,0},{2,3},{3,2},{4,5},{5,4},{6,7},{7,6},{8,9},{9,8},{10,11... | collective-permute-start | bytes 1572872 | tf_op jit(solution)/shard_map/ppermute | solution.py:265
  71.0 13.6 %copy-start.8 = (f32[1024,512]{1,0:T(8,128)S(1)}, f32[1024,512]{1,0:T(8,128)}, u32[]{:S(2)}) copy-start(f32[1024,512]{1,0:T(8,128)} %second.1) | copy-start | bytes 6291460
  89.7 15.3 %collective-permute-start.20 = (bf16[512,512]{1,0:T(8,128)(2,1)S(1)}, bf16[512,512]{1,0:T(8,128)(2,1)S(1)}, u32[]{:S(2)}, u32[]{:S(2)}) collective-permute-start(bf16[512,512]{1,0:T(8,128)(2,1)S(1)} %get-tuple-element.43), channel_id=1, source_target_pairs={{0,1},{1,0},{2,3},{3,2},{4,5},{5,4},{6,7},{7,6},{8,9},{9,8},{10,11... | collective-permute-start | bytes 1572872 | tf_op jit(solution)/shard_map/ppermute | solution.py:265

commit v4 on v3

--- a/solution.py
+++ b/solution.py
@@ -1,5 +1,3 @@
-import functools
-
 import jax
 import jax.numpy as jnp
 from jax import lax
@@ -39,18 +37,25 @@
     return pl.ds(pl.multiple_of(index * size, size), size)
 
 
-def call(kernel, outs, operands, specs, scratch=(), flops=0, moved=0, limit=24):
+def call(kernel, outs, operands, specs, scratch=(), flops=0, moved=0, limit=24, space=VMEM):
     return pl.pallas_call(
         kernel,
         out_shape=outs,
         in_specs=specs,
-        out_specs=[VMEM] * len(outs),
+        out_specs=[space] * len(outs),
         scratch_shapes=list(scratch),
         compiler_params=pltpu.CompilerParams(vmem_limit_bytes=limit * 2**20),
         cost_estimate=pl.CostEstimate(flops=flops, bytes_accessed=moved, transcendentals=0),
     )(*operands)
 
 
+def run_all(copies):
+    for copy in copies:
+        copy.start()
+    for copy in copies:
+        copy.wait()
+
+
 TILES = 4
 UPPER = [(i, j) for i in range(TILES) for j in range(i, TILES)]
 
@@ -60,18 +65,27 @@
     out[1] = right[...].astype(HALF)
 
 
-def stats_kernel(where, left, right, out):
-    size = left.shape[0] // TILES
-    count = len(UPPER) // 2
-    for core in range(2):
+def stats_kernel(where, left, right, out, sem):
+    size = out.shape[0]
+    rows = size * TILES
+    for core, stat in enumerate((left, right)):
 
         @pl.when(where[1] == core)
         def _():
-            for place, (i, j) in enumerate(UPPER[core * count : (core + 1) * count]):
-                for side, stat in enumerate((left, right)):
-                    out[side, :, place * size : (place + 1) * size] = stat[
-                        i * size : (i + 1) * size, j * size : (j + 1) * size
-                    ]
+            begin = where[0] * rows
+            run_all(
+                [
+                    pltpu.make_async_copy(
+                        stat.at[
+                            i * size : (i + 1) * size,
+                            pl.ds(pl.multiple_of(begin + j * size, size), size),
+                        ],
+                        out.at[:, place * size : (place + 1) * size],
+                        sem.at[place],
+                    )
+                    for place, (i, j) in enumerate(UPPER)
+                ]
+            )
 
 
 def first_sum_kernel(where, group, came, kept, sent):
@@ -104,147 +118,169 @@
         out[tile(z ^ k, size)] = part[...]
 
 
-def place_basis(where, out, own, mine, theirs, side, natural):
+def place_basis(where, out, own, mine, theirs, side):
     rows = own.shape[0]
     half = rows // 2
     position, core = where[0], where[1]
-    first = position if natural else 0
-    out[tile(first, rows)] = own[...].astype(HALF)
-    other = (1 - first) * 2
+    out[tile(position, rows)] = own[...].astype(HALF)
+    other = (1 - position) * 2
     out[tile(other + core, half)] = mine[side]
     out[tile(other + 1 - core, half)] = theirs[side]
 
 
-def place_stat(where, out, own, mine, theirs, side, natural):
-    rows = own.shape[0]
+def state_kernel(
+    where, left, right, mine, theirs, stat_left, stat_right, came, bases, turned, back, full, sem
+):
+    rows, width = left.shape
     size = rows // TILES
-    count = len(UPPER) // 2
     position, core = where[0], where[1]
-    first = position if natural else 0
-    here, there = tile(first, rows), tile(1 - first, rows)
-    out[here, here] = own[:, tile(position, rows)]
-    cross = own[:, tile(1 - position, rows)]
-    out[here, there] = cross
-    out[there, here] = cross.T
-    base = (1 - first) * TILES
+    here, there = tile(position, rows), tile(1 - position, rows)
+    for side, stat in enumerate((stat_left, stat_right)):
+
+        @pl.when(core == side)
+        def _():
+            pltpu.make_async_copy(stat, full.at[here], sem).start()
+
+    place_basis(where, bases.at[core], left, mine, theirs, 0)
+    place_basis(where, bases.at[1 - core], right, mine, theirs, 1)
+    turned[...] = bases[core].T
+    back[...] = bases[1 - core].T
+    base = (1 - position) * TILES
     for place, (i, j) in enumerate(UPPER):
-        from_mine = core == place // count
-        columns = slice(place % count * size, (place % count + 1) * size)
-        value = jnp.where(from_mine, mine[side, :, columns], theirs[side, :, columns])
-        out[tile(base + i, size), tile(base + j, size)] = value
+        value = came[:, place * size : (place + 1) * size]
+        full[tile(base + i, size), tile(base + j, size)] = value
         if i != j:
-            out[tile(base + j, size), tile(base + i, size)] = value.T
-
-
-def left_state_kernel(where, basis, bmine, btheirs, stat, smine, stheirs, rot, turned, full):
-    place_basis(where, rot, basis, bmine, btheirs, 0, False)
-    place_stat(where, full, stat, smine, stheirs, 0, False)
-    turned[...] = rot[...].T
-
-
-def right_state_kernel(where, basis, bmine, btheirs, stat, smine, stheirs, rot, near, back, full):
-    rows = basis.shape[0]
-    place_basis(where, rot, basis, bmine, btheirs, 1, True)
-    place_stat(where, full, stat, smine, stheirs, 1, True)
-    near[:, :rows] = rot[:, tile(where[0], rows)]
-    near[:, rows:] = rot[:, tile(1 - where[0], rows)]
-    back[...] = near[...].T
-
-
-def moment_kernel(where, moment, near, *refs):
-    parts, (gradient, turned, ours, others, sem) = refs[:-5], refs[-5:]
-    core, x = where[1], where[2]
+            full[tile(base + j, size), tile(base + i, size)] = value.T
+    pltpu.make_async_copy(stat_left, full.at[here], sem).wait()
+    full[there, here] = full[here, there].T
+
+
+def moment_kernel(where, moment, bases, *refs):
+    parts, (gradient, ours, others, sem) = refs[:-4], refs[-4:]
+    position, core, x = where[0], where[1], where[2]
     size = parts[0].shape[0]
     rows = moment.shape[0]
+    step = rows // 2
     copies = []
     for place, part in enumerate(parts):
         block = (
-            (place // 4) * 4 + (core ^ (place % 4 // 2)) * 2 + (x ^ (place % 2))
+            (position ^ (place // 4)) * 4 + (core ^ (place % 4 // 2)) * 2 + (x ^ (place % 2))
         )
         copies.append(
             pltpu.make_async_copy(part, gradient.at[tile(block, size)], sem.at[place])
         )
+    run_all(copies)
+    half = (
+        BETA_ONE * moment[...] + (1.0 - BETA_ONE) * gradient[tile(position, rows)].astype(FULL)
+    ).astype(HALF)
+    there, here = tile((1 - position) * 2 + core, step), tile(position * 2 + core, step)
+    others[...] = matmul(half, bases[1 - core, :, there]).astype(HALF)
+    ours[...] = matmul(half, bases[1 - core, :, here]).astype(HALF)
+
+
+def adam_kernel(where, gradient, bases, turned, mine, came, second, new, kept, sent):
+    width = gradient.shape[0]
+    rows, step = mine.shape
+    position, core = where[0], where[1]
+    here, there = tile(position, rows), tile(1 - position, rows)
+    block = matmul(gradient[...], bases[1 - core, :, tile(position * 2 + core, step)])
+    grad_rot = matmul(turned[...], block.astype(HALF)) * (1.0 / width)
+    moment_rot = (
+        matmul(turned[:, here], mine[...]) + matmul(turned[:, there], came[...])
+    ) * (1.0 / width)
+    value = BETA_TWO * second[:, tile(core, step)] + (1.0 - BETA_TWO) * grad_rot * grad_rot
+    new[...] = value
+    scaled = (moment_rot / (jnp.sqrt(value) + EPSILON)).astype(HALF)
+    sent[...] = matmul(bases[core, there], scaled).astype(HALF)
+    kept[...] = matmul(bases[core, here], scaled).astype(HALF)
+
+
+def update_kernel(
+    where, kept, came, kept_next, came_next, back, new, new_next, out, second_new, rows_back, sem
+):
+    rows, width = out.shape
+    step = kept.shape[1]
+    position, core = where[0], where[1]
+    copies = [
+        pltpu.make_async_copy(value, second_new.at[:, tile(place, step)], sem.at[i])
+        for i, (value, place) in enumerate(((new, core), (new_next, 1 - core)))
+    ]
     for copy in copies:
         copy.start()
+    for value, place in (
+        (kept, position * 2 + core),
+        (came, (1 - position) * 2 + core),
+        (kept_next, position * 2 + 1 - core),
+        (came_next, (1 - position) * 2 + 1 - core),
+    ):
+        rows_back[:, tile(place, step)] = value[...]
+    for here in [slice(i * step, (i + 1) * step) for i in range(4)]:
+        out[:, here] = (matmul(rows_back[...], back[:, here]) * (1.0 / width)).astype(HALF)
     for copy in copies:
         copy.wait()
-    half = (
-        BETA_ONE * moment[...] + (1.0 - BETA_ONE) * gradient[:rows].astype(FULL)
-    ).astype(HALF)
-    step = rows // 2
-    for i in range(2):
-        here = slice(i * step, (i + 1) * step)
-        others[:, here] = matmul(half, near[:, rows + i * step : rows + (i + 1) * step]).astype(HALF)
-        ours[:, here] = matmul(half, near[:, here]).astype(HALF)
-    step = gradient.shape[0] // 4
-    for i in range(4):
-        here = slice(i * step, (i + 1) * step)
-        turned[:, here] = gradient[here].T
-
-
-def adam_kernel(gradient, near, rot, turned, mine, came, second, new, kept, sent, block, scaled):
+
+
+def sides_kernel(where, mine, theirs, left, right, sem):
+    for core, (one, two) in enumerate(((mine, theirs), (theirs, mine))):
+
+        @pl.when(where[1] == core)
+        def _():
+            run_all(
+                [
+                    pltpu.make_async_copy(one, left, sem.at[0]),
+                    pltpu.make_async_copy(two, right, sem.at[1]),
+                ]
+            )
+
+
+def quarters(width):
+    step = width // 4
+    return [slice(i * step, (i + 1) * step) for i in range(4)]
+
+
+def power_kernel(where, gradient, bases, stat, start, turned, pair, half):
     width = gradient.shape[0]
-    rows = mine.shape[0]
-    step = rows // 2
-    columns = [slice(i * step, (i + 1) * step) for i in range(2)]
-    for here in columns:
-        block[:, here] = matmul(gradient[...], near[:, here]).astype(HALF)
-    for here in columns:
-        grad_rot = matmul(turned[...], block[:, here]) * (1.0 / width)
-        moment_rot = (
-            matmul(turned[:, :rows], mine[:, here]) + matmul(turned[:, rows:], came[:, here])
-        ) * (1.0 / width)
-        value = BETA_TWO * second[:, here] + (1.0 - BETA_TWO) * grad_rot * grad_rot
-        new[:, here] = value
-        scaled[:, here] = (moment_rot / (jnp.sqrt(value) + EPSILON)).astype(HALF)
-    for here in columns:
-        sent[:, here] = matmul(rot[rows:], scaled[:, here]).astype(HALF)
-        kept[:, here] = matmul(rot[:rows], scaled[:, here]).astype(HALF)
-
-
-def update_kernel(mine, came, back, out):
-    rows, width = out.shape
-    step = width // 4
-    for here in [slice(i * step, (i + 1) * step) for i in range(4)]:
-        total = matmul(mine[...], back[:rows, here]) + matmul(came[...], back[rows:, here])
-        out[:, here] = (total * (1.0 / width)).astype(HALF)
-
-
-def refresh_kernel(natural, where, one, two, rot, stat, out, half, first, second, turned, gram):
-    width = one.shape[0]
+    core = where[1]
+    for here in quarters(width):
+        value = gradient[here]
+        pair[core, here] = value
+        pair[1 - core, :, here] = value.T
+    for here in quarters(width):
+        grads = matmul(pair[0], pair[1, :, here])
+        half[:, here] = (BETA_STAT * stat[:, here] + (1.0 - BETA_STAT) * grads).astype(HALF)
+    for here in quarters(width):
+        product = matmul(half[...], bases[0, :, here])
+        square = jnp.sum(product * product, axis=0, keepdims=True) * (1.0 / width)
+        value = (product * lax.rsqrt(square + NORM_EPS)).astype(HALF)
+        start[:, here] = value
+        turned[here] = value.T
+
+
+def refresh_kernel(where, start, start_turned, out, following, following_turned, gram):
+    width = start.shape[0]
     rows = out.shape[0]
-    step = width // 4
-    columns = [slice(i * step, (i + 1) * step) for i in range(4)]
-    for here in columns:
-        grads = matmul(one[...], two[:, here])
-        half[:, here] = (BETA_STAT * stat[:, here] + (1.0 - BETA_STAT) * grads).astype(HALF)
-    for here in columns:
-        product = matmul(half[...], rot[:, here])
-        square = jnp.sum(product * product, axis=0, keepdims=True) * (1.0 / width)
-        start = (product * lax.rsqrt(square + NORM_EPS)).astype(HALF)
-        first[:, here] = start
-        turned[here] = start.T
-
-    def improved(current, kept, result, dtype, again):
+
+    def improved(current, turned, kept, result, result_turned):
         size = result.shape[0]
-        for here in columns:
+        for here in quarters(width):
             gram[:size, here] = (matmul(current[kept], turned[:, here]) * (1.0 / width)).astype(
                 HALF
             )
-        for here in columns:
+        for here in quarters(width):
             value = (
                 1.5 * current[kept, here].astype(FULL)
                 - 0.5 * matmul(gram[:size], current[:, here])
-            ).astype(dtype)
+            ).astype(result.dtype)
             result[:, here] = value
-            if again:
-                turned[here] = value.T
-
-    current, following = first, second
-    for _ in range(NS_ITERS - 1):
-        improved(current, slice(0, width), following, HALF, True)
-        current, following = following, current
-    improved(current, tile(where[0], rows) if natural else slice(0, rows), out, FULL, False)
+            if result_turned is not None:
+                result_turned[here] = value.T
+
+    current, turned = start, start_turned
+    for iteration in range(NS_ITERS - 1):
+        place = iteration % 2
+        improved(current, turned, slice(0, width), following.at[place], following_turned.at[place])
+        current, turned = following.at[place], following_turned.at[place]
+    improved(current, turned, tile(where[0], rows), out, None)
 
 
 def fast_body(group_grads, moment, second, stat_left, stat_right, basis_left, basis_right):
@@ -300,20 +336,15 @@
         [SMEM, VMEM, VMEM],
         moved=2**20,
     )
-    (stats_sent,) = pl.pallas_call(
+    (stats_sent,) = call(
         stats_kernel,
-        out_shape=[shaped((2, quarter, 5 * quarter), FULL)],
-        grid_spec=pltpu.PrefetchScalarGridSpec(
-            num_scalar_prefetch=1,
-            grid=(1,),
-            in_specs=[pl.BlockSpec((rows, rows), lambda i, where: (0, where[0]))] * 2,
-            out_specs=[
-                pl.BlockSpec((2, quarter, 5 * quarter), lambda i, where: (0, 0, 0)),
-            ],
-        ),
-        compiler_params=pltpu.CompilerParams(vmem_limit_bytes=56 * 2**20),
-        cost_estimate=pl.CostEstimate(flops=0, bytes_accessed=2**22, transcendentals=0),
-    )(where, stat_left, stat_right)
+        [shaped((quarter, len(UPPER) * quarter), FULL)],
+        (where, stat_left, stat_right),
+        [SMEM, ANY, ANY],
+        [pltpu.SemaphoreType.DMA((len(UPPER),))],
+        moved=2**21,
+        limit=56,
+    )
     stats_mine = shard_swap(stats_sent)
     pieces = [dp_swap(value, 4 * (k + 1)) for k, value in enumerate(sent)]
     (piece,) = call(
@@ -326,75 +357,99 @@
     )
     part, bases_mine, stats_mine = lax.optimization_barrier((part, bases_mine, stats_mine))
     parts = [part, dp_swap(part, 2), shard_swap(part), cross_swap(part)]
+
+    bases_theirs = dp_swap(bases_mine, 1)
+    square = shaped((width, width), HALF)
+    bases, left_turned, right_turned, stat = call(
+        state_kernel,
+        [shaped((2, width, width), HALF), square, square, shaped((width, width), FULL)],
+        (
+            where,
+            basis_left,
+            basis_right,
+            bases_mine,
+            bases_theirs,
+            stat_left,
+            stat_right,
+            stats_mine,
+        ),
+        [SMEM] + [VMEM] * 4 + [ANY] * 2 + [VMEM],
+        [pltpu.SemaphoreType.DMA(())],
+        moved=2**24,
+    )
+    parts[2], parts[3], bases = lax.optimization_barrier((parts[2], parts[3], bases))
     swapped = [dp_swap(value, 1) for value in parts]
-
-    bases_theirs = dp_swap(bases_mine, 1)
-    stats_theirs = dp_swap(stats_mine, 1)
-    bases = (bases_mine, bases_theirs)
-    stats = (stats_mine, stats_theirs)
-    state_outs = [
-        shaped((width, width), HALF),
-        shaped((width, width), HALF),
-        shaped((width, width), FULL),
-    ]
-    left_rot, left_turned, left_stat = call(
-        left_state_kernel,
-        state_outs,
-        (where, basis_left, *bases, stat_left, *stats),
-        [SMEM] + [VMEM] * 6,
-        moved=2**24,
-    )
-    right_rot, right_near, right_back, right_stat = call(
-        right_state_kernel,
-        state_outs[:1] + state_outs,
-        (where, basis_right, *bases, stat_right, *stats),
-        [SMEM] + [VMEM] * 6,
-        moved=2**24,
-    )
-
     ordered = [parts[0], parts[1], swapped[0], swapped[1], parts[2], parts[3], swapped[2], swapped[3]]
-    gradient, gradient_turned, moment_mine, moment_sent = call(
+    gradient, moment_mine, moment_sent = call(
         moment_kernel,
-        [shaped((width, width), HALF)] * 2 + [shaped((rows, rows), HALF)] * 2,
-        (where, moment, right_near, *ordered),
+        [square] + [shaped((rows, half), HALF)] * 2,
+        (where, moment, bases, *ordered),
         [SMEM, VMEM, VMEM] + [ANY] * 8,
         [pltpu.SemaphoreType.DMA((8,))],
-        flops=unit // 2,
-        moved=2**23,
+        flops=unit // 4,
+        moved=2**22,
     )
     moment_came = shard_swap(moment_sent)
-
-    def refreshed(natural, one, two, rot, stat):
-        (out,) = call(
-            functools.partial(refresh_kernel, natural),
-            [shaped((rows, width), FULL)],
-            (where, one, two, rot, stat),
-            [SMEM] + [VMEM] * 4,
-            [pltpu.VMEM((width, width), HALF)] * 5,
-            flops=5 * unit,
-            moved=2**23,
-        )
-        return out
-
-    left_new = refreshed(False, gradient, gradient_turned, left_rot, left_stat)
-    second_new, back_mine, back_sent = call(
-        adam_kernel,
-        [shaped((width, rows), FULL)] + [shaped((rows, rows), HALF)] * 2,
-        (gradient, right_near, left_rot, left_turned, moment_mine, moment_came, second),
-        [VMEM] * 7,
-        [pltpu.VMEM((width, rows), HALF)] * 2,
+    start, start_turned = call(
+        power_kernel,
+        [square] * 2,
+        (where, gradient, bases, stat),
+        [SMEM] + [VMEM] * 3,
+        [pltpu.VMEM((2, width, width), HALF), pltpu.VMEM((width, width), HALF)],
         flops=2 * unit,
         moved=2**23,
     )
+    new, back_kept, back_sent = call(
+        adam_kernel,
+        [shaped((width, half), FULL)] + [shaped((rows, half), HALF)] * 2,
+        (where, gradient, bases, left_turned, moment_mine, moment_came, second),
+        [SMEM] + [VMEM] * 6,
+        flops=unit,
+        moved=2**22,
+    )
+    start, back_sent = lax.optimization_barrier((start, back_sent))
     back_came = shard_swap(back_sent)
-    right_new = refreshed(True, gradient_turned, gradient, right_rot, right_stat)
-    (update,) = call(
+    new_next = dp_swap(new, 1)
+    back_kept_next = dp_swap(back_kept, 1)
+    (side_new,) = call(
+        refresh_kernel,
+        [shaped((rows, width), FULL)],
+        (where, start, start_turned),
+        [SMEM] + [VMEM] * 2,
+        [pltpu.VMEM((2, width, width), HALF)] * 2 + [pltpu.VMEM((width, width), HALF)],
+        flops=3 * unit,
+        moved=2**22,
+    )
+    side_next = dp_swap(side_new, 1)
+    back_came_next = dp_swap(back_came, 1)
+    update, second_new = pl.pallas_call(
         update_kernel,
-        [shaped((rows, width), HALF)],
-        (back_mine, back_came, right_back),
-        [VMEM] * 3,
-        flops=unit // 2,
-        moved=2**22,
+        out_shape=[shaped((rows, width), HALF), shaped((width, rows), FULL)],
+        in_specs=[SMEM] + [VMEM] * 5 + [ANY] * 2,
+        out_specs=[VMEM, ANY],
+        scratch_shapes=[pltpu.VMEM((rows, width), HALF), pltpu.SemaphoreType.DMA((2,))],
+        compiler_params=pltpu.CompilerParams(vmem_limit_bytes=24 * 2**20),
+        cost_estimate=pl.CostEstimate(
+            flops=unit // 2, bytes_accessed=2**23, transcendentals=0
+        ),
+    )(
+        where,
+        back_kept,
+        back_came,
+        back_kept_next,
+        back_came_next,
+        right_turned,
+        new,
+        new_next,
+    )
+    left_new, right_new = call(
+        sides_kernel,
+        [shaped((rows, width), FULL)] * 2,
+        (where, side_new, side_next),
+        [SMEM, ANY, ANY],
+        [pltpu.SemaphoreType.DMA((2,))],
+        moved=2**23,
+        space=ANY,
     )
     return (update, second_new, left_new, right_new)
 

time: 107 us -> 107 us (level)
  Pallas kernels: 49 us -> 38.3 us
  waiting for transfers between devices: 34.9 us -> 44.3 us
  local copies, waits for them, and re-layouts: 1.13 us -> 2.96 us
    pallas_call x12, Pallas kernels: 45.8 us -> 35.1 us  [the longest x11 31.3 us: call(): pl.pallas_call(kernel, out_shape=outs, in_specs=specs, out_specs=[space]...]
    ppermute x5, waiting for transfers between devices: 5.96 us -> 12.4 us  [shard_swap(): return lax.ppermute(value, 'shard', [(0, 1), (1, 0)])]
    ppermute x15 -> x18, waiting for transfers between devices: 28.9 us -> 31.9 us  [dp_swap(): return lax.ppermute(value, 'dp', [(i, i ^ distance) for i in range(16)])]
    unnamed x18 -> x22, local copies, waits for them, and re-layouts: 0.04 us -> 1.88 us
    ppermute x15 -> x18, starting transfers between devices: 13.7 us -> 13.7 us  [dp_swap(): return lax.ppermute(value, 'dp', [(i, i ^ distance) for i in range(16)])]
  transfers between devices with their start and end apart: 21 -> 24, of which waited for: 8 -> 13; matrix products, arithmetic and copies ran while one was open for 1% -> 1% of each run, Pallas kernels for 37% -> 21%
where the time goes in v4:
time: 107 us
  waiting for transfers between devices  44.3 us (41%)
  Pallas kernels  38.3 us (36%)
  starting transfers between devices  19.9 us (19%)
  local copies, waits for them, and re-layouts  2.96 us (3%)
    ppermute x18, waiting for transfers between devices, dp_swap(): return lax.ppermute(value, 'dp', [(i, i ^ distance) for i in range(16)])  31.9 us
    pallas_call x11, Pallas kernels, call(): pl.pallas_call(kernel, out_shape=outs, in_specs=specs, out_specs=[space]...  31.3 us
    ppermute x18, starting transfers between devices, dp_swap(): return lax.ppermute(value, 'dp', [(i, i ^ distance) for i in range(16)])  13.7 us
    ppermute x5, waiting for transfers between devices, shard_swap(): return lax.ppermute(value, 'shard', [(0, 1), (1, 0)])  12.4 us
    ppermute x5, starting transfers between devices, shard_swap(): return lax.ppermute(value, 'shard', [(0, 1), (1, 0)])  4.7 us
    pallas_call x1, Pallas kernels, fast_body(): pl.pallas_call(update_kernel, out_shape=[shaped((rows, width), HALF), sha...  3.88 us
    pallas_call x1, Pallas kernels, fast_body(): pl.pallas_call(bases_kernel, out_shape=[shaped((2, half, width), HALF)],...  3.18 us
  transfers between devices with their start and end apart: 24, of which 13 were waited for; matrix products, arithmetic and copies ran while one was open for 1% of the time, Pallas kernels for 21%

profile of v4, /device:TPU:0, one launch (start us, length us, event | category | flops | bytes accessed | tf_op | source)
XLA Modules:
  0.0 107.1 jit_solution(3499218925518841958)
XLA Ops:
  0.6 1.1 %dynamic-slice_bitcast_fusion = bf16[256,1024]{1,0:T(8,128)(2,1)S(1)} fusion(bf16[1,512,1024]{2,1,0:T(8,128)(2,1)} %group.1, s32[]{:T(128)S(6)} %select_n.3), kind=kLoop, calls=%fused_computation | loop fusion | bytes 1048580 | tf_op jit(solution)/shard_map/dynamic_slice | solution.py:322
  1.7 0.5 collective-permute-start
  2.2 0.6 pad_add_fusion.where
  2.8 3.2 %shard_map.106 = bf16[2,256,1024]{2,1,0:T(8,128)(2,1)} custom-call(s32[4]{0:T(128)} %pad_add_fusion.where, f32[512,1024]{1,0:T(8,128)} %left.5, f32[512,1024]{1,0:T(8,128)} %right.5), custom_call_target="tpu_custom_call" | custom-call | bytes 4194304 | tf_op jit(solution)/shard_map/pallas_call | solution.py:308
  6.0 2.5 %collective-permute-start.8 = (bf16[2,256,1024]{2,1,0:T(8,128)(2,1)}, bf16[2,256,1024]{2,1,0:T(8,128)(2,1)S(1)}, u32[]{:S(2)}, u32[]{:S(2)}) collective-permute-start(bf16[2,256,1024]{2,1,0:T(8,128)(2,1)} %shard_map.106), channel_id=1, source_target_pairs={{0,1},{1,0},{2,3},{3,2},{4,5},{5,4},{6,7},{7,6},{8,9},{9,8},{10,11... | collective-permute-start | bytes 3145736 | tf_op jit(solution)/shard_map/ppermute | solution.py:301
  8.6 0.0 collective-permute-done.came
  8.6 0.0 copy-start.3
  8.6 1.4 %shard_map.102 = (f32[128,1024]{1,0:T(8,128)S(1)}, f32[128,1024]{1,0:T(8,128)}) custom-call(s32[4]{0:T(128)S(1)} %copy-done.9, bf16[1,512,1024]{2,1,0:T(8,128)(2,1)S(1)} %copy-done.4, bf16[256,1024]{1,0:T(8,128)(2,1)S(1)} %collective-permute-done.came), custom_call_target="tpu_custom_call" | custom-call | bytes 2097152 | tf_op jit(solution)/shard_map/pallas_call | solution.py:41
  10.0 0.8 copy-done.7
  10.8 1.5 %collective-permute-start.1 = (f32[128,1024]{1,0:T(8,128)}, f32[128,1024]{1,0:T(8,128)S(1)}, u32[]{:S(2)}, u32[]{:S(2)}) collective-permute-start(f32[128,1024]{1,0:T(8,128)} %get-tuple-element.35), channel_id=1, source_target_pairs={{0,4},{2,6},{4,0},{6,2},{8,12},{10,14},{12,8},{14,10},{16,20},{18,... | collective-permute-start | bytes 1572872 | tf_op jit(solution)/shard_map/ppermute | solution.py:298
  12.3 3.2 %shard_map.107 = f32[128,1280]{1,0:T(8,128)} custom-call(s32[4]{0:T(128)} %pad_add_fusion.where, f32[512,1024]{1,0:T(8,128)} %stat_left.1, f32[512,1024]{1,0:T(8,128)} %stat_right.1), custom_call_target="tpu_custom_call" | custom-call | bytes 2097152 | tf_op jit(solution)/shard_map/pallas_call | solution.py:41
  15.5 0.0 copy-start
  15.5 0.6 collective-permute-start.9
  16.1 8.9 %collective-permute-done.1.came = f32[128,1024]{1,0:T(8,128)S(1)} collective-permute-done((f32[128,1024]{1,0:T(8,128)}, f32[128,1024]{1,0:T(8,128)S(1)}, u32[]{:S(2)}, u32[]{:S(2)}) %collective-permute-start.1) | collective-permute-done | bytes 524320 | tf_op jit(solution)/shard_map/ppermute | solution.py:298
  25.0 1.0 copy-done.8
  26.1 0.6 shard_map.103
  26.7 1.6 %collective-permute-start.2 = (f32[32,1024]{1,0:T(8,128)S(1)}, f32[32,1024]{1,0:T(8,128)S(1)}, u32[]{:S(2)}, u32[]{:S(2)}) collective-permute-start(f32[32,1024]{1,0:T(8,128)S(1)} %get-tuple-element.37), channel_id=1, source_target_pairs={{0,8},{2,10},{4,12},{6,14},{8,0},{10,2},{12,4},{14,6},{16,24},{18,... | collective-permute-start | bytes 393224 | tf_op jit(solution)/shard_map/ppermute | solution.py:298
  28.3 2.6 %collective-permute-start.3 = (f32[32,1024]{1,0:T(8,128)S(1)}, f32[32,1024]{1,0:T(8,128)S(1)}, u32[]{:S(2)}, u32[]{:S(2)}) collective-permute-start(f32[32,1024]{1,0:T(8,128)S(1)} %get-tuple-element.38), channel_id=1, source_target_pairs={{0,16},{2,18},{4,20},{6,22},{8,24},{10,26},{12,28},{14,30},{16,0},... | collective-permute-start | bytes 393224 | tf_op jit(solution)/shard_map/ppermute | solution.py:298
  30.9 0.2 collective-permute-start.4
  31.1 2.0 %collective-permute-done.2.one = f32[32,1024]{1,0:T(8,128)S(1)} collective-permute-done((f32[32,1024]{1,0:T(8,128)S(1)}, f32[32,1024]{1,0:T(8,128)S(1)}, u32[]{:S(2)}, u32[]{:S(2)}) %collective-permute-start.2) | collective-permute-done | bytes 131104 | tf_op jit(solution)/shard_map/ppermute | solution.py:298
  33.2 7.6 %collective-permute-done.3.two = f32[32,1024]{1,0:T(8,128)S(1)} collective-permute-done((f32[32,1024]{1,0:T(8,128)S(1)}, f32[32,1024]{1,0:T(8,128)S(1)}, u32[]{:S(2)}, u32[]{:S(2)}) %collective-permute-start.3) | collective-permute-done | bytes 131104 | tf_op jit(solution)/shard_map/ppermute | solution.py:298
  40.8 0.0 collective-permute-done.4.three
  40.8 2.0 %collective-permute-start.5 = (bf16[32,1024]{1,0:T(8,128)(2,1)S(1)}, bf16[32,1024]{1,0:T(8,128)(2,1)S(1)}, u32[]{:S(2)}, u32[]{:S(2)}) collective-permute-start(bf16[32,1024]{1,0:T(8,128)(2,1)S(1)} %shard_map.104.refs_0_), channel_id=1, source_target_pairs={{0,8},{2,10},{4,12},{6,14},{8,0},{10,2},{12,4},{14,6},{16,24},{18,... | collective-permute-start | bytes 196616 | tf_op jit(solution)/shard_map/ppermute | solution.py:298
  42.8 1.1 %collective-permute-start.6 = (bf16[32,1024]{1,0:T(8,128)(2,1)S(1)}, bf16[32,1024]{1,0:T(8,128)(2,1)S(1)}, u32[]{:S(2)}, u32[]{:S(2)}) collective-permute-start(bf16[32,1024]{1,0:T(8,128)(2,1)S(1)} %shard_map.104.refs_0_), channel_id=1, source_target_pairs={{0,16},{2,18},{4,20},{6,22},{8,24},{10,26},{12,28},{14,30},{16,0},... | collective-permute-start | bytes 196616 | tf_op jit(solution)/shard_map/ppermute | solution.py:298
  43.9 1.4 %collective-permute-start.7 = (bf16[32,1024]{1,0:T(8,128)(2,1)S(1)}, bf16[32,1024]{1,0:T(8,128)(2,1)S(1)}, u32[]{:S(2)}, u32[]{:S(2)}) collective-permute-start(bf16[32,1024]{1,0:T(8,128)(2,1)S(1)} %shard_map.104.refs_0_), channel_id=1, source_target_pairs={{0,24},{2,26},{4,28},{6,30},{8,16},{10,18},{12,20},{14,22},{16,8},... | collective-permute-start | bytes 196616 | tf_op jit(solution)/shard_map/ppermute | solution.py:298
  45.3 0.5 collective-permute-done.5.refs_1_
  45.8 3.3 %collective-permute-done.6.refs_2_ = bf16[32,1024]{1,0:T(8,128)(2,1)S(1)} collective-permute-done((bf16[32,1024]{1,0:T(8,128)(2,1)S(1)}, bf16[32,1024]{1,0:T(8,128)(2,1)S(1)}, u32[]{:S(2)}, u32[]{:S(2)}) %collective-permute-start.6) | collective-permute-done | bytes 65568 | tf_op jit(solution)/shard_map/ppermute | solution.py:298
  49.1 1.1 collective-permute-done.7.refs_3_
  50.1 0.6 shard_map.105.refs_0_
  50.7 0.0 copy-start.5
  50.7 0.0 collective-permute-done.9.came
  50.7 0.0 collective-permute-done.8.mine
  50.7 0.1 collective-permute-start.12
  50.8 1.6 %collective-permute-start.13 = (bf16[128,1024]{1,0:T(8,128)(2,1)S(1)}, bf16[128,1024]{1,0:T(8,128)(2,1)S(1)}, u32[]{:S(2)}, u32[]{:S(2)}) collective-permute-start(bf16[128,1024]{1,0:T(8,128)(2,1)S(1)} %shard_map.105.refs_0_), channel_id=1, source_target_pairs={{0,4},{2,6},{4,0},{6,2},{8,12},{10,14},{12,8},{14,10},{16,20},{18,... | collective-permute-start | bytes 786440 | tf_op jit(solution)/shard_map/ppermute | solution.py:298
  52.3 0.5 collective-permute-start.10
  52.9 1.5 %collective-permute-start.11 = (bf16[128,1024]{1,0:T(8,128)(2,1)S(1)}, bf16[128,1024]{1,0:T(8,128)(2,1)S(1)}, u32[]{:S(2)}, u32[]{:S(2)}) collective-permute-start(bf16[128,1024]{1,0:T(8,128)(2,1)S(1)} %shard_map.105.refs_0_), channel_id=1, source_target_pairs={{0,5},{1,4},{2,7},{3,6},{4,1},{5,0},{6,3},{7,2},{8,13},{9,12},{10,... | collective-permute-start | bytes 786440 | tf_op jit(solution)/shard_map/ppermute | solution.py:305
  54.3 0.0 collective-permute-start.14
  54.3 5.6 %collective-permute-done.13.refs_1_ = bf16[128,1024]{1,0:T(8,128)(2,1)S(1)} collective-permute-done((bf16[128,1024]{1,0:T(8,128)(2,1)S(1)}, bf16[128,1024]{1,0:T(8,128)(2,1)S(1)}, u32[]{:S(2)}, u32[]{:S(2)}) %collective-permute-start.13) | collective-permute-done | bytes 262176 | tf_op jit(solution)/shard_map/ppermute | solution.py:298
  60.0 0.0 collective-permute-start.15
  60.0 0.0 collective-permute-done.12.theirs
  60.0 2.8 %shard_map.108 = (bf16[2,1024,1024]{2,1,0:T(8,128)(2,1)S(1)}, bf16[1024,1024]{1,0:T(8,128)(2,1)S(1)}, bf16[1024,1024]{1,0:T(8,128)(2,1)S(1)}, f32[1024,1024]{1,0:T(8,128)S(1)}) custom-call(s32[4]{0:T(128)S(1)} %copy-done.10, f32[512,1024]{1,0:T(8,128)S(1)} %copy-done.2, f32[512,1024]{1,0:T(8,128)S(1)} %copy-done.3, ...), custom_call_target="tpu_custom_call" | custom-call | bytes 16777216 | tf_op jit(solution)/shard_map/pallas_call | solution.py:41
  62.8 3.5 %collective-permute-done.10.refs_4_ = bf16[128,1024]{1,0:T(8,128)(2,1)S(1)} collective-permute-done((bf16[128,1024]{1,0:T(8,128)(2,1)S(1)}, bf16[128,1024]{1,0:T(8,128)(2,1)S(1)}, u32[]{:S(2)}, u32[]{:S(2)}) %collective-permute-start.10) | collective-permute-done | bytes 262176 | tf_op jit(solution)/shard_map/ppermute | solution.py:301
  66.3 0.0 collective-permute-done.11.refs_5_
  66.3 0.0 collective-permute-start.16
  66.3 0.5 collective-permute-start.17
  66.9 0.0 collective-permute-done.14.refs_2_
  66.9 0.0 collective-permute-done.15.refs_3_
  66.9 1.0 collective-permute-done.16.refs_6_
  67.9 0.4 collective-permute-done.17.refs_7_
  68.3 1.7 %shard_map.109 = (bf16[1024,1024]{1,0:T(8,128)(2,1)S(1)}, bf16[512,256]{1,0:T(8,128)(2,1)S(1)}, bf16[512,256]{1,0:T(8,128)(2,1)S(1)}) custom-call(s32[4]{0:T(128)S(1)} %copy-done.10, f32[512,1024]{1,0:T(8,128)S(1)} %copy-done.5, bf16[2,1024,1024]{2,1,0:T(8,128)(2,1)S(1)} %get-tuple-element.44.bases, bf16[128,1024]{1,0:T(8,128)(2,1)S(1)} %shard_map.105.refs_0_, ...), custom_call_target="tpu_custom_call" | custom-call | flops 536870912 | bytes 4194304 | tf_op jit(solution)/shard_map/pallas_call | solution.py:41
  70.0 0.6 collective-permute-start.18
  70.6 6.7 %shard_map.111 = (bf16[1024,1024]{1,0:T(8,128)(2,1)S(1)}, bf16[1024,1024]{1,0:T(8,128)(2,1)S(1)}) custom-call(s32[4]{0:T(128)S(1)} %copy-done.10, bf16[1024,1024]{1,0:T(8,128)(2,1)S(1)} %get-tuple-element.47.gradient, bf16[2,1024,1024]{2,1,0:T(8,128)(2,1)S(1)} %get-tuple-element.44.bases, f32[1024,1024]{1,0:T(8,128)S(1)} %get-tuple-element.52.stat), custom_call_target="tpu_custom_call" | custom-call | flops 4294967296 | bytes 8388608 | tf_op jit(solution)/shard_map/pallas_call | solution.py:41
  77.3 1.1 %collective-permute-done.18.came = bf16[512,256]{1,0:T(8,128)(2,1)S(1)} collective-permute-done((bf16[512,256]{1,0:T(8,128)(2,1)S(1)}, bf16[512,256]{1,0:T(8,128)(2,1)S(1)}, u32[]{:S(2)}, u32[]{:S(2)}) %collective-permute-start.18) | collective-permute-done | bytes 262176 | tf_op jit(solution)/shard_map/ppermute | solution.py:301
  78.4 4.1 %shard_map.110 = (f32[1024,256]{1,0:T(8,128)S(1)}, bf16[512,256]{1,0:T(8,128)(2,1)S(1)}, bf16[512,256]{1,0:T(8,128)(2,1)S(1)}) custom-call(s32[4]{0:T(128)S(1)} %copy-done.10, bf16[1024,1024]{1,0:T(8,128)(2,1)S(1)} %get-tuple-element.47.gradient, bf16[2,1024,1024]{2,1,0:T(8,128)(2,1)S(1)} %get-tuple-element.44.bases, ...), custom_call_target="tpu_custom_call" | custom-call | flops 2147483648 | bytes 4194304 | tf_op jit(solution)/shard_map/pallas_call | solution.py:41
  82.5 7.5 %shard_map.113.mine = f32[512,1024]{1,0:T(8,128)S(1)} custom-call(s32[4]{0:T(128)S(1)} %copy-done.10, bf16[1024,1024]{1,0:T(8,128)(2,1)S(1)} %get-tuple-element.60.start, bf16[1024,1024]{1,0:T(8,128)(2,1)S(1)} %get-tuple-element.61.start_turned), custom_call_target="tpu_custom_call" | custom-call | flops 6442450944 | bytes 4194304 | tf_op jit(solution)/shard_map/pallas_call | solution.py:41
  90.0 0.1 collective-permute-start.23
  90.1 0.5 collective-permute-start.22
  90.6 0.5 collective-permute-start.19
  91.1 0.0 collective-permute-start.20
  91.1 7.8 %collective-permute-done.19.came = bf16[512,256]{1,0:T(8,128)(2,1)S(1)} collective-permute-done((bf16[512,256]{1,0:T(8,128)(2,1)S(1)}, bf16[512,256]{1,0:T(8,128)(2,1)S(1)}, u32[]{:S(2)}, u32[]{:S(2)}) %collective-permute-start.19) | collective-permute-done | bytes 262176 | tf_op jit(solution)/shard_map/ppermute | solution.py:301
  98.9 1.5 %collective-permute-done.21.came_next = bf16[512,256]{1,0:T(8,128)(2,1)S(1)} collective-permute-done((bf16[512,256]{1,0:T(8,128)(2,1)S(1)}, bf16[512,256]{1,0:T(8,128)(2,1)S(1)}, u32[]{:S(2)}, u32[]{:S(2)}) %collective-permute-start.21) | collective-permute-done | bytes 262176 | tf_op jit(solution)/shard_map/ppermute | solution.py:298
  100.4 3.9 %shard_map.112 = (bf16[512,1024]{1,0:T(8,128)(2,1)}, f32[1024,512]{1,0:T(8,128)}) custom-call(s32[4]{0:T(128)S(1)} %copy-done.10, bf16[512,256]{1,0:T(8,128)(2,1)S(1)} %get-tuple-element.51.kept, bf16[512,256]{1,0:T(8,128)(2,1)S(1)} %collective-permute-done.19.came, bf16[512,256]{1,0:T(8,128)(2,1)S(1)} %collective-permute-done.20.kept_next, ...), custom_call_target="tpu_custom_call" | custom-call | flops 1073741824 | bytes 8388608 | tf_op jit(solution)/shard_map/pallas_call | solution.py:425
  104.3 0.0 collective-permute-done.23.theirs
  104.3 2.6 %shard_map.114 = (f32[512,1024]{1,0:T(8,128)}, f32[512,1024]{1,0:T(8,128)}) custom-call(s32[4]{0:T(128)S(1)} %copy-done.10, f32[512,1024]{1,0:T(8,128)S(1)} %shard_map.113.mine, f32[512,1024]{1,0:T(8,128)S(1)} %collective-permute-done.23.theirs), custom_call_target="tpu_custom_call" | custom-call | bytes 8388608 | tf_op jit(solution)/shard_map/pallas_call | solution.py:41
  (21 shorter events, 0.1 us)
Async XLA Ops:
  1.7 6.8 %collective-permute-start = (bf16[256,1024]{1,0:T(8,128)(2,1)S(1)}, bf16[256,1024]{1,0:T(8,128)(2,1)S(1)}, u32[]{:S(2)}, u32[]{:S(2)}) collective-permute-start(bf16[256,1024]{1,0:T(8,128)(2,1)S(1)} %dynamic-slice_bitcast_fusion), channel_id=1, source_target_pairs={{0,2},{2,0},{4,6},{6,4},{8,10},{10,8},{12,14},{14,12},{16,18},{18,... | collective-permute-start | bytes 1572872 | tf_op jit(solution)/shard_map/ppermute | solution.py:298
  2.8 5.7 %copy-start.4 = (bf16[1,512,1024]{2,1,0:T(8,128)(2,1)S(1)}, bf16[1,512,1024]{2,1,0:T(8,128)(2,1)}, u32[]{:S(2)}) copy-start(bf16[1,512,1024]{2,1,0:T(8,128)(2,1)} %group.1) | copy-start | bytes 3145732
  2.8 5.7 %copy-start.9 = (s32[4]{0:T(128)S(1)}, s32[4]{0:T(128)}, u32[]{:S(2)}) copy-start(s32[4]{0:T(128)} %pad_add_fusion.where) | copy-start | bytes 52
  6.0 44.7 %collective-permute-start.8 = (bf16[2,256,1024]{2,1,0:T(8,128)(2,1)}, bf16[2,256,1024]{2,1,0:T(8,128)(2,1)S(1)}, u32[]{:S(2)}, u32[]{:S(2)}) collective-permute-start(bf16[2,256,1024]{2,1,0:T(8,128)(2,1)} %shard_map.106), channel_id=1, source_target_pairs={{0,1},{1,0},{2,3},{3,2},{4,5},{5,4},{6,7},{7,6},{8,9},{9,8},{10,11... | collective-permute-start | bytes 3145736 | tf_op jit(solution)/shard_map/ppermute | solution.py:301
  8.6 51.4 %copy-start.3 = (f32[512,1024]{1,0:T(8,128)S(1)}, f32[512,1024]{1,0:T(8,128)}, u32[]{:S(2)}) copy-start(f32[512,1024]{1,0:T(8,128)} %right.5) | copy-start | bytes 6291460
  10.0 0.8 copy-start.7
  10.8 14.3 %copy-start.10 = (s32[4]{0:T(128)S(1)}, s32[4]{0:T(128)}, u32[]{:S(2)}) copy-start(s32[4]{0:T(128)} %pad_add_fusion.where) | copy-start | bytes 52
  10.8 14.2 %collective-permute-start.1 = (f32[128,1024]{1,0:T(8,128)}, f32[128,1024]{1,0:T(8,128)S(1)}, u32[]{:S(2)}, u32[]{:S(2)}) collective-permute-start(f32[128,1024]{1,0:T(8,128)} %get-tuple-element.35), channel_id=1, source_target_pairs={{0,4},{2,6},{4,0},{6,2},{8,12},{10,14},{12,8},{14,10},{16,20},{18,... | collective-permute-start | bytes 1572872 | tf_op jit(solution)/shard_map/ppermute | solution.py:298
  12.3 47.7 %copy-start.1 = (f32[512,1024]{1,0:T(8,128)S(1)}, f32[512,1024]{1,0:T(8,128)}, u32[]{:S(2)}) copy-start(f32[512,1024]{1,0:T(8,128)} %stat_right.1) | copy-start | bytes 6291460
  12.3 47.7 %copy-start.2 = (f32[512,1024]{1,0:T(8,128)S(1)}, f32[512,1024]{1,0:T(8,128)}, u32[]{:S(2)}) copy-start(f32[512,1024]{1,0:T(8,128)} %left.5) | copy-start | bytes 6291460
  15.5 44.5 %copy-start = (f32[512,1024]{1,0:T(8,128)S(1)}, f32[512,1024]{1,0:T(8,128)}, u32[]{:S(2)}) copy-start(f32[512,1024]{1,0:T(8,128)} %stat_left.1) | copy-start | bytes 6291460
  15.5 35.2 %collective-permute-start.9 = (f32[128,1280]{1,0:T(8,128)}, f32[128,1280]{1,0:T(8,128)S(1)}, u32[]{:S(2)}, u32[]{:S(2)}) collective-permute-start(f32[128,1280]{1,0:T(8,128)} %shard_map.107), channel_id=1, source_target_pairs={{0,1},{1,0},{2,3},{3,2},{4,5},{5,4},{6,7},{7,6},{8,9},{9,8},{10,11... | collective-permute-start | bytes 1966088 | tf_op jit(solution)/shard_map/ppermute | solution.py:301
  25.0 1.0 copy-start.8
  26.7 6.5 %collective-permute-start.2 = (f32[32,1024]{1,0:T(8,128)S(1)}, f32[32,1024]{1,0:T(8,128)S(1)}, u32[]{:S(2)}, u32[]{:S(2)}) collective-permute-start(f32[32,1024]{1,0:T(8,128)S(1)} %get-tuple-element.37), channel_id=1, source_target_pairs={{0,8},{2,10},{4,12},{6,14},{8,0},{10,2},{12,4},{14,6},{16,24},{18,... | collective-permute-start | bytes 393224 | tf_op jit(solution)/shard_map/ppermute | solution.py:298
  28.3 12.5 %collective-permute-start.3 = (f32[32,1024]{1,0:T(8,128)S(1)}, f32[32,1024]{1,0:T(8,128)S(1)}, u32[]{:S(2)}, u32[]{:S(2)}) collective-permute-start(f32[32,1024]{1,0:T(8,128)S(1)} %get-tuple-element.38), channel_id=1, source_target_pairs={{0,16},{2,18},{4,20},{6,22},{8,24},{10,26},{12,28},{14,30},{16,0},... | collective-permute-start | bytes 393224 | tf_op jit(solution)/shard_map/ppermute | solution.py:298
  30.9 9.9 %collective-permute-start.4 = (f32[32,1024]{1,0:T(8,128)S(1)}, f32[32,1024]{1,0:T(8,128)S(1)}, u32[]{:S(2)}, u32[]{:S(2)}) collective-permute-start(f32[32,1024]{1,0:T(8,128)S(1)} %get-tuple-element.39), channel_id=1, source_target_pairs={{0,24},{2,26},{4,28},{6,30},{8,16},{10,18},{12,20},{14,22},{16,8},... | collective-permute-start | bytes 393224 | tf_op jit(solution)/shard_map/ppermute | solution.py:298
  40.8 5.0 %collective-permute-start.5 = (bf16[32,1024]{1,0:T(8,128)(2,1)S(1)}, bf16[32,1024]{1,0:T(8,128)(2,1)S(1)}, u32[]{:S(2)}, u32[]{:S(2)}) collective-permute-start(bf16[32,1024]{1,0:T(8,128)(2,1)S(1)} %shard_map.104.refs_0_), channel_id=1, source_target_pairs={{0,8},{2,10},{4,12},{6,14},{8,0},{10,2},{12,4},{14,6},{16,24},{18,... | collective-permute-start | bytes 196616 | tf_op jit(solution)/shard_map/ppermute | solution.py:298
  42.8 6.2 %collective-permute-start.6 = (bf16[32,1024]{1,0:T(8,128)(2,1)S(1)}, bf16[32,1024]{1,0:T(8,128)(2,1)S(1)}, u32[]{:S(2)}, u32[]{:S(2)}) collective-permute-start(bf16[32,1024]{1,0:T(8,128)(2,1)S(1)} %shard_map.104.refs_0_), channel_id=1, source_target_pairs={{0,16},{2,18},{4,20},{6,22},{8,24},{10,26},{12,28},{14,30},{16,0},... | collective-permute-start | bytes 196616 | tf_op jit(solution)/shard_map/ppermute | solution.py:298
  43.9 6.2 %collective-permute-start.7 = (bf16[32,1024]{1,0:T(8,128)(2,1)S(1)}, bf16[32,1024]{1,0:T(8,128)(2,1)S(1)}, u32[]{:S(2)}, u32[]{:S(2)}) collective-permute-start(bf16[32,1024]{1,0:T(8,128)(2,1)S(1)} %shard_map.104.refs_0_), channel_id=1, source_target_pairs={{0,24},{2,26},{4,28},{6,30},{8,16},{10,18},{12,20},{14,22},{16,8},... | collective-permute-start | bytes 196616 | tf_op jit(solution)/shard_map/ppermute | solution.py:298
  50.7 17.6 %copy-start.5 = (f32[512,1024]{1,0:T(8,128)S(1)}, f32[512,1024]{1,0:T(8,128)}, u32[]{:S(2)}) copy-start(f32[512,1024]{1,0:T(8,128)} %moment.1) | copy-start | bytes 6291460
  50.7 9.3 %collective-permute-start.12 = (bf16[2,256,1024]{2,1,0:T(8,128)(2,1)S(1)}, bf16[2,256,1024]{2,1,0:T(8,128)(2,1)S(1)}, u32[]{:S(2)}, u32[]{:S(2)}) collective-permute-start(bf16[2,256,1024]{2,1,0:T(8,128)(2,1)S(1)} %collective-permute-done.8.mine), channel_id=1, source_target_pairs={{0,2},{2,0},{4,6},{6,4},{8,10},{10,8},{12,14},{14,12},{16,18},{18,... | collective-permute-start | bytes 3145736 | tf_op jit(solution)/shard_map/ppermute | solution.py:298
  50.8 9.2 %collective-permute-start.13 = (bf16[128,1024]{1,0:T(8,128)(2,1)S(1)}, bf16[128,1024]{1,0:T(8,128)(2,1)S(1)}, u32[]{:S(2)}, u32[]{:S(2)}) collective-permute-start(bf16[128,1024]{1,0:T(8,128)(2,1)S(1)} %shard_map.105.refs_0_), channel_id=1, source_target_pairs={{0,4},{2,6},{4,0},{6,2},{8,12},{10,14},{12,8},{14,10},{16,20},{18,... | collective-permute-start | bytes 786440 | tf_op jit(solution)/shard_map/ppermute | solution.py:298
  52.3 14.0 %collective-permute-start.10 = (bf16[128,1024]{1,0:T(8,128)(2,1)S(1)}, bf16[128,1024]{1,0:T(8,128)(2,1)S(1)}, u32[]{:S(2)}, u32[]{:S(2)}) collective-permute-start(bf16[128,1024]{1,0:T(8,128)(2,1)S(1)} %shard_map.105.refs_0_), channel_id=1, source_target_pairs={{0,1},{1,0},{2,3},{3,2},{4,5},{5,4},{6,7},{7,6},{8,9},{9,8},{10,11... | collective-permute-start | bytes 786440 | tf_op jit(solution)/shard_map/ppermute | solution.py:301
  52.9 13.5 %collective-permute-start.11 = (bf16[128,1024]{1,0:T(8,128)(2,1)S(1)}, bf16[128,1024]{1,0:T(8,128)(2,1)S(1)}, u32[]{:S(2)}, u32[]{:S(2)}) collective-permute-start(bf16[128,1024]{1,0:T(8,128)(2,1)S(1)} %shard_map.105.refs_0_), channel_id=1, source_target_pairs={{0,5},{1,4},{2,7},{3,6},{4,1},{5,0},{6,3},{7,2},{8,13},{9,12},{10,... | collective-permute-start | bytes 786440 | tf_op jit(solution)/shard_map/ppermute | solution.py:305
  54.3 12.5 %collective-permute-start.14 = (bf16[128,1024]{1,0:T(8,128)(2,1)S(1)}, bf16[128,1024]{1,0:T(8,128)(2,1)S(1)}, u32[]{:S(2)}, u32[]{:S(2)}) collective-permute-start(bf16[128,1024]{1,0:T(8,128)(2,1)S(1)} %shard_map.105.refs_0_), channel_id=1, source_target_pairs={{0,2},{2,0},{4,6},{6,4},{8,10},{10,8},{12,14},{14,12},{16,18},{18,... | collective-permute-start | bytes 786440 | tf_op jit(solution)/shard_map/ppermute | solution.py:298
  60.0 6.9 %collective-permute-start.15 = (bf16[128,1024]{1,0:T(8,128)(2,1)S(1)}, bf16[128,1024]{1,0:T(8,128)(2,1)S(1)}, u32[]{:S(2)}, u32[]{:S(2)}) collective-permute-start(bf16[128,1024]{1,0:T(8,128)(2,1)S(1)} %collective-permute-done.13.refs_1_), channel_id=1, source_target_pairs={{0,2},{2,0},{4,6},{6,4},{8,10},{10,8},{12,14},{14,12},{16,18},{18,... | collective-permute-start | bytes 786440 | tf_op jit(solution)/shard_map/ppermute | solution.py:298
  66.3 1.5 %collective-permute-start.16 = (bf16[128,1024]{1,0:T(8,128)(2,1)S(1)}, bf16[128,1024]{1,0:T(8,128)(2,1)S(1)}, u32[]{:S(2)}, u32[]{:S(2)}) collective-permute-start(bf16[128,1024]{1,0:T(8,128)(2,1)S(1)} %collective-permute-done.10.refs_4_), channel_id=1, source_target_pairs={{0,2},{2,0},{4,6},{6,4},{8,10},{10,8},{12,14},{14,12},{16,18},{18,... | collective-permute-start | bytes 786440 | tf_op jit(solution)/shard_map/ppermute | solution.py:298
  66.3 1.9 %collective-permute-start.17 = (bf16[128,1024]{1,0:T(8,128)(2,1)S(1)}, bf16[128,1024]{1,0:T(8,128)(2,1)S(1)}, u32[]{:S(2)}, u32[]{:S(2)}) collective-permute-start(bf16[128,1024]{1,0:T(8,128)(2,1)S(1)} %collective-permute-done.11.refs_5_), channel_id=1, source_target_pairs={{0,2},{2,0},{4,6},{6,4},{8,10},{10,8},{12,14},{14,12},{16,18},{18,... | collective-permute-start | bytes 786440 | tf_op jit(solution)/shard_map/ppermute | solution.py:298
  70.0 8.4 %collective-permute-start.18 = (bf16[512,256]{1,0:T(8,128)(2,1)S(1)}, bf16[512,256]{1,0:T(8,128)(2,1)S(1)}, u32[]{:S(2)}, u32[]{:S(2)}) collective-permute-start(bf16[512,256]{1,0:T(8,128)(2,1)S(1)} %get-tuple-element.50), channel_id=1, source_target_pairs={{0,1},{1,0},{2,3},{3,2},{4,5},{5,4},{6,7},{7,6},{8,9},{9,8},{10,11... | collective-permute-start | bytes 786440 | tf_op jit(solution)/shard_map/ppermute | solution.py:301
  70.6 7.9 %copy-start.6 = (f32[1024,512]{1,0:T(8,128)S(1)}, f32[1024,512]{1,0:T(8,128)}, u32[]{:S(2)}) copy-start(f32[1024,512]{1,0:T(8,128)} %second.1) | copy-start | bytes 6291460
  90.0 14.3 %collective-permute-start.23 = (f32[512,1024]{1,0:T(8,128)S(1)}, f32[512,1024]{1,0:T(8,128)S(1)}, u32[]{:S(2)}, u32[]{:S(2)}) collective-permute-start(f32[512,1024]{1,0:T(8,128)S(1)} %shard_map.113.mine), channel_id=1, source_target_pairs={{0,2},{2,0},{4,6},{6,4},{8,10},{10,8},{12,14},{14,12},{16,18},{18,... | collective-permute-start | bytes 6291464 | tf_op jit(solution)/shard_map/ppermute | solution.py:298
  90.1 10.3 %collective-permute-start.22 = (f32[1024,256]{1,0:T(8,128)S(1)}, f32[1024,256]{1,0:T(8,128)S(1)}, u32[]{:S(2)}, u32[]{:S(2)}) collective-permute-start(f32[1024,256]{1,0:T(8,128)S(1)} %get-tuple-element.57.new), channel_id=1, source_target_pairs={{0,2},{2,0},{4,6},{6,4},{8,10},{10,8},{12,14},{14,12},{16,18},{18,... | collective-permute-start | bytes 3145736 | tf_op jit(solution)/shard_map/ppermute | solution.py:298
  90.6 8.3 %collective-permute-start.19 = (bf16[512,256]{1,0:T(8,128)(2,1)S(1)}, bf16[512,256]{1,0:T(8,128)(2,1)S(1)}, u32[]{:S(2)}, u32[]{:S(2)}) collective-permute-start(bf16[512,256]{1,0:T(8,128)(2,1)S(1)} %get-tuple-element.55), channel_id=1, source_target_pairs={{0,1},{1,0},{2,3},{3,2},{4,5},{5,4},{6,7},{7,6},{8,9},{9,8},{10,11... | collective-permute-start | bytes 786440 | tf_op jit(solution)/shard_map/ppermute | solution.py:301
  91.1 7.8 %collective-permute-start.20 = (bf16[512,256]{1,0:T(8,128)(2,1)S(1)}, bf16[512,256]{1,0:T(8,128)(2,1)S(1)}, u32[]{:S(2)}, u32[]{:S(2)}) collective-permute-start(bf16[512,256]{1,0:T(8,128)(2,1)S(1)} %get-tuple-element.51.kept), channel_id=1, source_target_pairs={{0,2},{2,0},{4,6},{6,4},{8,10},{10,8},{12,14},{14,12},{16,18},{18,... | collective-permute-start | bytes 786440 | tf_op jit(solution)/shard_map/ppermute | solution.py:298
  98.9 1.5 %collective-permute-start.21 = (bf16[512,256]{1,0:T(8,128)(2,1)S(1)}, bf16[512,256]{1,0:T(8,128)(2,1)S(1)}, u32[]{:S(2)}, u32[]{:S(2)}) collective-permute-start(bf16[512,256]{1,0:T(8,128)(2,1)S(1)} %collective-permute-done.19.came), channel_id=1, source_target_pairs={{0,2},{2,0},{4,6},{6,4},{8,10},{10,8},{12,14},{14,12},{16,18},{18,... | collective-permute-start | bytes 786440 | tf_op jit(solution)/shard_map/ppermute | solution.py:298

commit v5 on v4

--- a/solution.py
+++ b/solution.py
@@ -37,13 +37,16 @@
     return pl.ds(pl.multiple_of(index * size, size), size)
 
 
-def call(kernel, outs, operands, specs, scratch=(), flops=0, moved=0, limit=24, space=VMEM):
+def call(
+    kernel, outs, operands, specs, scratch=(), flops=0, moved=0, limit=24, space=VMEM, aliases=None
+):
     return pl.pallas_call(
         kernel,
         out_shape=outs,
         in_specs=specs,
         out_specs=[space] * len(outs),
         scratch_shapes=list(scratch),
+        input_output_aliases=aliases or {},
         compiler_params=pltpu.CompilerParams(vmem_limit_bytes=limit * 2**20),
         cost_estimate=pl.CostEstimate(flops=flops, bytes_accessed=moved, transcendentals=0),
     )(*operands)
@@ -60,54 +63,87 @@
 UPPER = [(i, j) for i in range(TILES) for j in range(i, TILES)]
 
 
-def bases_kernel(where, left, right, out):
-    out[0] = left[...].astype(HALF)
-    out[1] = right[...].astype(HALF)
-
-
-def stats_kernel(where, left, right, out, sem):
-    size = out.shape[0]
-    rows = size * TILES
-    for core, stat in enumerate((left, right)):
-
-        @pl.when(where[1] == core)
+def start_kernel(
+    where,
+    group,
+    came,
+    left,
+    right,
+    stat_left,
+    stat_right,
+    state,
+    near_kept,
+    near_sent,
+    kept,
+    far_1,
+    far_2,
+    far_3,
+    basis_in,
+    stat_in,
+    sem,
+):
+    position, core, x, z = where[0], where[1], where[2], where[3]
+    half, width = basis_in.shape[1:]
+    size = state.shape[1]
+    bases = [
+        pltpu.make_async_copy(basis.at[tile(core, half)], basis_in.at[i], sem.at[i])
+        for i, basis in enumerate((left, right))
+    ]
+    for copy in bases:
+        copy.start()
+    for side, stat in enumerate((stat_left, stat_right)):
+
+        @pl.when(core == side)
         def _():
-            begin = where[0] * rows
-            run_all(
-                [
-                    pltpu.make_async_copy(
-                        stat.at[
-                            i * size : (i + 1) * size,
-                            pl.ds(pl.multiple_of(begin + j * size, size), size),
-                        ],
-                        out.at[:, place * size : (place + 1) * size],
-                        sem.at[place],
-                    )
-                    for place, (i, j) in enumerate(UPPER)
-                ]
-            )
-
-
-def first_sum_kernel(where, group, came, kept, sent):
-    size = kept.shape[0]
-    core, x = where[1], where[2]
-    kept[...] = group[0, tile(core * 2 + x, size)].astype(FULL) + came[tile(x, size)].astype(FULL)
-    sent[...] = group[0, tile(core * 2 + 1 - x, size)].astype(FULL) + came[
-        tile(1 - x, size)
-    ].astype(FULL)
-
-
-def second_sum_kernel(where, kept, came, own, *sent):
-    size = own.shape[0]
-    z = where[3]
-    own[...] = kept[tile(z, size)] + came[tile(z, size)]
-    for k, out in enumerate(sent):
-        there = tile(z ^ (k + 1), size)
-        out[...] = kept[there] + came[there]
-
-
-def third_sum_kernel(own, one, two, three, out):
-    out[...] = ((own[...] + one[...]) + (two[...] + three[...])).astype(HALF)
+            pltpu.make_async_copy(stat.at[:, tile(position, size * TILES)], stat_in, sem.at[2]).start()
+
+    rows, cut = near_kept.shape
+    for out, there in ((near_kept, x), (near_sent, 1 - x)):
+        out[...] = group[0, tile(core * 2 + there, rows), :cut].astype(FULL) + came[
+            tile(there, rows), :cut
+        ].astype(FULL)
+    rows = kept.shape[0] // 2
+    for k, out in enumerate((kept, far_1, far_2, far_3)):
+        for i in range(2):
+            there = i * 4 + (z ^ k)
+            out[i * rows : (i + 1) * rows] = group[0, tile(core * 8 + there, rows), cut:].astype(
+                FULL
+            ) + came[tile(there, rows), cut:].astype(FULL)
+    for copy in bases:
+        copy.wait()
+    across = width // size
+    for band in range(2 * half // size):
+        for column in range(across):
+            begin = band * size % half
+            state[band * across + column] = basis_in[
+                band * size // half, begin : begin + size, column * size : (column + 1) * size
+            ].astype(HALF)
+    pltpu.make_async_copy(stat_left.at[:, : size * TILES], stat_in, sem.at[2]).wait()
+    base = 2 * half * width // size**2
+    for place, (i, j) in enumerate(UPPER):
+        value = stat_in[i * size : (i + 1) * size, j * size : (j + 1) * size]
+        high = value.astype(HALF)
+        state[base + place] = high
+        state[base + len(UPPER) + place] = (value - high.astype(FULL)).astype(HALF)
+
+
+def second_sum_kernel(
+    where, near_kept, near_came, kept, one, two, three, near_own, near_1, near_2, near_3, own, sent
+):
+    size = near_own.shape[0]
+    x, z = where[2], where[3]
+    for k, out in enumerate((near_own, near_1, near_2, near_3)):
+        there = tile(z ^ k, size)
+        out[...] = near_kept[there] + near_came[there]
+    for k, out in enumerate((own, sent)):
+        there = tile(x ^ k, size)
+        out[...] = (kept[there] + one[there]) + (two[there] + three[there])
+
+
+def third_sum_kernel(near_own, one, two, three, own, came, out):
+    cut = near_own.shape[1]
+    out[:, :cut] = ((near_own[...] + one[...]) + (two[...] + three[...])).astype(HALF)
+    out[:, cut:] = (own[...] + came[...]).astype(HALF)
 
 
 def joined_kernel(where, *refs):
@@ -119,17 +155,25 @@
 
 
 def place_basis(where, out, own, mine, theirs, side):
-    rows = own.shape[0]
+    rows, width = own.shape
     half = rows // 2
+    size = mine.shape[1]
     position, core = where[0], where[1]
+    across = width // size
+    count = half // size * across
     out[tile(position, rows)] = own[...].astype(HALF)
     other = (1 - position) * 2
-    out[tile(other + core, half)] = mine[side]
-    out[tile(other + 1 - core, half)] = theirs[side]
+    for part, block in ((mine, other + core), (theirs, other + 1 - core)):
+        for band in range(half // size):
+            here = tile(block * (half // size) + band, size)
+            for column in range(across):
+                out[here, column * size : (column + 1) * size] = part[
+                    side * count + band * across + column
+                ]
 
 
 def state_kernel(
-    where, left, right, mine, theirs, stat_left, stat_right, came, bases, turned, back, full, sem
+    where, left, right, mine, theirs, stat_left, stat_right, bases, turned, back, full, sem
 ):
     rows, width = left.shape
     size = rows // TILES
@@ -146,8 +190,9 @@
     turned[...] = bases[core].T
     back[...] = bases[1 - core].T
     base = (1 - position) * TILES
+    first = rows * width // size**2
     for place, (i, j) in enumerate(UPPER):
-        value = came[:, place * size : (place + 1) * size]
+        value = mine[first + place].astype(FULL) + mine[first + len(UPPER) + place].astype(FULL)
         full[tile(base + i, size), tile(base + j, size)] = value
         if i != j:
             full[tile(base + j, size), tile(base + i, size)] = value.T
@@ -158,17 +203,15 @@
 def moment_kernel(where, moment, bases, *refs):
     parts, (gradient, ours, others, sem) = refs[:-4], refs[-4:]
     position, core, x = where[0], where[1], where[2]
-    size = parts[0].shape[0]
     rows = moment.shape[0]
     step = rows // 2
     copies = []
     for place, part in enumerate(parts):
+        size = part.shape[0]
         block = (
-            (position ^ (place // 4)) * 4 + (core ^ (place % 4 // 2)) * 2 + (x ^ (place % 2))
+            (position ^ (place // 4)) * 4 + (core ^ (place // 2 % 2)) * 2 + (x ^ (place % 2))
         )
-        copies.append(
-            pltpu.make_async_copy(part, gradient.at[tile(block, size)], sem.at[place])
-        )
+        copies.append(pltpu.make_async_copy(part, gradient.at[tile(block, size)], sem.at[place]))
     run_all(copies)
     half = (
         BETA_ONE * moment[...] + (1.0 - BETA_ONE) * gradient[tile(position, rows)].astype(FULL)
@@ -220,17 +263,26 @@
         copy.wait()
 
 
-def sides_kernel(where, mine, theirs, left, right, sem):
-    for core, (one, two) in enumerate(((mine, theirs), (theirs, mine))):
-
-        @pl.when(where[1] == core)
+def write_sides(core, top, low, side, left, right, sem):
+    half = top.shape[0]
+    for place, out in enumerate((left, right)):
+
+        @pl.when((core ^ side) == place)
         def _():
             run_all(
                 [
-                    pltpu.make_async_copy(one, left, sem.at[0]),
-                    pltpu.make_async_copy(two, right, sem.at[1]),
+                    pltpu.make_async_copy(top, out.at[:half], sem.at[0]),
+                    pltpu.make_async_copy(low, out.at[half:], sem.at[1]),
                 ]
             )
+
+
+def own_side_kernel(where, top, low, left, right, sem):
+    write_sides(where[1], top, low, 0, left, right, sem)
+
+
+def next_side_kernel(where, top, low, left_in, right_in, left, right, sem):
+    write_sides(where[1], top, low, 1, left, right, sem)
 
 
 def quarters(width):
@@ -256,31 +308,37 @@
         turned[here] = value.T
 
 
-def refresh_kernel(where, start, start_turned, out, following, following_turned, gram):
+def improved(current, turned, kept, gram, result, result_turned):
+    size, width = result.shape
+    for here in quarters(width):
+        gram[:size, here] = (matmul(current[kept], turned[:, here]) * (1.0 / width)).astype(HALF)
+    for here in quarters(width):
+        value = (
+            1.5 * current[kept, here].astype(FULL) - 0.5 * matmul(gram[:size], current[:, here])
+        ).astype(result.dtype)
+        result[:, here] = value
+        if result_turned is not None:
+            result_turned[here] = value.T
+
+
+def refresh_kernel(where, start, start_turned, current, turned, out, *scratch):
     width = start.shape[0]
-    rows = out.shape[0]
-
-    def improved(current, turned, kept, result, result_turned):
-        size = result.shape[0]
-        for here in quarters(width):
-            gram[:size, here] = (matmul(current[kept], turned[:, here]) * (1.0 / width)).astype(
-                HALF
-            )
-        for here in quarters(width):
-            value = (
-                1.5 * current[kept, here].astype(FULL)
-                - 0.5 * matmul(gram[:size], current[:, here])
-            ).astype(result.dtype)
-            result[:, here] = value
-            if result_turned is not None:
-                result_turned[here] = value.T
-
-    current, turned = start, start_turned
+    rows = width // 2
+    gram, between = scratch[0], scratch[1:]
+    source, source_turned = start, start_turned
     for iteration in range(NS_ITERS - 1):
-        place = iteration % 2
-        improved(current, turned, slice(0, width), following.at[place], following_turned.at[place])
-        current, turned = following.at[place], following_turned.at[place]
-    improved(current, turned, tile(where[0], rows), out, None)
+        last = iteration + 2 == NS_ITERS
+        if last:
+            result, result_turned = current, turned
+        else:
+            result, result_turned = between[0].at[iteration % 2], between[1].at[iteration % 2]
+        improved(source, source_turned, slice(0, width), gram, result, result_turned)
+        source, source_turned = result, result_turned
+    improved(current, turned, tile(where[0] * 2, rows // 2), gram, out, None)
+
+
+def last_kernel(where, current, turned, out, gram):
+    improved(current, turned, tile(where[0] * 2 + 1, out.shape[0]), gram, out, None)
 
 
 def fast_body(group_grads, moment, second, stat_left, stat_right, basis_left, basis_right):
@@ -304,61 +362,57 @@
         pairs = [(i, i ^ 5) for i in range(32)]
         return lax.ppermute(value, ("dp", "shard"), pairs)
 
-    step = half // 2
-    (bases_sent,) = pl.pallas_call(
-        bases_kernel,
-        out_shape=[shaped((2, half, width), HALF)],
-        grid_spec=pltpu.PrefetchScalarGridSpec(
-            num_scalar_prefetch=1,
-            grid=(2,),
-            in_specs=[pl.BlockSpec((step, width), lambda i, where: (where[1] * 2 + i, 0))] * 2,
-            out_specs=[pl.BlockSpec((2, step, width), lambda i, where: (0, i, 0))],
-        ),
-        compiler_params=pltpu.CompilerParams(vmem_limit_bytes=56 * 2**20),
-        cost_estimate=pl.CostEstimate(flops=0, bytes_accessed=2**22, transcendentals=0),
-    )(where, basis_left, basis_right)
-    bases_mine = shard_swap(bases_sent)
-
     raw = lax.dynamic_slice_in_dim(group_grads[0], (1 - core) * half, half, 0)
     came = dp_swap(raw, 1)
-    kept, sent = call(
-        first_sum_kernel,
-        [shaped((quarter, width), FULL)] * 2,
-        (where, group_grads, came),
-        [SMEM, VMEM, VMEM],
-        moved=2**21,
-    )
+    cut = width * 5 // 8
+    rest = width - cut
+    tiles = rows * width // quarter**2 + 2 * len(UPPER)
+    state_sent, near_kept, near_sent, kept, *sent = call(
+        start_kernel,
+        [shaped((tiles, quarter, quarter), HALF)]
+        + [shaped((quarter, cut), FULL)] * 2
+        + [shaped((quarter // 2, rest), FULL)] * 4,
+        (where, group_grads, came, basis_left, basis_right, stat_left, stat_right),
+        [SMEM] + [VMEM] * 2 + [ANY] * 4,
+        [
+            pltpu.VMEM((2, half, width), FULL),
+            pltpu.VMEM((rows, rows), FULL),
+            pltpu.SemaphoreType.DMA((3,)),
+        ],
+        moved=2**22,
+        limit=52,
+    )
+    near_came = dp_swap(near_sent, 2)
+    came = [dp_swap(value, 4 * (k + 1)) for k, value in enumerate(sent)]
+    state_mine = shard_swap(state_sent)
+    near_own, *near_sent, own, sent = call(
+        second_sum_kernel,
+        [shaped((chunk, cut), FULL)] * 4 + [shaped((chunk, rest), FULL)] * 2,
+        (where, near_kept, near_came, kept, *came),
+        [SMEM] + [VMEM] * 6,
+        moved=2**20,
+    )
+    near_came = [dp_swap(value, 4 * (k + 1)) for k, value in enumerate(near_sent)]
     came = dp_swap(sent, 2)
-    own, *sent = call(
-        second_sum_kernel,
-        [shaped((chunk, width), FULL)] * 4,
-        (where, kept, came),
-        [SMEM, VMEM, VMEM],
-        moved=2**20,
-    )
-    (stats_sent,) = call(
-        stats_kernel,
-        [shaped((quarter, len(UPPER) * quarter), FULL)],
-        (where, stat_left, stat_right),
-        [SMEM, ANY, ANY],
-        [pltpu.SemaphoreType.DMA((len(UPPER),))],
-        moved=2**21,
-        limit=56,
-    )
-    stats_mine = shard_swap(stats_sent)
-    pieces = [dp_swap(value, 4 * (k + 1)) for k, value in enumerate(sent)]
     (piece,) = call(
-        third_sum_kernel, [shaped((chunk, width), HALF)], (own, *pieces), [VMEM] * 4, moved=2**19
+        third_sum_kernel,
+        [shaped((chunk, width), HALF)],
+        (near_own, *near_came, own, came),
+        [VMEM] * 6,
+        moved=2**19,
     )
     pieces = [piece] + [dp_swap(piece, 4 * k) for k in (1, 2, 3)]
     (part,) = call(
-        joined_kernel, [shaped((quarter, width), HALF)], (where, *pieces), [SMEM] + [VMEM] * 4,
+        joined_kernel,
+        [shaped((quarter, width), HALF)],
+        (where, *pieces),
+        [SMEM] + [VMEM] * 4,
         moved=2**19,
     )
-    part, bases_mine, stats_mine = lax.optimization_barrier((part, bases_mine, stats_mine))
+    part, state_mine = lax.optimization_barrier((part, state_mine))
     parts = [part, dp_swap(part, 2), shard_swap(part), cross_swap(part)]
 
-    bases_theirs = dp_swap(bases_mine, 1)
+    state_theirs = dp_swap(state_mine, 1)
     square = shaped((width, width), HALF)
     bases, left_turned, right_turned, stat = call(
         state_kernel,
@@ -367,19 +421,18 @@
             where,
             basis_left,
             basis_right,
-            bases_mine,
-            bases_theirs,
+            state_mine,
+            state_theirs,
             stat_left,
             stat_right,
-            stats_mine,
         ),
-        [SMEM] + [VMEM] * 4 + [ANY] * 2 + [VMEM],
+        [SMEM] + [VMEM] * 4 + [ANY] * 2,
         [pltpu.SemaphoreType.DMA(())],
         moved=2**24,
     )
     parts[2], parts[3], bases = lax.optimization_barrier((parts[2], parts[3], bases))
     swapped = [dp_swap(value, 1) for value in parts]
-    ordered = [parts[0], parts[1], swapped[0], swapped[1], parts[2], parts[3], swapped[2], swapped[3]]
+    ordered = parts[:2] + swapped[:2] + parts[2:] + swapped[2:]
     gradient, moment_mine, moment_sent = call(
         moment_kernel,
         [square] + [shaped((rows, half), HALF)] * 2,
@@ -411,16 +464,28 @@
     back_came = shard_swap(back_sent)
     new_next = dp_swap(new, 1)
     back_kept_next = dp_swap(back_kept, 1)
-    (side_new,) = call(
+    current, current_turned, top = call(
         refresh_kernel,
-        [shaped((rows, width), FULL)],
+        [square] * 2 + [shaped((half, width), FULL)],
         (where, start, start_turned),
         [SMEM] + [VMEM] * 2,
-        [pltpu.VMEM((2, width, width), HALF)] * 2 + [pltpu.VMEM((width, width), HALF)],
-        flops=3 * unit,
+        [pltpu.VMEM((width, width), HALF)]
+        + [pltpu.VMEM((2, width, width), HALF)] * (2 if NS_ITERS > 2 else 0),
+        flops=5 * unit // 2,
         moved=2**22,
     )
-    side_next = dp_swap(side_new, 1)
+    top_next = dp_swap(top, 1)
+    current, back_came = lax.optimization_barrier((current, back_came))
+    (low,) = call(
+        last_kernel,
+        [shaped((half, width), FULL)],
+        (where, current, current_turned),
+        [SMEM] + [VMEM] * 2,
+        [pltpu.VMEM((half, width), HALF)],
+        flops=unit // 2,
+        moved=2**21,
+    )
+    low_next = dp_swap(low, 1)
     back_came_next = dp_swap(back_came, 1)
     update, second_new = pl.pallas_call(
         update_kernel,
@@ -442,14 +507,25 @@
         new,
         new_next,
     )
+    sides = [shaped((rows, width), FULL)] * 2
     left_new, right_new = call(
-        sides_kernel,
-        [shaped((rows, width), FULL)] * 2,
-        (where, side_new, side_next),
+        own_side_kernel,
+        sides,
+        (where, top, low),
         [SMEM, ANY, ANY],
         [pltpu.SemaphoreType.DMA((2,))],
-        moved=2**23,
+        moved=2**22,
         space=ANY,
+    )
+    left_new, right_new = call(
+        next_side_kernel,
+        sides,
+        (where, top_next, low_next, left_new, right_new),
+        [SMEM] + [ANY] * 4,
+        [pltpu.SemaphoreType.DMA((2,))],
+        moved=2**22,
+        space=ANY,
+        aliases={3: 0, 4: 1},
     )
     return (update, second_new, left_new, right_new)
 

time: 107 us -> 102 us (0.953)
  waiting for transfers between devices: 44.3 us -> 34.1 us
  starting transfers between devices: 19.9 us -> 27.2 us
  local copies, waits for them, and re-layouts: 2.96 us -> 1.11 us
    ppermute x18 -> x23, waiting for transfers between devices: 31.9 us -> 26.3 us  [dp_swap(): return lax.ppermute(value, 'dp', [(i, i ^ distance) for i in range(16)])]
    ppermute x18 -> x23, starting transfers between devices: 13.7 us -> 19.3 us  [dp_swap(): return lax.ppermute(value, 'dp', [(i, i ^ distance) for i in range(16)])]
    ppermute x5 -> x4, waiting for transfers between devices: 12.4 us -> 7.79 us  [shard_swap(): return lax.ppermute(value, 'shard', [(0, 1), (1, 0)])]
    pallas_call x1 -> x0, Pallas kernels: 3.18 us -> none  [fast_body(): pl.pallas_call(bases_kernel, out_shape=[shaped((2, half, width), HALF)],...]
    ppermute x5 -> x4, starting transfers between devices: 4.7 us -> 7.65 us  [shard_swap(): return lax.ppermute(value, 'shard', [(0, 1), (1, 0)])]
    pallas_call x11 -> x12, Pallas kernels: 31.3 us -> 34.2 us  [call(): pl.pallas_call(kernel, out_shape=outs, in_specs=specs, out_specs=[space]...]
    unnamed x22 -> x12, local copies, waits for them, and re-layouts: 1.88 us -> 0.02 us
    ppermute x1, starting transfers between devices: 1.49 us -> 0.26 us  [cross_swap(): return lax.ppermute(value, ('dp', 'shard'), pairs)]
  transfers between devices with their start and end apart: 24 -> 28, of which waited for: 13 -> 16; matrix products, arithmetic and copies ran while one was open for 1% -> 0% of each run, Pallas kernels for 21% -> 25%
where the time goes in v5:
time: 102 us; the launch traced here: 101 us
  Pallas kernels  38 us (37%)
  waiting for transfers between devices  34.1 us (33%)
  starting transfers between devices  27.2 us (27%)
  local copies, waits for them, and re-layouts  1.11 us (1%)
    pallas_call x12, Pallas kernels, call(): pl.pallas_call(kernel, out_shape=outs, in_specs=specs, out_specs=[space]...  34.2 us
    ppermute x23, waiting for transfers between devices, dp_swap(): return lax.ppermute(value, 'dp', [(i, i ^ distance) for i in range(16)])  26.3 us
    ppermute x23, starting transfers between devices, dp_swap(): return lax.ppermute(value, 'dp', [(i, i ^ distance) for i in range(16)])  19.3 us
    ppermute x4, waiting for transfers between devices, shard_swap(): return lax.ppermute(value, 'shard', [(0, 1), (1, 0)])  7.79 us
    ppermute x4, starting transfers between devices, shard_swap(): return lax.ppermute(value, 'shard', [(0, 1), (1, 0)])  7.65 us
    pallas_call x1, Pallas kernels, fast_body(): pl.pallas_call(update_kernel, out_shape=[shaped((rows, width), HALF), sha...  3.86 us
  transfers between devices with their start and end apart: 28, of which 16 were waited for; matrix products, arithmetic and copies ran while one was open for 0% of the time, Pallas kernels for 25%

profile of v5, /device:TPU:0, one launch (start us, length us, event | category | flops | bytes accessed | tf_op | source)
XLA Modules:
  0.0 101.5 jit_solution(9958583026153490175)
XLA Ops:
  0.6 1.1 %dynamic-slice_bitcast_fusion = bf16[256,1024]{1,0:T(8,128)(2,1)S(1)} fusion(bf16[1,512,1024]{2,1,0:T(8,128)(2,1)} %group.1, s32[]{:T(128)S(6)} %select_n.3), kind=kLoop, calls=%fused_computation | loop fusion | bytes 1048580 | tf_op jit(solution)/shard_map/dynamic_slice | solution.py:365
  1.7 0.5 collective-permute-start
  2.2 0.1 pad_add_fusion.where
  2.3 1.5 %collective-permute-done.came = bf16[256,1024]{1,0:T(8,128)(2,1)S(1)} collective-permute-done((bf16[256,1024]{1,0:T(8,128)(2,1)S(1)}, bf16[256,1024]{1,0:T(8,128)(2,1)S(1)}, u32[]{:S(2)}, u32[]{:S(2)}) %collective-permute-start) | collective-permute-done | bytes 524320 | tf_op jit(solution)/shard_map/ppermute | solution.py:356
  3.8 5.2 %shard_map.102 = (bf16[52,128,128]{2,1,0:T(8,128)(2,1)}, f32[128,640]{1,0:T(8,128)S(1)}, f32[128,640]{1,0:T(8,128)S(1)}, f32[64,384]{1,0:T(8,128)S(1)}, f32[64,3...) custom-call(s32[4]{0:T(128)S(1)} %pad_add_fusion.where, bf16[1,512,1024]{2,1,0:T(8,128)(2,1)} %group.1, ...), custom_call_target="tpu_custom_call" | custom-call | bytes 4194304 | tf_op jit(solution)/shard_map/pallas_call | solution.py:43
  9.0 3.0 %collective-permute-start.12 = (bf16[52,128,128]{2,1,0:T(8,128)(2,1)}, bf16[52,128,128]{2,1,0:T(8,128)(2,1)S(1)}, u32[]{:S(2)}, u32[]{:S(2)}) collective-permute-start(bf16[52,128,128]{2,1,0:T(8,128)(2,1)} %get-tuple-element.59), channel_id=1, source_target_pairs={{0,1},{1,0},{2,3},{3,2},{4,5},{5,4},{6,7},{7,6},{8,9},{9,8},{10,11... | collective-permute-start | bytes 5111816 | tf_op jit(solution)/shard_map/ppermute | solution.py:359
  11.9 1.5 %collective-permute-start.1 = (f32[128,640]{1,0:T(8,128)S(1)}, f32[128,640]{1,0:T(8,128)S(1)}, u32[]{:S(2)}, u32[]{:S(2)}) collective-permute-start(f32[128,640]{1,0:T(8,128)S(1)} %get-tuple-element.48), channel_id=1, source_target_pairs={{0,4},{2,6},{4,0},{6,2},{8,12},{10,14},{12,8},{14,10},{16,20},{18,... | collective-permute-start | bytes 983048 | tf_op jit(solution)/shard_map/ppermute | solution.py:356
  13.4 1.6 %collective-permute-start.2 = (f32[64,384]{1,0:T(8,128)S(1)}, f32[64,384]{1,0:T(8,128)S(1)}, u32[]{:S(2)}, u32[]{:S(2)}) collective-permute-start(f32[64,384]{1,0:T(8,128)S(1)} %get-tuple-element.50), channel_id=1, source_target_pairs={{0,8},{2,10},{4,12},{6,14},{8,0},{10,2},{12,4},{14,6},{16,24},{18,... | collective-permute-start | bytes 294920 | tf_op jit(solution)/shard_map/ppermute | solution.py:356
  15.0 2.6 %collective-permute-start.3 = (f32[64,384]{1,0:T(8,128)S(1)}, f32[64,384]{1,0:T(8,128)S(1)}, u32[]{:S(2)}, u32[]{:S(2)}) collective-permute-start(f32[64,384]{1,0:T(8,128)S(1)} %get-tuple-element.51), channel_id=1, source_target_pairs={{0,16},{2,18},{4,20},{6,22},{8,24},{10,26},{12,28},{14,30},{16,0},... | collective-permute-start | bytes 294920 | tf_op jit(solution)/shard_map/ppermute | solution.py:356
  17.6 0.2 collective-permute-start.4
  17.8 1.2 %collective-permute-done.2.one = f32[64,384]{1,0:T(8,128)S(1)} collective-permute-done((f32[64,384]{1,0:T(8,128)S(1)}, f32[64,384]{1,0:T(8,128)S(1)}, u32[]{:S(2)}, u32[]{:S(2)}) %collective-permute-start.2) | collective-permute-done | bytes 98336 | tf_op jit(solution)/shard_map/ppermute | solution.py:356
  19.0 6.1 %collective-permute-done.3.two = f32[64,384]{1,0:T(8,128)S(1)} collective-permute-done((f32[64,384]{1,0:T(8,128)S(1)}, f32[64,384]{1,0:T(8,128)S(1)}, u32[]{:S(2)}, u32[]{:S(2)}) %collective-permute-start.3) | collective-permute-done | bytes 98336 | tf_op jit(solution)/shard_map/ppermute | solution.py:356
  25.2 0.0 collective-permute-done.4.three
  25.2 0.0 collective-permute-done.1.near_came
  25.2 0.6 shard_map.103
  25.8 1.7 %collective-permute-start.5 = (f32[32,640]{1,0:T(8,128)S(1)}, f32[32,640]{1,0:T(8,128)S(1)}, u32[]{:S(2)}, u32[]{:S(2)}) collective-permute-start(f32[32,640]{1,0:T(8,128)S(1)} %get-tuple-element.54), channel_id=1, source_target_pairs={{0,8},{2,10},{4,12},{6,14},{8,0},{10,2},{12,4},{14,6},{16,24},{18,... | collective-permute-start | bytes 245768 | tf_op jit(solution)/shard_map/ppermute | solution.py:356
  27.5 1.4 %collective-permute-start.6 = (f32[32,640]{1,0:T(8,128)S(1)}, f32[32,640]{1,0:T(8,128)S(1)}, u32[]{:S(2)}, u32[]{:S(2)}) collective-permute-start(f32[32,640]{1,0:T(8,128)S(1)} %get-tuple-element.55), channel_id=1, source_target_pairs={{0,16},{2,18},{4,20},{6,22},{8,24},{10,26},{12,28},{14,30},{16,0},... | collective-permute-start | bytes 245768 | tf_op jit(solution)/shard_map/ppermute | solution.py:356
  28.9 1.3 %collective-permute-start.7 = (f32[32,640]{1,0:T(8,128)S(1)}, f32[32,640]{1,0:T(8,128)S(1)}, u32[]{:S(2)}, u32[]{:S(2)}) collective-permute-start(f32[32,640]{1,0:T(8,128)S(1)} %get-tuple-element.56), channel_id=1, source_target_pairs={{0,24},{2,26},{4,28},{6,30},{8,16},{10,18},{12,20},{14,22},{16,8},... | collective-permute-start | bytes 245768 | tf_op jit(solution)/shard_map/ppermute | solution.py:356
  30.2 0.5 collective-permute-start.8
  30.8 3.6 %collective-permute-done.8.came = f32[32,384]{1,0:T(8,128)S(1)} collective-permute-done((f32[32,384]{1,0:T(8,128)S(1)}, f32[32,384]{1,0:T(8,128)S(1)}, u32[]{:S(2)}, u32[]{:S(2)}) %collective-permute-start.8) | collective-permute-done | bytes 49184 | tf_op jit(solution)/shard_map/ppermute | solution.py:356
  34.3 0.0 collective-permute-done.5.one
  34.3 1.5 %collective-permute-done.6.two = f32[32,640]{1,0:T(8,128)S(1)} collective-permute-done((f32[32,640]{1,0:T(8,128)S(1)}, f32[32,640]{1,0:T(8,128)S(1)}, u32[]{:S(2)}, u32[]{:S(2)}) %collective-permute-start.6) | collective-permute-done | bytes 81952 | tf_op jit(solution)/shard_map/ppermute | solution.py:356
  35.8 0.0 collective-permute-done.7.three
  35.8 1.5 %collective-permute-start.9 = (bf16[32,1024]{1,0:T(8,128)(2,1)S(1)}, bf16[32,1024]{1,0:T(8,128)(2,1)S(1)}, u32[]{:S(2)}, u32[]{:S(2)}) collective-permute-start(bf16[32,1024]{1,0:T(8,128)(2,1)S(1)} %shard_map.104.refs_0_), channel_id=1, source_target_pairs={{0,8},{2,10},{4,12},{6,14},{8,0},{10,2},{12,4},{14,6},{16,24},{18,... | collective-permute-start | bytes 196616 | tf_op jit(solution)/shard_map/ppermute | solution.py:356
  37.3 1.3 %collective-permute-start.10 = (bf16[32,1024]{1,0:T(8,128)(2,1)S(1)}, bf16[32,1024]{1,0:T(8,128)(2,1)S(1)}, u32[]{:S(2)}, u32[]{:S(2)}) collective-permute-start(bf16[32,1024]{1,0:T(8,128)(2,1)S(1)} %shard_map.104.refs_0_), channel_id=1, source_target_pairs={{0,16},{2,18},{4,20},{6,22},{8,24},{10,26},{12,28},{14,30},{16,0},... | collective-permute-start | bytes 196616 | tf_op jit(solution)/shard_map/ppermute | solution.py:356
  38.6 1.6 %collective-permute-start.11 = (bf16[32,1024]{1,0:T(8,128)(2,1)S(1)}, bf16[32,1024]{1,0:T(8,128)(2,1)S(1)}, u32[]{:S(2)}, u32[]{:S(2)}) collective-permute-start(bf16[32,1024]{1,0:T(8,128)(2,1)S(1)} %shard_map.104.refs_0_), channel_id=1, source_target_pairs={{0,24},{2,26},{4,28},{6,30},{8,16},{10,18},{12,20},{14,22},{16,8},... | collective-permute-start | bytes 196616 | tf_op jit(solution)/shard_map/ppermute | solution.py:356
  40.3 0.4 collective-permute-done.9.refs_1_
  40.6 3.0 %collective-permute-done.10.refs_2_ = bf16[32,1024]{1,0:T(8,128)(2,1)S(1)} collective-permute-done((bf16[32,1024]{1,0:T(8,128)(2,1)S(1)}, bf16[32,1024]{1,0:T(8,128)(2,1)S(1)}, u32[]{:S(2)}, u32[]{:S(2)}) %collective-permute-start.10) | collective-permute-done | bytes 65568 | tf_op jit(solution)/shard_map/ppermute | solution.py:356
  43.6 1.2 %collective-permute-done.11.refs_3_ = bf16[32,1024]{1,0:T(8,128)(2,1)S(1)} collective-permute-done((bf16[32,1024]{1,0:T(8,128)(2,1)S(1)}, bf16[32,1024]{1,0:T(8,128)(2,1)S(1)}, u32[]{:S(2)}, u32[]{:S(2)}) %collective-permute-start.11) | collective-permute-done | bytes 65568 | tf_op jit(solution)/shard_map/ppermute | solution.py:356
  44.8 0.6 shard_map.105.refs_0_
  45.4 0.0 copy-start.4
  45.4 4.3 %collective-permute-done.12.mine = bf16[52,128,128]{2,1,0:T(8,128)(2,1)S(1)} collective-permute-done((bf16[52,128,128]{2,1,0:T(8,128)(2,1)}, bf16[52,128,128]{2,1,0:T(8,128)(2,1)S(1)}, u32[]{:S(2)}, u32[]{:S(2)}) %collective-permute-start.12) | collective-permute-done | bytes 1703968 | tf_op jit(solution)/shard_map/ppermute | solution.py:359
  49.6 0.0 collective-permute-start.15
  49.6 1.7 %collective-permute-start.16 = (bf16[128,1024]{1,0:T(8,128)(2,1)S(1)}, bf16[128,1024]{1,0:T(8,128)(2,1)S(1)}, u32[]{:S(2)}, u32[]{:S(2)}) collective-permute-start(bf16[128,1024]{1,0:T(8,128)(2,1)S(1)} %shard_map.105.refs_0_), channel_id=1, source_target_pairs={{0,4},{2,6},{4,0},{6,2},{8,12},{10,14},{12,8},{14,10},{16,20},{18,... | collective-permute-start | bytes 786440 | tf_op jit(solution)/shard_map/ppermute | solution.py:356
  51.4 1.5 %collective-permute-start.13 = (bf16[128,1024]{1,0:T(8,128)(2,1)S(1)}, bf16[128,1024]{1,0:T(8,128)(2,1)S(1)}, u32[]{:S(2)}, u32[]{:S(2)}) collective-permute-start(bf16[128,1024]{1,0:T(8,128)(2,1)S(1)} %shard_map.105.refs_0_), channel_id=1, source_target_pairs={{0,1},{1,0},{2,3},{3,2},{4,5},{5,4},{6,7},{7,6},{8,9},{9,8},{10,11... | collective-permute-start | bytes 786440 | tf_op jit(solution)/shard_map/ppermute | solution.py:359
  52.9 0.3 collective-permute-start.14
  53.1 0.0 collective-permute-start.17
  53.1 5.6 %collective-permute-done.16.refs_1_ = bf16[128,1024]{1,0:T(8,128)(2,1)S(1)} collective-permute-done((bf16[128,1024]{1,0:T(8,128)(2,1)S(1)}, bf16[128,1024]{1,0:T(8,128)(2,1)S(1)}, u32[]{:S(2)}, u32[]{:S(2)}) %collective-permute-start.16) | collective-permute-done | bytes 262176 | tf_op jit(solution)/shard_map/ppermute | solution.py:356
  58.7 0.0 collective-permute-start.18
  58.8 0.0 collective-permute-done.15.theirs
  58.8 3.2 %shard_map.106 = (bf16[2,1024,1024]{2,1,0:T(8,128)(2,1)S(1)}, bf16[1024,1024]{1,0:T(8,128)(2,1)S(1)}, bf16[1024,1024]{1,0:T(8,128)(2,1)S(1)}, f32[1024,1024]{1,0:T(8,128)S(1)}) custom-call(s32[4]{0:T(128)S(1)} %pad_add_fusion.where, f32[512,1024]{1,0:T(8,128)S(1)} %copy-done, f32[512,1024]{1,0:T(8,128)S(1)} %copy-done.1, ...), custom_call_target="tpu_custom_call" | custom-call | bytes 16777216 | tf_op jit(solution)/shard_map/pallas_call | solution.py:43
  62.0 3.4 %collective-permute-done.13.refs_4_ = bf16[128,1024]{1,0:T(8,128)(2,1)S(1)} collective-permute-done((bf16[128,1024]{1,0:T(8,128)(2,1)S(1)}, bf16[128,1024]{1,0:T(8,128)(2,1)S(1)}, u32[]{:S(2)}, u32[]{:S(2)}) %collective-permute-start.13) | collective-permute-done | bytes 262176 | tf_op jit(solution)/shard_map/ppermute | solution.py:359
  65.4 0.5 collective-permute-start.20
  65.9 0.0 collective-permute-done.17.refs_2_
  65.9 1.0 %collective-permute-done.19.refs_6_ = bf16[128,1024]{1,0:T(8,128)(2,1)S(1)} collective-permute-done((bf16[128,1024]{1,0:T(8,128)(2,1)S(1)}, bf16[128,1024]{1,0:T(8,128)(2,1)S(1)}, u32[]{:S(2)}, u32[]{:S(2)}) %collective-permute-start.19) | collective-permute-done | bytes 262176 | tf_op jit(solution)/shard_map/ppermute | solution.py:356
  67.0 0.4 collective-permute-done.20.refs_7_
  67.3 1.7 %shard_map.107 = (bf16[1024,1024]{1,0:T(8,128)(2,1)S(1)}, bf16[512,256]{1,0:T(8,128)(2,1)S(1)}, bf16[512,256]{1,0:T(8,128)(2,1)S(1)}) custom-call(s32[4]{0:T(128)S(1)} %pad_add_fusion.where, f32[512,1024]{1,0:T(8,128)S(1)} %copy-done.4, bf16[2,1024,1024]{2,1,0:T(8,128)(2,1)S(1)} %get-tuple-element.63.bases, bf16[128,1024]{1,0:T(8,128)(2,1)S(1)} %shard_map.105.refs_0_, ...), custom_call_target="tpu_custom_call" | custom-call | flops 536870912 | bytes 4194304 | tf_op jit(solution)/shard_map/pallas_call | solution.py:43
  69.1 1.6 %collective-permute-start.21 = (bf16[512,256]{1,0:T(8,128)(2,1)S(1)}, bf16[512,256]{1,0:T(8,128)(2,1)S(1)}, u32[]{:S(2)}, u32[]{:S(2)}) collective-permute-start(bf16[512,256]{1,0:T(8,128)(2,1)S(1)} %get-tuple-element.69), channel_id=1, source_target_pairs={{0,1},{1,0},{2,3},{3,2},{4,5},{5,4},{6,7},{7,6},{8,9},{9,8},{10,11... | collective-permute-start | bytes 786440 | tf_op jit(solution)/shard_map/ppermute | solution.py:359
  70.6 6.7 %shard_map.109 = (bf16[1024,1024]{1,0:T(8,128)(2,1)S(1)}, bf16[1024,1024]{1,0:T(8,128)(2,1)S(1)}) custom-call(s32[4]{0:T(128)S(1)} %pad_add_fusion.where, bf16[1024,1024]{1,0:T(8,128)(2,1)S(1)} %get-tuple-element.66.gradient, bf16[2,1024,1024]{2,1,0:T(8,128)(2,1)S(1)} %get-tuple-element.63.bases, f32[1024,1024]{1,0:T(8,128)S(1)} %get-tuple-element.71.stat), custom_call_target="tpu_custom_call" | custom-call | flops 4294967296 | bytes 8388608 | tf_op jit(solution)/shard_map/pallas_call | solution.py:43
  77.4 0.1 collective-permute-done.21.came
  77.5 4.1 %shard_map.108 = (f32[1024,256]{1,0:T(8,128)S(1)}, bf16[512,256]{1,0:T(8,128)(2,1)S(1)}, bf16[512,256]{1,0:T(8,128)(2,1)S(1)}) custom-call(s32[4]{0:T(128)S(1)} %pad_add_fusion.where, bf16[1024,1024]{1,0:T(8,128)(2,1)S(1)} %get-tuple-element.66.gradient, bf16[2,1024,1024]{2,1,0:T(8,128)(2,1)S(1)} %get-tuple-element.63.bases, ...), custom_call_target="tpu_custom_call" | custom-call | flops 2147483648 | bytes 4194304 | tf_op jit(solution)/shard_map/pallas_call | solution.py:43
  81.6 1.6 %collective-permute-start.22 = (bf16[512,256]{1,0:T(8,128)(2,1)S(1)}, bf16[512,256]{1,0:T(8,128)(2,1)S(1)}, u32[]{:S(2)}, u32[]{:S(2)}) collective-permute-start(bf16[512,256]{1,0:T(8,128)(2,1)S(1)} %get-tuple-element.77), channel_id=1, source_target_pairs={{0,1},{1,0},{2,3},{3,2},{4,5},{5,4},{6,7},{7,6},{8,9},{9,8},{10,11... | collective-permute-start | bytes 786440 | tf_op jit(solution)/shard_map/ppermute | solution.py:359
  83.2 0.0 collective-permute-start.25
  83.2 6.5 %shard_map.110 = (bf16[1024,1024]{1,0:T(8,128)(2,1)S(1)}, bf16[1024,1024]{1,0:T(8,128)(2,1)S(1)}, f32[256,1024]{1,0:T(8,128)S(1)}) custom-call(s32[4]{0:T(128)S(1)} %pad_add_fusion.where, bf16[1024,1024]{1,0:T(8,128)(2,1)S(1)} %get-tuple-element.74.start, bf16[1024,1024]{1,0:T(8,128)(2,1)S(1)} %get-tuple-element.75.start_turned), custom_call_target="tpu_custom_call" | custom-call | flops 5368709120 | bytes 4194304 | tf_op jit(solution)/shard_map/pallas_call | solution.py:43
  89.7 0.6 collective-permute-start.26
  90.3 1.8 %shard_map.112.low = f32[256,1024]{1,0:T(8,128)S(1)} custom-call(s32[4]{0:T(128)S(1)} %pad_add_fusion.where, bf16[1024,1024]{1,0:T(8,128)(2,1)S(1)} %get-tuple-element.84.current, bf16[1024,1024]{1,0:T(8,128)(2,1)S(1)} %get-tuple-element.85.turned), custom_call_target="tpu_custom_call" | custom-call | flops 1073741824 | bytes 2097152 | tf_op jit(solution)/shard_map/pallas_call | solution.py:43
  92.1 0.1 collective-permute-start.27
  92.2 0.5 collective-permute-start.23
  92.7 0.1 collective-permute-start.24
  92.7 1.9 %shard_map.113 = (f32[512,1024]{1,0:T(8,128)}, f32[512,1024]{1,0:T(8,128)}) custom-call(s32[4]{0:T(128)S(1)} %pad_add_fusion.where, f32[256,1024]{1,0:T(8,128)S(1)} %get-tuple-element.83.top, f32[256,1024]{1,0:T(8,128)S(1)} %shard_map.112.low), custom_call_target="tpu_custom_call" | custom-call | bytes 4194304 | tf_op jit(solution)/shard_map/pallas_call | solution.py:43
  94.6 0.6 collective-permute-done.23.kept_next
  95.2 0.4 collective-permute-done.24.came_next
  95.6 3.9 %shard_map.111 = (bf16[512,1024]{1,0:T(8,128)(2,1)}, f32[1024,512]{1,0:T(8,128)}) custom-call(s32[4]{0:T(128)S(1)} %pad_add_fusion.where, bf16[512,256]{1,0:T(8,128)(2,1)S(1)} %get-tuple-element.70.kept, bf16[512,256]{1,0:T(8,128)(2,1)S(1)} %collective-permute-done.22.came, bf16[512,256]{1,0:T(8,128)(2,1)S(1)} %collective-permute-done.23.kept_next, ...), custom_call_target="tpu_custom_call" | custom-call | flops 1073741824 | bytes 8388608 | tf_op jit(solution)/shard_map/pallas_call | solution.py:490
  99.5 1.9 %shard_map.114 = (f32[512,1024]{1,0:T(8,128)}, f32[512,1024]{1,0:T(8,128)}) custom-call(s32[4]{0:T(128)S(1)} %pad_add_fusion.where, f32[256,1024]{1,0:T(8,128)S(1)} %collective-permute-done.26.top, f32[256,1024]{1,0:T(8,128)S(1)} %collective-permute-done.27.low, ...), custom_call_target="tpu_custom_call", output_to_operand_aliasing={{0}: (3, {}), {1}: (4, {})} | custom-call | bytes 4194304 | tf_op jit(solution)/shard_map/pallas_call | solution.py:43
  (19 shorter events, 0.1 us)
Async XLA Ops:
  1.7 2.1 %collective-permute-start = (bf16[256,1024]{1,0:T(8,128)(2,1)S(1)}, bf16[256,1024]{1,0:T(8,128)(2,1)S(1)}, u32[]{:S(2)}, u32[]{:S(2)}) collective-permute-start(bf16[256,1024]{1,0:T(8,128)(2,1)S(1)} %dynamic-slice_bitcast_fusion), channel_id=1, source_target_pairs={{0,2},{2,0},{4,6},{6,4},{8,10},{10,8},{12,14},{14,12},{16,18},{18,... | collective-permute-start | bytes 1572872 | tf_op jit(solution)/shard_map/ppermute | solution.py:356
  3.8 55.0 %copy-start = (f32[512,1024]{1,0:T(8,128)S(1)}, f32[512,1024]{1,0:T(8,128)}, u32[]{:S(2)}) copy-start(f32[512,1024]{1,0:T(8,128)} %left.3) | copy-start | bytes 6291460
  3.8 55.0 %copy-start.1 = (f32[512,1024]{1,0:T(8,128)S(1)}, f32[512,1024]{1,0:T(8,128)}, u32[]{:S(2)}) copy-start(f32[512,1024]{1,0:T(8,128)} %right.3) | copy-start | bytes 6291460
  3.8 55.0 %copy-start.2 = (f32[512,1024]{1,0:T(8,128)S(1)}, f32[512,1024]{1,0:T(8,128)}, u32[]{:S(2)}) copy-start(f32[512,1024]{1,0:T(8,128)} %stat_left.3) | copy-start | bytes 6291460
  3.8 55.0 %copy-start.3 = (f32[512,1024]{1,0:T(8,128)S(1)}, f32[512,1024]{1,0:T(8,128)}, u32[]{:S(2)}) copy-start(f32[512,1024]{1,0:T(8,128)} %stat_right.3) | copy-start | bytes 6291460
  9.0 40.7 %collective-permute-start.12 = (bf16[52,128,128]{2,1,0:T(8,128)(2,1)}, bf16[52,128,128]{2,1,0:T(8,128)(2,1)S(1)}, u32[]{:S(2)}, u32[]{:S(2)}) collective-permute-start(bf16[52,128,128]{2,1,0:T(8,128)(2,1)} %get-tuple-element.59), channel_id=1, source_target_pairs={{0,1},{1,0},{2,3},{3,2},{4,5},{5,4},{6,7},{7,6},{8,9},{9,8},{10,11... | collective-permute-start | bytes 5111816 | tf_op jit(solution)/shard_map/ppermute | solution.py:359
  11.9 13.2 %collective-permute-start.1 = (f32[128,640]{1,0:T(8,128)S(1)}, f32[128,640]{1,0:T(8,128)S(1)}, u32[]{:S(2)}, u32[]{:S(2)}) collective-permute-start(f32[128,640]{1,0:T(8,128)S(1)} %get-tuple-element.48), channel_id=1, source_target_pairs={{0,4},{2,6},{4,0},{6,2},{8,12},{10,14},{12,8},{14,10},{16,20},{18,... | collective-permute-start | bytes 983048 | tf_op jit(solution)/shard_map/ppermute | solution.py:356
  13.4 5.6 %collective-permute-start.2 = (f32[64,384]{1,0:T(8,128)S(1)}, f32[64,384]{1,0:T(8,128)S(1)}, u32[]{:S(2)}, u32[]{:S(2)}) collective-permute-start(f32[64,384]{1,0:T(8,128)S(1)} %get-tuple-element.50), channel_id=1, source_target_pairs={{0,8},{2,10},{4,12},{6,14},{8,0},{10,2},{12,4},{14,6},{16,24},{18,... | collective-permute-start | bytes 294920 | tf_op jit(solution)/shard_map/ppermute | solution.py:356
  15.0 10.2 %collective-permute-start.3 = (f32[64,384]{1,0:T(8,128)S(1)}, f32[64,384]{1,0:T(8,128)S(1)}, u32[]{:S(2)}, u32[]{:S(2)}) collective-permute-start(f32[64,384]{1,0:T(8,128)S(1)} %get-tuple-element.51), channel_id=1, source_target_pairs={{0,16},{2,18},{4,20},{6,22},{8,24},{10,26},{12,28},{14,30},{16,0},... | collective-permute-start | bytes 294920 | tf_op jit(solution)/shard_map/ppermute | solution.py:356
  17.6 7.6 %collective-permute-start.4 = (f32[64,384]{1,0:T(8,128)S(1)}, f32[64,384]{1,0:T(8,128)S(1)}, u32[]{:S(2)}, u32[]{:S(2)}) collective-permute-start(f32[64,384]{1,0:T(8,128)S(1)} %get-tuple-element.52), channel_id=1, source_target_pairs={{0,24},{2,26},{4,28},{6,30},{8,16},{10,18},{12,20},{14,22},{16,8},... | collective-permute-start | bytes 294920 | tf_op jit(solution)/shard_map/ppermute | solution.py:356
  25.8 8.5 %collective-permute-start.5 = (f32[32,640]{1,0:T(8,128)S(1)}, f32[32,640]{1,0:T(8,128)S(1)}, u32[]{:S(2)}, u32[]{:S(2)}) collective-permute-start(f32[32,640]{1,0:T(8,128)S(1)} %get-tuple-element.54), channel_id=1, source_target_pairs={{0,8},{2,10},{4,12},{6,14},{8,0},{10,2},{12,4},{14,6},{16,24},{18,... | collective-permute-start | bytes 245768 | tf_op jit(solution)/shard_map/ppermute | solution.py:356
  27.5 8.3 %collective-permute-start.6 = (f32[32,640]{1,0:T(8,128)S(1)}, f32[32,640]{1,0:T(8,128)S(1)}, u32[]{:S(2)}, u32[]{:S(2)}) collective-permute-start(f32[32,640]{1,0:T(8,128)S(1)} %get-tuple-element.55), channel_id=1, source_target_pairs={{0,16},{2,18},{4,20},{6,22},{8,24},{10,26},{12,28},{14,30},{16,0},... | collective-permute-start | bytes 245768 | tf_op jit(solution)/shard_map/ppermute | solution.py:356
  28.9 6.9 %collective-permute-start.7 = (f32[32,640]{1,0:T(8,128)S(1)}, f32[32,640]{1,0:T(8,128)S(1)}, u32[]{:S(2)}, u32[]{:S(2)}) collective-permute-start(f32[32,640]{1,0:T(8,128)S(1)} %get-tuple-element.56), channel_id=1, source_target_pairs={{0,24},{2,26},{4,28},{6,30},{8,16},{10,18},{12,20},{14,22},{16,8},... | collective-permute-start | bytes 245768 | tf_op jit(solution)/shard_map/ppermute | solution.py:356
  30.2 4.1 %collective-permute-start.8 = (f32[32,384]{1,0:T(8,128)S(1)}, f32[32,384]{1,0:T(8,128)S(1)}, u32[]{:S(2)}, u32[]{:S(2)}) collective-permute-start(f32[32,384]{1,0:T(8,128)S(1)} %get-tuple-element.58), channel_id=1, source_target_pairs={{0,4},{2,6},{4,0},{6,2},{8,12},{10,14},{12,8},{14,10},{16,20},{18,... | collective-permute-start | bytes 147464 | tf_op jit(solution)/shard_map/ppermute | solution.py:356
  35.8 4.8 %collective-permute-start.9 = (bf16[32,1024]{1,0:T(8,128)(2,1)S(1)}, bf16[32,1024]{1,0:T(8,128)(2,1)S(1)}, u32[]{:S(2)}, u32[]{:S(2)}) collective-permute-start(bf16[32,1024]{1,0:T(8,128)(2,1)S(1)} %shard_map.104.refs_0_), channel_id=1, source_target_pairs={{0,8},{2,10},{4,12},{6,14},{8,0},{10,2},{12,4},{14,6},{16,24},{18,... | collective-permute-start | bytes 196616 | tf_op jit(solution)/shard_map/ppermute | solution.py:356
  37.3 6.3 %collective-permute-start.10 = (bf16[32,1024]{1,0:T(8,128)(2,1)S(1)}, bf16[32,1024]{1,0:T(8,128)(2,1)S(1)}, u32[]{:S(2)}, u32[]{:S(2)}) collective-permute-start(bf16[32,1024]{1,0:T(8,128)(2,1)S(1)} %shard_map.104.refs_0_), channel_id=1, source_target_pairs={{0,16},{2,18},{4,20},{6,22},{8,24},{10,26},{12,28},{14,30},{16,0},... | collective-permute-start | bytes 196616 | tf_op jit(solution)/shard_map/ppermute | solution.py:356
  38.6 6.2 %collective-permute-start.11 = (bf16[32,1024]{1,0:T(8,128)(2,1)S(1)}, bf16[32,1024]{1,0:T(8,128)(2,1)S(1)}, u32[]{:S(2)}, u32[]{:S(2)}) collective-permute-start(bf16[32,1024]{1,0:T(8,128)(2,1)S(1)} %shard_map.104.refs_0_), channel_id=1, source_target_pairs={{0,24},{2,26},{4,28},{6,30},{8,16},{10,18},{12,20},{14,22},{16,8},... | collective-permute-start | bytes 196616 | tf_op jit(solution)/shard_map/ppermute | solution.py:356
  45.4 22.0 %copy-start.4 = (f32[512,1024]{1,0:T(8,128)S(1)}, f32[512,1024]{1,0:T(8,128)}, u32[]{:S(2)}) copy-start(f32[512,1024]{1,0:T(8,128)} %moment.1) | copy-start | bytes 6291460
  49.6 9.1 %collective-permute-start.15 = (bf16[52,128,128]{2,1,0:T(8,128)(2,1)S(1)}, bf16[52,128,128]{2,1,0:T(8,128)(2,1)S(1)}, u32[]{:S(2)}, u32[]{:S(2)}) collective-permute-start(bf16[52,128,128]{2,1,0:T(8,128)(2,1)S(1)} %collective-permute-done.12.mine), channel_id=1, source_target_pairs={{0,2},{2,0},{4,6},{6,4},{8,10},{10,8},{12,14},{14,12},{16,18},{18,... | collective-permute-start | bytes 5111816 | tf_op jit(solution)/shard_map/ppermute | solution.py:356
  49.6 9.1 %collective-permute-start.16 = (bf16[128,1024]{1,0:T(8,128)(2,1)S(1)}, bf16[128,1024]{1,0:T(8,128)(2,1)S(1)}, u32[]{:S(2)}, u32[]{:S(2)}) collective-permute-start(bf16[128,1024]{1,0:T(8,128)(2,1)S(1)} %shard_map.105.refs_0_), channel_id=1, source_target_pairs={{0,4},{2,6},{4,0},{6,2},{8,12},{10,14},{12,8},{14,10},{16,20},{18,... | collective-permute-start | bytes 786440 | tf_op jit(solution)/shard_map/ppermute | solution.py:356
  51.4 14.1 %collective-permute-start.13 = (bf16[128,1024]{1,0:T(8,128)(2,1)S(1)}, bf16[128,1024]{1,0:T(8,128)(2,1)S(1)}, u32[]{:S(2)}, u32[]{:S(2)}) collective-permute-start(bf16[128,1024]{1,0:T(8,128)(2,1)S(1)} %shard_map.105.refs_0_), channel_id=1, source_target_pairs={{0,1},{1,0},{2,3},{3,2},{4,5},{5,4},{6,7},{7,6},{8,9},{9,8},{10,11... | collective-permute-start | bytes 786440 | tf_op jit(solution)/shard_map/ppermute | solution.py:359
  52.9 12.5 %collective-permute-start.14 = (bf16[128,1024]{1,0:T(8,128)(2,1)S(1)}, bf16[128,1024]{1,0:T(8,128)(2,1)S(1)}, u32[]{:S(2)}, u32[]{:S(2)}) collective-permute-start(bf16[128,1024]{1,0:T(8,128)(2,1)S(1)} %shard_map.105.refs_0_), channel_id=1, source_target_pairs={{0,5},{1,4},{2,7},{3,6},{4,1},{5,0},{6,3},{7,2},{8,13},{9,12},{10,... | collective-permute-start | bytes 786440 | tf_op jit(solution)/shard_map/ppermute | solution.py:363
  53.1 12.8 %collective-permute-start.17 = (bf16[128,1024]{1,0:T(8,128)(2,1)S(1)}, bf16[128,1024]{1,0:T(8,128)(2,1)S(1)}, u32[]{:S(2)}, u32[]{:S(2)}) collective-permute-start(bf16[128,1024]{1,0:T(8,128)(2,1)S(1)} %shard_map.105.refs_0_), channel_id=1, source_target_pairs={{0,2},{2,0},{4,6},{6,4},{8,10},{10,8},{12,14},{14,12},{16,18},{18,... | collective-permute-start | bytes 786440 | tf_op jit(solution)/shard_map/ppermute | solution.py:356
  58.7 7.2 %collective-permute-start.18 = (bf16[128,1024]{1,0:T(8,128)(2,1)S(1)}, bf16[128,1024]{1,0:T(8,128)(2,1)S(1)}, u32[]{:S(2)}, u32[]{:S(2)}) collective-permute-start(bf16[128,1024]{1,0:T(8,128)(2,1)S(1)} %collective-permute-done.16.refs_1_), channel_id=1, source_target_pairs={{0,2},{2,0},{4,6},{6,4},{8,10},{10,8},{12,14},{14,12},{16,18},{18,... | collective-permute-start | bytes 786440 | tf_op jit(solution)/shard_map/ppermute | solution.py:356
  65.4 1.5 %collective-permute-start.19 = (bf16[128,1024]{1,0:T(8,128)(2,1)S(1)}, bf16[128,1024]{1,0:T(8,128)(2,1)S(1)}, u32[]{:S(2)}, u32[]{:S(2)}) collective-permute-start(bf16[128,1024]{1,0:T(8,128)(2,1)S(1)} %collective-permute-done.13.refs_4_), channel_id=1, source_target_pairs={{0,2},{2,0},{4,6},{6,4},{8,10},{10,8},{12,14},{14,12},{16,18},{18,... | collective-permute-start | bytes 786440 | tf_op jit(solution)/shard_map/ppermute | solution.py:356
  65.4 1.9 %collective-permute-start.20 = (bf16[128,1024]{1,0:T(8,128)(2,1)S(1)}, bf16[128,1024]{1,0:T(8,128)(2,1)S(1)}, u32[]{:S(2)}, u32[]{:S(2)}) collective-permute-start(bf16[128,1024]{1,0:T(8,128)(2,1)S(1)} %collective-permute-done.14.refs_5_), channel_id=1, source_target_pairs={{0,2},{2,0},{4,6},{6,4},{8,10},{10,8},{12,14},{14,12},{16,18},{18,... | collective-permute-start | bytes 786440 | tf_op jit(solution)/shard_map/ppermute | solution.py:356
  69.1 8.4 %collective-permute-start.21 = (bf16[512,256]{1,0:T(8,128)(2,1)S(1)}, bf16[512,256]{1,0:T(8,128)(2,1)S(1)}, u32[]{:S(2)}, u32[]{:S(2)}) collective-permute-start(bf16[512,256]{1,0:T(8,128)(2,1)S(1)} %get-tuple-element.69), channel_id=1, source_target_pairs={{0,1},{1,0},{2,3},{3,2},{4,5},{5,4},{6,7},{7,6},{8,9},{9,8},{10,11... | collective-permute-start | bytes 786440 | tf_op jit(solution)/shard_map/ppermute | solution.py:359
  70.6 6.8 %copy-start.5 = (f32[1024,512]{1,0:T(8,128)S(1)}, f32[1024,512]{1,0:T(8,128)}, u32[]{:S(2)}) copy-start(f32[1024,512]{1,0:T(8,128)} %second.1) | copy-start | bytes 6291460
  81.6 8.7 %collective-permute-start.22 = (bf16[512,256]{1,0:T(8,128)(2,1)S(1)}, bf16[512,256]{1,0:T(8,128)(2,1)S(1)}, u32[]{:S(2)}, u32[]{:S(2)}) collective-permute-start(bf16[512,256]{1,0:T(8,128)(2,1)S(1)} %get-tuple-element.77), channel_id=1, source_target_pairs={{0,1},{1,0},{2,3},{3,2},{4,5},{5,4},{6,7},{7,6},{8,9},{9,8},{10,11... | collective-permute-start | bytes 786440 | tf_op jit(solution)/shard_map/ppermute | solution.py:359
  83.2 12.4 %collective-permute-start.25 = (f32[1024,256]{1,0:T(8,128)S(1)}, f32[1024,256]{1,0:T(8,128)S(1)}, u32[]{:S(2)}, u32[]{:S(2)}) collective-permute-start(f32[1024,256]{1,0:T(8,128)S(1)} %get-tuple-element.80.new), channel_id=1, source_target_pairs={{0,2},{2,0},{4,6},{6,4},{8,10},{10,8},{12,14},{14,12},{16,18},{18,... | collective-permute-start | bytes 3145736 | tf_op jit(solution)/shard_map/ppermute | solution.py:356
  89.7 9.7 %collective-permute-start.26 = (f32[256,1024]{1,0:T(8,128)S(1)}, f32[256,1024]{1,0:T(8,128)S(1)}, u32[]{:S(2)}, u32[]{:S(2)}) collective-permute-start(f32[256,1024]{1,0:T(8,128)S(1)} %get-tuple-element.83.top), channel_id=1, source_target_pairs={{0,2},{2,0},{4,6},{6,4},{8,10},{10,8},{12,14},{14,12},{16,18},{18,... | collective-permute-start | bytes 3145736 | tf_op jit(solution)/shard_map/ppermute | solution.py:356
  92.1 7.4 %collective-permute-start.27 = (f32[256,1024]{1,0:T(8,128)S(1)}, f32[256,1024]{1,0:T(8,128)S(1)}, u32[]{:S(2)}, u32[]{:S(2)}) collective-permute-start(f32[256,1024]{1,0:T(8,128)S(1)} %shard_map.112.low), channel_id=1, source_target_pairs={{0,2},{2,0},{4,6},{6,4},{8,10},{10,8},{12,14},{14,12},{16,18},{18,... | collective-permute-start | bytes 3145736 | tf_op jit(solution)/shard_map/ppermute | solution.py:356
  92.2 3.0 %collective-permute-start.23 = (bf16[512,256]{1,0:T(8,128)(2,1)S(1)}, bf16[512,256]{1,0:T(8,128)(2,1)S(1)}, u32[]{:S(2)}, u32[]{:S(2)}) collective-permute-start(bf16[512,256]{1,0:T(8,128)(2,1)S(1)} %get-tuple-element.70.kept), channel_id=1, source_target_pairs={{0,2},{2,0},{4,6},{6,4},{8,10},{10,8},{12,14},{14,12},{16,18},{18,... | collective-permute-start | bytes 786440 | tf_op jit(solution)/shard_map/ppermute | solution.py:356
  92.7 2.9 %collective-permute-start.24 = (bf16[512,256]{1,0:T(8,128)(2,1)S(1)}, bf16[512,256]{1,0:T(8,128)(2,1)S(1)}, u32[]{:S(2)}, u32[]{:S(2)}) collective-permute-start(bf16[512,256]{1,0:T(8,128)(2,1)S(1)} %collective-permute-done.22.came), channel_id=1, source_target_pairs={{0,2},{2,0},{4,6},{6,4},{8,10},{10,8},{12,14},{14,12},{16,18},{18,... | collective-permute-start | bytes 786440 | tf_op jit(solution)/shard_map/ppermute | solution.py:356

commit v6 on v5

--- a/solution.py
+++ b/solution.py
@@ -63,6 +63,21 @@
 UPPER = [(i, j) for i in range(TILES) for j in range(i, TILES)]
 
 
+def pack(out, base, value):
+    size = out.shape[1]
+    across = value.shape[1] // size
+    for band in range(value.shape[0] // size):
+        for column in range(across):
+            out[base + band * across + column] = value[
+                band * size : (band + 1) * size, column * size : (column + 1) * size
+            ].astype(HALF)
+
+
+def diagonal(size):
+    shape = (size, size)
+    return lax.broadcasted_iota(jnp.int32, shape, 0) == lax.broadcasted_iota(jnp.int32, shape, 1)
+
+
 def start_kernel(
     where,
     group,
@@ -71,79 +86,74 @@
     right,
     stat_left,
     stat_right,
-    state,
-    near_kept,
-    near_sent,
+    first,
+    second,
     kept,
-    far_1,
-    far_2,
-    far_3,
+    sent,
     basis_in,
     stat_in,
     sem,
 ):
-    position, core, x, z = where[0], where[1], where[2], where[3]
+    position, core, x = where[0], where[1], where[2]
     half, width = basis_in.shape[1:]
-    size = state.shape[1]
-    bases = [
-        pltpu.make_async_copy(basis.at[tile(core, half)], basis_in.at[i], sem.at[i])
-        for i, basis in enumerate((left, right))
-    ]
-    for copy in bases:
-        copy.start()
+    size = first.shape[1]
+    mine = tile(core, half)
+    last = pltpu.make_async_copy(right.at[mine], basis_in.at[1], sem.at[1])
+
+    @pl.when(x == 0)
+    def _():
+        pltpu.make_async_copy(left.at[mine], basis_in.at[0], sem.at[0]).start()
+
     for side, stat in enumerate((stat_left, stat_right)):
 
-        @pl.when(core == side)
+        @pl.when((x == 1) & (core == side))
         def _():
-            pltpu.make_async_copy(stat.at[:, tile(position, size * TILES)], stat_in, sem.at[2]).start()
-
-    rows, cut = near_kept.shape
-    for out, there in ((near_kept, x), (near_sent, 1 - x)):
-        out[...] = group[0, tile(core * 2 + there, rows), :cut].astype(FULL) + came[
-            tile(there, rows), :cut
-        ].astype(FULL)
-    rows = kept.shape[0] // 2
-    for k, out in enumerate((kept, far_1, far_2, far_3)):
-        for i in range(2):
-            there = i * 4 + (z ^ k)
-            out[i * rows : (i + 1) * rows] = group[0, tile(core * 8 + there, rows), cut:].astype(
-                FULL
-            ) + came[tile(there, rows), cut:].astype(FULL)
-    for copy in bases:
-        copy.wait()
-    across = width // size
-    for band in range(2 * half // size):
-        for column in range(across):
-            begin = band * size % half
-            state[band * across + column] = basis_in[
-                band * size // half, begin : begin + size, column * size : (column + 1) * size
-            ].astype(HALF)
-    pltpu.make_async_copy(stat_left.at[:, : size * TILES], stat_in, sem.at[2]).wait()
-    base = 2 * half * width // size**2
-    for place, (i, j) in enumerate(UPPER):
-        value = stat_in[i * size : (i + 1) * size, j * size : (j + 1) * size]
-        high = value.astype(HALF)
-        state[base + place] = high
-        state[base + len(UPPER) + place] = (value - high.astype(FULL)).astype(HALF)
-
-
-def second_sum_kernel(
-    where, near_kept, near_came, kept, one, two, three, near_own, near_1, near_2, near_3, own, sent
-):
-    size = near_own.shape[0]
-    x, z = where[2], where[3]
-    for k, out in enumerate((near_own, near_1, near_2, near_3)):
+            pltpu.make_async_copy(stat.at[:, tile(position, size * TILES)], stat_in, sem.at[0]).start()
+
+    last.start()
+    rows = kept.shape[0]
+    for out, there in ((kept, x), (sent, 1 - x)):
+        out[...] = (
+            group[0, tile(core * 2 + there, rows)].astype(FULL)
+            + came[tile(there, rows)].astype(FULL)
+        ).astype(out.dtype)
+
+    @pl.when(x == 0)
+    def _():
+        pltpu.make_async_copy(left.at[mine], basis_in.at[0], sem.at[0]).wait()
+        pack(first, 0, basis_in.at[0])
+
+    @pl.when(x == 1)
+    def _():
+        pltpu.make_async_copy(stat_left.at[:, : size * TILES], stat_in, sem.at[0]).wait()
+        same = diagonal(size)
+        for place, (i, j) in enumerate(UPPER):
+            value = stat_in[i * size : (i + 1) * size, j * size : (j + 1) * size]
+            high = value.astype(HALF)
+            first[place] = high
+            if i == j:
+                low = jnp.where(same, value - high.astype(FULL), 0.0)
+                line = jnp.sum(low, axis=0, keepdims=True)
+                first[len(UPPER), i * 16 : (i + 1) * 16] = jnp.broadcast_to(
+                    line, (16, size)
+                ).astype(HALF)
+
+    last.wait()
+    pack(second, 0, basis_in.at[1])
+
+
+def second_sum_kernel(where, kept, came, own, *sent):
+    size = own.shape[0]
+    z = where[3]
+    for k, out in enumerate((own, *sent)):
         there = tile(z ^ k, size)
-        out[...] = near_kept[there] + near_came[there]
-    for k, out in enumerate((own, sent)):
-        there = tile(x ^ k, size)
-        out[...] = (kept[there] + one[there]) + (two[there] + three[there])
-
-
-def third_sum_kernel(near_own, one, two, three, own, came, out):
-    cut = near_own.shape[1]
-    out[:, :cut] = ((near_own[...] + one[...]) + (two[...] + three[...])).astype(HALF)
-    out[:, cut:] = (own[...] + came[...]).astype(HALF)
+        out[...] = (kept[there] + came[there].astype(FULL)).astype(out.dtype)
+
+
+def third_sum_kernel(own, one, two, three, out):
+    out[...] = (
+        (own[...] + one[...].astype(FULL)) + (two[...].astype(FULL) + three[...].astype(FULL))
+    ).astype(HALF)
 
 
 def joined_kernel(where, *refs):
@@ -154,30 +164,42 @@
         out[tile(z ^ k, size)] = part[...]
 
 
-def place_basis(where, out, own, mine, theirs, side):
+def place_basis(where, out, own, mine, theirs):
     rows, width = own.shape
     half = rows // 2
-    size = mine.shape[1]
     position, core = where[0], where[1]
-    across = width // size
-    count = half // size * across
     out[tile(position, rows)] = own[...].astype(HALF)
     other = (1 - position) * 2
     for part, block in ((mine, other + core), (theirs, other + 1 - core)):
+        size = part.shape[1]
+        across = width // size
         for band in range(half // size):
             here = tile(block * (half // size) + band, size)
             for column in range(across):
-                out[here, column * size : (column + 1) * size] = part[
-                    side * count + band * across + column
-                ]
+                out[here, column * size : (column + 1) * size] = part[band * across + column]
 
 
 def state_kernel(
-    where, left, right, mine, theirs, stat_left, stat_right, bases, turned, back, full, sem
+    where,
+    left,
+    right,
+    first,
+    first_x,
+    second,
+    first_next,
+    first_x_next,
+    second_next,
+    stat_left,
+    stat_right,
+    bases,
+    turned,
+    back,
+    full,
+    sem,
 ):
     rows, width = left.shape
     size = rows // TILES
-    position, core = where[0], where[1]
+    position, core, x = where[0], where[1], where[2]
     here, there = tile(position, rows), tile(1 - position, rows)
     for side, stat in enumerate((stat_left, stat_right)):
 
@@ -185,17 +207,30 @@
         def _():
             pltpu.make_async_copy(stat, full.at[here], sem).start()
 
-    place_basis(where, bases.at[core], left, mine, theirs, 0)
-    place_basis(where, bases.at[1 - core], right, mine, theirs, 1)
+    def place(basis_mine, basis_theirs, stats):
+        place_basis(where, bases.at[core], left, basis_mine, basis_theirs)
+        base = (1 - position) * TILES
+        same = diagonal(size)
+        for number, (i, j) in enumerate(UPPER):
+            value = stats[number].astype(FULL)
+            if i == j:
+                line = stats[len(UPPER), i * 16 : (i + 1) * 16].astype(FULL)[:1]
+                value = value + jnp.where(same, line, 0.0)
+            full[tile(base + i, size), tile(base + j, size)] = value
+            if i != j:
+                full[tile(base + j, size), tile(base + i, size)] = value.T
+
+    @pl.when(x == 0)
+    def _():
+        place(first, first_next, first_x)
+
+    @pl.when(x == 1)
+    def _():
+        place(first_x, first_x_next, first)
+
+    place_basis(where, bases.at[1 - core], right, second, second_next)
     turned[...] = bases[core].T
     back[...] = bases[1 - core].T
-    base = (1 - position) * TILES
-    first = rows * width // size**2
-    for place, (i, j) in enumerate(UPPER):
-        value = mine[first + place].astype(FULL) + mine[first + len(UPPER) + place].astype(FULL)
-        full[tile(base + i, size), tile(base + j, size)] = value
-        if i != j:
-            full[tile(base + j, size), tile(base + i, size)] = value.T
     pltpu.make_async_copy(stat_left, full.at[here], sem).wait()
     full[there, here] = full[here, there].T
 
@@ -238,8 +273,32 @@
     kept[...] = matmul(bases[core, here], scaled).astype(HALF)
 
 
+def side_copies(top, low, out, sem):
+    half = top.shape[0]
+    return [
+        pltpu.make_async_copy(top, out.at[:half], sem.at[0]),
+        pltpu.make_async_copy(low, out.at[half:], sem.at[1]),
+    ]
+
+
 def update_kernel(
-    where, kept, came, kept_next, came_next, back, new, new_next, out, second_new, rows_back, sem
+    where,
+    kept,
+    came,
+    kept_next,
+    came_next,
+    back,
+    new,
+    new_next,
+    top,
+    low,
+    out,
+    second_new,
+    left,
+    right,
+    rows_back,
+    sem,
+    side_sem,
 ):
     rows, width = out.shape
     step = kept.shape[1]
@@ -250,6 +309,13 @@
     ]
     for copy in copies:
         copy.start()
+    for side, target in enumerate((left, right)):
+
+        @pl.when(core == side)
+        def _():
+            for copy in side_copies(top, low, target, side_sem):
+                copy.start()
+
     for value, place in (
         (kept, position * 2 + core),
         (came, (1 - position) * 2 + core),
@@ -257,32 +323,18 @@
         (came_next, (1 - position) * 2 + 1 - core),
     ):
         rows_back[:, tile(place, step)] = value[...]
-    for here in [slice(i * step, (i + 1) * step) for i in range(4)]:
+    for here in quarters(width):
         out[:, here] = (matmul(rows_back[...], back[:, here]) * (1.0 / width)).astype(HALF)
-    for copy in copies:
+    for copy in copies + side_copies(top, low, left, side_sem):
         copy.wait()
 
 
-def write_sides(core, top, low, side, left, right, sem):
-    half = top.shape[0]
-    for place, out in enumerate((left, right)):
-
-        @pl.when((core ^ side) == place)
+def next_side_kernel(where, top, low, left_in, right_in, left, right, sem):
+    for side, out in enumerate((right, left)):
+
+        @pl.when(where[1] == side)
         def _():
-            run_all(
-                [
-                    pltpu.make_async_copy(top, out.at[:half], sem.at[0]),
-                    pltpu.make_async_copy(low, out.at[half:], sem.at[1]),
-                ]
-            )
-
-
-def own_side_kernel(where, top, low, left, right, sem):
-    write_sides(where[1], top, low, 0, left, right, sem)
-
-
-def next_side_kernel(where, top, low, left_in, right_in, left, right, sem):
-    write_sides(where[1], top, low, 1, left, right, sem)
+            run_all(side_copies(top, low, out, sem))
 
 
 def quarters(width):
@@ -364,41 +416,39 @@
 
     raw = lax.dynamic_slice_in_dim(group_grads[0], (1 - core) * half, half, 0)
     came = dp_swap(raw, 1)
-    cut = width * 5 // 8
-    rest = width - cut
-    tiles = rows * width // quarter**2 + 2 * len(UPPER)
-    state_sent, near_kept, near_sent, kept, *sent = call(
+    count = half * width // quarter**2
+    first_sent, second_sent, kept, sent = call(
         start_kernel,
-        [shaped((tiles, quarter, quarter), HALF)]
-        + [shaped((quarter, cut), FULL)] * 2
-        + [shaped((quarter // 2, rest), FULL)] * 4,
+        [shaped((count, quarter, quarter), HALF)] * 2
+        + [shaped((quarter, width), FULL), shaped((quarter, width), HALF)],
         (where, group_grads, came, basis_left, basis_right, stat_left, stat_right),
         [SMEM] + [VMEM] * 2 + [ANY] * 4,
         [
             pltpu.VMEM((2, half, width), FULL),
             pltpu.VMEM((rows, rows), FULL),
-            pltpu.SemaphoreType.DMA((3,)),
+            pltpu.SemaphoreType.DMA((2,)),
         ],
         moved=2**22,
-        limit=52,
-    )
-    near_came = dp_swap(near_sent, 2)
-    came = [dp_swap(value, 4 * (k + 1)) for k, value in enumerate(sent)]
-    state_mine = shard_swap(state_sent)
-    near_own, *near_sent, own, sent = call(
+        limit=50,
+    )
+    came = dp_swap(sent, 2)
+    first = shard_swap(first_sent)
+    second_half = shard_swap(second_sent)
+    own, *sent = call(
         second_sum_kernel,
-        [shaped((chunk, cut), FULL)] * 4 + [shaped((chunk, rest), FULL)] * 2,
-        (where, near_kept, near_came, kept, *came),
-        [SMEM] + [VMEM] * 6,
+        [shaped((chunk, width), FULL)] + [shaped((chunk, width), HALF)] * 3,
+        (where, kept, came),
+        [SMEM] + [VMEM] * 2,
         moved=2**20,
     )
-    near_came = [dp_swap(value, 4 * (k + 1)) for k, value in enumerate(near_sent)]
-    came = dp_swap(sent, 2)
+    pieces = [dp_swap(value, 4 * (k + 1)) for k, value in enumerate(sent)]
+    pieces[0], first = lax.optimization_barrier((pieces[0], first))
+    first_x = dp_swap(first, 2)
     (piece,) = call(
         third_sum_kernel,
         [shaped((chunk, width), HALF)],
-        (near_own, *near_came, own, came),
-        [VMEM] * 6,
+        (own, *pieces),
+        [VMEM] * 4,
         moved=2**19,
     )
     pieces = [piece] + [dp_swap(piece, 4 * k) for k in (1, 2, 3)]
@@ -409,10 +459,12 @@
         [SMEM] + [VMEM] * 4,
         moved=2**19,
     )
-    part, state_mine = lax.optimization_barrier((part, state_mine))
+    part, first, first_x, second_half = lax.optimization_barrier(
+        (part, first, first_x, second_half)
+    )
     parts = [part, dp_swap(part, 2), shard_swap(part), cross_swap(part)]
-
-    state_theirs = dp_swap(state_mine, 1)
+    state = [first, first_x, second_half]
+    state += [dp_swap(value, 1) for value in state]
     square = shaped((width, width), HALF)
     bases, left_turned, right_turned, stat = call(
         state_kernel,
@@ -421,12 +473,11 @@
             where,
             basis_left,
             basis_right,
-            state_mine,
-            state_theirs,
+            *state,
             stat_left,
             stat_right,
         ),
-        [SMEM] + [VMEM] * 4 + [ANY] * 2,
+        [SMEM] + [VMEM] * 8 + [ANY] * 2,
         [pltpu.SemaphoreType.DMA(())],
         moved=2**24,
     )
@@ -487,12 +538,17 @@
     )
     low_next = dp_swap(low, 1)
     back_came_next = dp_swap(back_came, 1)
-    update, second_new = pl.pallas_call(
+    side = shaped((rows, width), FULL)
+    update, second_new, left_new, right_new = pl.pallas_call(
         update_kernel,
-        out_shape=[shaped((rows, width), HALF), shaped((width, rows), FULL)],
-        in_specs=[SMEM] + [VMEM] * 5 + [ANY] * 2,
-        out_specs=[VMEM, ANY],
-        scratch_shapes=[pltpu.VMEM((rows, width), HALF), pltpu.SemaphoreType.DMA((2,))],
+        out_shape=[shaped((rows, width), HALF), shaped((width, rows), FULL), side, side],
+        in_specs=[SMEM] + [VMEM] * 5 + [ANY] * 4,
+        out_specs=[VMEM] + [ANY] * 3,
+        scratch_shapes=[
+            pltpu.VMEM((rows, width), HALF),
+            pltpu.SemaphoreType.DMA((2,)),
+            pltpu.SemaphoreType.DMA((2,)),
+        ],
         compiler_params=pltpu.CompilerParams(vmem_limit_bytes=24 * 2**20),
         cost_estimate=pl.CostEstimate(
             flops=unit // 2, bytes_accessed=2**23, transcendentals=0
@@ -506,20 +562,12 @@
         right_turned,
         new,
         new_next,
-    )
-    sides = [shaped((rows, width), FULL)] * 2
-    left_new, right_new = call(
-        own_side_kernel,
-        sides,
-        (where, top, low),
-        [SMEM, ANY, ANY],
-        [pltpu.SemaphoreType.DMA((2,))],
-        moved=2**22,
-        space=ANY,
+        top,
+        low,
     )
     left_new, right_new = call(
         next_side_kernel,
-        sides,
+        [side, side],
         (where, top_next, low_next, left_new, right_new),
         [SMEM] + [ANY] * 4,
         [pltpu.SemaphoreType.DMA((2,))],

time: 102 us -> 96.8 us (0.949)
  Pallas kernels: 38 us -> 33.3 us
  local copies, waits for them, and re-layouts: 1.11 us -> 2.33 us
    ppermute x4 -> x5, waiting for transfers between devices: 7.79 us -> 0.11 us  [shard_swap(): return lax.ppermute(value, 'shard', [(0, 1), (1, 0)])]
    pallas_call x12 -> x11, Pallas kernels: 34.2 us -> 29.6 us  [call(): pl.pallas_call(kernel, out_shape=outs, in_specs=specs, out_specs=[space]...]
    ppermute x1, waiting for transfers between devices: 0.01 us -> 3.49 us  [cross_swap(): return lax.ppermute(value, ('dp', 'shard'), pairs)]
    ppermute x23 -> x22, waiting for transfers between devices: 26.3 us -> 29.5 us  [dp_swap(): return lax.ppermute(value, 'dp', [(i, i ^ distance) for i in range(16)])]
    ppermute x23 -> x22, starting transfers between devices: 19.3 us -> 17.2 us  [dp_swap(): return lax.ppermute(value, 'dp', [(i, i ^ distance) for i in range(16)])]
    unnamed x12 -> x14, local copies, waits for them, and re-layouts: 0.02 us -> 1.25 us
    ppermute x1, starting transfers between devices: 0.26 us -> 1.48 us  [cross_swap(): return lax.ppermute(value, ('dp', 'shard'), pairs)]
    ppermute x4 -> x5, starting transfers between devices: 7.65 us -> 8.14 us  [shard_swap(): return lax.ppermute(value, 'shard', [(0, 1), (1, 0)])]
  transfers between devices with their start and end apart: 28 -> 28, of which waited for: 16 -> 15; matrix products, arithmetic and copies ran while one was open for 0% -> 0% of each run, Pallas kernels for 25% -> 24%
where the time goes in v6:
time: 96.8 us; the launch traced here: 96.6 us
  Pallas kernels  33.3 us (34%)
  waiting for transfers between devices  33.1 us (34%)
  starting transfers between devices  26.8 us (28%)
  local copies, waits for them, and re-layouts  2.33 us (2%)
  between operations  1 us (1%)
    pallas_call x11, Pallas kernels, call(): pl.pallas_call(kernel, out_shape=outs, in_specs=specs, out_specs=[space]...  29.6 us
    ppermute x22, waiting for transfers between devices, dp_swap(): return lax.ppermute(value, 'dp', [(i, i ^ distance) for i in range(16)])  29.5 us
    ppermute x22, starting transfers between devices, dp_swap(): return lax.ppermute(value, 'dp', [(i, i ^ distance) for i in range(16)])  17.2 us
    ppermute x5, starting transfers between devices, shard_swap(): return lax.ppermute(value, 'shard', [(0, 1), (1, 0)])  8.14 us
    pallas_call x1, Pallas kernels, fast_body(): pl.pallas_call(update_kernel, out_shape=[shaped((rows, width), HALF), sha...  3.66 us
    ppermute x1, waiting for transfers between devices, cross_swap(): return lax.ppermute(value, ('dp', 'shard'), pairs)  3.49 us
  transfers between devices with their start and end apart: 28, of which 15 were waited for; matrix products, arithmetic and copies ran while one was open for 0% of the time, Pallas kernels for 24%

profile of v6, /device:TPU:0, one launch (start us, length us, event | category | flops | bytes accessed | tf_op | source)
XLA Modules:
  0.0 96.6 jit_solution(2563866662978811290)
XLA Ops:
  0.6 1.1 %dynamic-slice_bitcast_fusion = bf16[256,1024]{1,0:T(8,128)(2,1)S(1)} fusion(bf16[1,512,1024]{2,1,0:T(8,128)(2,1)} %group.1, s32[]{:T(128)S(6)} %select_n.3), kind=kLoop, calls=%fused_computation | loop fusion | bytes 1048580 | tf_op jit(solution)/shard_map/dynamic_slice | solution.py:417
  1.7 0.5 collective-permute-start
  2.2 0.1 pad_add_fusion.where
  2.3 1.5 %collective-permute-done.came = bf16[256,1024]{1,0:T(8,128)(2,1)S(1)} collective-permute-done((bf16[256,1024]{1,0:T(8,128)(2,1)S(1)}, bf16[256,1024]{1,0:T(8,128)(2,1)S(1)}, u32[]{:S(2)}, u32[]{:S(2)}) %collective-permute-start) | collective-permute-done | bytes 524320 | tf_op jit(solution)/shard_map/ppermute | solution.py:408
  3.8 1.2 %copy-done.4 = bf16[1,512,1024]{2,1,0:T(8,128)(2,1)S(1)} copy-done((bf16[1,512,1024]{2,1,0:T(8,128)(2,1)S(1)}, bf16[1,512,1024]{2,1,0:T(8,128)(2,1)}, u32[]{:S(2)}) %copy-start.4) | copy-done | bytes 1048600
  5.0 2.4 %shard_map.102 = (bf16[16,128,128]{2,1,0:T(8,128)(2,1)S(1)}, bf16[16,128,128]{2,1,0:T(8,128)(2,1)S(1)}, f32[128,1024]{1,0:T(8,128)S(1)}, bf16[128,1024]{1,0:T(8,128)(2,1)S(1)}) custom-call(s32[4]{0:T(128)S(1)} %pad_add_fusion.where, bf16[1,512,1024]{2,1,0:T(8,128)(2,1)S(1)} %copy-done.4, bf16[256,1024]{1,0:T(8,128)(2,1)S(1)} %collective-permute-done.came, ...), custom_call_target="tpu_custom_call" | custom-call | bytes 4194304 | tf_op jit(solution)/shard_map/pallas_call | solution.py:43
  7.5 3.0 %collective-permute-start.3 = (bf16[16,128,128]{2,1,0:T(8,128)(2,1)S(1)}, bf16[16,128,128]{2,1,0:T(8,128)(2,1)S(1)}, u32[]{:S(2)}, u32[]{:S(2)}) collective-permute-start(bf16[16,128,128]{2,1,0:T(8,128)(2,1)S(1)} %get-tuple-element.50), channel_id=1, source_target_pairs={{0,1},{1,0},{2,3},{3,2},{4,5},{5,4},{6,7},{7,6},{8,9},{9,8},{10,11... | collective-permute-start | bytes 1572872 | tf_op jit(solution)/shard_map/ppermute | solution.py:411
  10.4 1.5 %collective-permute-start.1 = (bf16[128,1024]{1,0:T(8,128)(2,1)S(1)}, bf16[128,1024]{1,0:T(8,128)(2,1)S(1)}, u32[]{:S(2)}, u32[]{:S(2)}) collective-permute-start(bf16[128,1024]{1,0:T(8,128)(2,1)S(1)} %get-tuple-element.47), channel_id=1, source_target_pairs={{0,4},{2,6},{4,0},{6,2},{8,12},{10,14},{12,8},{14,10},{16,20},{18,... | collective-permute-start | bytes 786440 | tf_op jit(solution)/shard_map/ppermute | solution.py:408
  11.9 6.6 %collective-permute-done.1.came = bf16[128,1024]{1,0:T(8,128)(2,1)S(1)} collective-permute-done((bf16[128,1024]{1,0:T(8,128)(2,1)S(1)}, bf16[128,1024]{1,0:T(8,128)(2,1)S(1)}, u32[]{:S(2)}, u32[]{:S(2)}) %collective-permute-start.1) | collective-permute-done | bytes 262176 | tf_op jit(solution)/shard_map/ppermute | solution.py:408
  18.5 0.6 shard_map.103
  19.1 1.6 %collective-permute-start.2 = (bf16[32,1024]{1,0:T(8,128)(2,1)S(1)}, bf16[32,1024]{1,0:T(8,128)(2,1)S(1)}, u32[]{:S(2)}, u32[]{:S(2)}) collective-permute-start(bf16[32,1024]{1,0:T(8,128)(2,1)S(1)} %get-tuple-element.49), channel_id=1, source_target_pairs={{0,8},{2,10},{4,12},{6,14},{8,0},{10,2},{12,4},{14,6},{16,24},{18,... | collective-permute-start | bytes 196616 | tf_op jit(solution)/shard_map/ppermute | solution.py:408
  20.7 0.5 collective-permute-start.10
  21.2 2.2 %collective-permute-done.2.one = bf16[32,1024]{1,0:T(8,128)(2,1)S(1)} collective-permute-done((bf16[32,1024]{1,0:T(8,128)(2,1)S(1)}, bf16[32,1024]{1,0:T(8,128)(2,1)S(1)}, u32[]{:S(2)}, u32[]{:S(2)}) %collective-permute-start.2) | collective-permute-done | bytes 65568 | tf_op jit(solution)/shard_map/ppermute | solution.py:408
  23.4 0.0 collective-permute-done.3.first
  23.4 1.7 %collective-permute-start.9 = (bf16[16,128,128]{2,1,0:T(8,128)(2,1)S(1)}, bf16[16,128,128]{2,1,0:T(8,128)(2,1)S(1)}, u32[]{:S(2)}, u32[]{:S(2)}) collective-permute-start(bf16[16,128,128]{2,1,0:T(8,128)(2,1)S(1)} %collective-permute-done.3.first), channel_id=1, source_target_pairs={{0,4},{2,6},{4,0},{6,2},{8,12},{10,14},{12,8},{14,10},{16,20},{18,... | collective-permute-start | bytes 1572872 | tf_op jit(solution)/shard_map/ppermute | solution.py:408
  25.2 2.6 %collective-permute-start.4 = (bf16[32,1024]{1,0:T(8,128)(2,1)S(1)}, bf16[32,1024]{1,0:T(8,128)(2,1)S(1)}, u32[]{:S(2)}, u32[]{:S(2)}) collective-permute-start(bf16[32,1024]{1,0:T(8,128)(2,1)S(1)} %get-tuple-element.52), channel_id=1, source_target_pairs={{0,16},{2,18},{4,20},{6,22},{8,24},{10,26},{12,28},{14,30},{16,0},... | collective-permute-start | bytes 196616 | tf_op jit(solution)/shard_map/ppermute | solution.py:408
  27.7 1.3 %collective-permute-start.5 = (bf16[32,1024]{1,0:T(8,128)(2,1)S(1)}, bf16[32,1024]{1,0:T(8,128)(2,1)S(1)}, u32[]{:S(2)}, u32[]{:S(2)}) collective-permute-start(bf16[32,1024]{1,0:T(8,128)(2,1)S(1)} %get-tuple-element.53), channel_id=1, source_target_pairs={{0,24},{2,26},{4,28},{6,30},{8,16},{10,18},{12,20},{14,22},{16,8},... | collective-permute-start | bytes 196616 | tf_op jit(solution)/shard_map/ppermute | solution.py:408
  29.1 3.0 %collective-permute-done.4.two = bf16[32,1024]{1,0:T(8,128)(2,1)S(1)} collective-permute-done((bf16[32,1024]{1,0:T(8,128)(2,1)S(1)}, bf16[32,1024]{1,0:T(8,128)(2,1)S(1)}, u32[]{:S(2)}, u32[]{:S(2)}) %collective-permute-start.4) | collective-permute-done | bytes 65568 | tf_op jit(solution)/shard_map/ppermute | solution.py:408
  32.1 1.7 %collective-permute-done.5.three = bf16[32,1024]{1,0:T(8,128)(2,1)S(1)} collective-permute-done((bf16[32,1024]{1,0:T(8,128)(2,1)S(1)}, bf16[32,1024]{1,0:T(8,128)(2,1)S(1)}, u32[]{:S(2)}, u32[]{:S(2)}) %collective-permute-start.5) | collective-permute-done | bytes 65568 | tf_op jit(solution)/shard_map/ppermute | solution.py:408
  33.9 0.1 collective-permute-start.6
  33.9 2.0 %collective-permute-start.7 = (bf16[32,1024]{1,0:T(8,128)(2,1)S(1)}, bf16[32,1024]{1,0:T(8,128)(2,1)S(1)}, u32[]{:S(2)}, u32[]{:S(2)}) collective-permute-start(bf16[32,1024]{1,0:T(8,128)(2,1)S(1)} %shard_map.104.refs_0_), channel_id=1, source_target_pairs={{0,16},{2,18},{4,20},{6,22},{8,24},{10,26},{12,28},{14,30},{16,0},... | collective-permute-start | bytes 196616 | tf_op jit(solution)/shard_map/ppermute | solution.py:408
  36.0 2.3 %collective-permute-start.8 = (bf16[32,1024]{1,0:T(8,128)(2,1)S(1)}, bf16[32,1024]{1,0:T(8,128)(2,1)S(1)}, u32[]{:S(2)}, u32[]{:S(2)}) collective-permute-start(bf16[32,1024]{1,0:T(8,128)(2,1)S(1)} %shard_map.104.refs_0_), channel_id=1, source_target_pairs={{0,24},{2,26},{4,28},{6,30},{8,16},{10,18},{12,20},{14,22},{16,8},... | collective-permute-start | bytes 196616 | tf_op jit(solution)/shard_map/ppermute | solution.py:408
  38.3 0.2 collective-permute-done.6.refs_1_
  38.5 0.7 collective-permute-done.7.refs_2_
  39.2 2.8 %collective-permute-done.8.refs_3_ = bf16[32,1024]{1,0:T(8,128)(2,1)S(1)} collective-permute-done((bf16[32,1024]{1,0:T(8,128)(2,1)S(1)}, bf16[32,1024]{1,0:T(8,128)(2,1)S(1)}, u32[]{:S(2)}, u32[]{:S(2)}) %collective-permute-start.8) | collective-permute-done | bytes 65568 | tf_op jit(solution)/shard_map/ppermute | solution.py:408
  42.0 0.6 shard_map.105.refs_0_
  42.6 0.0 copy-start.5
  42.6 0.0 collective-permute-done.10.second
  42.7 0.1 collective-permute-start.13
  42.7 0.5 collective-permute-start.14
  43.2 0.1 collective-permute-start.15
  43.3 0.5 collective-permute-start.16
  43.8 1.5 %collective-permute-start.11 = (bf16[128,1024]{1,0:T(8,128)(2,1)S(1)}, bf16[128,1024]{1,0:T(8,128)(2,1)S(1)}, u32[]{:S(2)}, u32[]{:S(2)}) collective-permute-start(bf16[128,1024]{1,0:T(8,128)(2,1)S(1)} %shard_map.105.refs_0_), channel_id=1, source_target_pairs={{0,1},{1,0},{2,3},{3,2},{4,5},{5,4},{6,7},{7,6},{8,9},{9,8},{10,11... | collective-permute-start | bytes 786440 | tf_op jit(solution)/shard_map/ppermute | solution.py:411
  45.3 6.6 %collective-permute-done.16.refs_1_ = bf16[128,1024]{1,0:T(8,128)(2,1)S(1)} collective-permute-done((bf16[128,1024]{1,0:T(8,128)(2,1)S(1)}, bf16[128,1024]{1,0:T(8,128)(2,1)S(1)}, u32[]{:S(2)}, u32[]{:S(2)}) %collective-permute-start.16) | collective-permute-done | bytes 262176 | tf_op jit(solution)/shard_map/ppermute | solution.py:408
  52.0 1.5 %collective-permute-start.12 = (bf16[128,1024]{1,0:T(8,128)(2,1)S(1)}, bf16[128,1024]{1,0:T(8,128)(2,1)S(1)}, u32[]{:S(2)}, u32[]{:S(2)}) collective-permute-start(bf16[128,1024]{1,0:T(8,128)(2,1)S(1)} %shard_map.105.refs_0_), channel_id=1, source_target_pairs={{0,5},{1,4},{2,7},{3,6},{4,1},{5,0},{6,3},{7,2},{8,13},{9,12},{10,... | collective-permute-start | bytes 786440 | tf_op jit(solution)/shard_map/ppermute | solution.py:415
  53.4 0.0 collective-permute-done.13.first_next
  53.4 0.0 collective-permute-start.17
  53.4 0.0 collective-permute-done.14.first_x_next
  53.5 0.5 collective-permute-start.18
  54.0 3.2 %shard_map.106 = (bf16[2,1024,1024]{2,1,0:T(8,128)(2,1)S(1)}, bf16[1024,1024]{1,0:T(8,128)(2,1)S(1)}, bf16[1024,1024]{1,0:T(8,128)(2,1)S(1)}, f32[1024,1024]{1,0:T(8,128)S(1)}) custom-call(s32[4]{0:T(128)S(1)} %pad_add_fusion.where, f32[512,1024]{1,0:T(8,128)S(1)} %copy-done, f32[512,1024]{1,0:T(8,128)S(1)} %copy-done.1, ...), custom_call_target="tpu_custom_call" | custom-call | bytes 16777216 | tf_op jit(solution)/shard_map/pallas_call | solution.py:43
  57.2 0.0 collective-permute-done.11.refs_4_
  57.2 3.5 %collective-permute-done.12.refs_5_ = bf16[128,1024]{1,0:T(8,128)(2,1)S(1)} collective-permute-done((bf16[128,1024]{1,0:T(8,128)(2,1)S(1)}, bf16[128,1024]{1,0:T(8,128)(2,1)S(1)}, u32[]{:S(2)}, u32[]{:S(2)}) %collective-permute-start.12) | collective-permute-done | bytes 262176 | tf_op jit(solution)/shard_map/ppermute | solution.py:415
  60.7 0.5 collective-permute-start.20
  61.2 0.0 collective-permute-done.17.refs_2_
  61.2 0.0 collective-permute-done.18.refs_3_
  61.3 1.0 %collective-permute-done.19.refs_6_ = bf16[128,1024]{1,0:T(8,128)(2,1)S(1)} collective-permute-done((bf16[128,1024]{1,0:T(8,128)(2,1)S(1)}, bf16[128,1024]{1,0:T(8,128)(2,1)S(1)}, u32[]{:S(2)}, u32[]{:S(2)}) %collective-permute-start.19) | collective-permute-done | bytes 262176 | tf_op jit(solution)/shard_map/ppermute | solution.py:408
  62.3 0.4 collective-permute-done.20.refs_7_
  62.6 1.7 %shard_map.107 = (bf16[1024,1024]{1,0:T(8,128)(2,1)S(1)}, bf16[512,256]{1,0:T(8,128)(2,1)S(1)}, bf16[512,256]{1,0:T(8,128)(2,1)S(1)}) custom-call(s32[4]{0:T(128)S(1)} %pad_add_fusion.where, f32[512,1024]{1,0:T(8,128)S(1)} %copy-done.5, bf16[2,1024,1024]{2,1,0:T(8,128)(2,1)S(1)} %get-tuple-element.61.bases, bf16[128,1024]{1,0:T(8,128)(2,1)S(1)} %shard_map.105.refs_0_, ...), custom_call_target="tpu_custom_call" | custom-call | flops 536870912 | bytes 4194304 | tf_op jit(solution)/shard_map/pallas_call | solution.py:43
  64.4 1.6 %collective-permute-start.21 = (bf16[512,256]{1,0:T(8,128)(2,1)S(1)}, bf16[512,256]{1,0:T(8,128)(2,1)S(1)}, u32[]{:S(2)}, u32[]{:S(2)}) collective-permute-start(bf16[512,256]{1,0:T(8,128)(2,1)S(1)} %get-tuple-element.67), channel_id=1, source_target_pairs={{0,1},{1,0},{2,3},{3,2},{4,5},{5,4},{6,7},{7,6},{8,9},{9,8},{10,11... | collective-permute-start | bytes 786440 | tf_op jit(solution)/shard_map/ppermute | solution.py:411
  66.0 6.7 %shard_map.109 = (bf16[1024,1024]{1,0:T(8,128)(2,1)S(1)}, bf16[1024,1024]{1,0:T(8,128)(2,1)S(1)}) custom-call(s32[4]{0:T(128)S(1)} %pad_add_fusion.where, bf16[1024,1024]{1,0:T(8,128)(2,1)S(1)} %get-tuple-element.64.gradient, bf16[2,1024,1024]{2,1,0:T(8,128)(2,1)S(1)} %get-tuple-element.61.bases, f32[1024,1024]{1,0:T(8,128)S(1)} %get-tuple-element.69.stat), custom_call_target="tpu_custom_call" | custom-call | flops 4294967296 | bytes 8388608 | tf_op jit(solution)/shard_map/pallas_call | solution.py:43
  72.7 0.1 collective-permute-done.21.came
  72.8 4.1 %shard_map.108 = (f32[1024,256]{1,0:T(8,128)S(1)}, bf16[512,256]{1,0:T(8,128)(2,1)S(1)}, bf16[512,256]{1,0:T(8,128)(2,1)S(1)}) custom-call(s32[4]{0:T(128)S(1)} %pad_add_fusion.where, bf16[1024,1024]{1,0:T(8,128)(2,1)S(1)} %get-tuple-element.64.gradient, bf16[2,1024,1024]{2,1,0:T(8,128)(2,1)S(1)} %get-tuple-element.61.bases, ...), custom_call_target="tpu_custom_call" | custom-call | flops 2147483648 | bytes 4194304 | tf_op jit(solution)/shard_map/pallas_call | solution.py:43
  76.9 1.6 %collective-permute-start.22 = (bf16[512,256]{1,0:T(8,128)(2,1)S(1)}, bf16[512,256]{1,0:T(8,128)(2,1)S(1)}, u32[]{:S(2)}, u32[]{:S(2)}) collective-permute-start(bf16[512,256]{1,0:T(8,128)(2,1)S(1)} %get-tuple-element.75), channel_id=1, source_target_pairs={{0,1},{1,0},{2,3},{3,2},{4,5},{5,4},{6,7},{7,6},{8,9},{9,8},{10,11... | collective-permute-start | bytes 786440 | tf_op jit(solution)/shard_map/ppermute | solution.py:411
  78.5 6.5 %shard_map.110 = (bf16[1024,1024]{1,0:T(8,128)(2,1)S(1)}, bf16[1024,1024]{1,0:T(8,128)(2,1)S(1)}, f32[256,1024]{1,0:T(8,128)S(1)}) custom-call(s32[4]{0:T(128)S(1)} %pad_add_fusion.where, bf16[1024,1024]{1,0:T(8,128)(2,1)S(1)} %get-tuple-element.72.start, bf16[1024,1024]{1,0:T(8,128)(2,1)S(1)} %get-tuple-element.73.start_turned), custom_call_target="tpu_custom_call" | custom-call | flops 5368709120 | bytes 4194304 | tf_op jit(solution)/shard_map/pallas_call | solution.py:43
  85.0 0.6 collective-permute-start.26
  85.6 1.8 %shard_map.111.low = f32[256,1024]{1,0:T(8,128)S(1)} custom-call(s32[4]{0:T(128)S(1)} %pad_add_fusion.where, bf16[1024,1024]{1,0:T(8,128)(2,1)S(1)} %get-tuple-element.80.current, bf16[1024,1024]{1,0:T(8,128)(2,1)S(1)} %get-tuple-element.81.turned), custom_call_target="tpu_custom_call" | custom-call | flops 1073741824 | bytes 2097152 | tf_op jit(solution)/shard_map/pallas_call | solution.py:43
  87.4 0.1 collective-permute-start.27
  87.5 0.5 collective-permute-start.23
  88.0 0.1 collective-permute-start.24
  88.1 2.4 %collective-permute-done.23.kept_next = bf16[512,256]{1,0:T(8,128)(2,1)S(1)} collective-permute-done((bf16[512,256]{1,0:T(8,128)(2,1)S(1)}, bf16[512,256]{1,0:T(8,128)(2,1)S(1)}, u32[]{:S(2)}, u32[]{:S(2)}) %collective-permute-start.23) | collective-permute-done | bytes 262176 | tf_op jit(solution)/shard_map/ppermute | solution.py:408
  90.5 0.4 collective-permute-done.24.came_next
  90.9 0.0 collective-permute-done.25.new_next
  90.9 3.7 %shard_map.112 = (bf16[512,1024]{1,0:T(8,128)(2,1)}, f32[1024,512]{1,0:T(8,128)}, f32[512,1024]{1,0:T(8,128)}, f32[512,1024]{1,0:T(8,128)}) custom-call(s32[4]{0:T(128)S(1)} %pad_add_fusion.where, bf16[512,256]{1,0:T(8,128)(2,1)S(1)} %get-tuple-element.68.kept, bf16[512,256]{1,0:T(8,128)(2,1)S(1)} %collective-permute-done.22.came, ...), custom_call_target="tpu_custom_call" | custom-call | flops 1073741824 | bytes 8388608 | tf_op jit(solution)/shard_map/pallas_call | solution.py:542
  94.6 1.9 %shard_map.113 = (f32[512,1024]{1,0:T(8,128)}, f32[512,1024]{1,0:T(8,128)}) custom-call(s32[4]{0:T(128)S(1)} %pad_add_fusion.where, f32[256,1024]{1,0:T(8,128)S(1)} %collective-permute-done.26.top, f32[256,1024]{1,0:T(8,128)S(1)} %collective-permute-done.27.low, ...), custom_call_target="tpu_custom_call", output_to_operand_aliasing={{0}: (3, {}), {1}: (4, {})} | custom-call | bytes 4194304 | tf_op jit(solution)/shard_map/pallas_call | solution.py:43
  (20 shorter events, 0.1 us)
Async XLA Ops:
  1.7 2.1 %collective-permute-start = (bf16[256,1024]{1,0:T(8,128)(2,1)S(1)}, bf16[256,1024]{1,0:T(8,128)(2,1)S(1)}, u32[]{:S(2)}, u32[]{:S(2)}) collective-permute-start(bf16[256,1024]{1,0:T(8,128)(2,1)S(1)} %dynamic-slice_bitcast_fusion), channel_id=1, source_target_pairs={{0,2},{2,0},{4,6},{6,4},{8,10},{10,8},{12,14},{14,12},{16,18},{18,... | collective-permute-start | bytes 1572872 | tf_op jit(solution)/shard_map/ppermute | solution.py:408
  3.8 1.2 %copy-start.4 = (bf16[1,512,1024]{2,1,0:T(8,128)(2,1)S(1)}, bf16[1,512,1024]{2,1,0:T(8,128)(2,1)}, u32[]{:S(2)}) copy-start(bf16[1,512,1024]{2,1,0:T(8,128)(2,1)} %group.1) | copy-start | bytes 3145732
  5.0 49.0 %copy-start = (f32[512,1024]{1,0:T(8,128)S(1)}, f32[512,1024]{1,0:T(8,128)}, u32[]{:S(2)}) copy-start(f32[512,1024]{1,0:T(8,128)} %left.3) | copy-start | bytes 6291460
  5.0 49.0 %copy-start.1 = (f32[512,1024]{1,0:T(8,128)S(1)}, f32[512,1024]{1,0:T(8,128)}, u32[]{:S(2)}) copy-start(f32[512,1024]{1,0:T(8,128)} %right.3) | copy-start | bytes 6291460
  5.0 49.0 %copy-start.2 = (f32[512,1024]{1,0:T(8,128)S(1)}, f32[512,1024]{1,0:T(8,128)}, u32[]{:S(2)}) copy-start(f32[512,1024]{1,0:T(8,128)} %stat_left.3) | copy-start | bytes 6291460
  5.0 49.0 %copy-start.3 = (f32[512,1024]{1,0:T(8,128)S(1)}, f32[512,1024]{1,0:T(8,128)}, u32[]{:S(2)}) copy-start(f32[512,1024]{1,0:T(8,128)} %stat_right.3) | copy-start | bytes 6291460
  7.5 16.0 %collective-permute-start.3 = (bf16[16,128,128]{2,1,0:T(8,128)(2,1)S(1)}, bf16[16,128,128]{2,1,0:T(8,128)(2,1)S(1)}, u32[]{:S(2)}, u32[]{:S(2)}) collective-permute-start(bf16[16,128,128]{2,1,0:T(8,128)(2,1)S(1)} %get-tuple-element.50), channel_id=1, source_target_pairs={{0,1},{1,0},{2,3},{3,2},{4,5},{5,4},{6,7},{7,6},{8,9},{9,8},{10,11... | collective-permute-start | bytes 1572872 | tf_op jit(solution)/shard_map/ppermute | solution.py:411
  10.4 8.1 %collective-permute-start.1 = (bf16[128,1024]{1,0:T(8,128)(2,1)S(1)}, bf16[128,1024]{1,0:T(8,128)(2,1)S(1)}, u32[]{:S(2)}, u32[]{:S(2)}) collective-permute-start(bf16[128,1024]{1,0:T(8,128)(2,1)S(1)} %get-tuple-element.47), channel_id=1, source_target_pairs={{0,4},{2,6},{4,0},{6,2},{8,12},{10,14},{12,8},{14,10},{16,20},{18,... | collective-permute-start | bytes 786440 | tf_op jit(solution)/shard_map/ppermute | solution.py:408
  19.1 4.3 %collective-permute-start.2 = (bf16[32,1024]{1,0:T(8,128)(2,1)S(1)}, bf16[32,1024]{1,0:T(8,128)(2,1)S(1)}, u32[]{:S(2)}, u32[]{:S(2)}) collective-permute-start(bf16[32,1024]{1,0:T(8,128)(2,1)S(1)} %get-tuple-element.49), channel_id=1, source_target_pairs={{0,8},{2,10},{4,12},{6,14},{8,0},{10,2},{12,4},{14,6},{16,24},{18,... | collective-permute-start | bytes 196616 | tf_op jit(solution)/shard_map/ppermute | solution.py:408
  20.7 21.9 %collective-permute-start.10 = (bf16[16,128,128]{2,1,0:T(8,128)(2,1)S(1)}, bf16[16,128,128]{2,1,0:T(8,128)(2,1)S(1)}, u32[]{:S(2)}, u32[]{:S(2)}) collective-permute-start(bf16[16,128,128]{2,1,0:T(8,128)(2,1)S(1)} %get-tuple-element.55), channel_id=1, source_target_pairs={{0,1},{1,0},{2,3},{3,2},{4,5},{5,4},{6,7},{7,6},{8,9},{9,8},{10,11... | collective-permute-start | bytes 1572872 | tf_op jit(solution)/shard_map/ppermute | solution.py:411
  23.4 19.2 %collective-permute-start.9 = (bf16[16,128,128]{2,1,0:T(8,128)(2,1)S(1)}, bf16[16,128,128]{2,1,0:T(8,128)(2,1)S(1)}, u32[]{:S(2)}, u32[]{:S(2)}) collective-permute-start(bf16[16,128,128]{2,1,0:T(8,128)(2,1)S(1)} %collective-permute-done.3.first), channel_id=1, source_target_pairs={{0,4},{2,6},{4,0},{6,2},{8,12},{10,14},{12,8},{14,10},{16,20},{18,... | collective-permute-start | bytes 1572872 | tf_op jit(solution)/shard_map/ppermute | solution.py:408
  25.2 7.0 %collective-permute-start.4 = (bf16[32,1024]{1,0:T(8,128)(2,1)S(1)}, bf16[32,1024]{1,0:T(8,128)(2,1)S(1)}, u32[]{:S(2)}, u32[]{:S(2)}) collective-permute-start(bf16[32,1024]{1,0:T(8,128)(2,1)S(1)} %get-tuple-element.52), channel_id=1, source_target_pairs={{0,16},{2,18},{4,20},{6,22},{8,24},{10,26},{12,28},{14,30},{16,0},... | collective-permute-start | bytes 196616 | tf_op jit(solution)/shard_map/ppermute | solution.py:408
  27.7 6.1 %collective-permute-start.5 = (bf16[32,1024]{1,0:T(8,128)(2,1)S(1)}, bf16[32,1024]{1,0:T(8,128)(2,1)S(1)}, u32[]{:S(2)}, u32[]{:S(2)}) collective-permute-start(bf16[32,1024]{1,0:T(8,128)(2,1)S(1)} %get-tuple-element.53), channel_id=1, source_target_pairs={{0,24},{2,26},{4,28},{6,30},{8,16},{10,18},{12,20},{14,22},{16,8},... | collective-permute-start | bytes 196616 | tf_op jit(solution)/shard_map/ppermute | solution.py:408
  33.9 4.7 %collective-permute-start.6 = (bf16[32,1024]{1,0:T(8,128)(2,1)S(1)}, bf16[32,1024]{1,0:T(8,128)(2,1)S(1)}, u32[]{:S(2)}, u32[]{:S(2)}) collective-permute-start(bf16[32,1024]{1,0:T(8,128)(2,1)S(1)} %shard_map.104.refs_0_), channel_id=1, source_target_pairs={{0,8},{2,10},{4,12},{6,14},{8,0},{10,2},{12,4},{14,6},{16,24},{18,... | collective-permute-start | bytes 196616 | tf_op jit(solution)/shard_map/ppermute | solution.py:408
  33.9 5.3 %collective-permute-start.7 = (bf16[32,1024]{1,0:T(8,128)(2,1)S(1)}, bf16[32,1024]{1,0:T(8,128)(2,1)S(1)}, u32[]{:S(2)}, u32[]{:S(2)}) collective-permute-start(bf16[32,1024]{1,0:T(8,128)(2,1)S(1)} %shard_map.104.refs_0_), channel_id=1, source_target_pairs={{0,16},{2,18},{4,20},{6,22},{8,24},{10,26},{12,28},{14,30},{16,0},... | collective-permute-start | bytes 196616 | tf_op jit(solution)/shard_map/ppermute | solution.py:408
  36.0 6.1 %collective-permute-start.8 = (bf16[32,1024]{1,0:T(8,128)(2,1)S(1)}, bf16[32,1024]{1,0:T(8,128)(2,1)S(1)}, u32[]{:S(2)}, u32[]{:S(2)}) collective-permute-start(bf16[32,1024]{1,0:T(8,128)(2,1)S(1)} %shard_map.104.refs_0_), channel_id=1, source_target_pairs={{0,24},{2,26},{4,28},{6,30},{8,16},{10,18},{12,20},{14,22},{16,8},... | collective-permute-start | bytes 196616 | tf_op jit(solution)/shard_map/ppermute | solution.py:408
  42.6 20.0 %copy-start.5 = (f32[512,1024]{1,0:T(8,128)S(1)}, f32[512,1024]{1,0:T(8,128)}, u32[]{:S(2)}) copy-start(f32[512,1024]{1,0:T(8,128)} %moment.1) | copy-start | bytes 6291460
  42.7 10.8 %collective-permute-start.13 = (bf16[16,128,128]{2,1,0:T(8,128)(2,1)S(1)}, bf16[16,128,128]{2,1,0:T(8,128)(2,1)S(1)}, u32[]{:S(2)}, u32[]{:S(2)}) collective-permute-start(bf16[16,128,128]{2,1,0:T(8,128)(2,1)S(1)} %collective-permute-done.3.first), channel_id=1, source_target_pairs={{0,2},{2,0},{4,6},{6,4},{8,10},{10,8},{12,14},{14,12},{16,18},{18,... | collective-permute-start | bytes 1572872 | tf_op jit(solution)/shard_map/ppermute | solution.py:408
  42.7 10.7 %collective-permute-start.14 = (bf16[16,128,128]{2,1,0:T(8,128)(2,1)S(1)}, bf16[16,128,128]{2,1,0:T(8,128)(2,1)S(1)}, u32[]{:S(2)}, u32[]{:S(2)}) collective-permute-start(bf16[16,128,128]{2,1,0:T(8,128)(2,1)S(1)} %collective-permute-done.9.first_x), channel_id=1, source_target_pairs={{0,2},{2,0},{4,6},{6,4},{8,10},{10,8},{12,14},{14,12},{16,18},{18,... | collective-permute-start | bytes 1572872 | tf_op jit(solution)/shard_map/ppermute | solution.py:408
  43.2 10.7 %collective-permute-start.15 = (bf16[16,128,128]{2,1,0:T(8,128)(2,1)S(1)}, bf16[16,128,128]{2,1,0:T(8,128)(2,1)S(1)}, u32[]{:S(2)}, u32[]{:S(2)}) collective-permute-start(bf16[16,128,128]{2,1,0:T(8,128)(2,1)S(1)} %collective-permute-done.10.second), channel_id=1, source_target_pairs={{0,2},{2,0},{4,6},{6,4},{8,10},{10,8},{12,14},{14,12},{16,18},{18,... | collective-permute-start | bytes 1572872 | tf_op jit(solution)/shard_map/ppermute | solution.py:408
  43.3 8.7 %collective-permute-start.16 = (bf16[128,1024]{1,0:T(8,128)(2,1)S(1)}, bf16[128,1024]{1,0:T(8,128)(2,1)S(1)}, u32[]{:S(2)}, u32[]{:S(2)}) collective-permute-start(bf16[128,1024]{1,0:T(8,128)(2,1)S(1)} %shard_map.105.refs_0_), channel_id=1, source_target_pairs={{0,4},{2,6},{4,0},{6,2},{8,12},{10,14},{12,8},{14,10},{16,20},{18,... | collective-permute-start | bytes 786440 | tf_op jit(solution)/shard_map/ppermute | solution.py:408
  43.8 13.4 %collective-permute-start.11 = (bf16[128,1024]{1,0:T(8,128)(2,1)S(1)}, bf16[128,1024]{1,0:T(8,128)(2,1)S(1)}, u32[]{:S(2)}, u32[]{:S(2)}) collective-permute-start(bf16[128,1024]{1,0:T(8,128)(2,1)S(1)} %shard_map.105.refs_0_), channel_id=1, source_target_pairs={{0,1},{1,0},{2,3},{3,2},{4,5},{5,4},{6,7},{7,6},{8,9},{9,8},{10,11... | collective-permute-start | bytes 786440 | tf_op jit(solution)/shard_map/ppermute | solution.py:411
  52.0 8.8 %collective-permute-start.12 = (bf16[128,1024]{1,0:T(8,128)(2,1)S(1)}, bf16[128,1024]{1,0:T(8,128)(2,1)S(1)}, u32[]{:S(2)}, u32[]{:S(2)}) collective-permute-start(bf16[128,1024]{1,0:T(8,128)(2,1)S(1)} %shard_map.105.refs_0_), channel_id=1, source_target_pairs={{0,5},{1,4},{2,7},{3,6},{4,1},{5,0},{6,3},{7,2},{8,13},{9,12},{10,... | collective-permute-start | bytes 786440 | tf_op jit(solution)/shard_map/ppermute | solution.py:415
  53.4 7.8 %collective-permute-start.17 = (bf16[128,1024]{1,0:T(8,128)(2,1)S(1)}, bf16[128,1024]{1,0:T(8,128)(2,1)S(1)}, u32[]{:S(2)}, u32[]{:S(2)}) collective-permute-start(bf16[128,1024]{1,0:T(8,128)(2,1)S(1)} %shard_map.105.refs_0_), channel_id=1, source_target_pairs={{0,2},{2,0},{4,6},{6,4},{8,10},{10,8},{12,14},{14,12},{16,18},{18,... | collective-permute-start | bytes 786440 | tf_op jit(solution)/shard_map/ppermute | solution.py:408
  53.5 7.8 %collective-permute-start.18 = (bf16[128,1024]{1,0:T(8,128)(2,1)S(1)}, bf16[128,1024]{1,0:T(8,128)(2,1)S(1)}, u32[]{:S(2)}, u32[]{:S(2)}) collective-permute-start(bf16[128,1024]{1,0:T(8,128)(2,1)S(1)} %collective-permute-done.16.refs_1_), channel_id=1, source_target_pairs={{0,2},{2,0},{4,6},{6,4},{8,10},{10,8},{12,14},{14,12},{16,18},{18,... | collective-permute-start | bytes 786440 | tf_op jit(solution)/shard_map/ppermute | solution.py:408
  60.7 1.5 %collective-permute-start.19 = (bf16[128,1024]{1,0:T(8,128)(2,1)S(1)}, bf16[128,1024]{1,0:T(8,128)(2,1)S(1)}, u32[]{:S(2)}, u32[]{:S(2)}) collective-permute-start(bf16[128,1024]{1,0:T(8,128)(2,1)S(1)} %collective-permute-done.11.refs_4_), channel_id=1, source_target_pairs={{0,2},{2,0},{4,6},{6,4},{8,10},{10,8},{12,14},{14,12},{16,18},{18,... | collective-permute-start | bytes 786440 | tf_op jit(solution)/shard_map/ppermute | solution.py:408
  60.7 1.9 %collective-permute-start.20 = (bf16[128,1024]{1,0:T(8,128)(2,1)S(1)}, bf16[128,1024]{1,0:T(8,128)(2,1)S(1)}, u32[]{:S(2)}, u32[]{:S(2)}) collective-permute-start(bf16[128,1024]{1,0:T(8,128)(2,1)S(1)} %collective-permute-done.12.refs_5_), channel_id=1, source_target_pairs={{0,2},{2,0},{4,6},{6,4},{8,10},{10,8},{12,14},{14,12},{16,18},{18,... | collective-permute-start | bytes 786440 | tf_op jit(solution)/shard_map/ppermute | solution.py:408
  64.4 8.4 %collective-permute-start.21 = (bf16[512,256]{1,0:T(8,128)(2,1)S(1)}, bf16[512,256]{1,0:T(8,128)(2,1)S(1)}, u32[]{:S(2)}, u32[]{:S(2)}) collective-permute-start(bf16[512,256]{1,0:T(8,128)(2,1)S(1)} %get-tuple-element.67), channel_id=1, source_target_pairs={{0,1},{1,0},{2,3},{3,2},{4,5},{5,4},{6,7},{7,6},{8,9},{9,8},{10,11... | collective-permute-start | bytes 786440 | tf_op jit(solution)/shard_map/ppermute | solution.py:411
  66.0 6.8 %copy-start.6 = (f32[1024,512]{1,0:T(8,128)S(1)}, f32[1024,512]{1,0:T(8,128)}, u32[]{:S(2)}) copy-start(f32[1024,512]{1,0:T(8,128)} %second.1) | copy-start | bytes 6291460
  76.9 8.7 %collective-permute-start.22 = (bf16[512,256]{1,0:T(8,128)(2,1)S(1)}, bf16[512,256]{1,0:T(8,128)(2,1)S(1)}, u32[]{:S(2)}, u32[]{:S(2)}) collective-permute-start(bf16[512,256]{1,0:T(8,128)(2,1)S(1)} %get-tuple-element.75), channel_id=1, source_target_pairs={{0,1},{1,0},{2,3},{3,2},{4,5},{5,4},{6,7},{7,6},{8,9},{9,8},{10,11... | collective-permute-start | bytes 786440 | tf_op jit(solution)/shard_map/ppermute | solution.py:411
  78.5 12.4 %collective-permute-start.25 = (f32[1024,256]{1,0:T(8,128)S(1)}, f32[1024,256]{1,0:T(8,128)S(1)}, u32[]{:S(2)}, u32[]{:S(2)}) collective-permute-start(f32[1024,256]{1,0:T(8,128)S(1)} %get-tuple-element.78.new), channel_id=1, source_target_pairs={{0,2},{2,0},{4,6},{6,4},{8,10},{10,8},{12,14},{14,12},{16,18},{18,... | collective-permute-start | bytes 3145736 | tf_op jit(solution)/shard_map/ppermute | solution.py:408
  85.0 9.5 %collective-permute-start.26 = (f32[256,1024]{1,0:T(8,128)S(1)}, f32[256,1024]{1,0:T(8,128)S(1)}, u32[]{:S(2)}, u32[]{:S(2)}) collective-permute-start(f32[256,1024]{1,0:T(8,128)S(1)} %get-tuple-element.79.top), channel_id=1, source_target_pairs={{0,2},{2,0},{4,6},{6,4},{8,10},{10,8},{12,14},{14,12},{16,18},{18,... | collective-permute-start | bytes 3145736 | tf_op jit(solution)/shard_map/ppermute | solution.py:408
  87.4 7.2 %collective-permute-start.27 = (f32[256,1024]{1,0:T(8,128)S(1)}, f32[256,1024]{1,0:T(8,128)S(1)}, u32[]{:S(2)}, u32[]{:S(2)}) collective-permute-start(f32[256,1024]{1,0:T(8,128)S(1)} %shard_map.111.low), channel_id=1, source_target_pairs={{0,2},{2,0},{4,6},{6,4},{8,10},{10,8},{12,14},{14,12},{16,18},{18,... | collective-permute-start | bytes 3145736 | tf_op jit(solution)/shard_map/ppermute | solution.py:408
  87.5 3.0 %collective-permute-start.23 = (bf16[512,256]{1,0:T(8,128)(2,1)S(1)}, bf16[512,256]{1,0:T(8,128)(2,1)S(1)}, u32[]{:S(2)}, u32[]{:S(2)}) collective-permute-start(bf16[512,256]{1,0:T(8,128)(2,1)S(1)} %get-tuple-element.68.kept), channel_id=1, source_target_pairs={{0,2},{2,0},{4,6},{6,4},{8,10},{10,8},{12,14},{14,12},{16,18},{18,... | collective-permute-start | bytes 786440 | tf_op jit(solution)/shard_map/ppermute | solution.py:408
  88.0 2.9 %collective-permute-start.24 = (bf16[512,256]{1,0:T(8,128)(2,1)S(1)}, bf16[512,256]{1,0:T(8,128)(2,1)S(1)}, u32[]{:S(2)}, u32[]{:S(2)}) collective-permute-start(bf16[512,256]{1,0:T(8,128)(2,1)S(1)} %collective-permute-done.22.came), channel_id=1, source_target_pairs={{0,2},{2,0},{4,6},{6,4},{8,10},{10,8},{12,14},{14,12},{16,18},{18,... | collective-permute-start | bytes 786440 | tf_op jit(solution)/shard_map/ppermute | solution.py:408

commit v7 on v5

--- a/solution.py
+++ b/solution.py
@@ -63,33 +63,44 @@
 UPPER = [(i, j) for i in range(TILES) for j in range(i, TILES)]
 
 
+def pack(out, base, value):
+    size = out.shape[1]
+    across = value.shape[1] // size
+    for band in range(value.shape[0] // size):
+        for column in range(across):
+            out[base + band * across + column] = value[
+                band * size : (band + 1) * size, column * size : (column + 1) * size
+            ].astype(HALF)
+
+
+def diagonal(size):
+    shape = (size, size)
+    return lax.broadcasted_iota(jnp.int32, shape, 0) == lax.broadcasted_iota(jnp.int32, shape, 1)
+
+
 def start_kernel(
     where,
-    group,
+    raw,
     came,
     left,
     right,
     stat_left,
     stat_right,
     state,
-    near_kept,
-    near_sent,
     kept,
-    far_1,
-    far_2,
-    far_3,
+    sent,
     basis_in,
     stat_in,
     sem,
 ):
-    position, core, x, z = where[0], where[1], where[2], where[3]
+    position, core, x = where[0], where[1], where[2]
     half, width = basis_in.shape[1:]
     size = state.shape[1]
-    bases = [
+    copies = [
         pltpu.make_async_copy(basis.at[tile(core, half)], basis_in.at[i], sem.at[i])
         for i, basis in enumerate((left, right))
     ]
-    for copy in bases:
+    for copy in copies:
         copy.start()
     for side, stat in enumerate((stat_left, stat_right)):
 
@@ -97,53 +108,40 @@
         def _():
             pltpu.make_async_copy(stat.at[:, tile(position, size * TILES)], stat_in, sem.at[2]).start()
 
-    rows, cut = near_kept.shape
-    for out, there in ((near_kept, x), (near_sent, 1 - x)):
-        out[...] = group[0, tile(core * 2 + there, rows), :cut].astype(FULL) + came[
-            tile(there, rows), :cut
-        ].astype(FULL)
-    rows = kept.shape[0] // 2
-    for k, out in enumerate((kept, far_1, far_2, far_3)):
-        for i in range(2):
-            there = i * 4 + (z ^ k)
-            out[i * rows : (i + 1) * rows] = group[0, tile(core * 8 + there, rows), cut:].astype(
-                FULL
-            ) + came[tile(there, rows), cut:].astype(FULL)
-    for copy in bases:
+    rows = kept.shape[0]
+    for out, there in ((kept, tile(x, rows)), (sent, tile(1 - x, rows))):
+        out[...] = (raw[there].astype(FULL) + came[there].astype(FULL)).astype(out.dtype)
+    count = half * width // size**2
+    for i, copy in enumerate(copies):
         copy.wait()
-    across = width // size
-    for band in range(2 * half // size):
-        for column in range(across):
-            begin = band * size % half
-            state[band * across + column] = basis_in[
-                band * size // half, begin : begin + size, column * size : (column + 1) * size
-            ].astype(HALF)
+        pack(state, i * count, basis_in.at[i])
     pltpu.make_async_copy(stat_left.at[:, : size * TILES], stat_in, sem.at[2]).wait()
-    base = 2 * half * width // size**2
+    same = diagonal(size)
+    base = 2 * count
     for place, (i, j) in enumerate(UPPER):
         value = stat_in[i * size : (i + 1) * size, j * size : (j + 1) * size]
         high = value.astype(HALF)
         state[base + place] = high
-        state[base + len(UPPER) + place] = (value - high.astype(FULL)).astype(HALF)
-
-
-def second_sum_kernel(
-    where, near_kept, near_came, kept, one, two, three, near_own, near_1, near_2, near_3, own, sent
-):
-    size = near_own.shape[0]
-    x, z = where[2], where[3]
-    for k, out in enumerate((near_own, near_1, near_2, near_3)):
+        if i == j:
+            low = jnp.where(same, value - high.astype(FULL), 0.0)
+            line = jnp.sum(low, axis=0, keepdims=True)
+            state[base + len(UPPER), i * 16 : (i + 1) * 16] = jnp.broadcast_to(
+                line, (16, size)
+            ).astype(HALF)
+
+
+def second_sum_kernel(where, kept, came, own, *sent):
+    size = own.shape[0]
+    z = where[3]
+    for k, out in enumerate((own, *sent)):
         there = tile(z ^ k, size)
-        out[...] = near_kept[there] + near_came[there]
-    for k, out in enumerate((own, sent)):
-        there = tile(x ^ k, size)
-        out[...] = (kept[there] + one[there]) + (two[there] + three[there])
-
-
-def third_sum_kernel(near_own, one, two, three, own, came, out):
-    cut = near_own.shape[1]
-    out[:, :cut] = ((near_own[...] + one[...]) + (two[...] + three[...])).astype(HALF)
-    out[:, cut:] = (own[...] + came[...]).astype(HALF)
+        out[...] = (kept[there] + came[there].astype(FULL)).astype(out.dtype)
+
+
+def third_sum_kernel(own, one, two, three, out):
+    out[...] = (
+        (own[...] + one[...].astype(FULL)) + (two[...].astype(FULL) + three[...].astype(FULL))
+    ).astype(HALF)
 
 
 def joined_kernel(where, *refs):
@@ -160,16 +158,14 @@
     size = mine.shape[1]
     position, core = where[0], where[1]
     across = width // size
-    count = half // size * across
+    base = side * half * width // size**2
     out[tile(position, rows)] = own[...].astype(HALF)
     other = (1 - position) * 2
     for part, block in ((mine, other + core), (theirs, other + 1 - core)):
         for band in range(half // size):
             here = tile(block * (half // size) + band, size)
             for column in range(across):
-                out[here, column * size : (column + 1) * size] = part[
-                    side * count + band * across + column
-                ]
+                out[here, column * size : (column + 1) * size] = part[base + band * across + column]
 
 
 def state_kernel(
@@ -191,8 +187,12 @@
     back[...] = bases[1 - core].T
     base = (1 - position) * TILES
     first = rows * width // size**2
-    for place, (i, j) in enumerate(UPPER):
-        value = mine[first + place].astype(FULL) + mine[first + len(UPPER) + place].astype(FULL)
+    same = diagonal(size)
+    for number, (i, j) in enumerate(UPPER):
+        value = mine[first + number].astype(FULL)
+        if i == j:
+            line = mine[first + len(UPPER), i * 16 : (i + 1) * 16].astype(FULL)[:1]
+            value = value + jnp.where(same, line, 0.0)
         full[tile(base + i, size), tile(base + j, size)] = value
         if i != j:
             full[tile(base + j, size), tile(base + i, size)] = value.T
@@ -238,18 +238,42 @@
     kept[...] = matmul(bases[core, here], scaled).astype(HALF)
 
 
+def write_part(core, side, block, part, left, right, sem):
+    size = part.shape[0]
+    here = slice(block * size, (block + 1) * size)
+    for place, out in enumerate((left, right)):
+
+        @pl.when((core ^ side) == place)
+        def _():
+            pltpu.make_async_copy(part, out.at[here], sem).start()
+
+    return pltpu.make_async_copy(part, left.at[here], sem)
+
+
 def update_kernel(
-    where, kept, came, kept_next, came_next, back, new, new_next, out, second_new, rows_back, sem
+    where,
+    kept,
+    came,
+    kept_next,
+    came_next,
+    back,
+    low,
+    top_next,
+    left_in,
+    right_in,
+    out,
+    left,
+    right,
+    rows_back,
+    sem,
 ):
     rows, width = out.shape
     step = kept.shape[1]
     position, core = where[0], where[1]
     copies = [
-        pltpu.make_async_copy(value, second_new.at[:, tile(place, step)], sem.at[i])
-        for i, (value, place) in enumerate(((new, core), (new_next, 1 - core)))
+        write_part(core, 0, 1, low, left, right, sem.at[0]),
+        write_part(core, 1, 0, top_next, left, right, sem.at[1]),
     ]
-    for copy in copies:
-        copy.start()
     for value, place in (
         (kept, position * 2 + core),
         (came, (1 - position) * 2 + core),
@@ -257,32 +281,14 @@
         (came_next, (1 - position) * 2 + 1 - core),
     ):
         rows_back[:, tile(place, step)] = value[...]
-    for here in [slice(i * step, (i + 1) * step) for i in range(4)]:
+    for here in quarters(width):
         out[:, here] = (matmul(rows_back[...], back[:, here]) * (1.0 / width)).astype(HALF)
     for copy in copies:
         copy.wait()
 
 
-def write_sides(core, top, low, side, left, right, sem):
-    half = top.shape[0]
-    for place, out in enumerate((left, right)):
-
-        @pl.when((core ^ side) == place)
-        def _():
-            run_all(
-                [
-                    pltpu.make_async_copy(top, out.at[:half], sem.at[0]),
-                    pltpu.make_async_copy(low, out.at[half:], sem.at[1]),
-                ]
-            )
-
-
-def own_side_kernel(where, top, low, left, right, sem):
-    write_sides(where[1], top, low, 0, left, right, sem)
-
-
-def next_side_kernel(where, top, low, left_in, right_in, left, right, sem):
-    write_sides(where[1], top, low, 1, left, right, sem)
+def next_side_kernel(where, low, left_in, right_in, left, right, sem):
+    write_part(where[1], 1, 1, low, left, right, sem.at[0]).wait()
 
 
 def quarters(width):
@@ -337,8 +343,19 @@
     improved(current, turned, tile(where[0] * 2, rows // 2), gram, out, None)
 
 
-def last_kernel(where, current, turned, out, gram):
+def last_kernel(
+    where, current, turned, top, new, new_next, out, left, right, second_new, gram, sem
+):
+    core = where[1]
+    step = new.shape[1]
+    copies = [write_part(core, 0, 0, top, left, right, sem.at[0])]
+    for i, (value, place) in enumerate(((new, core), (new_next, 1 - core))):
+        copy = pltpu.make_async_copy(value, second_new.at[:, tile(place, step)], sem.at[i + 1])
+        copy.start()
+        copies.append(copy)
     improved(current, turned, tile(where[0] * 2 + 1, out.shape[0]), gram, out, None)
+    for copy in copies:
+        copy.wait()
 
 
 def fast_body(group_grads, moment, second, stat_left, stat_right, basis_left, basis_right):
@@ -364,15 +381,16 @@
 
     raw = lax.dynamic_slice_in_dim(group_grads[0], (1 - core) * half, half, 0)
     came = dp_swap(raw, 1)
-    cut = width * 5 // 8
-    rest = width - cut
-    tiles = rows * width // quarter**2 + 2 * len(UPPER)
-    state_sent, near_kept, near_sent, kept, *sent = call(
+    raw = lax.dynamic_slice_in_dim(group_grads[0], core * half, half, 0)
+    count = rows * width // quarter**2 + len(UPPER) + 1
+    state_sent, kept, sent = call(
         start_kernel,
-        [shaped((tiles, quarter, quarter), HALF)]
-        + [shaped((quarter, cut), FULL)] * 2
-        + [shaped((quarter // 2, rest), FULL)] * 4,
-        (where, group_grads, came, basis_left, basis_right, stat_left, stat_right),
+        [
+            shaped((count, quarter, quarter), HALF),
+            shaped((quarter, width), FULL),
+            shaped((quarter, width), HALF),
+        ],
+        (where, raw, came, basis_left, basis_right, stat_left, stat_right),
         [SMEM] + [VMEM] * 2 + [ANY] * 4,
         [
             pltpu.VMEM((2, half, width), FULL),
@@ -380,25 +398,23 @@
             pltpu.SemaphoreType.DMA((3,)),
         ],
         moved=2**22,
-        limit=52,
-    )
-    near_came = dp_swap(near_sent, 2)
-    came = [dp_swap(value, 4 * (k + 1)) for k, value in enumerate(sent)]
+        limit=50,
+    )
+    came = dp_swap(sent, 2)
     state_mine = shard_swap(state_sent)
-    near_own, *near_sent, own, sent = call(
+    own, *sent = call(
         second_sum_kernel,
-        [shaped((chunk, cut), FULL)] * 4 + [shaped((chunk, rest), FULL)] * 2,
-        (where, near_kept, near_came, kept, *came),
-        [SMEM] + [VMEM] * 6,
+        [shaped((chunk, width), FULL)] + [shaped((chunk, width), HALF)] * 3,
+        (where, kept, came),
+        [SMEM] + [VMEM] * 2,
         moved=2**20,
     )
-    near_came = [dp_swap(value, 4 * (k + 1)) for k, value in enumerate(near_sent)]
-    came = dp_swap(sent, 2)
+    pieces = [dp_swap(value, 4 * (k + 1)) for k, value in enumerate(sent)]
     (piece,) = call(
         third_sum_kernel,
         [shaped((chunk, width), HALF)],
-        (near_own, *near_came, own, came),
-        [VMEM] * 6,
+        (own, *pieces),
+        [VMEM] * 4,
         moved=2**19,
     )
     pieces = [piece] + [dp_swap(piece, 4 * k) for k in (1, 2, 3)]
@@ -411,7 +427,6 @@
     )
     part, state_mine = lax.optimization_barrier((part, state_mine))
     parts = [part, dp_swap(part, 2), shard_swap(part), cross_swap(part)]
-
     state_theirs = dp_swap(state_mine, 1)
     square = shaped((width, width), HALF)
     bases, left_turned, right_turned, stat = call(
@@ -452,6 +467,7 @@
         flops=2 * unit,
         moved=2**23,
     )
+    start, moment_came = lax.optimization_barrier((start, moment_came))
     new, back_kept, back_sent = call(
         adam_kernel,
         [shaped((width, half), FULL)] + [shaped((rows, half), HALF)] * 2,
@@ -475,28 +491,31 @@
         moved=2**22,
     )
     top_next = dp_swap(top, 1)
-    current, back_came = lax.optimization_barrier((current, back_came))
-    (low,) = call(
+    current, back_came, back_kept_next, new_next = lax.optimization_barrier(
+        (current, back_came, back_kept_next, new_next)
+    )
+    back_came_next = dp_swap(back_came, 1)
+    side = shaped((rows, width), FULL)
+    low, left_new, right_new, second_new = pl.pallas_call(
         last_kernel,
-        [shaped((half, width), FULL)],
-        (where, current, current_turned),
-        [SMEM] + [VMEM] * 2,
-        [pltpu.VMEM((half, width), HALF)],
-        flops=unit // 2,
-        moved=2**21,
-    )
+        out_shape=[shaped((half, width), FULL), side, side, shaped((width, rows), FULL)],
+        in_specs=[SMEM] + [VMEM] * 2 + [ANY] * 3,
+        out_specs=[VMEM] + [ANY] * 3,
+        scratch_shapes=[pltpu.VMEM((half, width), HALF), pltpu.SemaphoreType.DMA((3,))],
+        compiler_params=pltpu.CompilerParams(vmem_limit_bytes=24 * 2**20),
+        cost_estimate=pl.CostEstimate(flops=unit // 2, bytes_accessed=2**22, transcendentals=0),
+    )(where, current, current_turned, top, new, new_next)
+    low, back_came_next = lax.optimization_barrier((low, back_came_next))
     low_next = dp_swap(low, 1)
-    back_came_next = dp_swap(back_came, 1)
-    update, second_new = pl.pallas_call(
+    update, left_new, right_new = pl.pallas_call(
         update_kernel,
-        out_shape=[shaped((rows, width), HALF), shaped((width, rows), FULL)],
-        in_specs=[SMEM] + [VMEM] * 5 + [ANY] * 2,
-        out_specs=[VMEM, ANY],
+        out_shape=[shaped((rows, width), HALF), side, side],
+        in_specs=[SMEM] + [VMEM] * 5 + [ANY] * 4,
+        out_specs=[VMEM] + [ANY] * 2,
         scratch_shapes=[pltpu.VMEM((rows, width), HALF), pltpu.SemaphoreType.DMA((2,))],
+        input_output_aliases={8: 1, 9: 2},
         compiler_params=pltpu.CompilerParams(vmem_limit_bytes=24 * 2**20),
-        cost_estimate=pl.CostEstimate(
-            flops=unit // 2, bytes_accessed=2**23, transcendentals=0
-        ),
+        cost_estimate=pl.CostEstimate(flops=unit // 2, bytes_accessed=2**22, transcendentals=0),
     )(
         where,
         back_kept,
@@ -504,28 +523,20 @@
         back_kept_next,
         back_came_next,
         right_turned,
-        new,
-        new_next,
-    )
-    sides = [shaped((rows, width), FULL)] * 2
-    left_new, right_new = call(
-        own_side_kernel,
-        sides,
-        (where, top, low),
-        [SMEM, ANY, ANY],
-        [pltpu.SemaphoreType.DMA((2,))],
-        moved=2**22,
-        space=ANY,
+        low,
+        top_next,
+        left_new,
+        right_new,
     )
     left_new, right_new = call(
         next_side_kernel,
-        sides,
-        (where, top_next, low_next, left_new, right_new),
-        [SMEM] + [ANY] * 4,
-        [pltpu.SemaphoreType.DMA((2,))],
-        moved=2**22,
+        [side, side],
+        (where, low_next, left_new, right_new),
+        [SMEM] + [ANY] * 3,
+        [pltpu.SemaphoreType.DMA((1,))],
+        moved=2**21,
         space=ANY,
-        aliases={3: 0, 4: 1},
+        aliases={2: 0, 3: 1},
     )
     return (update, second_new, left_new, right_new)
 

time: 102 us -> 91.6 us (0.90)
  starting transfers between devices: 27.2 us -> 19.6 us
  Pallas kernels: 38 us -> 33.9 us
  waiting for transfers between devices: 34.1 us -> 35.6 us
    pallas_call x12 -> x10, Pallas kernels: 34.2 us -> 27.7 us  [call(): pl.pallas_call(kernel, out_shape=outs, in_specs=specs, out_specs=[space]...]
    ppermute x23 -> x19, starting transfers between devices: 19.3 us -> 14 us  [dp_swap(): return lax.ppermute(value, 'dp', [(i, i ^ distance) for i in range(16)])]
    ppermute x4, starting transfers between devices: 7.65 us -> 4.1 us  [shard_swap(): return lax.ppermute(value, 'shard', [(0, 1), (1, 0)])]
    ppermute x1, waiting for transfers between devices: 0.01 us -> 3.26 us  [cross_swap(): return lax.ppermute(value, ('dp', 'shard'), pairs)]
    pallas_call x1 -> x2, Pallas kernels: 3.86 us -> 6.19 us  [the longest x1 3.26 us: fast_body(): pl.pallas_call(last_kernel, out_shape=[shaped((half, width), FULL), side,...]
    ppermute x23 -> x19, waiting for transfers between devices: 26.3 us -> 24 us  [dp_swap(): return lax.ppermute(value, 'dp', [(i, i ^ distance) for i in range(16)])]
    ppermute x1, starting transfers between devices: 0.26 us -> 1.49 us  [cross_swap(): return lax.ppermute(value, ('dp', 'shard'), pairs)]
  transfers between devices with their start and end apart: 28 -> 24, of which waited for: 16 -> 15; matrix products, arithmetic and copies ran while one was open for 0% -> 0% of each run, Pallas kernels for 25% -> 26%
where the time goes in v7:
time: 91.6 us; the launch traced here: 91.4 us
  waiting for transfers between devices  35.6 us (39%)
  Pallas kernels  33.9 us (37%)
  starting transfers between devices  19.6 us (21%)
  local copies, waits for them, and re-layouts  1.3 us (1%)
  between operations  0.98 us (1%)
    pallas_call x10, Pallas kernels, call(): pl.pallas_call(kernel, out_shape=outs, in_specs=specs, out_specs=[space]...  27.7 us
    ppermute x19, waiting for transfers between devices, dp_swap(): return lax.ppermute(value, 'dp', [(i, i ^ distance) for i in range(16)])  24 us
    ppermute x19, starting transfers between devices, dp_swap(): return lax.ppermute(value, 'dp', [(i, i ^ distance) for i in range(16)])  14 us
    ppermute x4, waiting for transfers between devices, shard_swap(): return lax.ppermute(value, 'shard', [(0, 1), (1, 0)])  8.31 us
    ppermute x4, starting transfers between devices, shard_swap(): return lax.ppermute(value, 'shard', [(0, 1), (1, 0)])  4.1 us
    ppermute x1, waiting for transfers between devices, cross_swap(): return lax.ppermute(value, ('dp', 'shard'), pairs)  3.26 us
    pallas_call x1, Pallas kernels, fast_body(): pl.pallas_call(last_kernel, out_shape=[shaped((half, width), FULL), side,...  3.26 us
    pallas_call x1, Pallas kernels, fast_body(): pl.pallas_call(update_kernel, out_shape=[shaped((rows, width), HALF), sid...  2.92 us
  transfers between devices with their start and end apart: 24, of which 15 were waited for; matrix products, arithmetic and copies ran while one was open for 0% of the time, Pallas kernels for 26%

profile of v7, /device:TPU:0, one launch (start us, length us, event | category | flops | bytes accessed | tf_op | source)
XLA Modules:
  0.0 91.4 jit_solution(9368725416878031853)
XLA Ops:
  0.6 1.3 %dynamic-slice_bitcast_fusion = (bf16[256,1024]{1,0:T(8,128)(2,1)S(1)}, bf16[256,1024]{1,0:T(8,128)(2,1)S(1)}) fusion(bf16[1,512,1024]{2,1,0:T(8,128)(2,1)} %param.7, s32[]{:T(128)S(6)} %select_n.7, s32[]{:T(128)S(6)} %select_n.6), kind=kLoop, calls=%fused_computation | loop fusion | bytes 2097160 | tf_op jit(solution)/shard_map/dynamic_slice | solution.py:382
  1.9 0.5 collective-permute-start
  2.4 0.1 pad_add_fusion.where
  2.5 1.5 %collective-permute-done.came = bf16[256,1024]{1,0:T(8,128)(2,1)S(1)} collective-permute-done((bf16[256,1024]{1,0:T(8,128)(2,1)S(1)}, bf16[256,1024]{1,0:T(8,128)(2,1)S(1)}, u32[]{:S(2)}, u32[]{:S(2)}) %collective-permute-start) | collective-permute-done | bytes 524320 | tf_op jit(solution)/shard_map/ppermute | solution.py:373
  4.0 2.8 %shard_map.102 = (bf16[43,128,128]{2,1,0:T(8,128)(2,1)S(1)}, f32[128,1024]{1,0:T(8,128)S(1)}, bf16[128,1024]{1,0:T(8,128)(2,1)S(1)}) custom-call(s32[4]{0:T(128)S(1)} %pad_add_fusion.where, bf16[256,1024]{1,0:T(8,128)(2,1)S(1)} %get-tuple-element.97.raw, bf16[256,1024]{1,0:T(8,128)(2,1)S(1)} %collective-permute-done.came, f32[512,1024]{1,0:T(8,128)} %left.3, ...), custom_call_target="tpu_custom_call" | custom-call | bytes 4194304 | tf_op jit(solution)/shard_map/pallas_call | solution.py:43
  6.8 3.0 %collective-permute-start.8 = (bf16[43,128,128]{2,1,0:T(8,128)(2,1)S(1)}, bf16[43,128,128]{2,1,0:T(8,128)(2,1)S(1)}, u32[]{:S(2)}, u32[]{:S(2)}) collective-permute-start(bf16[43,128,128]{2,1,0:T(8,128)(2,1)S(1)} %get-tuple-element.56), channel_id=1, source_target_pairs={{0,1},{1,0},{2,3},{3,2},{4,5},{5,4},{6,7},{7,6},{8,9},{9,8},{10,11... | collective-permute-start | bytes 4227080 | tf_op jit(solution)/shard_map/ppermute | solution.py:376
  9.7 1.5 %collective-permute-start.1 = (bf16[128,1024]{1,0:T(8,128)(2,1)S(1)}, bf16[128,1024]{1,0:T(8,128)(2,1)S(1)}, u32[]{:S(2)}, u32[]{:S(2)}) collective-permute-start(bf16[128,1024]{1,0:T(8,128)(2,1)S(1)} %get-tuple-element.51), channel_id=1, source_target_pairs={{0,4},{2,6},{4,0},{6,2},{8,12},{10,14},{12,8},{14,10},{16,20},{18,... | collective-permute-start | bytes 786440 | tf_op jit(solution)/shard_map/ppermute | solution.py:373
  11.2 6.6 %collective-permute-done.1.came = bf16[128,1024]{1,0:T(8,128)(2,1)S(1)} collective-permute-done((bf16[128,1024]{1,0:T(8,128)(2,1)S(1)}, bf16[128,1024]{1,0:T(8,128)(2,1)S(1)}, u32[]{:S(2)}, u32[]{:S(2)}) %collective-permute-start.1) | collective-permute-done | bytes 262176 | tf_op jit(solution)/shard_map/ppermute | solution.py:373
  17.8 0.6 shard_map.103
  18.4 1.6 %collective-permute-start.2 = (bf16[32,1024]{1,0:T(8,128)(2,1)S(1)}, bf16[32,1024]{1,0:T(8,128)(2,1)S(1)}, u32[]{:S(2)}, u32[]{:S(2)}) collective-permute-start(bf16[32,1024]{1,0:T(8,128)(2,1)S(1)} %get-tuple-element.53), channel_id=1, source_target_pairs={{0,8},{2,10},{4,12},{6,14},{8,0},{10,2},{12,4},{14,6},{16,24},{18,... | collective-permute-start | bytes 196616 | tf_op jit(solution)/shard_map/ppermute | solution.py:373
  20.0 2.6 %collective-permute-start.3 = (bf16[32,1024]{1,0:T(8,128)(2,1)S(1)}, bf16[32,1024]{1,0:T(8,128)(2,1)S(1)}, u32[]{:S(2)}, u32[]{:S(2)}) collective-permute-start(bf16[32,1024]{1,0:T(8,128)(2,1)S(1)} %get-tuple-element.54), channel_id=1, source_target_pairs={{0,16},{2,18},{4,20},{6,22},{8,24},{10,26},{12,28},{14,30},{16,0},... | collective-permute-start | bytes 196616 | tf_op jit(solution)/shard_map/ppermute | solution.py:373
  22.6 0.2 collective-permute-start.4
  22.8 0.5 collective-permute-done.2.one
  23.3 3.2 %collective-permute-done.3.two = bf16[32,1024]{1,0:T(8,128)(2,1)S(1)} collective-permute-done((bf16[32,1024]{1,0:T(8,128)(2,1)S(1)}, bf16[32,1024]{1,0:T(8,128)(2,1)S(1)}, u32[]{:S(2)}, u32[]{:S(2)}) %collective-permute-start.3) | collective-permute-done | bytes 65568 | tf_op jit(solution)/shard_map/ppermute | solution.py:373
  26.6 2.1 %collective-permute-done.4.three = bf16[32,1024]{1,0:T(8,128)(2,1)S(1)} collective-permute-done((bf16[32,1024]{1,0:T(8,128)(2,1)S(1)}, bf16[32,1024]{1,0:T(8,128)(2,1)S(1)}, u32[]{:S(2)}, u32[]{:S(2)}) %collective-permute-start.4) | collective-permute-done | bytes 65568 | tf_op jit(solution)/shard_map/ppermute | solution.py:373
  28.7 1.1 %collective-permute-start.7 = (bf16[32,1024]{1,0:T(8,128)(2,1)S(1)}, bf16[32,1024]{1,0:T(8,128)(2,1)S(1)}, u32[]{:S(2)}, u32[]{:S(2)}) collective-permute-start(bf16[32,1024]{1,0:T(8,128)(2,1)S(1)} %shard_map.104.refs_0_), channel_id=1, source_target_pairs={{0,24},{2,26},{4,28},{6,30},{8,16},{10,18},{12,20},{14,22},{16,8},... | collective-permute-start | bytes 196616 | tf_op jit(solution)/shard_map/ppermute | solution.py:373
  29.8 0.4 collective-permute-start.6
  30.3 2.9 %collective-permute-start.5 = (bf16[32,1024]{1,0:T(8,128)(2,1)S(1)}, bf16[32,1024]{1,0:T(8,128)(2,1)S(1)}, u32[]{:S(2)}, u32[]{:S(2)}) collective-permute-start(bf16[32,1024]{1,0:T(8,128)(2,1)S(1)} %shard_map.104.refs_0_), channel_id=1, source_target_pairs={{0,8},{2,10},{4,12},{6,14},{8,0},{10,2},{12,4},{14,6},{16,24},{18,... | collective-permute-start | bytes 196616 | tf_op jit(solution)/shard_map/ppermute | solution.py:373
  33.2 1.7 %collective-permute-done.7.refs_3_ = bf16[32,1024]{1,0:T(8,128)(2,1)S(1)} collective-permute-done((bf16[32,1024]{1,0:T(8,128)(2,1)S(1)}, bf16[32,1024]{1,0:T(8,128)(2,1)S(1)}, u32[]{:S(2)}, u32[]{:S(2)}) %collective-permute-start.7) | collective-permute-done | bytes 65568 | tf_op jit(solution)/shard_map/ppermute | solution.py:373
  34.9 1.3 %collective-permute-done.6.refs_2_ = bf16[32,1024]{1,0:T(8,128)(2,1)S(1)} collective-permute-done((bf16[32,1024]{1,0:T(8,128)(2,1)S(1)}, bf16[32,1024]{1,0:T(8,128)(2,1)S(1)}, u32[]{:S(2)}, u32[]{:S(2)}) %collective-permute-start.6) | collective-permute-done | bytes 65568 | tf_op jit(solution)/shard_map/ppermute | solution.py:373
  36.3 0.0 collective-permute-done.5.refs_1_
  36.3 0.6 shard_map.105.refs_0_
  36.8 0.0 copy-start.4
  36.8 4.0 %collective-permute-done.8.mine = bf16[43,128,128]{2,1,0:T(8,128)(2,1)S(1)} collective-permute-done((bf16[43,128,128]{2,1,0:T(8,128)(2,1)S(1)}, bf16[43,128,128]{2,1,0:T(8,128)(2,1)S(1)}, u32[]{:S(2)}, u32[]{:S(2)}) %collective-permute-start.8) | collective-permute-done | bytes 1409056 | tf_op jit(solution)/shard_map/ppermute | solution.py:376
  40.9 0.0 collective-permute-start.11
  40.9 1.7 %collective-permute-start.12 = (bf16[128,1024]{1,0:T(8,128)(2,1)S(1)}, bf16[128,1024]{1,0:T(8,128)(2,1)S(1)}, u32[]{:S(2)}, u32[]{:S(2)}) collective-permute-start(bf16[128,1024]{1,0:T(8,128)(2,1)S(1)} %shard_map.105.refs_0_), channel_id=1, source_target_pairs={{0,4},{2,6},{4,0},{6,2},{8,12},{10,14},{12,8},{14,10},{16,20},{18,... | collective-permute-start | bytes 786440 | tf_op jit(solution)/shard_map/ppermute | solution.py:373
  42.6 1.5 %collective-permute-start.10 = (bf16[128,1024]{1,0:T(8,128)(2,1)S(1)}, bf16[128,1024]{1,0:T(8,128)(2,1)S(1)}, u32[]{:S(2)}, u32[]{:S(2)}) collective-permute-start(bf16[128,1024]{1,0:T(8,128)(2,1)S(1)} %shard_map.105.refs_0_), channel_id=1, source_target_pairs={{0,5},{1,4},{2,7},{3,6},{4,1},{5,0},{6,3},{7,2},{8,13},{9,12},{10,... | collective-permute-start | bytes 786440 | tf_op jit(solution)/shard_map/ppermute | solution.py:380
  44.1 0.3 collective-permute-start.9
  44.4 0.0 collective-permute-start.13
  44.4 5.6 %collective-permute-done.12.refs_1_ = bf16[128,1024]{1,0:T(8,128)(2,1)S(1)} collective-permute-done((bf16[128,1024]{1,0:T(8,128)(2,1)S(1)}, bf16[128,1024]{1,0:T(8,128)(2,1)S(1)}, u32[]{:S(2)}, u32[]{:S(2)}) %collective-permute-start.12) | collective-permute-done | bytes 262176 | tf_op jit(solution)/shard_map/ppermute | solution.py:373
  50.0 0.0 collective-permute-start.14
  50.0 0.0 collective-permute-done.11.theirs
  50.0 0.0 copy-done
  50.0 3.2 %shard_map.106 = (bf16[2,1024,1024]{2,1,0:T(8,128)(2,1)S(1)}, bf16[1024,1024]{1,0:T(8,128)(2,1)S(1)}, bf16[1024,1024]{1,0:T(8,128)(2,1)S(1)}, f32[1024,1024]{1,0:T(8,128)S(1)}) custom-call(s32[4]{0:T(128)S(1)} %pad_add_fusion.where, f32[512,1024]{1,0:T(8,128)S(1)} %copy-done, f32[512,1024]{1,0:T(8,128)S(1)} %copy-done.1, ...), custom_call_target="tpu_custom_call" | custom-call | bytes 16777216 | tf_op jit(solution)/shard_map/pallas_call | solution.py:43
  53.2 3.3 %collective-permute-done.10.refs_5_ = bf16[128,1024]{1,0:T(8,128)(2,1)S(1)} collective-permute-done((bf16[128,1024]{1,0:T(8,128)(2,1)S(1)}, bf16[128,1024]{1,0:T(8,128)(2,1)S(1)}, u32[]{:S(2)}, u32[]{:S(2)}) %collective-permute-start.10) | collective-permute-done | bytes 262176 | tf_op jit(solution)/shard_map/ppermute | solution.py:380
  56.5 1.4 %collective-permute-done.9.refs_4_ = bf16[128,1024]{1,0:T(8,128)(2,1)S(1)} collective-permute-done((bf16[128,1024]{1,0:T(8,128)(2,1)S(1)}, bf16[128,1024]{1,0:T(8,128)(2,1)S(1)}, u32[]{:S(2)}, u32[]{:S(2)}) %collective-permute-start.9) | collective-permute-done | bytes 262176 | tf_op jit(solution)/shard_map/ppermute | solution.py:376
  57.9 0.0 collective-permute-start.15
  57.9 0.5 collective-permute-start.16
  58.4 0.0 collective-permute-done.13.refs_2_
  58.4 0.0 collective-permute-done.14.refs_3_
  58.4 1.0 %collective-permute-done.15.refs_6_ = bf16[128,1024]{1,0:T(8,128)(2,1)S(1)} collective-permute-done((bf16[128,1024]{1,0:T(8,128)(2,1)S(1)}, bf16[128,1024]{1,0:T(8,128)(2,1)S(1)}, u32[]{:S(2)}, u32[]{:S(2)}) %collective-permute-start.15) | collective-permute-done | bytes 262176 | tf_op jit(solution)/shard_map/ppermute | solution.py:373
  59.4 0.4 collective-permute-done.16.refs_7_
  59.8 0.0 copy-done.4
  59.8 1.7 %shard_map.107 = (bf16[1024,1024]{1,0:T(8,128)(2,1)S(1)}, bf16[512,256]{1,0:T(8,128)(2,1)S(1)}, bf16[512,256]{1,0:T(8,128)(2,1)S(1)}) custom-call(s32[4]{0:T(128)S(1)} %pad_add_fusion.where, f32[512,1024]{1,0:T(8,128)S(1)} %copy-done.4, bf16[2,1024,1024]{2,1,0:T(8,128)(2,1)S(1)} %get-tuple-element.60.bases, bf16[128,1024]{1,0:T(8,128)(2,1)S(1)} %shard_map.105.refs_0_, ...), custom_call_target="tpu_custom_call" | custom-call | flops 536870912 | bytes 4194304 | tf_op jit(solution)/shard_map/pallas_call | solution.py:43
  61.5 0.4 collective-permute-start.17
  61.9 6.7 %shard_map.108 = (bf16[1024,1024]{1,0:T(8,128)(2,1)S(1)}, bf16[1024,1024]{1,0:T(8,128)(2,1)S(1)}) custom-call(s32[4]{0:T(128)S(1)} %pad_add_fusion.where, bf16[1024,1024]{1,0:T(8,128)(2,1)S(1)} %get-tuple-element.63.gradient, bf16[2,1024,1024]{2,1,0:T(8,128)(2,1)S(1)} %get-tuple-element.60.bases, f32[1024,1024]{1,0:T(8,128)S(1)} %get-tuple-element.66.stat), custom_call_target="tpu_custom_call" | custom-call | flops 4294967296 | bytes 8388608 | tf_op jit(solution)/shard_map/pallas_call | solution.py:43
  68.6 1.3 %collective-permute-done.17.came = bf16[512,256]{1,0:T(8,128)(2,1)S(1)} collective-permute-done((bf16[512,256]{1,0:T(8,128)(2,1)S(1)}, bf16[512,256]{1,0:T(8,128)(2,1)S(1)}, u32[]{:S(2)}, u32[]{:S(2)}) %collective-permute-start.17) | collective-permute-done | bytes 262176 | tf_op jit(solution)/shard_map/ppermute | solution.py:376
  69.9 4.1 %shard_map.109 = (f32[1024,256]{1,0:T(8,128)S(1)}, bf16[512,256]{1,0:T(8,128)(2,1)S(1)}, bf16[512,256]{1,0:T(8,128)(2,1)S(1)}) custom-call(s32[4]{0:T(128)S(1)} %pad_add_fusion.where, bf16[1024,1024]{1,0:T(8,128)(2,1)S(1)} %get-tuple-element.63.gradient, bf16[2,1024,1024]{2,1,0:T(8,128)(2,1)S(1)} %get-tuple-element.60.bases, ...), custom_call_target="tpu_custom_call" | custom-call | flops 2147483648 | bytes 4194304 | tf_op jit(solution)/shard_map/pallas_call | solution.py:43
  74.1 0.1 collective-permute-start.20
  74.1 0.5 collective-permute-start.18
  74.6 0.2 collective-permute-start.19
  74.8 6.5 %shard_map.110 = (bf16[1024,1024]{1,0:T(8,128)(2,1)S(1)}, bf16[1024,1024]{1,0:T(8,128)(2,1)S(1)}, f32[256,1024]{1,0:T(8,128)S(1)}) custom-call(s32[4]{0:T(128)S(1)} %pad_add_fusion.where, bf16[1024,1024]{1,0:T(8,128)(2,1)S(1)} %get-tuple-element.73.start, bf16[1024,1024]{1,0:T(8,128)(2,1)S(1)} %get-tuple-element.74.start_turned), custom_call_target="tpu_custom_call" | custom-call | flops 5368709120 | bytes 4194304 | tf_op jit(solution)/shard_map/pallas_call | solution.py:43
  81.3 1.6 %collective-permute-done.18.came = bf16[512,256]{1,0:T(8,128)(2,1)S(1)} collective-permute-done((bf16[512,256]{1,0:T(8,128)(2,1)S(1)}, bf16[512,256]{1,0:T(8,128)(2,1)S(1)}, u32[]{:S(2)}, u32[]{:S(2)}) %collective-permute-start.18) | collective-permute-done | bytes 262176 | tf_op jit(solution)/shard_map/ppermute | solution.py:376
  82.9 0.0 collective-permute-done.19.kept_next
  82.9 0.0 collective-permute-done.20.new_next
  82.9 0.0 collective-permute-start.21
  82.9 0.5 collective-permute-start.22
  83.4 3.3 %shard_map.111 = (f32[256,1024]{1,0:T(8,128)S(1)}, f32[512,1024]{1,0:T(8,128)}, f32[512,1024]{1,0:T(8,128)}, f32[1024,512]{1,0:T(8,128)}) custom-call(s32[4]{0:T(128)S(1)} %pad_add_fusion.where, bf16[1024,1024]{1,0:T(8,128)(2,1)S(1)} %get-tuple-element.80.current, bf16[1024,1024]{1,0:T(8,128)(2,1)S(1)} %get-tuple-element.81.turned, ...), custom_call_target="tpu_custom_call" | custom-call | flops 1073741824 | bytes 4194304 | tf_op jit(solution)/shard_map/pallas_call | solution.py:499
  86.6 0.0 collective-permute-done.21.came_next
  86.7 0.1 collective-permute-start.23
  86.8 0.0 collective-permute-done.22.top_next
  86.8 2.9 %shard_map.112 = (bf16[512,1024]{1,0:T(8,128)(2,1)}, f32[512,1024]{1,0:T(8,128)}, f32[512,1024]{1,0:T(8,128)}) custom-call(s32[4]{0:T(128)S(1)} %pad_add_fusion.where, bf16[512,256]{1,0:T(8,128)(2,1)S(1)} %get-tuple-element.70.kept, bf16[512,256]{1,0:T(8,128)(2,1)S(1)} %collective-permute-done.18.came, ...), custom_call_target="tpu_custom_call", output_to_operand_aliasing={{1}: (8, {}), {2}: (9, {})} | custom-call | flops 1073741824 | bytes 4194304 | tf_op jit(solution)/shard_map/pallas_call | solution.py:510
  89.7 0.0 collective-permute-done.23.low
  89.7 1.5 %shard_map.113 = (f32[512,1024]{1,0:T(8,128)}, f32[512,1024]{1,0:T(8,128)}) custom-call(s32[4]{0:T(128)S(1)} %pad_add_fusion.where, f32[256,1024]{1,0:T(8,128)S(1)} %collective-permute-done.23.low, f32[512,1024]{1,0:T(8,128)} %get-tuple-element.92.left_in, f32[512,1024]{1,0:T(8,128)} %get-tuple-element.93.right_in), custom_call_target="tpu_custom_call", output_to_operand_aliasing={{0}: (2, {}), {1}: (3, {})} | custom-call | bytes 2097152 | tf_op jit(solution)/shard_map/pallas_call | solution.py:43
  (10 shorter events, 0.0 us)
Async XLA Ops:
  1.9 2.1 %collective-permute-start = (bf16[256,1024]{1,0:T(8,128)(2,1)S(1)}, bf16[256,1024]{1,0:T(8,128)(2,1)S(1)}, u32[]{:S(2)}, u32[]{:S(2)}) collective-permute-start(bf16[256,1024]{1,0:T(8,128)(2,1)S(1)} %get-tuple-element.96), channel_id=1, source_target_pairs={{0,2},{2,0},{4,6},{6,4},{8,10},{10,8},{12,14},{14,12},{16,18},{18,... | collective-permute-start | bytes 1572872 | tf_op jit(solution)/shard_map/ppermute | solution.py:373
  4.0 46.0 %copy-start = (f32[512,1024]{1,0:T(8,128)S(1)}, f32[512,1024]{1,0:T(8,128)}, u32[]{:S(2)}) copy-start(f32[512,1024]{1,0:T(8,128)} %left.3) | copy-start | bytes 6291460
  4.0 46.0 %copy-start.1 = (f32[512,1024]{1,0:T(8,128)S(1)}, f32[512,1024]{1,0:T(8,128)}, u32[]{:S(2)}) copy-start(f32[512,1024]{1,0:T(8,128)} %right.3) | copy-start | bytes 6291460
  4.0 46.0 %copy-start.2 = (f32[512,1024]{1,0:T(8,128)S(1)}, f32[512,1024]{1,0:T(8,128)}, u32[]{:S(2)}) copy-start(f32[512,1024]{1,0:T(8,128)} %stat_left.3) | copy-start | bytes 6291460
  4.0 46.1 %copy-start.3 = (f32[512,1024]{1,0:T(8,128)S(1)}, f32[512,1024]{1,0:T(8,128)}, u32[]{:S(2)}) copy-start(f32[512,1024]{1,0:T(8,128)} %stat_right.3) | copy-start | bytes 6291460
  6.8 34.1 %collective-permute-start.8 = (bf16[43,128,128]{2,1,0:T(8,128)(2,1)S(1)}, bf16[43,128,128]{2,1,0:T(8,128)(2,1)S(1)}, u32[]{:S(2)}, u32[]{:S(2)}) collective-permute-start(bf16[43,128,128]{2,1,0:T(8,128)(2,1)S(1)} %get-tuple-element.56), channel_id=1, source_target_pairs={{0,1},{1,0},{2,3},{3,2},{4,5},{5,4},{6,7},{7,6},{8,9},{9,8},{10,11... | collective-permute-start | bytes 4227080 | tf_op jit(solution)/shard_map/ppermute | solution.py:376
  9.7 8.1 %collective-permute-start.1 = (bf16[128,1024]{1,0:T(8,128)(2,1)S(1)}, bf16[128,1024]{1,0:T(8,128)(2,1)S(1)}, u32[]{:S(2)}, u32[]{:S(2)}) collective-permute-start(bf16[128,1024]{1,0:T(8,128)(2,1)S(1)} %get-tuple-element.51), channel_id=1, source_target_pairs={{0,4},{2,6},{4,0},{6,2},{8,12},{10,14},{12,8},{14,10},{16,20},{18,... | collective-permute-start | bytes 786440 | tf_op jit(solution)/shard_map/ppermute | solution.py:373
  18.4 5.0 %collective-permute-start.2 = (bf16[32,1024]{1,0:T(8,128)(2,1)S(1)}, bf16[32,1024]{1,0:T(8,128)(2,1)S(1)}, u32[]{:S(2)}, u32[]{:S(2)}) collective-permute-start(bf16[32,1024]{1,0:T(8,128)(2,1)S(1)} %get-tuple-element.53), channel_id=1, source_target_pairs={{0,8},{2,10},{4,12},{6,14},{8,0},{10,2},{12,4},{14,6},{16,24},{18,... | collective-permute-start | bytes 196616 | tf_op jit(solution)/shard_map/ppermute | solution.py:373
  20.0 6.6 %collective-permute-start.3 = (bf16[32,1024]{1,0:T(8,128)(2,1)S(1)}, bf16[32,1024]{1,0:T(8,128)(2,1)S(1)}, u32[]{:S(2)}, u32[]{:S(2)}) collective-permute-start(bf16[32,1024]{1,0:T(8,128)(2,1)S(1)} %get-tuple-element.54), channel_id=1, source_target_pairs={{0,16},{2,18},{4,20},{6,22},{8,24},{10,26},{12,28},{14,30},{16,0},... | collective-permute-start | bytes 196616 | tf_op jit(solution)/shard_map/ppermute | solution.py:373
  22.6 6.1 %collective-permute-start.4 = (bf16[32,1024]{1,0:T(8,128)(2,1)S(1)}, bf16[32,1024]{1,0:T(8,128)(2,1)S(1)}, u32[]{:S(2)}, u32[]{:S(2)}) collective-permute-start(bf16[32,1024]{1,0:T(8,128)(2,1)S(1)} %get-tuple-element.55), channel_id=1, source_target_pairs={{0,24},{2,26},{4,28},{6,30},{8,16},{10,18},{12,20},{14,22},{16,8},... | collective-permute-start | bytes 196616 | tf_op jit(solution)/shard_map/ppermute | solution.py:373
  28.7 6.2 %collective-permute-start.7 = (bf16[32,1024]{1,0:T(8,128)(2,1)S(1)}, bf16[32,1024]{1,0:T(8,128)(2,1)S(1)}, u32[]{:S(2)}, u32[]{:S(2)}) collective-permute-start(bf16[32,1024]{1,0:T(8,128)(2,1)S(1)} %shard_map.104.refs_0_), channel_id=1, source_target_pairs={{0,24},{2,26},{4,28},{6,30},{8,16},{10,18},{12,20},{14,22},{16,8},... | collective-permute-start | bytes 196616 | tf_op jit(solution)/shard_map/ppermute | solution.py:373
  29.8 6.4 %collective-permute-start.6 = (bf16[32,1024]{1,0:T(8,128)(2,1)S(1)}, bf16[32,1024]{1,0:T(8,128)(2,1)S(1)}, u32[]{:S(2)}, u32[]{:S(2)}) collective-permute-start(bf16[32,1024]{1,0:T(8,128)(2,1)S(1)} %shard_map.104.refs_0_), channel_id=1, source_target_pairs={{0,16},{2,18},{4,20},{6,22},{8,24},{10,26},{12,28},{14,30},{16,0},... | collective-permute-start | bytes 196616 | tf_op jit(solution)/shard_map/ppermute | solution.py:373
  30.3 6.0 %collective-permute-start.5 = (bf16[32,1024]{1,0:T(8,128)(2,1)S(1)}, bf16[32,1024]{1,0:T(8,128)(2,1)S(1)}, u32[]{:S(2)}, u32[]{:S(2)}) collective-permute-start(bf16[32,1024]{1,0:T(8,128)(2,1)S(1)} %shard_map.104.refs_0_), channel_id=1, source_target_pairs={{0,8},{2,10},{4,12},{6,14},{8,0},{10,2},{12,4},{14,6},{16,24},{18,... | collective-permute-start | bytes 196616 | tf_op jit(solution)/shard_map/ppermute | solution.py:373
  36.8 23.0 %copy-start.4 = (f32[512,1024]{1,0:T(8,128)S(1)}, f32[512,1024]{1,0:T(8,128)}, u32[]{:S(2)}) copy-start(f32[512,1024]{1,0:T(8,128)} %moment.1) | copy-start | bytes 6291460
  40.9 9.1 %collective-permute-start.11 = (bf16[43,128,128]{2,1,0:T(8,128)(2,1)S(1)}, bf16[43,128,128]{2,1,0:T(8,128)(2,1)S(1)}, u32[]{:S(2)}, u32[]{:S(2)}) collective-permute-start(bf16[43,128,128]{2,1,0:T(8,128)(2,1)S(1)} %collective-permute-done.8.mine), channel_id=1, source_target_pairs={{0,2},{2,0},{4,6},{6,4},{8,10},{10,8},{12,14},{14,12},{16,18},{18,... | collective-permute-start | bytes 4227080 | tf_op jit(solution)/shard_map/ppermute | solution.py:373
  40.9 9.1 %collective-permute-start.12 = (bf16[128,1024]{1,0:T(8,128)(2,1)S(1)}, bf16[128,1024]{1,0:T(8,128)(2,1)S(1)}, u32[]{:S(2)}, u32[]{:S(2)}) collective-permute-start(bf16[128,1024]{1,0:T(8,128)(2,1)S(1)} %shard_map.105.refs_0_), channel_id=1, source_target_pairs={{0,4},{2,6},{4,0},{6,2},{8,12},{10,14},{12,8},{14,10},{16,20},{18,... | collective-permute-start | bytes 786440 | tf_op jit(solution)/shard_map/ppermute | solution.py:373
  42.6 13.9 %collective-permute-start.10 = (bf16[128,1024]{1,0:T(8,128)(2,1)S(1)}, bf16[128,1024]{1,0:T(8,128)(2,1)S(1)}, u32[]{:S(2)}, u32[]{:S(2)}) collective-permute-start(bf16[128,1024]{1,0:T(8,128)(2,1)S(1)} %shard_map.105.refs_0_), channel_id=1, source_target_pairs={{0,5},{1,4},{2,7},{3,6},{4,1},{5,0},{6,3},{7,2},{8,13},{9,12},{10,... | collective-permute-start | bytes 786440 | tf_op jit(solution)/shard_map/ppermute | solution.py:380
  44.1 13.8 %collective-permute-start.9 = (bf16[128,1024]{1,0:T(8,128)(2,1)S(1)}, bf16[128,1024]{1,0:T(8,128)(2,1)S(1)}, u32[]{:S(2)}, u32[]{:S(2)}) collective-permute-start(bf16[128,1024]{1,0:T(8,128)(2,1)S(1)} %shard_map.105.refs_0_), channel_id=1, source_target_pairs={{0,1},{1,0},{2,3},{3,2},{4,5},{5,4},{6,7},{7,6},{8,9},{9,8},{10,11... | collective-permute-start | bytes 786440 | tf_op jit(solution)/shard_map/ppermute | solution.py:376
  44.4 14.0 %collective-permute-start.13 = (bf16[128,1024]{1,0:T(8,128)(2,1)S(1)}, bf16[128,1024]{1,0:T(8,128)(2,1)S(1)}, u32[]{:S(2)}, u32[]{:S(2)}) collective-permute-start(bf16[128,1024]{1,0:T(8,128)(2,1)S(1)} %shard_map.105.refs_0_), channel_id=1, source_target_pairs={{0,2},{2,0},{4,6},{6,4},{8,10},{10,8},{12,14},{14,12},{16,18},{18,... | collective-permute-start | bytes 786440 | tf_op jit(solution)/shard_map/ppermute | solution.py:373
  50.0 8.4 %collective-permute-start.14 = (bf16[128,1024]{1,0:T(8,128)(2,1)S(1)}, bf16[128,1024]{1,0:T(8,128)(2,1)S(1)}, u32[]{:S(2)}, u32[]{:S(2)}) collective-permute-start(bf16[128,1024]{1,0:T(8,128)(2,1)S(1)} %collective-permute-done.12.refs_1_), channel_id=1, source_target_pairs={{0,2},{2,0},{4,6},{6,4},{8,10},{10,8},{12,14},{14,12},{16,18},{18,... | collective-permute-start | bytes 786440 | tf_op jit(solution)/shard_map/ppermute | solution.py:373
  57.9 1.5 %collective-permute-start.15 = (bf16[128,1024]{1,0:T(8,128)(2,1)S(1)}, bf16[128,1024]{1,0:T(8,128)(2,1)S(1)}, u32[]{:S(2)}, u32[]{:S(2)}) collective-permute-start(bf16[128,1024]{1,0:T(8,128)(2,1)S(1)} %collective-permute-done.9.refs_4_), channel_id=1, source_target_pairs={{0,2},{2,0},{4,6},{6,4},{8,10},{10,8},{12,14},{14,12},{16,18},{18,... | collective-permute-start | bytes 786440 | tf_op jit(solution)/shard_map/ppermute | solution.py:373
  57.9 1.9 %collective-permute-start.16 = (bf16[128,1024]{1,0:T(8,128)(2,1)S(1)}, bf16[128,1024]{1,0:T(8,128)(2,1)S(1)}, u32[]{:S(2)}, u32[]{:S(2)}) collective-permute-start(bf16[128,1024]{1,0:T(8,128)(2,1)S(1)} %collective-permute-done.10.refs_5_), channel_id=1, source_target_pairs={{0,2},{2,0},{4,6},{6,4},{8,10},{10,8},{12,14},{14,12},{16,18},{18,... | collective-permute-start | bytes 786440 | tf_op jit(solution)/shard_map/ppermute | solution.py:373
  61.5 8.4 %collective-permute-start.17 = (bf16[512,256]{1,0:T(8,128)(2,1)S(1)}, bf16[512,256]{1,0:T(8,128)(2,1)S(1)}, u32[]{:S(2)}, u32[]{:S(2)}) collective-permute-start(bf16[512,256]{1,0:T(8,128)(2,1)S(1)} %get-tuple-element.68), channel_id=1, source_target_pairs={{0,1},{1,0},{2,3},{3,2},{4,5},{5,4},{6,7},{7,6},{8,9},{9,8},{10,11... | collective-permute-start | bytes 786440 | tf_op jit(solution)/shard_map/ppermute | solution.py:376
  61.9 8.0 %copy-start.5 = (f32[1024,512]{1,0:T(8,128)S(1)}, f32[1024,512]{1,0:T(8,128)}, u32[]{:S(2)}) copy-start(f32[1024,512]{1,0:T(8,128)} %second.1) | copy-start | bytes 6291460
  74.1 8.8 %collective-permute-start.20 = (f32[1024,256]{1,0:T(8,128)S(1)}, f32[1024,256]{1,0:T(8,128)S(1)}, u32[]{:S(2)}, u32[]{:S(2)}) collective-permute-start(f32[1024,256]{1,0:T(8,128)S(1)} %get-tuple-element.77.new), channel_id=1, source_target_pairs={{0,2},{2,0},{4,6},{6,4},{8,10},{10,8},{12,14},{14,12},{16,18},{18,... | collective-permute-start | bytes 3145736 | tf_op jit(solution)/shard_map/ppermute | solution.py:373
  74.1 8.7 %collective-permute-start.18 = (bf16[512,256]{1,0:T(8,128)(2,1)S(1)}, bf16[512,256]{1,0:T(8,128)(2,1)S(1)}, u32[]{:S(2)}, u32[]{:S(2)}) collective-permute-start(bf16[512,256]{1,0:T(8,128)(2,1)S(1)} %get-tuple-element.76), channel_id=1, source_target_pairs={{0,1},{1,0},{2,3},{3,2},{4,5},{5,4},{6,7},{7,6},{8,9},{9,8},{10,11... | collective-permute-start | bytes 786440 | tf_op jit(solution)/shard_map/ppermute | solution.py:376
  74.6 8.3 %collective-permute-start.19 = (bf16[512,256]{1,0:T(8,128)(2,1)S(1)}, bf16[512,256]{1,0:T(8,128)(2,1)S(1)}, u32[]{:S(2)}, u32[]{:S(2)}) collective-permute-start(bf16[512,256]{1,0:T(8,128)(2,1)S(1)} %get-tuple-element.70.kept), channel_id=1, source_target_pairs={{0,2},{2,0},{4,6},{6,4},{8,10},{10,8},{12,14},{14,12},{16,18},{18,... | collective-permute-start | bytes 786440 | tf_op jit(solution)/shard_map/ppermute | solution.py:373
  82.9 3.8 %collective-permute-start.21 = (bf16[512,256]{1,0:T(8,128)(2,1)S(1)}, bf16[512,256]{1,0:T(8,128)(2,1)S(1)}, u32[]{:S(2)}, u32[]{:S(2)}) collective-permute-start(bf16[512,256]{1,0:T(8,128)(2,1)S(1)} %collective-permute-done.18.came), channel_id=1, source_target_pairs={{0,2},{2,0},{4,6},{6,4},{8,10},{10,8},{12,14},{14,12},{16,18},{18,... | collective-permute-start | bytes 786440 | tf_op jit(solution)/shard_map/ppermute | solution.py:373
  82.9 3.9 %collective-permute-start.22 = (f32[256,1024]{1,0:T(8,128)S(1)}, f32[256,1024]{1,0:T(8,128)S(1)}, u32[]{:S(2)}, u32[]{:S(2)}) collective-permute-start(f32[256,1024]{1,0:T(8,128)S(1)} %get-tuple-element.82.top), channel_id=1, source_target_pairs={{0,2},{2,0},{4,6},{6,4},{8,10},{10,8},{12,14},{14,12},{16,18},{18,... | collective-permute-start | bytes 3145736 | tf_op jit(solution)/shard_map/ppermute | solution.py:373
  86.7 3.1 %collective-permute-start.23 = (f32[256,1024]{1,0:T(8,128)S(1)}, f32[256,1024]{1,0:T(8,128)S(1)}, u32[]{:S(2)}, u32[]{:S(2)}) collective-permute-start(f32[256,1024]{1,0:T(8,128)S(1)} %get-tuple-element.87.low), channel_id=1, source_target_pairs={{0,2},{2,0},{4,6},{6,4},{8,10},{10,8},{12,14},{14,12},{16,18},{18,... | collective-permute-start | bytes 3145736 | tf_op jit(solution)/shard_map/ppermute | solution.py:373

commit v8 on v7

--- a/solution.py
+++ b/solution.py
@@ -200,11 +200,26 @@
     full[there, here] = full[here, there].T
 
 
-def moment_kernel(where, moment, bases, *refs):
-    parts, (gradient, ours, others, sem) = refs[:-4], refs[-4:]
+def moment_kernel(where, moment, bases, own, over_x, next_own, next_over_x, ours, others, half):
     position, core, x = where[0], where[1], where[2]
-    rows = moment.shape[0]
-    step = rows // 2
+    size = own.shape[0]
+    step = ours.shape[1]
+    for place, part in enumerate((own, over_x, next_own, next_over_x)):
+        here = tile((core ^ (place // 2)) * 2 + (x ^ (place % 2)), size)
+        half[here] = (
+            BETA_ONE * moment[here] + (1.0 - BETA_ONE) * part[...].astype(FULL)
+        ).astype(HALF)
+    there, here = tile((1 - position) * 2 + core, step), tile(position * 2 + core, step)
+    others[...] = matmul(half[...], bases[1 - core, :, there]).astype(HALF)
+    ours[...] = matmul(half[...], bases[1 - core, :, here]).astype(HALF)
+
+
+def statistic_kernel(where, bases, turned, stat, second, *refs):
+    parts, (half, new, pair, sem) = refs[:-4], refs[-4:]
+    position, core, x = where[0], where[1], where[2]
+    width = half.shape[0]
+    step = new.shape[1]
+    gradient = pair.at[core]
     copies = []
     for place, part in enumerate(parts):
         size = part.shape[0]
@@ -213,27 +228,25 @@
         )
         copies.append(pltpu.make_async_copy(part, gradient.at[tile(block, size)], sem.at[place]))
     run_all(copies)
-    half = (
-        BETA_ONE * moment[...] + (1.0 - BETA_ONE) * gradient[tile(position, rows)].astype(FULL)
-    ).astype(HALF)
-    there, here = tile((1 - position) * 2 + core, step), tile(position * 2 + core, step)
-    others[...] = matmul(half, bases[1 - core, :, there]).astype(HALF)
-    ours[...] = matmul(half, bases[1 - core, :, here]).astype(HALF)
-
-
-def adam_kernel(where, gradient, bases, turned, mine, came, second, new, kept, sent):
-    width = gradient.shape[0]
-    rows, step = mine.shape
+    for here in quarters(width):
+        pair[1 - core, :, here] = gradient[here].T
+    block = matmul(gradient[...], bases[1 - core, :, tile(position * 2 + core, step)])
+    for here in quarters(width):
+        grads = matmul(pair[0], pair[1, :, here])
+        half[:, here] = (BETA_STAT * stat[:, here] + (1.0 - BETA_STAT) * grads).astype(HALF)
+    grad_rot = matmul(turned[...], block.astype(HALF)) * (1.0 / width)
+    new[...] = BETA_TWO * second[:, tile(core, step)] + (1.0 - BETA_TWO) * grad_rot * grad_rot
+
+
+def adam_kernel(where, bases, turned, mine, came, new, kept, sent):
+    width = new.shape[0]
+    rows = mine.shape[0]
     position, core = where[0], where[1]
     here, there = tile(position, rows), tile(1 - position, rows)
-    block = matmul(gradient[...], bases[1 - core, :, tile(position * 2 + core, step)])
-    grad_rot = matmul(turned[...], block.astype(HALF)) * (1.0 / width)
     moment_rot = (
         matmul(turned[:, here], mine[...]) + matmul(turned[:, there], came[...])
     ) * (1.0 / width)
-    value = BETA_TWO * second[:, tile(core, step)] + (1.0 - BETA_TWO) * grad_rot * grad_rot
-    new[...] = value
-    scaled = (moment_rot / (jnp.sqrt(value) + EPSILON)).astype(HALF)
+    scaled = (moment_rot / (jnp.sqrt(new[...]) + EPSILON)).astype(HALF)
     sent[...] = matmul(bases[core, there], scaled).astype(HALF)
     kept[...] = matmul(bases[core, here], scaled).astype(HALF)
 
@@ -296,24 +309,6 @@
     return [slice(i * step, (i + 1) * step) for i in range(4)]
 
 
-def power_kernel(where, gradient, bases, stat, start, turned, pair, half):
-    width = gradient.shape[0]
-    core = where[1]
-    for here in quarters(width):
-        value = gradient[here]
-        pair[core, here] = value
-        pair[1 - core, :, here] = value.T
-    for here in quarters(width):
-        grads = matmul(pair[0], pair[1, :, here])
-        half[:, here] = (BETA_STAT * stat[:, here] + (1.0 - BETA_STAT) * grads).astype(HALF)
-    for here in quarters(width):
-        product = matmul(half[...], bases[0, :, here])
-        square = jnp.sum(product * product, axis=0, keepdims=True) * (1.0 / width)
-        value = (product * lax.rsqrt(square + NORM_EPS)).astype(HALF)
-        start[:, here] = value
-        turned[here] = value.T
-
-
 def improved(current, turned, kept, gram, result, result_turned):
     size, width = result.shape
     for here in quarters(width):
@@ -327,32 +322,43 @@
             result_turned[here] = value.T
 
 
-def refresh_kernel(where, start, start_turned, current, turned, out, *scratch):
-    width = start.shape[0]
+def refresh_kernel(
+    where, stat, bases, new, current, turned, out, second_new, start, start_turned, gram, *scratch
+):
+    width = stat.shape[0]
     rows = width // 2
-    gram, between = scratch[0], scratch[1:]
+    between, sem = scratch[:-1], scratch[-1]
+    copy = pltpu.make_async_copy(new, second_new.at[:, tile(where[1], new.shape[1])], sem)
+    copy.start()
+    for here in quarters(width):
+        product = matmul(stat[...], bases[0, :, here])
+        square = jnp.sum(product * product, axis=0, keepdims=True) * (1.0 / width)
+        value = (product * lax.rsqrt(square + NORM_EPS)).astype(HALF)
+        start[:, here] = value
+        start_turned[here] = value.T
     source, source_turned = start, start_turned
     for iteration in range(NS_ITERS - 1):
-        last = iteration + 2 == NS_ITERS
-        if last:
+        if iteration + 2 == NS_ITERS:
             result, result_turned = current, turned
         else:
             result, result_turned = between[0].at[iteration % 2], between[1].at[iteration % 2]
         improved(source, source_turned, slice(0, width), gram, result, result_turned)
         source, source_turned = result, result_turned
     improved(current, turned, tile(where[0] * 2, rows // 2), gram, out, None)
+    copy.wait()
 
 
 def last_kernel(
-    where, current, turned, top, new, new_next, out, left, right, second_new, gram, sem
+    where, current, turned, top, new_next, second_in, out, left, right, second_new, gram, sem
 ):
     core = where[1]
-    step = new.shape[1]
-    copies = [write_part(core, 0, 0, top, left, right, sem.at[0])]
-    for i, (value, place) in enumerate(((new, core), (new_next, 1 - core))):
-        copy = pltpu.make_async_copy(value, second_new.at[:, tile(place, step)], sem.at[i + 1])
-        copy.start()
-        copies.append(copy)
+    copies = [
+        write_part(core, 0, 0, top, left, right, sem.at[0]),
+        pltpu.make_async_copy(
+            new_next, second_new.at[:, tile(1 - core, new_next.shape[1])], sem.at[1]
+        ),
+    ]
+    copies[1].start()
     improved(current, turned, tile(where[0] * 2 + 1, out.shape[0]), gram, out, None)
     for copy in copies:
         copy.wait()
@@ -445,51 +451,54 @@
         [pltpu.SemaphoreType.DMA(())],
         moved=2**24,
     )
-    parts[2], parts[3], bases = lax.optimization_barrier((parts[2], parts[3], bases))
-    swapped = [dp_swap(value, 1) for value in parts]
-    ordered = parts[:2] + swapped[:2] + parts[2:] + swapped[2:]
-    gradient, moment_mine, moment_sent = call(
+    near = parts[:2] + [dp_swap(value, 1) for value in parts[:2]]
+    moment_mine, moment_sent = call(
         moment_kernel,
-        [square] + [shaped((rows, half), HALF)] * 2,
-        (where, moment, bases, *ordered),
-        [SMEM, VMEM, VMEM] + [ANY] * 8,
-        [pltpu.SemaphoreType.DMA((8,))],
+        [shaped((rows, half), HALF)] * 2,
+        (where, moment, bases, *near),
+        [SMEM] + [VMEM] * 6,
+        [pltpu.VMEM((rows, width), HALF)],
         flops=unit // 4,
         moved=2**22,
     )
     moment_came = shard_swap(moment_sent)
-    start, start_turned = call(
-        power_kernel,
-        [square] * 2,
-        (where, gradient, bases, stat),
-        [SMEM] + [VMEM] * 3,
-        [pltpu.VMEM((2, width, width), HALF), pltpu.VMEM((width, width), HALF)],
-        flops=2 * unit,
+    far = list(lax.optimization_barrier((parts[2], parts[3], bases)))[:2]
+    far += [dp_swap(value, 1) for value in far]
+    stat, new = call(
+        statistic_kernel,
+        [square, shaped((width, half), FULL)],
+        (where, bases, left_turned, stat, second, *near, *far),
+        [SMEM] + [VMEM] * 4 + [ANY] * 8,
+        [pltpu.VMEM((2, width, width), HALF), pltpu.SemaphoreType.DMA((8,))],
+        flops=3 * unit // 2,
         moved=2**23,
     )
-    start, moment_came = lax.optimization_barrier((start, moment_came))
-    new, back_kept, back_sent = call(
+    new_next = dp_swap(new, 1)
+    stat, moment_came = lax.optimization_barrier((stat, moment_came))
+    back_kept, back_sent = call(
         adam_kernel,
-        [shaped((width, half), FULL)] + [shaped((rows, half), HALF)] * 2,
-        (where, gradient, bases, left_turned, moment_mine, moment_came, second),
-        [SMEM] + [VMEM] * 6,
-        flops=unit,
+        [shaped((rows, half), HALF)] * 2,
+        (where, bases, left_turned, moment_mine, moment_came, new),
+        [SMEM] + [VMEM] * 5,
+        flops=unit // 2,
         moved=2**22,
     )
-    start, back_sent = lax.optimization_barrier((start, back_sent))
+    stat, back_sent = lax.optimization_barrier((stat, back_sent))
     back_came = shard_swap(back_sent)
-    new_next = dp_swap(new, 1)
     back_kept_next = dp_swap(back_kept, 1)
-    current, current_turned, top = call(
+    current, current_turned, top, second_new = pl.pallas_call(
         refresh_kernel,
-        [square] * 2 + [shaped((half, width), FULL)],
-        (where, start, start_turned),
-        [SMEM] + [VMEM] * 2,
-        [pltpu.VMEM((width, width), HALF)]
-        + [pltpu.VMEM((2, width, width), HALF)] * (2 if NS_ITERS > 2 else 0),
-        flops=5 * unit // 2,
-        moved=2**22,
-    )
+        out_shape=[square, square, shaped((half, width), FULL), shaped((width, rows), FULL)],
+        in_specs=[SMEM] + [VMEM] * 2 + [ANY],
+        out_specs=[VMEM] * 3 + [ANY],
+        scratch_shapes=[pltpu.VMEM((width, width), HALF)] * 3
+        + [pltpu.VMEM((2, width, width), HALF)] * (2 if NS_ITERS > 2 else 0)
+        + [pltpu.SemaphoreType.DMA(())],
+        compiler_params=pltpu.CompilerParams(vmem_limit_bytes=24 * 2**20),
+        cost_estimate=pl.CostEstimate(
+            flops=7 * unit // 2, bytes_accessed=2**23, transcendentals=0
+        ),
+    )(where, stat, bases, new)
     top_next = dp_swap(top, 1)
     current, back_came, back_kept_next, new_next = lax.optimization_barrier(
         (current, back_came, back_kept_next, new_next)
@@ -501,10 +510,11 @@
         out_shape=[shaped((half, width), FULL), side, side, shaped((width, rows), FULL)],
         in_specs=[SMEM] + [VMEM] * 2 + [ANY] * 3,
         out_specs=[VMEM] + [ANY] * 3,
-        scratch_shapes=[pltpu.VMEM((half, width), HALF), pltpu.SemaphoreType.DMA((3,))],
+        scratch_shapes=[pltpu.VMEM((half, width), HALF), pltpu.SemaphoreType.DMA((2,))],
+        input_output_aliases={5: 3},
         compiler_params=pltpu.CompilerParams(vmem_limit_bytes=24 * 2**20),
         cost_estimate=pl.CostEstimate(flops=unit // 2, bytes_accessed=2**22, transcendentals=0),
-    )(where, current, current_turned, top, new, new_next)
+    )(where, current, current_turned, top, new_next, second_new)
     low, back_came_next = lax.optimization_barrier((low, back_came_next))
     low_next = dp_swap(low, 1)
     update, left_new, right_new = pl.pallas_call(

time: 91.6 us -> 90.6 us (0.989)
  waiting for transfers between devices: 35.6 us -> 31.3 us
  starting transfers between devices: 19.6 us -> 22.3 us
    pallas_call x0 -> x1, Pallas kernels: none -> 9.88 us  [fast_body(): pl.pallas_call(refresh_kernel, out_shape=[square, square, shaped((half, w...]
    pallas_call x10 -> x9, Pallas kernels: 27.7 us -> 18.8 us  [call(): pl.pallas_call(kernel, out_shape=outs, in_specs=specs, out_specs=[space]...]
    ppermute x4, starting transfers between devices: 4.1 us -> 7.65 us  [shard_swap(): return lax.ppermute(value, 'shard', [(0, 1), (1, 0)])]
    ppermute x1, waiting for transfers between devices: 3.26 us -> 0.01 us  [cross_swap(): return lax.ppermute(value, ('dp', 'shard'), pairs)]
    ppermute x1, starting transfers between devices: 1.49 us -> 0.26 us  [cross_swap(): return lax.ppermute(value, ('dp', 'shard'), pairs)]
    ppermute x19, waiting for transfers between devices: 24 us -> 23 us  [dp_swap(): return lax.ppermute(value, 'dp', [(i, i ^ distance) for i in range(16)])]
  transfers between devices with their start and end apart: 24 -> 24, of which waited for: 15 -> 11; matrix products, arithmetic and copies ran while one was open for 0% -> 0% of each run, Pallas kernels for 26% -> 33%
where the time goes in v8:
time: 90.6 us; the launch traced here: 90.5 us
  Pallas kernels  34.5 us (38%)
  waiting for transfers between devices  31.3 us (35%)
  starting transfers between devices  22.3 us (25%)
  local copies, waits for them, and re-layouts  1.3 us (1%)
  between operations  1.01 us (1%)
    ppermute x19, waiting for transfers between devices, dp_swap(): return lax.ppermute(value, 'dp', [(i, i ^ distance) for i in range(16)])  23 us
    pallas_call x9, Pallas kernels, call(): pl.pallas_call(kernel, out_shape=outs, in_specs=specs, out_specs=[space]...  18.8 us
    ppermute x19, starting transfers between devices, dp_swap(): return lax.ppermute(value, 'dp', [(i, i ^ distance) for i in range(16)])  14.4 us
    pallas_call x1, Pallas kernels, fast_body(): pl.pallas_call(refresh_kernel, out_shape=[square, square, shaped((half, w...  9.88 us
    ppermute x4, waiting for transfers between devices, shard_swap(): return lax.ppermute(value, 'shard', [(0, 1), (1, 0)])  8.33 us
    ppermute x4, starting transfers between devices, shard_swap(): return lax.ppermute(value, 'shard', [(0, 1), (1, 0)])  7.65 us
    pallas_call x1, Pallas kernels, fast_body(): pl.pallas_call(update_kernel, out_shape=[shaped((rows, width), HALF), sid...  2.92 us
    pallas_call x1, Pallas kernels, fast_body(): pl.pallas_call(last_kernel, out_shape=[shaped((half, width), FULL), side,...  2.91 us
  transfers between devices with their start and end apart: 24, of which 11 were waited for; matrix products, arithmetic and copies ran while one was open for 0% of the time, Pallas kernels for 33%

profile of v8, /device:TPU:0, one launch (start us, length us, event | category | flops | bytes accessed | tf_op | source)
XLA Modules:
  0.0 90.5 jit_solution(3856501513319074970)
XLA Ops:
  0.6 1.3 %dynamic-slice_bitcast_fusion = (bf16[256,1024]{1,0:T(8,128)(2,1)S(1)}, bf16[256,1024]{1,0:T(8,128)(2,1)S(1)}) fusion(bf16[1,512,1024]{2,1,0:T(8,128)(2,1)} %param.7, s32[]{:T(128)S(6)} %select_n.7, s32[]{:T(128)S(6)} %select_n.6), kind=kLoop, calls=%fused_computation | loop fusion | bytes 2097160 | tf_op jit(solution)/shard_map/dynamic_slice | solution.py:388
  1.9 0.5 collective-permute-start
  2.4 0.1 pad_add_fusion.where
  2.5 1.5 %collective-permute-done.came = bf16[256,1024]{1,0:T(8,128)(2,1)S(1)} collective-permute-done((bf16[256,1024]{1,0:T(8,128)(2,1)S(1)}, bf16[256,1024]{1,0:T(8,128)(2,1)S(1)}, u32[]{:S(2)}, u32[]{:S(2)}) %collective-permute-start) | collective-permute-done | bytes 524320 | tf_op jit(solution)/shard_map/ppermute | solution.py:379
  4.0 2.8 %shard_map.102 = (bf16[43,128,128]{2,1,0:T(8,128)(2,1)S(1)}, f32[128,1024]{1,0:T(8,128)S(1)}, bf16[128,1024]{1,0:T(8,128)(2,1)S(1)}) custom-call(s32[4]{0:T(128)S(1)} %pad_add_fusion.where, bf16[256,1024]{1,0:T(8,128)(2,1)S(1)} %get-tuple-element.93.raw, bf16[256,1024]{1,0:T(8,128)(2,1)S(1)} %collective-permute-done.came, f32[512,1024]{1,0:T(8,128)} %left.3, ...), custom_call_target="tpu_custom_call" | custom-call | bytes 4194304 | tf_op jit(solution)/shard_map/pallas_call | solution.py:43
  6.8 3.0 %collective-permute-start.8 = (bf16[43,128,128]{2,1,0:T(8,128)(2,1)S(1)}, bf16[43,128,128]{2,1,0:T(8,128)(2,1)S(1)}, u32[]{:S(2)}, u32[]{:S(2)}) collective-permute-start(bf16[43,128,128]{2,1,0:T(8,128)(2,1)S(1)} %get-tuple-element.54), channel_id=1, source_target_pairs={{0,1},{1,0},{2,3},{3,2},{4,5},{5,4},{6,7},{7,6},{8,9},{9,8},{10,11... | collective-permute-start | bytes 4227080 | tf_op jit(solution)/shard_map/ppermute | solution.py:382
  9.7 1.5 %collective-permute-start.1 = (bf16[128,1024]{1,0:T(8,128)(2,1)S(1)}, bf16[128,1024]{1,0:T(8,128)(2,1)S(1)}, u32[]{:S(2)}, u32[]{:S(2)}) collective-permute-start(bf16[128,1024]{1,0:T(8,128)(2,1)S(1)} %get-tuple-element.49), channel_id=1, source_target_pairs={{0,4},{2,6},{4,0},{6,2},{8,12},{10,14},{12,8},{14,10},{16,20},{18,... | collective-permute-start | bytes 786440 | tf_op jit(solution)/shard_map/ppermute | solution.py:379
  11.2 6.6 %collective-permute-done.1.came = bf16[128,1024]{1,0:T(8,128)(2,1)S(1)} collective-permute-done((bf16[128,1024]{1,0:T(8,128)(2,1)S(1)}, bf16[128,1024]{1,0:T(8,128)(2,1)S(1)}, u32[]{:S(2)}, u32[]{:S(2)}) %collective-permute-start.1) | collective-permute-done | bytes 262176 | tf_op jit(solution)/shard_map/ppermute | solution.py:379
  17.8 0.6 shard_map.103
  18.4 1.6 %collective-permute-start.2 = (bf16[32,1024]{1,0:T(8,128)(2,1)S(1)}, bf16[32,1024]{1,0:T(8,128)(2,1)S(1)}, u32[]{:S(2)}, u32[]{:S(2)}) collective-permute-start(bf16[32,1024]{1,0:T(8,128)(2,1)S(1)} %get-tuple-element.51), channel_id=1, source_target_pairs={{0,8},{2,10},{4,12},{6,14},{8,0},{10,2},{12,4},{14,6},{16,24},{18,... | collective-permute-start | bytes 196616 | tf_op jit(solution)/shard_map/ppermute | solution.py:379
  20.0 2.6 %collective-permute-start.3 = (bf16[32,1024]{1,0:T(8,128)(2,1)S(1)}, bf16[32,1024]{1,0:T(8,128)(2,1)S(1)}, u32[]{:S(2)}, u32[]{:S(2)}) collective-permute-start(bf16[32,1024]{1,0:T(8,128)(2,1)S(1)} %get-tuple-element.52), channel_id=1, source_target_pairs={{0,16},{2,18},{4,20},{6,22},{8,24},{10,26},{12,28},{14,30},{16,0},... | collective-permute-start | bytes 196616 | tf_op jit(solution)/shard_map/ppermute | solution.py:379
  22.6 0.2 collective-permute-start.4
  22.8 0.5 collective-permute-done.2.one
  23.3 3.2 %collective-permute-done.3.two = bf16[32,1024]{1,0:T(8,128)(2,1)S(1)} collective-permute-done((bf16[32,1024]{1,0:T(8,128)(2,1)S(1)}, bf16[32,1024]{1,0:T(8,128)(2,1)S(1)}, u32[]{:S(2)}, u32[]{:S(2)}) %collective-permute-start.3) | collective-permute-done | bytes 65568 | tf_op jit(solution)/shard_map/ppermute | solution.py:379
  26.6 2.5 %collective-permute-done.4.three = bf16[32,1024]{1,0:T(8,128)(2,1)S(1)} collective-permute-done((bf16[32,1024]{1,0:T(8,128)(2,1)S(1)}, bf16[32,1024]{1,0:T(8,128)(2,1)S(1)}, u32[]{:S(2)}, u32[]{:S(2)}) %collective-permute-start.4) | collective-permute-done | bytes 65568 | tf_op jit(solution)/shard_map/ppermute | solution.py:379
  29.1 0.1 collective-permute-start.5
  29.2 1.0 %collective-permute-start.6 = (bf16[32,1024]{1,0:T(8,128)(2,1)S(1)}, bf16[32,1024]{1,0:T(8,128)(2,1)S(1)}, u32[]{:S(2)}, u32[]{:S(2)}) collective-permute-start(bf16[32,1024]{1,0:T(8,128)(2,1)S(1)} %shard_map.104.refs_0_), channel_id=1, source_target_pairs={{0,16},{2,18},{4,20},{6,22},{8,24},{10,26},{12,28},{14,30},{16,0},... | collective-permute-start | bytes 196616 | tf_op jit(solution)/shard_map/ppermute | solution.py:379
  30.3 3.3 %collective-permute-start.7 = (bf16[32,1024]{1,0:T(8,128)(2,1)S(1)}, bf16[32,1024]{1,0:T(8,128)(2,1)S(1)}, u32[]{:S(2)}, u32[]{:S(2)}) collective-permute-start(bf16[32,1024]{1,0:T(8,128)(2,1)S(1)} %shard_map.104.refs_0_), channel_id=1, source_target_pairs={{0,24},{2,26},{4,28},{6,30},{8,16},{10,18},{12,20},{14,22},{16,8},... | collective-permute-start | bytes 196616 | tf_op jit(solution)/shard_map/ppermute | solution.py:379
  33.6 0.0 collective-permute-done.5.refs_1_
  33.6 0.9 collective-permute-done.6.refs_2_
  34.5 2.2 %collective-permute-done.7.refs_3_ = bf16[32,1024]{1,0:T(8,128)(2,1)S(1)} collective-permute-done((bf16[32,1024]{1,0:T(8,128)(2,1)S(1)}, bf16[32,1024]{1,0:T(8,128)(2,1)S(1)}, u32[]{:S(2)}, u32[]{:S(2)}) %collective-permute-start.7) | collective-permute-done | bytes 65568 | tf_op jit(solution)/shard_map/ppermute | solution.py:379
  36.6 0.6 shard_map.105.own.refs_0_
  37.2 0.0 copy-start.4
  37.2 3.7 %collective-permute-done.8.mine = bf16[43,128,128]{2,1,0:T(8,128)(2,1)S(1)} collective-permute-done((bf16[43,128,128]{2,1,0:T(8,128)(2,1)S(1)}, bf16[43,128,128]{2,1,0:T(8,128)(2,1)S(1)}, u32[]{:S(2)}, u32[]{:S(2)}) %collective-permute-start.8) | collective-permute-done | bytes 1409056 | tf_op jit(solution)/shard_map/ppermute | solution.py:382
  40.9 0.0 collective-permute-start.9
  40.9 1.7 %collective-permute-start.10 = (bf16[128,1024]{1,0:T(8,128)(2,1)S(1)}, bf16[128,1024]{1,0:T(8,128)(2,1)S(1)}, u32[]{:S(2)}, u32[]{:S(2)}) collective-permute-start(bf16[128,1024]{1,0:T(8,128)(2,1)S(1)} %shard_map.105.own.refs_0_), channel_id=1, source_target_pairs={{0,4},{2,6},{4,0},{6,2},{8,12},{10,14},{12,8},{14,10},{16,20},{18,... | collective-permute-start | bytes 786440 | tf_op jit(solution)/shard_map/ppermute | solution.py:379
  42.6 1.5 %collective-permute-start.13 = (bf16[128,1024]{1,0:T(8,128)(2,1)S(1)}, bf16[128,1024]{1,0:T(8,128)(2,1)S(1)}, u32[]{:S(2)}, u32[]{:S(2)}) collective-permute-start(bf16[128,1024]{1,0:T(8,128)(2,1)S(1)} %shard_map.105.own.refs_0_), channel_id=1, source_target_pairs={{0,1},{1,0},{2,3},{3,2},{4,5},{5,4},{6,7},{7,6},{8,9},{9,8},{10,11... | collective-permute-start | bytes 786440 | tf_op jit(solution)/shard_map/ppermute | solution.py:382
  44.1 0.3 collective-permute-start.14
  44.4 0.0 collective-permute-start.11
  44.4 5.6 %collective-permute-done.10.over_x.refs_1_ = bf16[128,1024]{1,0:T(8,128)(2,1)S(1)} collective-permute-done((bf16[128,1024]{1,0:T(8,128)(2,1)S(1)}, bf16[128,1024]{1,0:T(8,128)(2,1)S(1)}, u32[]{:S(2)}, u32[]{:S(2)}) %collective-permute-start.10) | collective-permute-done | bytes 262176 | tf_op jit(solution)/shard_map/ppermute | solution.py:379
  50.0 0.0 collective-permute-start.12
  50.0 0.0 collective-permute-done.9.theirs
  50.0 0.0 copy-done
  50.0 3.2 %shard_map.106 = (bf16[2,1024,1024]{2,1,0:T(8,128)(2,1)S(1)}, bf16[1024,1024]{1,0:T(8,128)(2,1)S(1)}, bf16[1024,1024]{1,0:T(8,128)(2,1)S(1)}, f32[1024,1024]{1,0:T(8,128)S(1)}) custom-call(s32[4]{0:T(128)S(1)} %pad_add_fusion.where, f32[512,1024]{1,0:T(8,128)S(1)} %copy-done, f32[512,1024]{1,0:T(8,128)S(1)} %copy-done.1, ...), custom_call_target="tpu_custom_call" | custom-call | bytes 16777216 | tf_op jit(solution)/shard_map/pallas_call | solution.py:43
  53.2 3.4 %collective-permute-done.13.refs_4_ = bf16[128,1024]{1,0:T(8,128)(2,1)S(1)} collective-permute-done((bf16[128,1024]{1,0:T(8,128)(2,1)S(1)}, bf16[128,1024]{1,0:T(8,128)(2,1)S(1)}, u32[]{:S(2)}, u32[]{:S(2)}) %collective-permute-start.13) | collective-permute-done | bytes 262176 | tf_op jit(solution)/shard_map/ppermute | solution.py:382
  56.7 0.0 collective-permute-done.14.refs_5_
  56.7 0.0 collective-permute-start.15
  56.7 0.5 collective-permute-start.16
  57.2 0.0 collective-permute-done.11.next_own.refs_2_
  57.2 0.0 collective-permute-done.12.next_over_x.refs_3_
  57.2 0.0 copy-done.4
  57.2 1.9 %shard_map.107 = (bf16[512,256]{1,0:T(8,128)(2,1)S(1)}, bf16[512,256]{1,0:T(8,128)(2,1)S(1)}) custom-call(s32[4]{0:T(128)S(1)} %pad_add_fusion.where, f32[512,1024]{1,0:T(8,128)S(1)} %copy-done.4, bf16[2,1024,1024]{2,1,0:T(8,128)(2,1)S(1)} %get-tuple-element.56.bases, bf16[128,1024]{1,0:T(8,128)(2,1)S(1)} %shard_map.105.own.refs_0_, ...), custom_call_target="tpu_custom_call" | custom-call | flops 536870912 | bytes 4194304 | tf_op jit(solution)/shard_map/pallas_call | solution.py:43
  59.1 1.6 %collective-permute-start.17 = (bf16[512,256]{1,0:T(8,128)(2,1)S(1)}, bf16[512,256]{1,0:T(8,128)(2,1)S(1)}, u32[]{:S(2)}, u32[]{:S(2)}) collective-permute-start(bf16[512,256]{1,0:T(8,128)(2,1)S(1)} %get-tuple-element.64), channel_id=1, source_target_pairs={{0,1},{1,0},{2,3},{3,2},{4,5},{5,4},{6,7},{7,6},{8,9},{9,8},{10,11... | collective-permute-start | bytes 786440 | tf_op jit(solution)/shard_map/ppermute | solution.py:382
  60.6 0.0 collective-permute-done.15.refs_6_
  60.7 0.0 collective-permute-done.16.refs_7_
  60.7 5.4 %shard_map.108 = (bf16[1024,1024]{1,0:T(8,128)(2,1)S(1)}, f32[1024,256]{1,0:T(8,128)S(1)}) custom-call(s32[4]{0:T(128)S(1)} %pad_add_fusion.where, bf16[2,1024,1024]{2,1,0:T(8,128)(2,1)S(1)} %get-tuple-element.56.bases, bf16[1024,1024]{1,0:T(8,128)(2,1)S(1)} %get-tuple-element.57.turned, f32[1024,1024]{1,0:T(8,128)S(1)} %get-tuple-element.60.stat, ...), custom_call_target="tpu_custom_call" | custom-call | flops 3221225472 | bytes 8388608 | tf_op jit(solution)/shard_map/pallas_call | solution.py:43
  66.1 0.1 collective-permute-start.20
  66.2 1.2 %collective-permute-done.17.came = bf16[512,256]{1,0:T(8,128)(2,1)S(1)} collective-permute-done((bf16[512,256]{1,0:T(8,128)(2,1)S(1)}, bf16[512,256]{1,0:T(8,128)(2,1)S(1)}, u32[]{:S(2)}, u32[]{:S(2)}) %collective-permute-start.17) | collective-permute-done | bytes 262176 | tf_op jit(solution)/shard_map/ppermute | solution.py:382
  67.4 2.8 %shard_map.109 = (bf16[512,256]{1,0:T(8,128)(2,1)S(1)}, bf16[512,256]{1,0:T(8,128)(2,1)S(1)}) custom-call(s32[4]{0:T(128)S(1)} %pad_add_fusion.where, bf16[2,1024,1024]{2,1,0:T(8,128)(2,1)S(1)} %get-tuple-element.56.bases, bf16[1024,1024]{1,0:T(8,128)(2,1)S(1)} %get-tuple-element.57.turned, bf16[512,256]{1,0:T(8,128)(2,1)S(1)} %get-tuple-element.59.mine, ...), custom_call_target="tpu_custom_call" | custom-call | flops 1073741824 | bytes 4194304 | tf_op jit(solution)/shard_map/pallas_call | solution.py:43
  70.3 1.6 %collective-permute-start.18 = (bf16[512,256]{1,0:T(8,128)(2,1)S(1)}, bf16[512,256]{1,0:T(8,128)(2,1)S(1)}, u32[]{:S(2)}, u32[]{:S(2)}) collective-permute-start(bf16[512,256]{1,0:T(8,128)(2,1)S(1)} %get-tuple-element.72), channel_id=1, source_target_pairs={{0,1},{1,0},{2,3},{3,2},{4,5},{5,4},{6,7},{7,6},{8,9},{9,8},{10,11... | collective-permute-start | bytes 786440 | tf_op jit(solution)/shard_map/ppermute | solution.py:382
  71.9 0.0 collective-permute-start.19
  71.9 9.9 %shard_map.110 = (bf16[1024,1024]{1,0:T(8,128)(2,1)S(1)}, bf16[1024,1024]{1,0:T(8,128)(2,1)S(1)}, f32[256,1024]{1,0:T(8,128)S(1)}, f32[1024,512]{1,0:T(8,128)}) custom-call(s32[4]{0:T(128)S(1)} %pad_add_fusion.where, bf16[1024,1024]{1,0:T(8,128)(2,1)S(1)} %get-tuple-element.70.stat, bf16[2,1024,1024]{2,1,0:T(8,128)(2,1)S(1)} %get-tuple-element.56.bases, ...), custom_call_target="tpu_custom_call" | custom-call | flops 7516192768 | bytes 8388608 | tf_op jit(solution)/shard_map/pallas_call | solution.py:489
  81.7 0.0 collective-permute-done.18.came
  81.8 0.0 collective-permute-done.19.kept_next
  81.8 0.0 collective-permute-done.20.new_next
  81.8 0.6 collective-permute-start.21
  82.4 0.1 collective-permute-start.22
  82.4 2.9 %shard_map.111 = (f32[256,1024]{1,0:T(8,128)S(1)}, f32[512,1024]{1,0:T(8,128)}, f32[512,1024]{1,0:T(8,128)}, f32[1024,512]{1,0:T(8,128)}) custom-call(s32[4]{0:T(128)S(1)} %pad_add_fusion.where, bf16[1024,1024]{1,0:T(8,128)(2,1)S(1)} %get-tuple-element.75.current, bf16[1024,1024]{1,0:T(8,128)(2,1)S(1)} %get-tuple-element.76.turned, ...), custom_call_target="tpu_custom_call", output_to_operand_aliasing={{3}: (5, {})} | custom-call | flops 1073741824 | bytes 4194304 | tf_op jit(solution)/shard_map/pallas_call | solution.py:508
  85.3 0.0 collective-permute-done.21.came_next
  85.4 0.5 collective-permute-start.23
  85.9 0.0 collective-permute-done.22.top_next
  85.9 2.9 %shard_map.112 = (bf16[512,1024]{1,0:T(8,128)(2,1)}, f32[512,1024]{1,0:T(8,128)}, f32[512,1024]{1,0:T(8,128)}) custom-call(s32[4]{0:T(128)S(1)} %pad_add_fusion.where, bf16[512,256]{1,0:T(8,128)(2,1)S(1)} %get-tuple-element.67.kept, bf16[512,256]{1,0:T(8,128)(2,1)S(1)} %collective-permute-done.18.came, ...), custom_call_target="tpu_custom_call", output_to_operand_aliasing={{1}: (8, {}), {2}: (9, {})} | custom-call | flops 1073741824 | bytes 4194304 | tf_op jit(solution)/shard_map/pallas_call | solution.py:520
  88.8 0.0 collective-permute-done.23.low
  88.8 1.5 %shard_map.113 = (f32[512,1024]{1,0:T(8,128)}, f32[512,1024]{1,0:T(8,128)}) custom-call(s32[4]{0:T(128)S(1)} %pad_add_fusion.where, f32[256,1024]{1,0:T(8,128)S(1)} %collective-permute-done.23.low, f32[512,1024]{1,0:T(8,128)} %get-tuple-element.88.left_in, f32[512,1024]{1,0:T(8,128)} %get-tuple-element.89.right_in), custom_call_target="tpu_custom_call", output_to_operand_aliasing={{0}: (2, {}), {1}: (3, {})} | custom-call | bytes 2097152 | tf_op jit(solution)/shard_map/pallas_call | solution.py:43
  (10 shorter events, 0.0 us)
Async XLA Ops:
  1.9 2.1 %collective-permute-start = (bf16[256,1024]{1,0:T(8,128)(2,1)S(1)}, bf16[256,1024]{1,0:T(8,128)(2,1)S(1)}, u32[]{:S(2)}, u32[]{:S(2)}) collective-permute-start(bf16[256,1024]{1,0:T(8,128)(2,1)S(1)} %get-tuple-element.92), channel_id=1, source_target_pairs={{0,2},{2,0},{4,6},{6,4},{8,10},{10,8},{12,14},{14,12},{16,18},{18,... | collective-permute-start | bytes 1572872 | tf_op jit(solution)/shard_map/ppermute | solution.py:379
  4.0 46.0 %copy-start = (f32[512,1024]{1,0:T(8,128)S(1)}, f32[512,1024]{1,0:T(8,128)}, u32[]{:S(2)}) copy-start(f32[512,1024]{1,0:T(8,128)} %left.3) | copy-start | bytes 6291460
  4.0 46.0 %copy-start.1 = (f32[512,1024]{1,0:T(8,128)S(1)}, f32[512,1024]{1,0:T(8,128)}, u32[]{:S(2)}) copy-start(f32[512,1024]{1,0:T(8,128)} %right.3) | copy-start | bytes 6291460
  4.0 46.0 %copy-start.2 = (f32[512,1024]{1,0:T(8,128)S(1)}, f32[512,1024]{1,0:T(8,128)}, u32[]{:S(2)}) copy-start(f32[512,1024]{1,0:T(8,128)} %stat_left.3) | copy-start | bytes 6291460
  4.0 46.1 %copy-start.3 = (f32[512,1024]{1,0:T(8,128)S(1)}, f32[512,1024]{1,0:T(8,128)}, u32[]{:S(2)}) copy-start(f32[512,1024]{1,0:T(8,128)} %stat_right.3) | copy-start | bytes 6291460
  6.8 34.1 %collective-permute-start.8 = (bf16[43,128,128]{2,1,0:T(8,128)(2,1)S(1)}, bf16[43,128,128]{2,1,0:T(8,128)(2,1)S(1)}, u32[]{:S(2)}, u32[]{:S(2)}) collective-permute-start(bf16[43,128,128]{2,1,0:T(8,128)(2,1)S(1)} %get-tuple-element.54), channel_id=1, source_target_pairs={{0,1},{1,0},{2,3},{3,2},{4,5},{5,4},{6,7},{7,6},{8,9},{9,8},{10,11... | collective-permute-start | bytes 4227080 | tf_op jit(solution)/shard_map/ppermute | solution.py:382
  9.7 8.1 %collective-permute-start.1 = (bf16[128,1024]{1,0:T(8,128)(2,1)S(1)}, bf16[128,1024]{1,0:T(8,128)(2,1)S(1)}, u32[]{:S(2)}, u32[]{:S(2)}) collective-permute-start(bf16[128,1024]{1,0:T(8,128)(2,1)S(1)} %get-tuple-element.49), channel_id=1, source_target_pairs={{0,4},{2,6},{4,0},{6,2},{8,12},{10,14},{12,8},{14,10},{16,20},{18,... | collective-permute-start | bytes 786440 | tf_op jit(solution)/shard_map/ppermute | solution.py:379
  18.4 5.0 %collective-permute-start.2 = (bf16[32,1024]{1,0:T(8,128)(2,1)S(1)}, bf16[32,1024]{1,0:T(8,128)(2,1)S(1)}, u32[]{:S(2)}, u32[]{:S(2)}) collective-permute-start(bf16[32,1024]{1,0:T(8,128)(2,1)S(1)} %get-tuple-element.51), channel_id=1, source_target_pairs={{0,8},{2,10},{4,12},{6,14},{8,0},{10,2},{12,4},{14,6},{16,24},{18,... | collective-permute-start | bytes 196616 | tf_op jit(solution)/shard_map/ppermute | solution.py:379
  20.0 6.6 %collective-permute-start.3 = (bf16[32,1024]{1,0:T(8,128)(2,1)S(1)}, bf16[32,1024]{1,0:T(8,128)(2,1)S(1)}, u32[]{:S(2)}, u32[]{:S(2)}) collective-permute-start(bf16[32,1024]{1,0:T(8,128)(2,1)S(1)} %get-tuple-element.52), channel_id=1, source_target_pairs={{0,16},{2,18},{4,20},{6,22},{8,24},{10,26},{12,28},{14,30},{16,0},... | collective-permute-start | bytes 196616 | tf_op jit(solution)/shard_map/ppermute | solution.py:379
  22.6 6.5 %collective-permute-start.4 = (bf16[32,1024]{1,0:T(8,128)(2,1)S(1)}, bf16[32,1024]{1,0:T(8,128)(2,1)S(1)}, u32[]{:S(2)}, u32[]{:S(2)}) collective-permute-start(bf16[32,1024]{1,0:T(8,128)(2,1)S(1)} %get-tuple-element.53), channel_id=1, source_target_pairs={{0,24},{2,26},{4,28},{6,30},{8,16},{10,18},{12,20},{14,22},{16,8},... | collective-permute-start | bytes 196616 | tf_op jit(solution)/shard_map/ppermute | solution.py:379
  29.1 4.5 %collective-permute-start.5 = (bf16[32,1024]{1,0:T(8,128)(2,1)S(1)}, bf16[32,1024]{1,0:T(8,128)(2,1)S(1)}, u32[]{:S(2)}, u32[]{:S(2)}) collective-permute-start(bf16[32,1024]{1,0:T(8,128)(2,1)S(1)} %shard_map.104.refs_0_), channel_id=1, source_target_pairs={{0,8},{2,10},{4,12},{6,14},{8,0},{10,2},{12,4},{14,6},{16,24},{18,... | collective-permute-start | bytes 196616 | tf_op jit(solution)/shard_map/ppermute | solution.py:379
  29.2 5.2 %collective-permute-start.6 = (bf16[32,1024]{1,0:T(8,128)(2,1)S(1)}, bf16[32,1024]{1,0:T(8,128)(2,1)S(1)}, u32[]{:S(2)}, u32[]{:S(2)}) collective-permute-start(bf16[32,1024]{1,0:T(8,128)(2,1)S(1)} %shard_map.104.refs_0_), channel_id=1, source_target_pairs={{0,16},{2,18},{4,20},{6,22},{8,24},{10,26},{12,28},{14,30},{16,0},... | collective-permute-start | bytes 196616 | tf_op jit(solution)/shard_map/ppermute | solution.py:379
  30.3 6.4 %collective-permute-start.7 = (bf16[32,1024]{1,0:T(8,128)(2,1)S(1)}, bf16[32,1024]{1,0:T(8,128)(2,1)S(1)}, u32[]{:S(2)}, u32[]{:S(2)}) collective-permute-start(bf16[32,1024]{1,0:T(8,128)(2,1)S(1)} %shard_map.104.refs_0_), channel_id=1, source_target_pairs={{0,24},{2,26},{4,28},{6,30},{8,16},{10,18},{12,20},{14,22},{16,8},... | collective-permute-start | bytes 196616 | tf_op jit(solution)/shard_map/ppermute | solution.py:379
  37.2 20.0 %copy-start.4 = (f32[512,1024]{1,0:T(8,128)S(1)}, f32[512,1024]{1,0:T(8,128)}, u32[]{:S(2)}) copy-start(f32[512,1024]{1,0:T(8,128)} %moment.1) | copy-start | bytes 6291460
  40.9 9.1 %collective-permute-start.9 = (bf16[43,128,128]{2,1,0:T(8,128)(2,1)S(1)}, bf16[43,128,128]{2,1,0:T(8,128)(2,1)S(1)}, u32[]{:S(2)}, u32[]{:S(2)}) collective-permute-start(bf16[43,128,128]{2,1,0:T(8,128)(2,1)S(1)} %collective-permute-done.8.mine), channel_id=1, source_target_pairs={{0,2},{2,0},{4,6},{6,4},{8,10},{10,8},{12,14},{14,12},{16,18},{18,... | collective-permute-start | bytes 4227080 | tf_op jit(solution)/shard_map/ppermute | solution.py:379
  40.9 9.1 %collective-permute-start.10 = (bf16[128,1024]{1,0:T(8,128)(2,1)S(1)}, bf16[128,1024]{1,0:T(8,128)(2,1)S(1)}, u32[]{:S(2)}, u32[]{:S(2)}) collective-permute-start(bf16[128,1024]{1,0:T(8,128)(2,1)S(1)} %shard_map.105.own.refs_0_), channel_id=1, source_target_pairs={{0,4},{2,6},{4,0},{6,2},{8,12},{10,14},{12,8},{14,10},{16,20},{18,... | collective-permute-start | bytes 786440 | tf_op jit(solution)/shard_map/ppermute | solution.py:379
  42.6 14.1 %collective-permute-start.13 = (bf16[128,1024]{1,0:T(8,128)(2,1)S(1)}, bf16[128,1024]{1,0:T(8,128)(2,1)S(1)}, u32[]{:S(2)}, u32[]{:S(2)}) collective-permute-start(bf16[128,1024]{1,0:T(8,128)(2,1)S(1)} %shard_map.105.own.refs_0_), channel_id=1, source_target_pairs={{0,1},{1,0},{2,3},{3,2},{4,5},{5,4},{6,7},{7,6},{8,9},{9,8},{10,11... | collective-permute-start | bytes 786440 | tf_op jit(solution)/shard_map/ppermute | solution.py:382
  44.1 12.5 %collective-permute-start.14 = (bf16[128,1024]{1,0:T(8,128)(2,1)S(1)}, bf16[128,1024]{1,0:T(8,128)(2,1)S(1)}, u32[]{:S(2)}, u32[]{:S(2)}) collective-permute-start(bf16[128,1024]{1,0:T(8,128)(2,1)S(1)} %shard_map.105.own.refs_0_), channel_id=1, source_target_pairs={{0,5},{1,4},{2,7},{3,6},{4,1},{5,0},{6,3},{7,2},{8,13},{9,12},{10,... | collective-permute-start | bytes 786440 | tf_op jit(solution)/shard_map/ppermute | solution.py:386
  44.4 12.8 %collective-permute-start.11 = (bf16[128,1024]{1,0:T(8,128)(2,1)S(1)}, bf16[128,1024]{1,0:T(8,128)(2,1)S(1)}, u32[]{:S(2)}, u32[]{:S(2)}) collective-permute-start(bf16[128,1024]{1,0:T(8,128)(2,1)S(1)} %shard_map.105.own.refs_0_), channel_id=1, source_target_pairs={{0,2},{2,0},{4,6},{6,4},{8,10},{10,8},{12,14},{14,12},{16,18},{18,... | collective-permute-start | bytes 786440 | tf_op jit(solution)/shard_map/ppermute | solution.py:379
  50.0 7.2 %collective-permute-start.12 = (bf16[128,1024]{1,0:T(8,128)(2,1)S(1)}, bf16[128,1024]{1,0:T(8,128)(2,1)S(1)}, u32[]{:S(2)}, u32[]{:S(2)}) collective-permute-start(bf16[128,1024]{1,0:T(8,128)(2,1)S(1)} %collective-permute-done.10.over_x.refs_1_), channel_id=1, source_target_pairs={{0,2},{2,0},{4,6},{6,4},{8,10},{10,8},{12,14},{14,12},{16,18},{18,... | collective-permute-start | bytes 786440 | tf_op jit(solution)/shard_map/ppermute | solution.py:379
  56.7 4.0 %copy-start.5 = (f32[1024,512]{1,0:T(8,128)S(1)}, f32[1024,512]{1,0:T(8,128)}, u32[]{:S(2)}) copy-start(f32[1024,512]{1,0:T(8,128)} %second.1) | copy-start | bytes 6291460
  56.7 4.0 %collective-permute-start.15 = (bf16[128,1024]{1,0:T(8,128)(2,1)S(1)}, bf16[128,1024]{1,0:T(8,128)(2,1)S(1)}, u32[]{:S(2)}, u32[]{:S(2)}) collective-permute-start(bf16[128,1024]{1,0:T(8,128)(2,1)S(1)} %collective-permute-done.13.refs_4_), channel_id=1, source_target_pairs={{0,2},{2,0},{4,6},{6,4},{8,10},{10,8},{12,14},{14,12},{16,18},{18,... | collective-permute-start | bytes 786440 | tf_op jit(solution)/shard_map/ppermute | solution.py:379
  56.7 4.0 %collective-permute-start.16 = (bf16[128,1024]{1,0:T(8,128)(2,1)S(1)}, bf16[128,1024]{1,0:T(8,128)(2,1)S(1)}, u32[]{:S(2)}, u32[]{:S(2)}) collective-permute-start(bf16[128,1024]{1,0:T(8,128)(2,1)S(1)} %collective-permute-done.14.refs_5_), channel_id=1, source_target_pairs={{0,2},{2,0},{4,6},{6,4},{8,10},{10,8},{12,14},{14,12},{16,18},{18,... | collective-permute-start | bytes 786440 | tf_op jit(solution)/shard_map/ppermute | solution.py:379
  59.1 8.4 %collective-permute-start.17 = (bf16[512,256]{1,0:T(8,128)(2,1)S(1)}, bf16[512,256]{1,0:T(8,128)(2,1)S(1)}, u32[]{:S(2)}, u32[]{:S(2)}) collective-permute-start(bf16[512,256]{1,0:T(8,128)(2,1)S(1)} %get-tuple-element.64), channel_id=1, source_target_pairs={{0,1},{1,0},{2,3},{3,2},{4,5},{5,4},{6,7},{7,6},{8,9},{9,8},{10,11... | collective-permute-start | bytes 786440 | tf_op jit(solution)/shard_map/ppermute | solution.py:382
  66.1 15.7 %collective-permute-start.20 = (f32[1024,256]{1,0:T(8,128)S(1)}, f32[1024,256]{1,0:T(8,128)S(1)}, u32[]{:S(2)}, u32[]{:S(2)}) collective-permute-start(f32[1024,256]{1,0:T(8,128)S(1)} %get-tuple-element.66.new), channel_id=1, source_target_pairs={{0,2},{2,0},{4,6},{6,4},{8,10},{10,8},{12,14},{14,12},{16,18},{18,... | collective-permute-start | bytes 3145736 | tf_op jit(solution)/shard_map/ppermute | solution.py:379
  70.3 11.5 %collective-permute-start.18 = (bf16[512,256]{1,0:T(8,128)(2,1)S(1)}, bf16[512,256]{1,0:T(8,128)(2,1)S(1)}, u32[]{:S(2)}, u32[]{:S(2)}) collective-permute-start(bf16[512,256]{1,0:T(8,128)(2,1)S(1)} %get-tuple-element.72), channel_id=1, source_target_pairs={{0,1},{1,0},{2,3},{3,2},{4,5},{5,4},{6,7},{7,6},{8,9},{9,8},{10,11... | collective-permute-start | bytes 786440 | tf_op jit(solution)/shard_map/ppermute | solution.py:382
  71.9 9.9 %collective-permute-start.19 = (bf16[512,256]{1,0:T(8,128)(2,1)S(1)}, bf16[512,256]{1,0:T(8,128)(2,1)S(1)}, u32[]{:S(2)}, u32[]{:S(2)}) collective-permute-start(bf16[512,256]{1,0:T(8,128)(2,1)S(1)} %get-tuple-element.67.kept), channel_id=1, source_target_pairs={{0,2},{2,0},{4,6},{6,4},{8,10},{10,8},{12,14},{14,12},{16,18},{18,... | collective-permute-start | bytes 786440 | tf_op jit(solution)/shard_map/ppermute | solution.py:379
  81.8 3.6 %collective-permute-start.21 = (bf16[512,256]{1,0:T(8,128)(2,1)S(1)}, bf16[512,256]{1,0:T(8,128)(2,1)S(1)}, u32[]{:S(2)}, u32[]{:S(2)}) collective-permute-start(bf16[512,256]{1,0:T(8,128)(2,1)S(1)} %collective-permute-done.18.came), channel_id=1, source_target_pairs={{0,2},{2,0},{4,6},{6,4},{8,10},{10,8},{12,14},{14,12},{16,18},{18,... | collective-permute-start | bytes 786440 | tf_op jit(solution)/shard_map/ppermute | solution.py:379
  82.4 3.5 %collective-permute-start.22 = (f32[256,1024]{1,0:T(8,128)S(1)}, f32[256,1024]{1,0:T(8,128)S(1)}, u32[]{:S(2)}, u32[]{:S(2)}) collective-permute-start(f32[256,1024]{1,0:T(8,128)S(1)} %get-tuple-element.77.top), channel_id=1, source_target_pairs={{0,2},{2,0},{4,6},{6,4},{8,10},{10,8},{12,14},{14,12},{16,18},{18,... | collective-permute-start | bytes 3145736 | tf_op jit(solution)/shard_map/ppermute | solution.py:379
  85.4 3.4 %collective-permute-start.23 = (f32[256,1024]{1,0:T(8,128)S(1)}, f32[256,1024]{1,0:T(8,128)S(1)}, u32[]{:S(2)}, u32[]{:S(2)}) collective-permute-start(f32[256,1024]{1,0:T(8,128)S(1)} %get-tuple-element.83.low), channel_id=1, source_target_pairs={{0,2},{2,0},{4,6},{6,4},{8,10},{10,8},{12,14},{14,12},{16,18},{18,... | collective-permute-start | bytes 3145736 | tf_op jit(solution)/shard_map/ppermute | solution.py:379

commit v9 on v8

--- a/solution.py
+++ b/solution.py
@@ -214,6 +214,12 @@
     ours[...] = matmul(half[...], bases[1 - core, :, here]).astype(HALF)
 
 
+def place_symmetric(out, here, value):
+    out[: here.stop, here] = value
+    if here.start:
+        out[here, : here.start] = value[: here.start].T
+
+
 def statistic_kernel(where, bases, turned, stat, second, *refs):
     parts, (half, new, pair, sem) = refs[:-4], refs[-4:]
     position, core, x = where[0], where[1], where[2]
@@ -231,9 +237,11 @@
     for here in quarters(width):
         pair[1 - core, :, here] = gradient[here].T
     block = matmul(gradient[...], bases[1 - core, :, tile(position * 2 + core, step)])
-    for here in quarters(width):
-        grads = matmul(pair[0], pair[1, :, here])
-        half[:, here] = (BETA_STAT * stat[:, here] + (1.0 - BETA_STAT) * grads).astype(HALF)
+    for here in reversed(quarters(width)):
+        above = slice(0, here.stop)
+        grads = matmul(pair[0, above], pair[1, :, here])
+        value = (BETA_STAT * stat[above, here] + (1.0 - BETA_STAT) * grads).astype(HALF)
+        place_symmetric(half, here, value)
     grad_rot = matmul(turned[...], block.astype(HALF)) * (1.0 / width)
     new[...] = BETA_TWO * second[:, tile(core, step)] + (1.0 - BETA_TWO) * grad_rot * grad_rot
 
@@ -311,8 +319,14 @@
 
 def improved(current, turned, kept, gram, result, result_turned):
     size, width = result.shape
-    for here in quarters(width):
-        gram[:size, here] = (matmul(current[kept], turned[:, here]) * (1.0 / width)).astype(HALF)
+    if size == width:
+        for here in reversed(quarters(width)):
+            product = matmul(current[: here.stop], turned[:, here]) * (1.0 / width)
+            place_symmetric(gram, here, product.astype(HALF))
+    else:
+        for here in quarters(width):
+            product = matmul(current[kept], turned[:, here]) * (1.0 / width)
+            gram[:size, here] = product.astype(HALF)
     for here in quarters(width):
         value = (
             1.5 * current[kept, here].astype(FULL) - 0.5 * matmul(gram[:size], current[:, here])

time: 90.6 us -> 89.5 us (0.988)
  Pallas kernels: 34.5 us -> 32.4 us
  waiting for transfers between devices: 31.3 us -> 32.3 us
    pallas_call x1, Pallas kernels: 9.88 us -> 8.75 us  [fast_body(): pl.pallas_call(refresh_kernel, out_shape=[square, square, shaped((half, w...]
    pallas_call x9, Pallas kernels: 18.8 us -> 17.9 us  [call(): pl.pallas_call(kernel, out_shape=outs, in_specs=specs, out_specs=[space]...]
    ppermute x4, waiting for transfers between devices: 8.33 us -> 9.3 us  [shard_swap(): return lax.ppermute(value, 'shard', [(0, 1), (1, 0)])]
  transfers between devices with their start and end apart: 24 -> 24, of which waited for: 11 -> 11; matrix products, arithmetic and copies ran while one was open for 0% -> 0% of each run, Pallas kernels for 33% -> 32%
where the time goes in v9:
time: 89.5 us; the launch traced here: 89.3 us
  Pallas kernels  32.4 us (36%)
  waiting for transfers between devices  32.3 us (36%)
  starting transfers between devices  22.3 us (25%)
  local copies, waits for them, and re-layouts  1.3 us (1%)
  between operations  1.01 us (1%)
    ppermute x19, waiting for transfers between devices, dp_swap(): return lax.ppermute(value, 'dp', [(i, i ^ distance) for i in range(16)])  23 us
    pallas_call x9, Pallas kernels, call(): pl.pallas_call(kernel, out_shape=outs, in_specs=specs, out_specs=[space]...  17.9 us
    ppermute x19, starting transfers between devices, dp_swap(): return lax.ppermute(value, 'dp', [(i, i ^ distance) for i in range(16)])  14.4 us
    ppermute x4, waiting for transfers between devices, shard_swap(): return lax.ppermute(value, 'shard', [(0, 1), (1, 0)])  9.3 us
    pallas_call x1, Pallas kernels, fast_body(): pl.pallas_call(refresh_kernel, out_shape=[square, square, shaped((half, w...  8.75 us
    ppermute x4, starting transfers between devices, shard_swap(): return lax.ppermute(value, 'shard', [(0, 1), (1, 0)])  7.65 us
    pallas_call x1, Pallas kernels, fast_body(): pl.pallas_call(update_kernel, out_shape=[shaped((rows, width), HALF), sid...  2.92 us
    pallas_call x1, Pallas kernels, fast_body(): pl.pallas_call(last_kernel, out_shape=[shaped((half, width), FULL), side,...  2.91 us
  transfers between devices with their start and end apart: 24, of which 11 were waited for; matrix products, arithmetic and copies ran while one was open for 0% of the time, Pallas kernels for 32%

profile of v9, /device:TPU:0, one launch (start us, length us, event | category | flops | bytes accessed | tf_op | source)
XLA Modules:
  0.0 89.3 jit_solution(9577455101256169644)
XLA Ops:
  0.6 1.3 %dynamic-slice_bitcast_fusion = (bf16[256,1024]{1,0:T(8,128)(2,1)S(1)}, bf16[256,1024]{1,0:T(8,128)(2,1)S(1)}) fusion(bf16[1,512,1024]{2,1,0:T(8,128)(2,1)} %param.7, s32[]{:T(128)S(6)} %select_n.7, s32[]{:T(128)S(6)} %select_n.6), kind=kLoop, calls=%fused_computation | loop fusion | bytes 2097160 | tf_op jit(solution)/shard_map/dynamic_slice | solution.py:402
  1.9 0.5 collective-permute-start
  2.4 0.1 pad_add_fusion.where
  2.5 1.5 %collective-permute-done.came = bf16[256,1024]{1,0:T(8,128)(2,1)S(1)} collective-permute-done((bf16[256,1024]{1,0:T(8,128)(2,1)S(1)}, bf16[256,1024]{1,0:T(8,128)(2,1)S(1)}, u32[]{:S(2)}, u32[]{:S(2)}) %collective-permute-start) | collective-permute-done | bytes 524320 | tf_op jit(solution)/shard_map/ppermute | solution.py:393
  4.0 2.8 %shard_map.102 = (bf16[43,128,128]{2,1,0:T(8,128)(2,1)S(1)}, f32[128,1024]{1,0:T(8,128)S(1)}, bf16[128,1024]{1,0:T(8,128)(2,1)S(1)}) custom-call(s32[4]{0:T(128)S(1)} %pad_add_fusion.where, bf16[256,1024]{1,0:T(8,128)(2,1)S(1)} %get-tuple-element.93.raw, bf16[256,1024]{1,0:T(8,128)(2,1)S(1)} %collective-permute-done.came, f32[512,1024]{1,0:T(8,128)} %left.3, ...), custom_call_target="tpu_custom_call" | custom-call | bytes 4194304 | tf_op jit(solution)/shard_map/pallas_call | solution.py:43
  6.8 3.0 %collective-permute-start.8 = (bf16[43,128,128]{2,1,0:T(8,128)(2,1)S(1)}, bf16[43,128,128]{2,1,0:T(8,128)(2,1)S(1)}, u32[]{:S(2)}, u32[]{:S(2)}) collective-permute-start(bf16[43,128,128]{2,1,0:T(8,128)(2,1)S(1)} %get-tuple-element.54), channel_id=1, source_target_pairs={{0,1},{1,0},{2,3},{3,2},{4,5},{5,4},{6,7},{7,6},{8,9},{9,8},{10,11... | collective-permute-start | bytes 4227080 | tf_op jit(solution)/shard_map/ppermute | solution.py:396
  9.7 1.5 %collective-permute-start.1 = (bf16[128,1024]{1,0:T(8,128)(2,1)S(1)}, bf16[128,1024]{1,0:T(8,128)(2,1)S(1)}, u32[]{:S(2)}, u32[]{:S(2)}) collective-permute-start(bf16[128,1024]{1,0:T(8,128)(2,1)S(1)} %get-tuple-element.49), channel_id=1, source_target_pairs={{0,4},{2,6},{4,0},{6,2},{8,12},{10,14},{12,8},{14,10},{16,20},{18,... | collective-permute-start | bytes 786440 | tf_op jit(solution)/shard_map/ppermute | solution.py:393
  11.2 6.6 %collective-permute-done.1.came = bf16[128,1024]{1,0:T(8,128)(2,1)S(1)} collective-permute-done((bf16[128,1024]{1,0:T(8,128)(2,1)S(1)}, bf16[128,1024]{1,0:T(8,128)(2,1)S(1)}, u32[]{:S(2)}, u32[]{:S(2)}) %collective-permute-start.1) | collective-permute-done | bytes 262176 | tf_op jit(solution)/shard_map/ppermute | solution.py:393
  17.8 0.6 shard_map.103
  18.4 1.6 %collective-permute-start.2 = (bf16[32,1024]{1,0:T(8,128)(2,1)S(1)}, bf16[32,1024]{1,0:T(8,128)(2,1)S(1)}, u32[]{:S(2)}, u32[]{:S(2)}) collective-permute-start(bf16[32,1024]{1,0:T(8,128)(2,1)S(1)} %get-tuple-element.51), channel_id=1, source_target_pairs={{0,8},{2,10},{4,12},{6,14},{8,0},{10,2},{12,4},{14,6},{16,24},{18,... | collective-permute-start | bytes 196616 | tf_op jit(solution)/shard_map/ppermute | solution.py:393
  20.0 2.6 %collective-permute-start.3 = (bf16[32,1024]{1,0:T(8,128)(2,1)S(1)}, bf16[32,1024]{1,0:T(8,128)(2,1)S(1)}, u32[]{:S(2)}, u32[]{:S(2)}) collective-permute-start(bf16[32,1024]{1,0:T(8,128)(2,1)S(1)} %get-tuple-element.52), channel_id=1, source_target_pairs={{0,16},{2,18},{4,20},{6,22},{8,24},{10,26},{12,28},{14,30},{16,0},... | collective-permute-start | bytes 196616 | tf_op jit(solution)/shard_map/ppermute | solution.py:393
  22.6 0.2 collective-permute-start.4
  22.8 0.5 collective-permute-done.2.one
  23.3 3.2 %collective-permute-done.3.two = bf16[32,1024]{1,0:T(8,128)(2,1)S(1)} collective-permute-done((bf16[32,1024]{1,0:T(8,128)(2,1)S(1)}, bf16[32,1024]{1,0:T(8,128)(2,1)S(1)}, u32[]{:S(2)}, u32[]{:S(2)}) %collective-permute-start.3) | collective-permute-done | bytes 65568 | tf_op jit(solution)/shard_map/ppermute | solution.py:393
  26.6 2.5 %collective-permute-done.4.three = bf16[32,1024]{1,0:T(8,128)(2,1)S(1)} collective-permute-done((bf16[32,1024]{1,0:T(8,128)(2,1)S(1)}, bf16[32,1024]{1,0:T(8,128)(2,1)S(1)}, u32[]{:S(2)}, u32[]{:S(2)}) %collective-permute-start.4) | collective-permute-done | bytes 65568 | tf_op jit(solution)/shard_map/ppermute | solution.py:393
  29.1 0.1 collective-permute-start.5
  29.2 1.0 %collective-permute-start.6 = (bf16[32,1024]{1,0:T(8,128)(2,1)S(1)}, bf16[32,1024]{1,0:T(8,128)(2,1)S(1)}, u32[]{:S(2)}, u32[]{:S(2)}) collective-permute-start(bf16[32,1024]{1,0:T(8,128)(2,1)S(1)} %shard_map.104.refs_0_), channel_id=1, source_target_pairs={{0,16},{2,18},{4,20},{6,22},{8,24},{10,26},{12,28},{14,30},{16,0},... | collective-permute-start | bytes 196616 | tf_op jit(solution)/shard_map/ppermute | solution.py:393
  30.3 3.3 %collective-permute-start.7 = (bf16[32,1024]{1,0:T(8,128)(2,1)S(1)}, bf16[32,1024]{1,0:T(8,128)(2,1)S(1)}, u32[]{:S(2)}, u32[]{:S(2)}) collective-permute-start(bf16[32,1024]{1,0:T(8,128)(2,1)S(1)} %shard_map.104.refs_0_), channel_id=1, source_target_pairs={{0,24},{2,26},{4,28},{6,30},{8,16},{10,18},{12,20},{14,22},{16,8},... | collective-permute-start | bytes 196616 | tf_op jit(solution)/shard_map/ppermute | solution.py:393
  33.6 0.0 collective-permute-done.5.refs_1_
  33.6 0.9 collective-permute-done.6.refs_2_
  34.5 2.2 %collective-permute-done.7.refs_3_ = bf16[32,1024]{1,0:T(8,128)(2,1)S(1)} collective-permute-done((bf16[32,1024]{1,0:T(8,128)(2,1)S(1)}, bf16[32,1024]{1,0:T(8,128)(2,1)S(1)}, u32[]{:S(2)}, u32[]{:S(2)}) %collective-permute-start.7) | collective-permute-done | bytes 65568 | tf_op jit(solution)/shard_map/ppermute | solution.py:393
  36.6 0.6 shard_map.105.own.refs_0_
  37.2 0.0 copy-start.4
  37.2 3.7 %collective-permute-done.8.mine = bf16[43,128,128]{2,1,0:T(8,128)(2,1)S(1)} collective-permute-done((bf16[43,128,128]{2,1,0:T(8,128)(2,1)S(1)}, bf16[43,128,128]{2,1,0:T(8,128)(2,1)S(1)}, u32[]{:S(2)}, u32[]{:S(2)}) %collective-permute-start.8) | collective-permute-done | bytes 1409056 | tf_op jit(solution)/shard_map/ppermute | solution.py:396
  40.9 0.0 collective-permute-start.9
  40.9 1.7 %collective-permute-start.10 = (bf16[128,1024]{1,0:T(8,128)(2,1)S(1)}, bf16[128,1024]{1,0:T(8,128)(2,1)S(1)}, u32[]{:S(2)}, u32[]{:S(2)}) collective-permute-start(bf16[128,1024]{1,0:T(8,128)(2,1)S(1)} %shard_map.105.own.refs_0_), channel_id=1, source_target_pairs={{0,4},{2,6},{4,0},{6,2},{8,12},{10,14},{12,8},{14,10},{16,20},{18,... | collective-permute-start | bytes 786440 | tf_op jit(solution)/shard_map/ppermute | solution.py:393
  42.6 1.5 %collective-permute-start.13 = (bf16[128,1024]{1,0:T(8,128)(2,1)S(1)}, bf16[128,1024]{1,0:T(8,128)(2,1)S(1)}, u32[]{:S(2)}, u32[]{:S(2)}) collective-permute-start(bf16[128,1024]{1,0:T(8,128)(2,1)S(1)} %shard_map.105.own.refs_0_), channel_id=1, source_target_pairs={{0,1},{1,0},{2,3},{3,2},{4,5},{5,4},{6,7},{7,6},{8,9},{9,8},{10,11... | collective-permute-start | bytes 786440 | tf_op jit(solution)/shard_map/ppermute | solution.py:396
  44.1 0.3 collective-permute-start.14
  44.4 0.0 collective-permute-start.11
  44.4 5.6 %collective-permute-done.10.over_x.refs_1_ = bf16[128,1024]{1,0:T(8,128)(2,1)S(1)} collective-permute-done((bf16[128,1024]{1,0:T(8,128)(2,1)S(1)}, bf16[128,1024]{1,0:T(8,128)(2,1)S(1)}, u32[]{:S(2)}, u32[]{:S(2)}) %collective-permute-start.10) | collective-permute-done | bytes 262176 | tf_op jit(solution)/shard_map/ppermute | solution.py:393
  50.0 0.0 collective-permute-start.12
  50.0 0.0 collective-permute-done.9.theirs
  50.0 3.2 %shard_map.106 = (bf16[2,1024,1024]{2,1,0:T(8,128)(2,1)S(1)}, bf16[1024,1024]{1,0:T(8,128)(2,1)S(1)}, bf16[1024,1024]{1,0:T(8,128)(2,1)S(1)}, f32[1024,1024]{1,0:T(8,128)S(1)}) custom-call(s32[4]{0:T(128)S(1)} %pad_add_fusion.where, f32[512,1024]{1,0:T(8,128)S(1)} %copy-done, f32[512,1024]{1,0:T(8,128)S(1)} %copy-done.1, ...), custom_call_target="tpu_custom_call" | custom-call | bytes 16777216 | tf_op jit(solution)/shard_map/pallas_call | solution.py:43
  53.2 3.4 %collective-permute-done.13.refs_4_ = bf16[128,1024]{1,0:T(8,128)(2,1)S(1)} collective-permute-done((bf16[128,1024]{1,0:T(8,128)(2,1)S(1)}, bf16[128,1024]{1,0:T(8,128)(2,1)S(1)}, u32[]{:S(2)}, u32[]{:S(2)}) %collective-permute-start.13) | collective-permute-done | bytes 262176 | tf_op jit(solution)/shard_map/ppermute | solution.py:396
  56.7 0.0 collective-permute-done.14.refs_5_
  56.7 0.0 collective-permute-start.15
  56.7 0.5 collective-permute-start.16
  57.2 0.0 collective-permute-done.11.next_own.refs_2_
  57.2 0.0 collective-permute-done.12.next_over_x.refs_3_
  57.2 0.0 copy-done.4
  57.2 1.9 %shard_map.107 = (bf16[512,256]{1,0:T(8,128)(2,1)S(1)}, bf16[512,256]{1,0:T(8,128)(2,1)S(1)}) custom-call(s32[4]{0:T(128)S(1)} %pad_add_fusion.where, f32[512,1024]{1,0:T(8,128)S(1)} %copy-done.4, bf16[2,1024,1024]{2,1,0:T(8,128)(2,1)S(1)} %get-tuple-element.56.bases, bf16[128,1024]{1,0:T(8,128)(2,1)S(1)} %shard_map.105.own.refs_0_, ...), custom_call_target="tpu_custom_call" | custom-call | flops 536870912 | bytes 4194304 | tf_op jit(solution)/shard_map/pallas_call | solution.py:43
  59.1 1.6 %collective-permute-start.17 = (bf16[512,256]{1,0:T(8,128)(2,1)S(1)}, bf16[512,256]{1,0:T(8,128)(2,1)S(1)}, u32[]{:S(2)}, u32[]{:S(2)}) collective-permute-start(bf16[512,256]{1,0:T(8,128)(2,1)S(1)} %get-tuple-element.64), channel_id=1, source_target_pairs={{0,1},{1,0},{2,3},{3,2},{4,5},{5,4},{6,7},{7,6},{8,9},{9,8},{10,11... | collective-permute-start | bytes 786440 | tf_op jit(solution)/shard_map/ppermute | solution.py:396
  60.6 0.0 collective-permute-done.15.refs_6_
  60.7 0.0 collective-permute-done.16.refs_7_
  60.7 0.0 copy-done.5
  60.7 4.5 %shard_map.108 = (bf16[1024,1024]{1,0:T(8,128)(2,1)S(1)}, f32[1024,256]{1,0:T(8,128)S(1)}) custom-call(s32[4]{0:T(128)S(1)} %pad_add_fusion.where, bf16[2,1024,1024]{2,1,0:T(8,128)(2,1)S(1)} %get-tuple-element.56.bases, bf16[1024,1024]{1,0:T(8,128)(2,1)S(1)} %get-tuple-element.57.turned, f32[1024,1024]{1,0:T(8,128)S(1)} %get-tuple-element.60.stat, ...), custom_call_target="tpu_custom_call" | custom-call | flops 3221225472 | bytes 8388608 | tf_op jit(solution)/shard_map/pallas_call | solution.py:43
  65.1 0.1 collective-permute-start.20
  65.2 2.2 %collective-permute-done.17.came = bf16[512,256]{1,0:T(8,128)(2,1)S(1)} collective-permute-done((bf16[512,256]{1,0:T(8,128)(2,1)S(1)}, bf16[512,256]{1,0:T(8,128)(2,1)S(1)}, u32[]{:S(2)}, u32[]{:S(2)}) %collective-permute-start.17) | collective-permute-done | bytes 262176 | tf_op jit(solution)/shard_map/ppermute | solution.py:396
  67.4 2.8 %shard_map.109 = (bf16[512,256]{1,0:T(8,128)(2,1)S(1)}, bf16[512,256]{1,0:T(8,128)(2,1)S(1)}) custom-call(s32[4]{0:T(128)S(1)} %pad_add_fusion.where, bf16[2,1024,1024]{2,1,0:T(8,128)(2,1)S(1)} %get-tuple-element.56.bases, bf16[1024,1024]{1,0:T(8,128)(2,1)S(1)} %get-tuple-element.57.turned, bf16[512,256]{1,0:T(8,128)(2,1)S(1)} %get-tuple-element.59.mine, ...), custom_call_target="tpu_custom_call" | custom-call | flops 1073741824 | bytes 4194304 | tf_op jit(solution)/shard_map/pallas_call | solution.py:43
  70.3 1.6 %collective-permute-start.18 = (bf16[512,256]{1,0:T(8,128)(2,1)S(1)}, bf16[512,256]{1,0:T(8,128)(2,1)S(1)}, u32[]{:S(2)}, u32[]{:S(2)}) collective-permute-start(bf16[512,256]{1,0:T(8,128)(2,1)S(1)} %get-tuple-element.72), channel_id=1, source_target_pairs={{0,1},{1,0},{2,3},{3,2},{4,5},{5,4},{6,7},{7,6},{8,9},{9,8},{10,11... | collective-permute-start | bytes 786440 | tf_op jit(solution)/shard_map/ppermute | solution.py:396
  71.9 0.0 collective-permute-start.19
  71.9 8.7 %shard_map.110 = (bf16[1024,1024]{1,0:T(8,128)(2,1)S(1)}, bf16[1024,1024]{1,0:T(8,128)(2,1)S(1)}, f32[256,1024]{1,0:T(8,128)S(1)}, f32[1024,512]{1,0:T(8,128)}) custom-call(s32[4]{0:T(128)S(1)} %pad_add_fusion.where, bf16[1024,1024]{1,0:T(8,128)(2,1)S(1)} %get-tuple-element.70.stat, bf16[2,1024,1024]{2,1,0:T(8,128)(2,1)S(1)} %get-tuple-element.56.bases, ...), custom_call_target="tpu_custom_call" | custom-call | flops 7516192768 | bytes 8388608 | tf_op jit(solution)/shard_map/pallas_call | solution.py:503
  80.6 0.0 collective-permute-done.18.came
  80.6 0.0 collective-permute-done.19.kept_next
  80.6 0.0 collective-permute-done.20.new_next
  80.6 0.6 collective-permute-start.21
  81.2 0.1 collective-permute-start.22
  81.3 2.9 %shard_map.111 = (f32[256,1024]{1,0:T(8,128)S(1)}, f32[512,1024]{1,0:T(8,128)}, f32[512,1024]{1,0:T(8,128)}, f32[1024,512]{1,0:T(8,128)}) custom-call(s32[4]{0:T(128)S(1)} %pad_add_fusion.where, bf16[1024,1024]{1,0:T(8,128)(2,1)S(1)} %get-tuple-element.75.current, bf16[1024,1024]{1,0:T(8,128)(2,1)S(1)} %get-tuple-element.76.turned, ...), custom_call_target="tpu_custom_call", output_to_operand_aliasing={{3}: (5, {})} | custom-call | flops 1073741824 | bytes 4194304 | tf_op jit(solution)/shard_map/pallas_call | solution.py:522
  84.2 0.0 collective-permute-done.21.came_next
  84.2 0.5 collective-permute-start.23
  84.7 0.0 collective-permute-done.22.top_next
  84.7 2.9 %shard_map.112 = (bf16[512,1024]{1,0:T(8,128)(2,1)}, f32[512,1024]{1,0:T(8,128)}, f32[512,1024]{1,0:T(8,128)}) custom-call(s32[4]{0:T(128)S(1)} %pad_add_fusion.where, bf16[512,256]{1,0:T(8,128)(2,1)S(1)} %get-tuple-element.67.kept, bf16[512,256]{1,0:T(8,128)(2,1)S(1)} %collective-permute-done.18.came, ...), custom_call_target="tpu_custom_call", output_to_operand_aliasing={{1}: (8, {}), {2}: (9, {})} | custom-call | flops 1073741824 | bytes 4194304 | tf_op jit(solution)/shard_map/pallas_call | solution.py:534
  87.7 0.0 collective-permute-done.23.low
  87.7 1.5 %shard_map.113 = (f32[512,1024]{1,0:T(8,128)}, f32[512,1024]{1,0:T(8,128)}) custom-call(s32[4]{0:T(128)S(1)} %pad_add_fusion.where, f32[256,1024]{1,0:T(8,128)S(1)} %collective-permute-done.23.low, f32[512,1024]{1,0:T(8,128)} %get-tuple-element.88.left_in, f32[512,1024]{1,0:T(8,128)} %get-tuple-element.89.right_in), custom_call_target="tpu_custom_call", output_to_operand_aliasing={{0}: (2, {}), {1}: (3, {})} | custom-call | bytes 2097152 | tf_op jit(solution)/shard_map/pallas_call | solution.py:43
  (10 shorter events, 0.0 us)
Async XLA Ops:
  1.9 2.1 %collective-permute-start = (bf16[256,1024]{1,0:T(8,128)(2,1)S(1)}, bf16[256,1024]{1,0:T(8,128)(2,1)S(1)}, u32[]{:S(2)}, u32[]{:S(2)}) collective-permute-start(bf16[256,1024]{1,0:T(8,128)(2,1)S(1)} %get-tuple-element.92), channel_id=1, source_target_pairs={{0,2},{2,0},{4,6},{6,4},{8,10},{10,8},{12,14},{14,12},{16,18},{18,... | collective-permute-start | bytes 1572872 | tf_op jit(solution)/shard_map/ppermute | solution.py:393
  4.0 46.0 %copy-start = (f32[512,1024]{1,0:T(8,128)S(1)}, f32[512,1024]{1,0:T(8,128)}, u32[]{:S(2)}) copy-start(f32[512,1024]{1,0:T(8,128)} %left.3) | copy-start | bytes 6291460
  4.0 46.0 %copy-start.1 = (f32[512,1024]{1,0:T(8,128)S(1)}, f32[512,1024]{1,0:T(8,128)}, u32[]{:S(2)}) copy-start(f32[512,1024]{1,0:T(8,128)} %right.3) | copy-start | bytes 6291460
  4.0 46.0 %copy-start.2 = (f32[512,1024]{1,0:T(8,128)S(1)}, f32[512,1024]{1,0:T(8,128)}, u32[]{:S(2)}) copy-start(f32[512,1024]{1,0:T(8,128)} %stat_left.3) | copy-start | bytes 6291460
  4.0 46.1 %copy-start.3 = (f32[512,1024]{1,0:T(8,128)S(1)}, f32[512,1024]{1,0:T(8,128)}, u32[]{:S(2)}) copy-start(f32[512,1024]{1,0:T(8,128)} %stat_right.3) | copy-start | bytes 6291460
  6.8 34.1 %collective-permute-start.8 = (bf16[43,128,128]{2,1,0:T(8,128)(2,1)S(1)}, bf16[43,128,128]{2,1,0:T(8,128)(2,1)S(1)}, u32[]{:S(2)}, u32[]{:S(2)}) collective-permute-start(bf16[43,128,128]{2,1,0:T(8,128)(2,1)S(1)} %get-tuple-element.54), channel_id=1, source_target_pairs={{0,1},{1,0},{2,3},{3,2},{4,5},{5,4},{6,7},{7,6},{8,9},{9,8},{10,11... | collective-permute-start | bytes 4227080 | tf_op jit(solution)/shard_map/ppermute | solution.py:396
  9.7 8.1 %collective-permute-start.1 = (bf16[128,1024]{1,0:T(8,128)(2,1)S(1)}, bf16[128,1024]{1,0:T(8,128)(2,1)S(1)}, u32[]{:S(2)}, u32[]{:S(2)}) collective-permute-start(bf16[128,1024]{1,0:T(8,128)(2,1)S(1)} %get-tuple-element.49), channel_id=1, source_target_pairs={{0,4},{2,6},{4,0},{6,2},{8,12},{10,14},{12,8},{14,10},{16,20},{18,... | collective-permute-start | bytes 786440 | tf_op jit(solution)/shard_map/ppermute | solution.py:393
  18.4 5.0 %collective-permute-start.2 = (bf16[32,1024]{1,0:T(8,128)(2,1)S(1)}, bf16[32,1024]{1,0:T(8,128)(2,1)S(1)}, u32[]{:S(2)}, u32[]{:S(2)}) collective-permute-start(bf16[32,1024]{1,0:T(8,128)(2,1)S(1)} %get-tuple-element.51), channel_id=1, source_target_pairs={{0,8},{2,10},{4,12},{6,14},{8,0},{10,2},{12,4},{14,6},{16,24},{18,... | collective-permute-start | bytes 196616 | tf_op jit(solution)/shard_map/ppermute | solution.py:393
  20.0 6.6 %collective-permute-start.3 = (bf16[32,1024]{1,0:T(8,128)(2,1)S(1)}, bf16[32,1024]{1,0:T(8,128)(2,1)S(1)}, u32[]{:S(2)}, u32[]{:S(2)}) collective-permute-start(bf16[32,1024]{1,0:T(8,128)(2,1)S(1)} %get-tuple-element.52), channel_id=1, source_target_pairs={{0,16},{2,18},{4,20},{6,22},{8,24},{10,26},{12,28},{14,30},{16,0},... | collective-permute-start | bytes 196616 | tf_op jit(solution)/shard_map/ppermute | solution.py:393
  22.6 6.5 %collective-permute-start.4 = (bf16[32,1024]{1,0:T(8,128)(2,1)S(1)}, bf16[32,1024]{1,0:T(8,128)(2,1)S(1)}, u32[]{:S(2)}, u32[]{:S(2)}) collective-permute-start(bf16[32,1024]{1,0:T(8,128)(2,1)S(1)} %get-tuple-element.53), channel_id=1, source_target_pairs={{0,24},{2,26},{4,28},{6,30},{8,16},{10,18},{12,20},{14,22},{16,8},... | collective-permute-start | bytes 196616 | tf_op jit(solution)/shard_map/ppermute | solution.py:393
  29.1 4.5 %collective-permute-start.5 = (bf16[32,1024]{1,0:T(8,128)(2,1)S(1)}, bf16[32,1024]{1,0:T(8,128)(2,1)S(1)}, u32[]{:S(2)}, u32[]{:S(2)}) collective-permute-start(bf16[32,1024]{1,0:T(8,128)(2,1)S(1)} %shard_map.104.refs_0_), channel_id=1, source_target_pairs={{0,8},{2,10},{4,12},{6,14},{8,0},{10,2},{12,4},{14,6},{16,24},{18,... | collective-permute-start | bytes 196616 | tf_op jit(solution)/shard_map/ppermute | solution.py:393
  29.2 5.2 %collective-permute-start.6 = (bf16[32,1024]{1,0:T(8,128)(2,1)S(1)}, bf16[32,1024]{1,0:T(8,128)(2,1)S(1)}, u32[]{:S(2)}, u32[]{:S(2)}) collective-permute-start(bf16[32,1024]{1,0:T(8,128)(2,1)S(1)} %shard_map.104.refs_0_), channel_id=1, source_target_pairs={{0,16},{2,18},{4,20},{6,22},{8,24},{10,26},{12,28},{14,30},{16,0},... | collective-permute-start | bytes 196616 | tf_op jit(solution)/shard_map/ppermute | solution.py:393
  30.3 6.4 %collective-permute-start.7 = (bf16[32,1024]{1,0:T(8,128)(2,1)S(1)}, bf16[32,1024]{1,0:T(8,128)(2,1)S(1)}, u32[]{:S(2)}, u32[]{:S(2)}) collective-permute-start(bf16[32,1024]{1,0:T(8,128)(2,1)S(1)} %shard_map.104.refs_0_), channel_id=1, source_target_pairs={{0,24},{2,26},{4,28},{6,30},{8,16},{10,18},{12,20},{14,22},{16,8},... | collective-permute-start | bytes 196616 | tf_op jit(solution)/shard_map/ppermute | solution.py:393
  37.2 20.0 %copy-start.4 = (f32[512,1024]{1,0:T(8,128)S(1)}, f32[512,1024]{1,0:T(8,128)}, u32[]{:S(2)}) copy-start(f32[512,1024]{1,0:T(8,128)} %moment.1) | copy-start | bytes 6291460
  40.9 9.1 %collective-permute-start.9 = (bf16[43,128,128]{2,1,0:T(8,128)(2,1)S(1)}, bf16[43,128,128]{2,1,0:T(8,128)(2,1)S(1)}, u32[]{:S(2)}, u32[]{:S(2)}) collective-permute-start(bf16[43,128,128]{2,1,0:T(8,128)(2,1)S(1)} %collective-permute-done.8.mine), channel_id=1, source_target_pairs={{0,2},{2,0},{4,6},{6,4},{8,10},{10,8},{12,14},{14,12},{16,18},{18,... | collective-permute-start | bytes 4227080 | tf_op jit(solution)/shard_map/ppermute | solution.py:393
  40.9 9.1 %collective-permute-start.10 = (bf16[128,1024]{1,0:T(8,128)(2,1)S(1)}, bf16[128,1024]{1,0:T(8,128)(2,1)S(1)}, u32[]{:S(2)}, u32[]{:S(2)}) collective-permute-start(bf16[128,1024]{1,0:T(8,128)(2,1)S(1)} %shard_map.105.own.refs_0_), channel_id=1, source_target_pairs={{0,4},{2,6},{4,0},{6,2},{8,12},{10,14},{12,8},{14,10},{16,20},{18,... | collective-permute-start | bytes 786440 | tf_op jit(solution)/shard_map/ppermute | solution.py:393
  42.6 14.1 %collective-permute-start.13 = (bf16[128,1024]{1,0:T(8,128)(2,1)S(1)}, bf16[128,1024]{1,0:T(8,128)(2,1)S(1)}, u32[]{:S(2)}, u32[]{:S(2)}) collective-permute-start(bf16[128,1024]{1,0:T(8,128)(2,1)S(1)} %shard_map.105.own.refs_0_), channel_id=1, source_target_pairs={{0,1},{1,0},{2,3},{3,2},{4,5},{5,4},{6,7},{7,6},{8,9},{9,8},{10,11... | collective-permute-start | bytes 786440 | tf_op jit(solution)/shard_map/ppermute | solution.py:396
  44.1 12.5 %collective-permute-start.14 = (bf16[128,1024]{1,0:T(8,128)(2,1)S(1)}, bf16[128,1024]{1,0:T(8,128)(2,1)S(1)}, u32[]{:S(2)}, u32[]{:S(2)}) collective-permute-start(bf16[128,1024]{1,0:T(8,128)(2,1)S(1)} %shard_map.105.own.refs_0_), channel_id=1, source_target_pairs={{0,5},{1,4},{2,7},{3,6},{4,1},{5,0},{6,3},{7,2},{8,13},{9,12},{10,... | collective-permute-start | bytes 786440 | tf_op jit(solution)/shard_map/ppermute | solution.py:400
  44.4 12.8 %collective-permute-start.11 = (bf16[128,1024]{1,0:T(8,128)(2,1)S(1)}, bf16[128,1024]{1,0:T(8,128)(2,1)S(1)}, u32[]{:S(2)}, u32[]{:S(2)}) collective-permute-start(bf16[128,1024]{1,0:T(8,128)(2,1)S(1)} %shard_map.105.own.refs_0_), channel_id=1, source_target_pairs={{0,2},{2,0},{4,6},{6,4},{8,10},{10,8},{12,14},{14,12},{16,18},{18,... | collective-permute-start | bytes 786440 | tf_op jit(solution)/shard_map/ppermute | solution.py:393
  50.0 7.2 %collective-permute-start.12 = (bf16[128,1024]{1,0:T(8,128)(2,1)S(1)}, bf16[128,1024]{1,0:T(8,128)(2,1)S(1)}, u32[]{:S(2)}, u32[]{:S(2)}) collective-permute-start(bf16[128,1024]{1,0:T(8,128)(2,1)S(1)} %collective-permute-done.10.over_x.refs_1_), channel_id=1, source_target_pairs={{0,2},{2,0},{4,6},{6,4},{8,10},{10,8},{12,14},{14,12},{16,18},{18,... | collective-permute-start | bytes 786440 | tf_op jit(solution)/shard_map/ppermute | solution.py:393
  56.7 4.0 %copy-start.5 = (f32[1024,512]{1,0:T(8,128)S(1)}, f32[1024,512]{1,0:T(8,128)}, u32[]{:S(2)}) copy-start(f32[1024,512]{1,0:T(8,128)} %second.1) | copy-start | bytes 6291460
  56.7 4.0 %collective-permute-start.15 = (bf16[128,1024]{1,0:T(8,128)(2,1)S(1)}, bf16[128,1024]{1,0:T(8,128)(2,1)S(1)}, u32[]{:S(2)}, u32[]{:S(2)}) collective-permute-start(bf16[128,1024]{1,0:T(8,128)(2,1)S(1)} %collective-permute-done.13.refs_4_), channel_id=1, source_target_pairs={{0,2},{2,0},{4,6},{6,4},{8,10},{10,8},{12,14},{14,12},{16,18},{18,... | collective-permute-start | bytes 786440 | tf_op jit(solution)/shard_map/ppermute | solution.py:393
  56.7 4.0 %collective-permute-start.16 = (bf16[128,1024]{1,0:T(8,128)(2,1)S(1)}, bf16[128,1024]{1,0:T(8,128)(2,1)S(1)}, u32[]{:S(2)}, u32[]{:S(2)}) collective-permute-start(bf16[128,1024]{1,0:T(8,128)(2,1)S(1)} %collective-permute-done.14.refs_5_), channel_id=1, source_target_pairs={{0,2},{2,0},{4,6},{6,4},{8,10},{10,8},{12,14},{14,12},{16,18},{18,... | collective-permute-start | bytes 786440 | tf_op jit(solution)/shard_map/ppermute | solution.py:393
  59.1 8.4 %collective-permute-start.17 = (bf16[512,256]{1,0:T(8,128)(2,1)S(1)}, bf16[512,256]{1,0:T(8,128)(2,1)S(1)}, u32[]{:S(2)}, u32[]{:S(2)}) collective-permute-start(bf16[512,256]{1,0:T(8,128)(2,1)S(1)} %get-tuple-element.64), channel_id=1, source_target_pairs={{0,1},{1,0},{2,3},{3,2},{4,5},{5,4},{6,7},{7,6},{8,9},{9,8},{10,11... | collective-permute-start | bytes 786440 | tf_op jit(solution)/shard_map/ppermute | solution.py:396
  65.1 15.5 %collective-permute-start.20 = (f32[1024,256]{1,0:T(8,128)S(1)}, f32[1024,256]{1,0:T(8,128)S(1)}, u32[]{:S(2)}, u32[]{:S(2)}) collective-permute-start(f32[1024,256]{1,0:T(8,128)S(1)} %get-tuple-element.66.new), channel_id=1, source_target_pairs={{0,2},{2,0},{4,6},{6,4},{8,10},{10,8},{12,14},{14,12},{16,18},{18,... | collective-permute-start | bytes 3145736 | tf_op jit(solution)/shard_map/ppermute | solution.py:393
  70.3 10.3 %collective-permute-start.18 = (bf16[512,256]{1,0:T(8,128)(2,1)S(1)}, bf16[512,256]{1,0:T(8,128)(2,1)S(1)}, u32[]{:S(2)}, u32[]{:S(2)}) collective-permute-start(bf16[512,256]{1,0:T(8,128)(2,1)S(1)} %get-tuple-element.72), channel_id=1, source_target_pairs={{0,1},{1,0},{2,3},{3,2},{4,5},{5,4},{6,7},{7,6},{8,9},{9,8},{10,11... | collective-permute-start | bytes 786440 | tf_op jit(solution)/shard_map/ppermute | solution.py:396
  71.9 8.8 %collective-permute-start.19 = (bf16[512,256]{1,0:T(8,128)(2,1)S(1)}, bf16[512,256]{1,0:T(8,128)(2,1)S(1)}, u32[]{:S(2)}, u32[]{:S(2)}) collective-permute-start(bf16[512,256]{1,0:T(8,128)(2,1)S(1)} %get-tuple-element.67.kept), channel_id=1, source_target_pairs={{0,2},{2,0},{4,6},{6,4},{8,10},{10,8},{12,14},{14,12},{16,18},{18,... | collective-permute-start | bytes 786440 | tf_op jit(solution)/shard_map/ppermute | solution.py:393
  80.6 3.6 %collective-permute-start.21 = (bf16[512,256]{1,0:T(8,128)(2,1)S(1)}, bf16[512,256]{1,0:T(8,128)(2,1)S(1)}, u32[]{:S(2)}, u32[]{:S(2)}) collective-permute-start(bf16[512,256]{1,0:T(8,128)(2,1)S(1)} %collective-permute-done.18.came), channel_id=1, source_target_pairs={{0,2},{2,0},{4,6},{6,4},{8,10},{10,8},{12,14},{14,12},{16,18},{18,... | collective-permute-start | bytes 786440 | tf_op jit(solution)/shard_map/ppermute | solution.py:393
  81.2 3.5 %collective-permute-start.22 = (f32[256,1024]{1,0:T(8,128)S(1)}, f32[256,1024]{1,0:T(8,128)S(1)}, u32[]{:S(2)}, u32[]{:S(2)}) collective-permute-start(f32[256,1024]{1,0:T(8,128)S(1)} %get-tuple-element.77.top), channel_id=1, source_target_pairs={{0,2},{2,0},{4,6},{6,4},{8,10},{10,8},{12,14},{14,12},{16,18},{18,... | collective-permute-start | bytes 3145736 | tf_op jit(solution)/shard_map/ppermute | solution.py:393
  84.2 3.4 %collective-permute-start.23 = (f32[256,1024]{1,0:T(8,128)S(1)}, f32[256,1024]{1,0:T(8,128)S(1)}, u32[]{:S(2)}, u32[]{:S(2)}) collective-permute-start(f32[256,1024]{1,0:T(8,128)S(1)} %get-tuple-element.83.low), channel_id=1, source_target_pairs={{0,2},{2,0},{4,6},{6,4},{8,10},{10,8},{12,14},{14,12},{16,18},{18,... | collective-permute-start | bytes 3145736 | tf_op jit(solution)/shard_map/ppermute | solution.py:393

commit v10 on v9

--- a/solution.py
+++ b/solution.py
@@ -221,7 +221,7 @@
 
 
 def statistic_kernel(where, bases, turned, stat, second, *refs):
-    parts, (half, new, pair, sem) = refs[:-4], refs[-4:]
+    parts, (start, start_turned, new, pair, half, sem) = refs[:-6], refs[-6:]
     position, core, x = where[0], where[1], where[2]
     width = half.shape[0]
     step = new.shape[1]
@@ -244,6 +244,12 @@
         place_symmetric(half, here, value)
     grad_rot = matmul(turned[...], block.astype(HALF)) * (1.0 / width)
     new[...] = BETA_TWO * second[:, tile(core, step)] + (1.0 - BETA_TWO) * grad_rot * grad_rot
+    for here in quarters(width):
+        product = matmul(half[...], bases[0, :, here])
+        square = jnp.sum(product * product, axis=0, keepdims=True) * (1.0 / width)
+        value = (product * lax.rsqrt(square + NORM_EPS)).astype(HALF)
+        start[:, here] = value
+        start_turned[here] = value.T
 
 
 def adam_kernel(where, bases, turned, mine, came, new, kept, sent):
@@ -286,6 +292,7 @@
     left,
     right,
     rows_back,
+    product,
     sem,
 ):
     rows, width = out.shape
@@ -302,8 +309,10 @@
         (came_next, (1 - position) * 2 + 1 - core),
     ):
         rows_back[:, tile(place, step)] = value[...]
-    for here in quarters(width):
-        out[:, here] = (matmul(rows_back[...], back[:, here]) * (1.0 / width)).astype(HALF)
+    for i, here in enumerate(quarters(width)):
+        product[:, here] = (matmul(rows_back[...], back[:, here]) * (1.0 / width)).astype(HALF)
+        copies.append(pltpu.make_async_copy(product.at[:, here], out.at[:, here], sem.at[2 + i]))
+        copies[-1].start()
     for copy in copies:
         copy.wait()
 
@@ -337,19 +346,13 @@
 
 
 def refresh_kernel(
-    where, stat, bases, new, current, turned, out, second_new, start, start_turned, gram, *scratch
+    where, start, start_turned, new, current, turned, out, second_new, gram, *scratch
 ):
-    width = stat.shape[0]
+    width = start.shape[0]
     rows = width // 2
     between, sem = scratch[:-1], scratch[-1]
     copy = pltpu.make_async_copy(new, second_new.at[:, tile(where[1], new.shape[1])], sem)
     copy.start()
-    for here in quarters(width):
-        product = matmul(stat[...], bases[0, :, here])
-        square = jnp.sum(product * product, axis=0, keepdims=True) * (1.0 / width)
-        value = (product * lax.rsqrt(square + NORM_EPS)).astype(HALF)
-        start[:, here] = value
-        start_turned[here] = value.T
     source, source_turned = start, start_turned
     for iteration in range(NS_ITERS - 1):
         if iteration + 2 == NS_ITERS:
@@ -478,17 +481,21 @@
     moment_came = shard_swap(moment_sent)
     far = list(lax.optimization_barrier((parts[2], parts[3], bases)))[:2]
     far += [dp_swap(value, 1) for value in far]
-    stat, new = call(
+    start, start_turned, new = call(
         statistic_kernel,
-        [square, shaped((width, half), FULL)],
+        [square, square, shaped((width, half), FULL)],
         (where, bases, left_turned, stat, second, *near, *far),
         [SMEM] + [VMEM] * 4 + [ANY] * 8,
-        [pltpu.VMEM((2, width, width), HALF), pltpu.SemaphoreType.DMA((8,))],
+        [
+            pltpu.VMEM((2, width, width), HALF),
+            pltpu.VMEM((width, width), HALF),
+            pltpu.SemaphoreType.DMA((8,)),
+        ],
         flops=3 * unit // 2,
         moved=2**23,
     )
     new_next = dp_swap(new, 1)
-    stat, moment_came = lax.optimization_barrier((stat, moment_came))
+    start, moment_came = lax.optimization_barrier((start, moment_came))
     back_kept, back_sent = call(
         adam_kernel,
         [shaped((rows, half), HALF)] * 2,
@@ -497,7 +504,7 @@
         flops=unit // 2,
         moved=2**22,
     )
-    stat, back_sent = lax.optimization_barrier((stat, back_sent))
+    start, back_sent = lax.optimization_barrier((start, back_sent))
     back_came = shard_swap(back_sent)
     back_kept_next = dp_swap(back_kept, 1)
     current, current_turned, top, second_new = pl.pallas_call(
@@ -505,14 +512,14 @@
         out_shape=[square, square, shaped((half, width), FULL), shaped((width, rows), FULL)],
         in_specs=[SMEM] + [VMEM] * 2 + [ANY],
         out_specs=[VMEM] * 3 + [ANY],
-        scratch_shapes=[pltpu.VMEM((width, width), HALF)] * 3
+        scratch_shapes=[pltpu.VMEM((width, width), HALF)]
         + [pltpu.VMEM((2, width, width), HALF)] * (2 if NS_ITERS > 2 else 0)
         + [pltpu.SemaphoreType.DMA(())],
         compiler_params=pltpu.CompilerParams(vmem_limit_bytes=24 * 2**20),
         cost_estimate=pl.CostEstimate(
-            flops=7 * unit // 2, bytes_accessed=2**23, transcendentals=0
+            flops=6 * unit, bytes_accessed=2**23, transcendentals=0
         ),
-    )(where, stat, bases, new)
+    )(where, start, start_turned, new)
     top_next = dp_swap(top, 1)
     current, back_came, back_kept_next, new_next = lax.optimization_barrier(
         (current, back_came, back_kept_next, new_next)
@@ -535,8 +542,8 @@
         update_kernel,
         out_shape=[shaped((rows, width), HALF), side, side],
         in_specs=[SMEM] + [VMEM] * 5 + [ANY] * 4,
-        out_specs=[VMEM] + [ANY] * 2,
-        scratch_shapes=[pltpu.VMEM((rows, width), HALF), pltpu.SemaphoreType.DMA((2,))],
+        out_specs=[ANY] * 3,
+        scratch_shapes=[pltpu.VMEM((rows, width), HALF)] * 2 + [pltpu.SemaphoreType.DMA((6,))],
         input_output_aliases={8: 1, 9: 2},
         compiler_params=pltpu.CompilerParams(vmem_limit_bytes=24 * 2**20),
         cost_estimate=pl.CostEstimate(flops=unit // 2, bytes_accessed=2**22, transcendentals=0),

time: 89.5 us -> 88.4 us (0.988)
  starting transfers between devices: 22.3 us -> 20.6 us
    ppermute x1, waiting for transfers between devices: 0.01 us -> 3.26 us  [cross_swap(): return lax.ppermute(value, ('dp', 'shard'), pairs)]
    pallas_call x9, Pallas kernels: 17.9 us -> 20.9 us  [call(): pl.pallas_call(kernel, out_shape=outs, in_specs=specs, out_specs=[space]...]
    ppermute x4, waiting for transfers between devices: 9.3 us -> 6.44 us  [shard_swap(): return lax.ppermute(value, 'shard', [(0, 1), (1, 0)])]
    ppermute x4, starting transfers between devices: 7.65 us -> 5.07 us  [shard_swap(): return lax.ppermute(value, 'shard', [(0, 1), (1, 0)])]
    pallas_call x1, Pallas kernels: 8.75 us -> 6.49 us  [fast_body(): pl.pallas_call(refresh_kernel, out_shape=[square, square, shaped((half, w...]
    ppermute x1, starting transfers between devices: 0.26 us -> 1.49 us  [cross_swap(): return lax.ppermute(value, ('dp', 'shard'), pairs)]
  transfers between devices with their start and end apart: 24 -> 24, of which waited for: 11 -> 13; matrix products, arithmetic and copies ran while one was open for 0% -> 0% of each run, Pallas kernels for 32% -> 33%
where the time goes in v10:
time: 88.4 us; the launch traced here: 88.3 us
  Pallas kernels  33.1 us (37%)
  waiting for transfers between devices  32.3 us (37%)
  starting transfers between devices  20.6 us (23%)
  local copies, waits for them, and re-layouts  1.3 us (1%)
  between operations  0.97 us (1%)
    ppermute x19, waiting for transfers between devices, dp_swap(): return lax.ppermute(value, 'dp', [(i, i ^ distance) for i in range(16)])  22.6 us
    pallas_call x9, Pallas kernels, call(): pl.pallas_call(kernel, out_shape=outs, in_specs=specs, out_specs=[space]...  20.9 us
    ppermute x19, starting transfers between devices, dp_swap(): return lax.ppermute(value, 'dp', [(i, i ^ distance) for i in range(16)])  14 us
    pallas_call x1, Pallas kernels, fast_body(): pl.pallas_call(refresh_kernel, out_shape=[square, square, shaped((half, w...  6.49 us
    ppermute x4, waiting for transfers between devices, shard_swap(): return lax.ppermute(value, 'shard', [(0, 1), (1, 0)])  6.44 us
    ppermute x4, starting transfers between devices, shard_swap(): return lax.ppermute(value, 'shard', [(0, 1), (1, 0)])  5.07 us
    ppermute x1, waiting for transfers between devices, cross_swap(): return lax.ppermute(value, ('dp', 'shard'), pairs)  3.26 us
    pallas_call x1, Pallas kernels, fast_body(): pl.pallas_call(last_kernel, out_shape=[shaped((half, width), FULL), side,...  2.91 us
  transfers between devices with their start and end apart: 24, of which 13 were waited for; matrix products, arithmetic and copies ran while one was open for 0% of the time, Pallas kernels for 33%

profile of v10, /device:TPU:0, one launch (start us, length us, event | category | flops | bytes accessed | tf_op | source)
XLA Modules:
  0.0 88.3 jit_solution(17653648442201295978)
XLA Ops:
  0.6 1.3 %dynamic-slice_bitcast_fusion = (bf16[256,1024]{1,0:T(8,128)(2,1)S(1)}, bf16[256,1024]{1,0:T(8,128)(2,1)S(1)}) fusion(bf16[1,512,1024]{2,1,0:T(8,128)(2,1)} %param.7, s32[]{:T(128)S(6)} %select_n.7, s32[]{:T(128)S(6)} %select_n.6), kind=kLoop, calls=%fused_computation | loop fusion | bytes 2097160 | tf_op jit(solution)/shard_map/dynamic_slice | solution.py:405
  1.9 0.5 collective-permute-start
  2.4 0.1 pad_add_fusion.where
  2.5 1.5 %collective-permute-done.came = bf16[256,1024]{1,0:T(8,128)(2,1)S(1)} collective-permute-done((bf16[256,1024]{1,0:T(8,128)(2,1)S(1)}, bf16[256,1024]{1,0:T(8,128)(2,1)S(1)}, u32[]{:S(2)}, u32[]{:S(2)}) %collective-permute-start) | collective-permute-done | bytes 524320 | tf_op jit(solution)/shard_map/ppermute | solution.py:396
  4.0 2.8 %shard_map.102 = (bf16[43,128,128]{2,1,0:T(8,128)(2,1)S(1)}, f32[128,1024]{1,0:T(8,128)S(1)}, bf16[128,1024]{1,0:T(8,128)(2,1)S(1)}) custom-call(s32[4]{0:T(128)S(1)} %pad_add_fusion.where, bf16[256,1024]{1,0:T(8,128)(2,1)S(1)} %get-tuple-element.95.raw, bf16[256,1024]{1,0:T(8,128)(2,1)S(1)} %collective-permute-done.came, f32[512,1024]{1,0:T(8,128)} %left.3, ...), custom_call_target="tpu_custom_call" | custom-call | bytes 4194304 | tf_op jit(solution)/shard_map/pallas_call | solution.py:43
  6.8 3.0 %collective-permute-start.8 = (bf16[43,128,128]{2,1,0:T(8,128)(2,1)S(1)}, bf16[43,128,128]{2,1,0:T(8,128)(2,1)S(1)}, u32[]{:S(2)}, u32[]{:S(2)}) collective-permute-start(bf16[43,128,128]{2,1,0:T(8,128)(2,1)S(1)} %get-tuple-element.55), channel_id=1, source_target_pairs={{0,1},{1,0},{2,3},{3,2},{4,5},{5,4},{6,7},{7,6},{8,9},{9,8},{10,11... | collective-permute-start | bytes 4227080 | tf_op jit(solution)/shard_map/ppermute | solution.py:399
  9.7 1.5 %collective-permute-start.1 = (bf16[128,1024]{1,0:T(8,128)(2,1)S(1)}, bf16[128,1024]{1,0:T(8,128)(2,1)S(1)}, u32[]{:S(2)}, u32[]{:S(2)}) collective-permute-start(bf16[128,1024]{1,0:T(8,128)(2,1)S(1)} %get-tuple-element.50), channel_id=1, source_target_pairs={{0,4},{2,6},{4,0},{6,2},{8,12},{10,14},{12,8},{14,10},{16,20},{18,... | collective-permute-start | bytes 786440 | tf_op jit(solution)/shard_map/ppermute | solution.py:396
  11.2 6.6 %collective-permute-done.1.came = bf16[128,1024]{1,0:T(8,128)(2,1)S(1)} collective-permute-done((bf16[128,1024]{1,0:T(8,128)(2,1)S(1)}, bf16[128,1024]{1,0:T(8,128)(2,1)S(1)}, u32[]{:S(2)}, u32[]{:S(2)}) %collective-permute-start.1) | collective-permute-done | bytes 262176 | tf_op jit(solution)/shard_map/ppermute | solution.py:396
  17.8 0.6 shard_map.103
  18.4 1.6 %collective-permute-start.2 = (bf16[32,1024]{1,0:T(8,128)(2,1)S(1)}, bf16[32,1024]{1,0:T(8,128)(2,1)S(1)}, u32[]{:S(2)}, u32[]{:S(2)}) collective-permute-start(bf16[32,1024]{1,0:T(8,128)(2,1)S(1)} %get-tuple-element.52), channel_id=1, source_target_pairs={{0,8},{2,10},{4,12},{6,14},{8,0},{10,2},{12,4},{14,6},{16,24},{18,... | collective-permute-start | bytes 196616 | tf_op jit(solution)/shard_map/ppermute | solution.py:396
  20.0 2.6 %collective-permute-start.3 = (bf16[32,1024]{1,0:T(8,128)(2,1)S(1)}, bf16[32,1024]{1,0:T(8,128)(2,1)S(1)}, u32[]{:S(2)}, u32[]{:S(2)}) collective-permute-start(bf16[32,1024]{1,0:T(8,128)(2,1)S(1)} %get-tuple-element.53), channel_id=1, source_target_pairs={{0,16},{2,18},{4,20},{6,22},{8,24},{10,26},{12,28},{14,30},{16,0},... | collective-permute-start | bytes 196616 | tf_op jit(solution)/shard_map/ppermute | solution.py:396
  22.6 0.2 collective-permute-start.4
  22.8 0.5 collective-permute-done.2.one
  23.3 3.2 %collective-permute-done.3.two = bf16[32,1024]{1,0:T(8,128)(2,1)S(1)} collective-permute-done((bf16[32,1024]{1,0:T(8,128)(2,1)S(1)}, bf16[32,1024]{1,0:T(8,128)(2,1)S(1)}, u32[]{:S(2)}, u32[]{:S(2)}) %collective-permute-start.3) | collective-permute-done | bytes 65568 | tf_op jit(solution)/shard_map/ppermute | solution.py:396
  26.6 2.1 %collective-permute-done.4.three = bf16[32,1024]{1,0:T(8,128)(2,1)S(1)} collective-permute-done((bf16[32,1024]{1,0:T(8,128)(2,1)S(1)}, bf16[32,1024]{1,0:T(8,128)(2,1)S(1)}, u32[]{:S(2)}, u32[]{:S(2)}) %collective-permute-start.4) | collective-permute-done | bytes 65568 | tf_op jit(solution)/shard_map/ppermute | solution.py:396
  28.7 1.1 %collective-permute-start.7 = (bf16[32,1024]{1,0:T(8,128)(2,1)S(1)}, bf16[32,1024]{1,0:T(8,128)(2,1)S(1)}, u32[]{:S(2)}, u32[]{:S(2)}) collective-permute-start(bf16[32,1024]{1,0:T(8,128)(2,1)S(1)} %shard_map.104.refs_0_), channel_id=1, source_target_pairs={{0,24},{2,26},{4,28},{6,30},{8,16},{10,18},{12,20},{14,22},{16,8},... | collective-permute-start | bytes 196616 | tf_op jit(solution)/shard_map/ppermute | solution.py:396
  29.8 0.4 collective-permute-start.6
  30.3 2.9 %collective-permute-start.5 = (bf16[32,1024]{1,0:T(8,128)(2,1)S(1)}, bf16[32,1024]{1,0:T(8,128)(2,1)S(1)}, u32[]{:S(2)}, u32[]{:S(2)}) collective-permute-start(bf16[32,1024]{1,0:T(8,128)(2,1)S(1)} %shard_map.104.refs_0_), channel_id=1, source_target_pairs={{0,8},{2,10},{4,12},{6,14},{8,0},{10,2},{12,4},{14,6},{16,24},{18,... | collective-permute-start | bytes 196616 | tf_op jit(solution)/shard_map/ppermute | solution.py:396
  33.2 1.7 %collective-permute-done.7.refs_3_ = bf16[32,1024]{1,0:T(8,128)(2,1)S(1)} collective-permute-done((bf16[32,1024]{1,0:T(8,128)(2,1)S(1)}, bf16[32,1024]{1,0:T(8,128)(2,1)S(1)}, u32[]{:S(2)}, u32[]{:S(2)}) %collective-permute-start.7) | collective-permute-done | bytes 65568 | tf_op jit(solution)/shard_map/ppermute | solution.py:396
  34.9 1.3 %collective-permute-done.6.refs_2_ = bf16[32,1024]{1,0:T(8,128)(2,1)S(1)} collective-permute-done((bf16[32,1024]{1,0:T(8,128)(2,1)S(1)}, bf16[32,1024]{1,0:T(8,128)(2,1)S(1)}, u32[]{:S(2)}, u32[]{:S(2)}) %collective-permute-start.6) | collective-permute-done | bytes 65568 | tf_op jit(solution)/shard_map/ppermute | solution.py:396
  36.3 0.0 collective-permute-done.5.refs_1_
  36.3 0.6 shard_map.105.own.refs_0_
  36.8 0.0 copy-start.4
  36.8 4.0 %collective-permute-done.8.mine = bf16[43,128,128]{2,1,0:T(8,128)(2,1)S(1)} collective-permute-done((bf16[43,128,128]{2,1,0:T(8,128)(2,1)S(1)}, bf16[43,128,128]{2,1,0:T(8,128)(2,1)S(1)}, u32[]{:S(2)}, u32[]{:S(2)}) %collective-permute-start.8) | collective-permute-done | bytes 1409056 | tf_op jit(solution)/shard_map/ppermute | solution.py:399
  40.9 0.0 collective-permute-start.9
  40.9 1.7 %collective-permute-start.10 = (bf16[128,1024]{1,0:T(8,128)(2,1)S(1)}, bf16[128,1024]{1,0:T(8,128)(2,1)S(1)}, u32[]{:S(2)}, u32[]{:S(2)}) collective-permute-start(bf16[128,1024]{1,0:T(8,128)(2,1)S(1)} %shard_map.105.own.refs_0_), channel_id=1, source_target_pairs={{0,4},{2,6},{4,0},{6,2},{8,12},{10,14},{12,8},{14,10},{16,20},{18,... | collective-permute-start | bytes 786440 | tf_op jit(solution)/shard_map/ppermute | solution.py:396
  42.6 1.5 %collective-permute-start.14 = (bf16[128,1024]{1,0:T(8,128)(2,1)S(1)}, bf16[128,1024]{1,0:T(8,128)(2,1)S(1)}, u32[]{:S(2)}, u32[]{:S(2)}) collective-permute-start(bf16[128,1024]{1,0:T(8,128)(2,1)S(1)} %shard_map.105.own.refs_0_), channel_id=1, source_target_pairs={{0,5},{1,4},{2,7},{3,6},{4,1},{5,0},{6,3},{7,2},{8,13},{9,12},{10,... | collective-permute-start | bytes 786440 | tf_op jit(solution)/shard_map/ppermute | solution.py:403
  44.1 0.3 collective-permute-start.13
  44.4 0.0 collective-permute-start.11
  44.4 5.6 %collective-permute-done.10.over_x.refs_1_ = bf16[128,1024]{1,0:T(8,128)(2,1)S(1)} collective-permute-done((bf16[128,1024]{1,0:T(8,128)(2,1)S(1)}, bf16[128,1024]{1,0:T(8,128)(2,1)S(1)}, u32[]{:S(2)}, u32[]{:S(2)}) %collective-permute-start.10) | collective-permute-done | bytes 262176 | tf_op jit(solution)/shard_map/ppermute | solution.py:396
  50.0 0.0 collective-permute-start.12
  50.0 0.0 collective-permute-done.9.theirs
  50.0 0.0 copy-done
  50.0 3.2 %shard_map.106 = (bf16[2,1024,1024]{2,1,0:T(8,128)(2,1)S(1)}, bf16[1024,1024]{1,0:T(8,128)(2,1)S(1)}, bf16[1024,1024]{1,0:T(8,128)(2,1)S(1)}, f32[1024,1024]{1,0:T(8,128)S(1)}) custom-call(s32[4]{0:T(128)S(1)} %pad_add_fusion.where, f32[512,1024]{1,0:T(8,128)S(1)} %copy-done, f32[512,1024]{1,0:T(8,128)S(1)} %copy-done.1, ...), custom_call_target="tpu_custom_call" | custom-call | bytes 16777216 | tf_op jit(solution)/shard_map/pallas_call | solution.py:43
  53.2 3.3 %collective-permute-done.14.refs_5_ = bf16[128,1024]{1,0:T(8,128)(2,1)S(1)} collective-permute-done((bf16[128,1024]{1,0:T(8,128)(2,1)S(1)}, bf16[128,1024]{1,0:T(8,128)(2,1)S(1)}, u32[]{:S(2)}, u32[]{:S(2)}) %collective-permute-start.14) | collective-permute-done | bytes 262176 | tf_op jit(solution)/shard_map/ppermute | solution.py:403
  56.5 1.4 %collective-permute-done.13.refs_4_ = bf16[128,1024]{1,0:T(8,128)(2,1)S(1)} collective-permute-done((bf16[128,1024]{1,0:T(8,128)(2,1)S(1)}, bf16[128,1024]{1,0:T(8,128)(2,1)S(1)}, u32[]{:S(2)}, u32[]{:S(2)}) %collective-permute-start.13) | collective-permute-done | bytes 262176 | tf_op jit(solution)/shard_map/ppermute | solution.py:399
  57.9 0.0 collective-permute-start.15
  57.9 0.5 collective-permute-start.16
  58.4 0.0 collective-permute-done.11.next_own.refs_2_
  58.4 0.0 collective-permute-done.12.next_over_x.refs_3_
  58.4 0.0 copy-done.4
  58.4 1.9 %shard_map.107 = (bf16[512,256]{1,0:T(8,128)(2,1)S(1)}, bf16[512,256]{1,0:T(8,128)(2,1)S(1)}) custom-call(s32[4]{0:T(128)S(1)} %pad_add_fusion.where, f32[512,1024]{1,0:T(8,128)S(1)} %copy-done.4, bf16[2,1024,1024]{2,1,0:T(8,128)(2,1)S(1)} %get-tuple-element.57.bases, bf16[128,1024]{1,0:T(8,128)(2,1)S(1)} %shard_map.105.own.refs_0_, ...), custom_call_target="tpu_custom_call" | custom-call | flops 536870912 | bytes 4194304 | tf_op jit(solution)/shard_map/pallas_call | solution.py:43
  60.3 0.4 collective-permute-start.17
  60.6 0.0 collective-permute-done.15.refs_6_
  60.7 0.0 collective-permute-done.16.refs_7_
  60.7 7.5 %shard_map.108 = (bf16[1024,1024]{1,0:T(8,128)(2,1)S(1)}, bf16[1024,1024]{1,0:T(8,128)(2,1)S(1)}, f32[1024,256]{1,0:T(8,128)S(1)}) custom-call(s32[4]{0:T(128)S(1)} %pad_add_fusion.where, bf16[2,1024,1024]{2,1,0:T(8,128)(2,1)S(1)} %get-tuple-element.57.bases, bf16[1024,1024]{1,0:T(8,128)(2,1)S(1)} %get-tuple-element.58.turned, ...), custom_call_target="tpu_custom_call" | custom-call | flops 3221225472 | bytes 8388608 | tf_op jit(solution)/shard_map/pallas_call | solution.py:43
  68.1 0.4 collective-permute-done.17.came
  68.6 0.0 collective-permute-start.20
  68.6 2.8 %shard_map.109 = (bf16[512,256]{1,0:T(8,128)(2,1)S(1)}, bf16[512,256]{1,0:T(8,128)(2,1)S(1)}) custom-call(s32[4]{0:T(128)S(1)} %pad_add_fusion.where, bf16[2,1024,1024]{2,1,0:T(8,128)(2,1)S(1)} %get-tuple-element.57.bases, bf16[1024,1024]{1,0:T(8,128)(2,1)S(1)} %get-tuple-element.58.turned, bf16[512,256]{1,0:T(8,128)(2,1)S(1)} %get-tuple-element.60.mine, ...), custom_call_target="tpu_custom_call" | custom-call | flops 1073741824 | bytes 4194304 | tf_op jit(solution)/shard_map/pallas_call | solution.py:43
  71.4 1.5 %collective-permute-start.18 = (bf16[512,256]{1,0:T(8,128)(2,1)S(1)}, bf16[512,256]{1,0:T(8,128)(2,1)S(1)}, u32[]{:S(2)}, u32[]{:S(2)}) collective-permute-start(bf16[512,256]{1,0:T(8,128)(2,1)S(1)} %get-tuple-element.74), channel_id=1, source_target_pairs={{0,1},{1,0},{2,3},{3,2},{4,5},{5,4},{6,7},{7,6},{8,9},{9,8},{10,11... | collective-permute-start | bytes 786440 | tf_op jit(solution)/shard_map/ppermute | solution.py:399
  72.9 0.2 collective-permute-start.19
  73.1 6.5 %shard_map.110 = (bf16[1024,1024]{1,0:T(8,128)(2,1)S(1)}, bf16[1024,1024]{1,0:T(8,128)(2,1)S(1)}, f32[256,1024]{1,0:T(8,128)S(1)}, f32[1024,512]{1,0:T(8,128)}) custom-call(s32[4]{0:T(128)S(1)} %pad_add_fusion.where, bf16[1024,1024]{1,0:T(8,128)(2,1)S(1)} %get-tuple-element.71.start, bf16[1024,1024]{1,0:T(8,128)(2,1)S(1)} %get-tuple-element.72.start_turned, ...), custom_call_target="tpu_custom_call" | custom-call | flops 12884901888 | bytes 8388608 | tf_op jit(solution)/shard_map/pallas_call | solution.py:510
  79.6 0.6 collective-permute-done.18.came
  80.2 0.0 collective-permute-done.19.kept_next
  80.2 0.0 collective-permute-done.20.new_next
  80.2 0.0 collective-permute-start.21
  80.2 0.5 collective-permute-start.22
  80.7 2.9 %shard_map.111 = (f32[256,1024]{1,0:T(8,128)S(1)}, f32[512,1024]{1,0:T(8,128)}, f32[512,1024]{1,0:T(8,128)}, f32[1024,512]{1,0:T(8,128)}) custom-call(s32[4]{0:T(128)S(1)} %pad_add_fusion.where, bf16[1024,1024]{1,0:T(8,128)(2,1)S(1)} %get-tuple-element.77.current, bf16[1024,1024]{1,0:T(8,128)(2,1)S(1)} %get-tuple-element.78.turned, ...), custom_call_target="tpu_custom_call", output_to_operand_aliasing={{3}: (5, {})} | custom-call | flops 1073741824 | bytes 4194304 | tf_op jit(solution)/shard_map/pallas_call | solution.py:529
  83.6 0.0 collective-permute-done.21.came_next
  83.6 0.1 collective-permute-start.23
  83.8 0.0 collective-permute-done.22.top_next
  83.8 2.8 %shard_map.112 = (bf16[512,1024]{1,0:T(8,128)(2,1)}, f32[512,1024]{1,0:T(8,128)}, f32[512,1024]{1,0:T(8,128)}) custom-call(s32[4]{0:T(128)S(1)} %pad_add_fusion.where, bf16[512,256]{1,0:T(8,128)(2,1)S(1)} %get-tuple-element.68.kept, bf16[512,256]{1,0:T(8,128)(2,1)S(1)} %collective-permute-done.18.came, ...), custom_call_target="tpu_custom_call", output_to_operand_aliasing={{1}: (8, {}), {2}: (9, {})} | custom-call | flops 1073741824 | bytes 4194304 | tf_op jit(solution)/shard_map/pallas_call | solution.py:541
  86.6 0.0 collective-permute-done.23.low
  86.6 1.5 %shard_map.113 = (f32[512,1024]{1,0:T(8,128)}, f32[512,1024]{1,0:T(8,128)}) custom-call(s32[4]{0:T(128)S(1)} %pad_add_fusion.where, f32[256,1024]{1,0:T(8,128)S(1)} %collective-permute-done.23.low, f32[512,1024]{1,0:T(8,128)} %get-tuple-element.90.left_in, f32[512,1024]{1,0:T(8,128)} %get-tuple-element.91.right_in), custom_call_target="tpu_custom_call", output_to_operand_aliasing={{0}: (2, {}), {1}: (3, {})} | custom-call | bytes 2097152 | tf_op jit(solution)/shard_map/pallas_call | solution.py:43
  (10 shorter events, 0.0 us)
Async XLA Ops:
  1.9 2.1 %collective-permute-start = (bf16[256,1024]{1,0:T(8,128)(2,1)S(1)}, bf16[256,1024]{1,0:T(8,128)(2,1)S(1)}, u32[]{:S(2)}, u32[]{:S(2)}) collective-permute-start(bf16[256,1024]{1,0:T(8,128)(2,1)S(1)} %get-tuple-element.94), channel_id=1, source_target_pairs={{0,2},{2,0},{4,6},{6,4},{8,10},{10,8},{12,14},{14,12},{16,18},{18,... | collective-permute-start | bytes 1572872 | tf_op jit(solution)/shard_map/ppermute | solution.py:396
  4.0 46.0 %copy-start = (f32[512,1024]{1,0:T(8,128)S(1)}, f32[512,1024]{1,0:T(8,128)}, u32[]{:S(2)}) copy-start(f32[512,1024]{1,0:T(8,128)} %left.3) | copy-start | bytes 6291460
  4.0 46.0 %copy-start.1 = (f32[512,1024]{1,0:T(8,128)S(1)}, f32[512,1024]{1,0:T(8,128)}, u32[]{:S(2)}) copy-start(f32[512,1024]{1,0:T(8,128)} %right.3) | copy-start | bytes 6291460
  4.0 46.0 %copy-start.2 = (f32[512,1024]{1,0:T(8,128)S(1)}, f32[512,1024]{1,0:T(8,128)}, u32[]{:S(2)}) copy-start(f32[512,1024]{1,0:T(8,128)} %stat_left.3) | copy-start | bytes 6291460
  4.0 46.1 %copy-start.3 = (f32[512,1024]{1,0:T(8,128)S(1)}, f32[512,1024]{1,0:T(8,128)}, u32[]{:S(2)}) copy-start(f32[512,1024]{1,0:T(8,128)} %stat_right.3) | copy-start | bytes 6291460
  6.8 34.1 %collective-permute-start.8 = (bf16[43,128,128]{2,1,0:T(8,128)(2,1)S(1)}, bf16[43,128,128]{2,1,0:T(8,128)(2,1)S(1)}, u32[]{:S(2)}, u32[]{:S(2)}) collective-permute-start(bf16[43,128,128]{2,1,0:T(8,128)(2,1)S(1)} %get-tuple-element.55), channel_id=1, source_target_pairs={{0,1},{1,0},{2,3},{3,2},{4,5},{5,4},{6,7},{7,6},{8,9},{9,8},{10,11... | collective-permute-start | bytes 4227080 | tf_op jit(solution)/shard_map/ppermute | solution.py:399
  9.7 8.1 %collective-permute-start.1 = (bf16[128,1024]{1,0:T(8,128)(2,1)S(1)}, bf16[128,1024]{1,0:T(8,128)(2,1)S(1)}, u32[]{:S(2)}, u32[]{:S(2)}) collective-permute-start(bf16[128,1024]{1,0:T(8,128)(2,1)S(1)} %get-tuple-element.50), channel_id=1, source_target_pairs={{0,4},{2,6},{4,0},{6,2},{8,12},{10,14},{12,8},{14,10},{16,20},{18,... | collective-permute-start | bytes 786440 | tf_op jit(solution)/shard_map/ppermute | solution.py:396
  18.4 5.0 %collective-permute-start.2 = (bf16[32,1024]{1,0:T(8,128)(2,1)S(1)}, bf16[32,1024]{1,0:T(8,128)(2,1)S(1)}, u32[]{:S(2)}, u32[]{:S(2)}) collective-permute-start(bf16[32,1024]{1,0:T(8,128)(2,1)S(1)} %get-tuple-element.52), channel_id=1, source_target_pairs={{0,8},{2,10},{4,12},{6,14},{8,0},{10,2},{12,4},{14,6},{16,24},{18,... | collective-permute-start | bytes 196616 | tf_op jit(solution)/shard_map/ppermute | solution.py:396
  20.0 6.6 %collective-permute-start.3 = (bf16[32,1024]{1,0:T(8,128)(2,1)S(1)}, bf16[32,1024]{1,0:T(8,128)(2,1)S(1)}, u32[]{:S(2)}, u32[]{:S(2)}) collective-permute-start(bf16[32,1024]{1,0:T(8,128)(2,1)S(1)} %get-tuple-element.53), channel_id=1, source_target_pairs={{0,16},{2,18},{4,20},{6,22},{8,24},{10,26},{12,28},{14,30},{16,0},... | collective-permute-start | bytes 196616 | tf_op jit(solution)/shard_map/ppermute | solution.py:396
  22.6 6.1 %collective-permute-start.4 = (bf16[32,1024]{1,0:T(8,128)(2,1)S(1)}, bf16[32,1024]{1,0:T(8,128)(2,1)S(1)}, u32[]{:S(2)}, u32[]{:S(2)}) collective-permute-start(bf16[32,1024]{1,0:T(8,128)(2,1)S(1)} %get-tuple-element.54), channel_id=1, source_target_pairs={{0,24},{2,26},{4,28},{6,30},{8,16},{10,18},{12,20},{14,22},{16,8},... | collective-permute-start | bytes 196616 | tf_op jit(solution)/shard_map/ppermute | solution.py:396
  28.7 6.2 %collective-permute-start.7 = (bf16[32,1024]{1,0:T(8,128)(2,1)S(1)}, bf16[32,1024]{1,0:T(8,128)(2,1)S(1)}, u32[]{:S(2)}, u32[]{:S(2)}) collective-permute-start(bf16[32,1024]{1,0:T(8,128)(2,1)S(1)} %shard_map.104.refs_0_), channel_id=1, source_target_pairs={{0,24},{2,26},{4,28},{6,30},{8,16},{10,18},{12,20},{14,22},{16,8},... | collective-permute-start | bytes 196616 | tf_op jit(solution)/shard_map/ppermute | solution.py:396
  29.8 6.4 %collective-permute-start.6 = (bf16[32,1024]{1,0:T(8,128)(2,1)S(1)}, bf16[32,1024]{1,0:T(8,128)(2,1)S(1)}, u32[]{:S(2)}, u32[]{:S(2)}) collective-permute-start(bf16[32,1024]{1,0:T(8,128)(2,1)S(1)} %shard_map.104.refs_0_), channel_id=1, source_target_pairs={{0,16},{2,18},{4,20},{6,22},{8,24},{10,26},{12,28},{14,30},{16,0},... | collective-permute-start | bytes 196616 | tf_op jit(solution)/shard_map/ppermute | solution.py:396
  30.3 6.0 %collective-permute-start.5 = (bf16[32,1024]{1,0:T(8,128)(2,1)S(1)}, bf16[32,1024]{1,0:T(8,128)(2,1)S(1)}, u32[]{:S(2)}, u32[]{:S(2)}) collective-permute-start(bf16[32,1024]{1,0:T(8,128)(2,1)S(1)} %shard_map.104.refs_0_), channel_id=1, source_target_pairs={{0,8},{2,10},{4,12},{6,14},{8,0},{10,2},{12,4},{14,6},{16,24},{18,... | collective-permute-start | bytes 196616 | tf_op jit(solution)/shard_map/ppermute | solution.py:396
  36.8 21.6 %copy-start.4 = (f32[512,1024]{1,0:T(8,128)S(1)}, f32[512,1024]{1,0:T(8,128)}, u32[]{:S(2)}) copy-start(f32[512,1024]{1,0:T(8,128)} %moment.1) | copy-start | bytes 6291460
  40.9 9.1 %collective-permute-start.9 = (bf16[43,128,128]{2,1,0:T(8,128)(2,1)S(1)}, bf16[43,128,128]{2,1,0:T(8,128)(2,1)S(1)}, u32[]{:S(2)}, u32[]{:S(2)}) collective-permute-start(bf16[43,128,128]{2,1,0:T(8,128)(2,1)S(1)} %collective-permute-done.8.mine), channel_id=1, source_target_pairs={{0,2},{2,0},{4,6},{6,4},{8,10},{10,8},{12,14},{14,12},{16,18},{18,... | collective-permute-start | bytes 4227080 | tf_op jit(solution)/shard_map/ppermute | solution.py:396
  40.9 9.1 %collective-permute-start.10 = (bf16[128,1024]{1,0:T(8,128)(2,1)S(1)}, bf16[128,1024]{1,0:T(8,128)(2,1)S(1)}, u32[]{:S(2)}, u32[]{:S(2)}) collective-permute-start(bf16[128,1024]{1,0:T(8,128)(2,1)S(1)} %shard_map.105.own.refs_0_), channel_id=1, source_target_pairs={{0,4},{2,6},{4,0},{6,2},{8,12},{10,14},{12,8},{14,10},{16,20},{18,... | collective-permute-start | bytes 786440 | tf_op jit(solution)/shard_map/ppermute | solution.py:396
  42.6 13.9 %collective-permute-start.14 = (bf16[128,1024]{1,0:T(8,128)(2,1)S(1)}, bf16[128,1024]{1,0:T(8,128)(2,1)S(1)}, u32[]{:S(2)}, u32[]{:S(2)}) collective-permute-start(bf16[128,1024]{1,0:T(8,128)(2,1)S(1)} %shard_map.105.own.refs_0_), channel_id=1, source_target_pairs={{0,5},{1,4},{2,7},{3,6},{4,1},{5,0},{6,3},{7,2},{8,13},{9,12},{10,... | collective-permute-start | bytes 786440 | tf_op jit(solution)/shard_map/ppermute | solution.py:403
  44.1 13.8 %collective-permute-start.13 = (bf16[128,1024]{1,0:T(8,128)(2,1)S(1)}, bf16[128,1024]{1,0:T(8,128)(2,1)S(1)}, u32[]{:S(2)}, u32[]{:S(2)}) collective-permute-start(bf16[128,1024]{1,0:T(8,128)(2,1)S(1)} %shard_map.105.own.refs_0_), channel_id=1, source_target_pairs={{0,1},{1,0},{2,3},{3,2},{4,5},{5,4},{6,7},{7,6},{8,9},{9,8},{10,11... | collective-permute-start | bytes 786440 | tf_op jit(solution)/shard_map/ppermute | solution.py:399
  44.4 14.0 %collective-permute-start.11 = (bf16[128,1024]{1,0:T(8,128)(2,1)S(1)}, bf16[128,1024]{1,0:T(8,128)(2,1)S(1)}, u32[]{:S(2)}, u32[]{:S(2)}) collective-permute-start(bf16[128,1024]{1,0:T(8,128)(2,1)S(1)} %shard_map.105.own.refs_0_), channel_id=1, source_target_pairs={{0,2},{2,0},{4,6},{6,4},{8,10},{10,8},{12,14},{14,12},{16,18},{18,... | collective-permute-start | bytes 786440 | tf_op jit(solution)/shard_map/ppermute | solution.py:396
  50.0 8.4 %collective-permute-start.12 = (bf16[128,1024]{1,0:T(8,128)(2,1)S(1)}, bf16[128,1024]{1,0:T(8,128)(2,1)S(1)}, u32[]{:S(2)}, u32[]{:S(2)}) collective-permute-start(bf16[128,1024]{1,0:T(8,128)(2,1)S(1)} %collective-permute-done.10.over_x.refs_1_), channel_id=1, source_target_pairs={{0,2},{2,0},{4,6},{6,4},{8,10},{10,8},{12,14},{14,12},{16,18},{18,... | collective-permute-start | bytes 786440 | tf_op jit(solution)/shard_map/ppermute | solution.py:396
  57.9 2.8 %copy-start.5 = (f32[1024,512]{1,0:T(8,128)S(1)}, f32[1024,512]{1,0:T(8,128)}, u32[]{:S(2)}) copy-start(f32[1024,512]{1,0:T(8,128)} %second.1) | copy-start | bytes 6291460
  57.9 2.8 %collective-permute-start.15 = (bf16[128,1024]{1,0:T(8,128)(2,1)S(1)}, bf16[128,1024]{1,0:T(8,128)(2,1)S(1)}, u32[]{:S(2)}, u32[]{:S(2)}) collective-permute-start(bf16[128,1024]{1,0:T(8,128)(2,1)S(1)} %collective-permute-done.13.refs_4_), channel_id=1, source_target_pairs={{0,2},{2,0},{4,6},{6,4},{8,10},{10,8},{12,14},{14,12},{16,18},{18,... | collective-permute-start | bytes 786440 | tf_op jit(solution)/shard_map/ppermute | solution.py:396
  57.9 2.8 %collective-permute-start.16 = (bf16[128,1024]{1,0:T(8,128)(2,1)S(1)}, bf16[128,1024]{1,0:T(8,128)(2,1)S(1)}, u32[]{:S(2)}, u32[]{:S(2)}) collective-permute-start(bf16[128,1024]{1,0:T(8,128)(2,1)S(1)} %collective-permute-done.14.refs_5_), channel_id=1, source_target_pairs={{0,2},{2,0},{4,6},{6,4},{8,10},{10,8},{12,14},{14,12},{16,18},{18,... | collective-permute-start | bytes 786440 | tf_op jit(solution)/shard_map/ppermute | solution.py:396
  60.3 8.3 %collective-permute-start.17 = (bf16[512,256]{1,0:T(8,128)(2,1)S(1)}, bf16[512,256]{1,0:T(8,128)(2,1)S(1)}, u32[]{:S(2)}, u32[]{:S(2)}) collective-permute-start(bf16[512,256]{1,0:T(8,128)(2,1)S(1)} %get-tuple-element.65), channel_id=1, source_target_pairs={{0,1},{1,0},{2,3},{3,2},{4,5},{5,4},{6,7},{7,6},{8,9},{9,8},{10,11... | collective-permute-start | bytes 786440 | tf_op jit(solution)/shard_map/ppermute | solution.py:399
  68.6 11.6 %collective-permute-start.20 = (f32[1024,256]{1,0:T(8,128)S(1)}, f32[1024,256]{1,0:T(8,128)S(1)}, u32[]{:S(2)}, u32[]{:S(2)}) collective-permute-start(f32[1024,256]{1,0:T(8,128)S(1)} %get-tuple-element.67.new), channel_id=1, source_target_pairs={{0,2},{2,0},{4,6},{6,4},{8,10},{10,8},{12,14},{14,12},{16,18},{18,... | collective-permute-start | bytes 3145736 | tf_op jit(solution)/shard_map/ppermute | solution.py:396
  71.4 8.8 %collective-permute-start.18 = (bf16[512,256]{1,0:T(8,128)(2,1)S(1)}, bf16[512,256]{1,0:T(8,128)(2,1)S(1)}, u32[]{:S(2)}, u32[]{:S(2)}) collective-permute-start(bf16[512,256]{1,0:T(8,128)(2,1)S(1)} %get-tuple-element.74), channel_id=1, source_target_pairs={{0,1},{1,0},{2,3},{3,2},{4,5},{5,4},{6,7},{7,6},{8,9},{9,8},{10,11... | collective-permute-start | bytes 786440 | tf_op jit(solution)/shard_map/ppermute | solution.py:399
  72.9 7.3 %collective-permute-start.19 = (bf16[512,256]{1,0:T(8,128)(2,1)S(1)}, bf16[512,256]{1,0:T(8,128)(2,1)S(1)}, u32[]{:S(2)}, u32[]{:S(2)}) collective-permute-start(bf16[512,256]{1,0:T(8,128)(2,1)S(1)} %get-tuple-element.68.kept), channel_id=1, source_target_pairs={{0,2},{2,0},{4,6},{6,4},{8,10},{10,8},{12,14},{14,12},{16,18},{18,... | collective-permute-start | bytes 786440 | tf_op jit(solution)/shard_map/ppermute | solution.py:396
  80.2 3.4 %collective-permute-start.21 = (bf16[512,256]{1,0:T(8,128)(2,1)S(1)}, bf16[512,256]{1,0:T(8,128)(2,1)S(1)}, u32[]{:S(2)}, u32[]{:S(2)}) collective-permute-start(bf16[512,256]{1,0:T(8,128)(2,1)S(1)} %collective-permute-done.18.came), channel_id=1, source_target_pairs={{0,2},{2,0},{4,6},{6,4},{8,10},{10,8},{12,14},{14,12},{16,18},{18,... | collective-permute-start | bytes 786440 | tf_op jit(solution)/shard_map/ppermute | solution.py:396
  80.2 3.6 %collective-permute-start.22 = (f32[256,1024]{1,0:T(8,128)S(1)}, f32[256,1024]{1,0:T(8,128)S(1)}, u32[]{:S(2)}, u32[]{:S(2)}) collective-permute-start(f32[256,1024]{1,0:T(8,128)S(1)} %get-tuple-element.79.top), channel_id=1, source_target_pairs={{0,2},{2,0},{4,6},{6,4},{8,10},{10,8},{12,14},{14,12},{16,18},{18,... | collective-permute-start | bytes 3145736 | tf_op jit(solution)/shard_map/ppermute | solution.py:396
  83.6 3.0 %collective-permute-start.23 = (f32[256,1024]{1,0:T(8,128)S(1)}, f32[256,1024]{1,0:T(8,128)S(1)}, u32[]{:S(2)}, u32[]{:S(2)}) collective-permute-start(f32[256,1024]{1,0:T(8,128)S(1)} %get-tuple-element.85.low), channel_id=1, source_target_pairs={{0,2},{2,0},{4,6},{6,4},{8,10},{10,8},{12,14},{14,12},{16,18},{18,... | collective-permute-start | bytes 3145736 | tf_op jit(solution)/shard_map/ppermute | solution.py:396

commit v11 on v10

--- a/solution.py
+++ b/solution.py
@@ -61,6 +61,7 @@
 
 TILES = 4
 UPPER = [(i, j) for i in range(TILES) for j in range(i, TILES)]
+SPLIT = len(UPPER) // 2
 
 
 def pack(out, base, value):
@@ -118,16 +119,26 @@
     pltpu.make_async_copy(stat_left.at[:, : size * TILES], stat_in, sem.at[2]).wait()
     same = diagonal(size)
     base = 2 * count
-    for place, (i, j) in enumerate(UPPER):
-        value = stat_in[i * size : (i + 1) * size, j * size : (j + 1) * size]
-        high = value.astype(HALF)
-        state[base + place] = high
-        if i == j:
-            low = jnp.where(same, value - high.astype(FULL), 0.0)
+
+    def tile_of(i, j):
+        return stat_in[i * size : (i + 1) * size, j * size : (j + 1) * size]
+
+    @pl.when(x == 0)
+    def _():
+        for place in range(SPLIT + 1):
+            state[base + place] = tile_of(*UPPER[place]).astype(HALF)
+
+    @pl.when(x == 1)
+    def _():
+        for place in range(SPLIT, len(UPPER)):
+            state[base + place - SPLIT] = tile_of(*UPPER[place]).astype(HALF)
+        for i in range(TILES):
+            value = tile_of(i, i)
+            low = jnp.where(same, value - value.astype(HALF).astype(FULL), 0.0)
             line = jnp.sum(low, axis=0, keepdims=True)
-            state[base + len(UPPER), i * 16 : (i + 1) * 16] = jnp.broadcast_to(
-                line, (16, size)
-            ).astype(HALF)
+            state[base + SPLIT, i * 16 : (i + 1) * 16] = jnp.broadcast_to(line, (16, size)).astype(
+                HALF
+            )
 
 
 def second_sum_kernel(where, kept, came, own, *sent):
@@ -169,7 +180,7 @@
 
 
 def state_kernel(
-    where, left, right, mine, theirs, stat_left, stat_right, bases, turned, back, full, sem
+    where, left, right, mine, theirs, relayed, stat_left, stat_right, bases, turned, back, full, sem
 ):
     rows, width = left.shape
     size = rows // TILES
@@ -188,10 +199,22 @@
     base = (1 - position) * TILES
     first = rows * width // size**2
     same = diagonal(size)
+    near_x = where[2] == 0
     for number, (i, j) in enumerate(UPPER):
-        value = mine[first + number].astype(FULL)
+        if number < SPLIT:
+            pair = mine[first + number], relayed[number]
+        elif number == SPLIT:
+            pair = mine[first + SPLIT], mine[first]
+        else:
+            pair = relayed[number - SPLIT], mine[first + number - SPLIT]
+        value = jnp.where(near_x, pair[0].astype(FULL), pair[1].astype(FULL))
         if i == j:
-            line = mine[first + len(UPPER), i * 16 : (i + 1) * 16].astype(FULL)[:1]
+            lines = slice(i * 16, (i + 1) * 16)
+            line = jnp.where(
+                near_x,
+                relayed[SPLIT, lines].astype(FULL),
+                mine[first + SPLIT, lines].astype(FULL),
+            )[:1]
             value = value + jnp.where(same, line, 0.0)
         full[tile(base + i, size), tile(base + j, size)] = value
         if i != j:
@@ -405,7 +428,8 @@
     raw = lax.dynamic_slice_in_dim(group_grads[0], (1 - core) * half, half, 0)
     came = dp_swap(raw, 1)
     raw = lax.dynamic_slice_in_dim(group_grads[0], core * half, half, 0)
-    count = rows * width // quarter**2 + len(UPPER) + 1
+    tiles = rows * width // quarter**2
+    count = tiles + SPLIT + 1
     state_sent, kept, sent = call(
         start_kernel,
         [
@@ -451,6 +475,7 @@
     part, state_mine = lax.optimization_barrier((part, state_mine))
     parts = [part, dp_swap(part, 2), shard_swap(part), cross_swap(part)]
     state_theirs = dp_swap(state_mine, 1)
+    state_relayed = dp_swap(state_mine[tiles:], 2)
     square = shaped((width, width), HALF)
     bases, left_turned, right_turned, stat = call(
         state_kernel,
@@ -461,10 +486,11 @@
             basis_right,
             state_mine,
             state_theirs,
+            state_relayed,
             stat_left,
             stat_right,
         ),
-        [SMEM] + [VMEM] * 4 + [ANY] * 2,
+        [SMEM] + [VMEM] * 5 + [ANY] * 2,
         [pltpu.SemaphoreType.DMA(())],
         moved=2**24,
     )

time: 88.4 us -> 91.4 us (1.034)
  starting transfers between devices: 20.6 us -> 23.8 us
    ppermute x19 -> x20, waiting for transfers between devices: 22.6 us -> 30.2 us  [dp_swap(): return lax.ppermute(value, 'dp', [(i, i ^ distance) for i in range(16)])]
    ppermute x4, waiting for transfers between devices: 6.44 us -> 1.81 us  [shard_swap(): return lax.ppermute(value, 'shard', [(0, 1), (1, 0)])]
    ppermute x1, waiting for transfers between devices: 3.26 us -> 0.01 us  [cross_swap(): return lax.ppermute(value, ('dp', 'shard'), pairs)]
    ppermute x19 -> x20, starting transfers between devices: 14 us -> 16.6 us  [dp_swap(): return lax.ppermute(value, 'dp', [(i, i ^ distance) for i in range(16)])]
  transfers between devices with their start and end apart: 24 -> 25, of which waited for: 13 -> 10; matrix products, arithmetic and copies ran while one was open for 0% -> 0% of each run, Pallas kernels for 33% -> 32%
where the time goes in v11:
time: 91.4 us; the launch traced here: 91.3 us
  Pallas kernels  33 us (36%)
  waiting for transfers between devices  32 us (35%)
  starting transfers between devices  23.8 us (26%)
  local copies, waits for them, and re-layouts  1.32 us (1%)
  between operations  1.01 us (1%)
    ppermute x20, waiting for transfers between devices, dp_swap(): return lax.ppermute(value, 'dp', [(i, i ^ distance) for i in range(16)])  30.2 us
    pallas_call x9, Pallas kernels, call(): pl.pallas_call(kernel, out_shape=outs, in_specs=specs, out_specs=[space]...  20.8 us
    ppermute x20, starting transfers between devices, dp_swap(): return lax.ppermute(value, 'dp', [(i, i ^ distance) for i in range(16)])  16.6 us
    pallas_call x1, Pallas kernels, fast_body(): pl.pallas_call(refresh_kernel, out_shape=[square, square, shaped((half, w...  6.49 us
    ppermute x4, starting transfers between devices, shard_swap(): return lax.ppermute(value, 'shard', [(0, 1), (1, 0)])  5.79 us
    pallas_call x1, Pallas kernels, fast_body(): pl.pallas_call(last_kernel, out_shape=[shaped((half, width), FULL), side,...  2.91 us
    pallas_call x1, Pallas kernels, fast_body(): pl.pallas_call(update_kernel, out_shape=[shaped((rows, width), HALF), sid...  2.8 us
  transfers between devices with their start and end apart: 25, of which 10 were waited for; matrix products, arithmetic and copies ran while one was open for 0% of the time, Pallas kernels for 32%

profile of v11, /device:TPU:0, one launch (start us, length us, event | category | flops | bytes accessed | tf_op | source)
XLA Modules:
  0.0 91.3 jit_solution(518861773070296837)
XLA Ops:
  0.6 1.3 %dynamic-slice_bitcast_fusion = (bf16[256,1024]{1,0:T(8,128)(2,1)S(1)}, bf16[256,1024]{1,0:T(8,128)(2,1)S(1)}) fusion(bf16[1,512,1024]{2,1,0:T(8,128)(2,1)} %param.7, s32[]{:T(128)S(6)} %select_n.7, s32[]{:T(128)S(6)} %select_n.6), kind=kLoop, calls=%fused_computation | loop fusion | bytes 2097160 | tf_op jit(solution)/shard_map/dynamic_slice | solution.py:428
  1.9 0.5 collective-permute-start
  2.4 0.1 pad_add_fusion.where
  2.5 1.5 %collective-permute-done.came = bf16[256,1024]{1,0:T(8,128)(2,1)S(1)} collective-permute-done((bf16[256,1024]{1,0:T(8,128)(2,1)S(1)}, bf16[256,1024]{1,0:T(8,128)(2,1)S(1)}, u32[]{:S(2)}, u32[]{:S(2)}) %collective-permute-start) | collective-permute-done | bytes 524320 | tf_op jit(solution)/shard_map/ppermute | solution.py:419
  4.0 2.7 %shard_map.102 = (bf16[38,128,128]{2,1,0:T(8,128)(2,1)S(1)}, f32[128,1024]{1,0:T(8,128)S(1)}, bf16[128,1024]{1,0:T(8,128)(2,1)S(1)}) custom-call(s32[4]{0:T(128)S(1)} %pad_add_fusion.where, bf16[256,1024]{1,0:T(8,128)(2,1)S(1)} %get-tuple-element.95.raw, bf16[256,1024]{1,0:T(8,128)(2,1)S(1)} %collective-permute-done.came, f32[512,1024]{1,0:T(8,128)} %left.3, ...), custom_call_target="tpu_custom_call" | custom-call | bytes 4194304 | tf_op jit(solution)/shard_map/pallas_call | solution.py:43
  6.7 0.0 copy-start
  6.7 3.0 %collective-permute-start.8 = (bf16[38,128,128]{2,1,0:T(8,128)(2,1)S(1)}, bf16[38,128,128]{2,1,0:T(8,128)(2,1)S(1)}, u32[]{:S(2)}, u32[]{:S(2)}) collective-permute-start(bf16[38,128,128]{2,1,0:T(8,128)(2,1)S(1)} %get-tuple-element.55), channel_id=1, source_target_pairs={{0,1},{1,0},{2,3},{3,2},{4,5},{5,4},{6,7},{7,6},{8,9},{9,8},{10,11... | collective-permute-start | bytes 3735560 | tf_op jit(solution)/shard_map/ppermute | solution.py:422
  9.7 1.5 %collective-permute-start.1 = (bf16[128,1024]{1,0:T(8,128)(2,1)S(1)}, bf16[128,1024]{1,0:T(8,128)(2,1)S(1)}, u32[]{:S(2)}, u32[]{:S(2)}) collective-permute-start(bf16[128,1024]{1,0:T(8,128)(2,1)S(1)} %get-tuple-element.50), channel_id=1, source_target_pairs={{0,4},{2,6},{4,0},{6,2},{8,12},{10,14},{12,8},{14,10},{16,20},{18,... | collective-permute-start | bytes 786440 | tf_op jit(solution)/shard_map/ppermute | solution.py:419
  11.2 6.5 %collective-permute-done.1.came = bf16[128,1024]{1,0:T(8,128)(2,1)S(1)} collective-permute-done((bf16[128,1024]{1,0:T(8,128)(2,1)S(1)}, bf16[128,1024]{1,0:T(8,128)(2,1)S(1)}, u32[]{:S(2)}, u32[]{:S(2)}) %collective-permute-start.1) | collective-permute-done | bytes 262176 | tf_op jit(solution)/shard_map/ppermute | solution.py:419
  17.7 0.6 shard_map.103
  18.3 1.6 %collective-permute-start.2 = (bf16[32,1024]{1,0:T(8,128)(2,1)S(1)}, bf16[32,1024]{1,0:T(8,128)(2,1)S(1)}, u32[]{:S(2)}, u32[]{:S(2)}) collective-permute-start(bf16[32,1024]{1,0:T(8,128)(2,1)S(1)} %get-tuple-element.52), channel_id=1, source_target_pairs={{0,8},{2,10},{4,12},{6,14},{8,0},{10,2},{12,4},{14,6},{16,24},{18,... | collective-permute-start | bytes 196616 | tf_op jit(solution)/shard_map/ppermute | solution.py:419
  20.0 2.6 %collective-permute-start.3 = (bf16[32,1024]{1,0:T(8,128)(2,1)S(1)}, bf16[32,1024]{1,0:T(8,128)(2,1)S(1)}, u32[]{:S(2)}, u32[]{:S(2)}) collective-permute-start(bf16[32,1024]{1,0:T(8,128)(2,1)S(1)} %get-tuple-element.53), channel_id=1, source_target_pairs={{0,16},{2,18},{4,20},{6,22},{8,24},{10,26},{12,28},{14,30},{16,0},... | collective-permute-start | bytes 196616 | tf_op jit(solution)/shard_map/ppermute | solution.py:419
  22.6 0.2 collective-permute-start.4
  22.8 0.5 collective-permute-done.2.one
  23.3 3.2 %collective-permute-done.3.two = bf16[32,1024]{1,0:T(8,128)(2,1)S(1)} collective-permute-done((bf16[32,1024]{1,0:T(8,128)(2,1)S(1)}, bf16[32,1024]{1,0:T(8,128)(2,1)S(1)}, u32[]{:S(2)}, u32[]{:S(2)}) %collective-permute-start.3) | collective-permute-done | bytes 65568 | tf_op jit(solution)/shard_map/ppermute | solution.py:419
  26.5 2.1 %collective-permute-done.4.three = bf16[32,1024]{1,0:T(8,128)(2,1)S(1)} collective-permute-done((bf16[32,1024]{1,0:T(8,128)(2,1)S(1)}, bf16[32,1024]{1,0:T(8,128)(2,1)S(1)}, u32[]{:S(2)}, u32[]{:S(2)}) %collective-permute-start.4) | collective-permute-done | bytes 65568 | tf_op jit(solution)/shard_map/ppermute | solution.py:419
  28.7 1.1 %collective-permute-start.7 = (bf16[32,1024]{1,0:T(8,128)(2,1)S(1)}, bf16[32,1024]{1,0:T(8,128)(2,1)S(1)}, u32[]{:S(2)}, u32[]{:S(2)}) collective-permute-start(bf16[32,1024]{1,0:T(8,128)(2,1)S(1)} %shard_map.104.refs_0_), channel_id=1, source_target_pairs={{0,24},{2,26},{4,28},{6,30},{8,16},{10,18},{12,20},{14,22},{16,8},... | collective-permute-start | bytes 196616 | tf_op jit(solution)/shard_map/ppermute | solution.py:419
  29.8 0.4 collective-permute-start.6
  30.3 2.9 %collective-permute-start.5 = (bf16[32,1024]{1,0:T(8,128)(2,1)S(1)}, bf16[32,1024]{1,0:T(8,128)(2,1)S(1)}, u32[]{:S(2)}, u32[]{:S(2)}) collective-permute-start(bf16[32,1024]{1,0:T(8,128)(2,1)S(1)} %shard_map.104.refs_0_), channel_id=1, source_target_pairs={{0,8},{2,10},{4,12},{6,14},{8,0},{10,2},{12,4},{14,6},{16,24},{18,... | collective-permute-start | bytes 196616 | tf_op jit(solution)/shard_map/ppermute | solution.py:419
  33.1 1.7 %collective-permute-done.7.refs_3_ = bf16[32,1024]{1,0:T(8,128)(2,1)S(1)} collective-permute-done((bf16[32,1024]{1,0:T(8,128)(2,1)S(1)}, bf16[32,1024]{1,0:T(8,128)(2,1)S(1)}, u32[]{:S(2)}, u32[]{:S(2)}) %collective-permute-start.7) | collective-permute-done | bytes 65568 | tf_op jit(solution)/shard_map/ppermute | solution.py:419
  34.9 1.3 %collective-permute-done.6.refs_2_ = bf16[32,1024]{1,0:T(8,128)(2,1)S(1)} collective-permute-done((bf16[32,1024]{1,0:T(8,128)(2,1)S(1)}, bf16[32,1024]{1,0:T(8,128)(2,1)S(1)}, u32[]{:S(2)}, u32[]{:S(2)}) %collective-permute-start.6) | collective-permute-done | bytes 65568 | tf_op jit(solution)/shard_map/ppermute | solution.py:419
  36.2 0.0 collective-permute-done.5.refs_1_
  36.2 0.6 shard_map.105.own.refs_0_
  36.8 0.5 collective-permute-done.8.mine
  37.3 0.0 collective-permute-start.9
  37.3 1.8 %collective-permute-start.11 = (bf16[128,1024]{1,0:T(8,128)(2,1)S(1)}, bf16[128,1024]{1,0:T(8,128)(2,1)S(1)}, u32[]{:S(2)}, u32[]{:S(2)}) collective-permute-start(bf16[128,1024]{1,0:T(8,128)(2,1)S(1)} %shard_map.105.own.refs_0_), channel_id=1, source_target_pairs={{0,4},{2,6},{4,0},{6,2},{8,12},{10,14},{12,8},{14,10},{16,20},{18,... | collective-permute-start | bytes 786440 | tf_op jit(solution)/shard_map/ppermute | solution.py:419
  39.1 1.4 %collective-permute-start.15 = (bf16[128,1024]{1,0:T(8,128)(2,1)S(1)}, bf16[128,1024]{1,0:T(8,128)(2,1)S(1)}, u32[]{:S(2)}, u32[]{:S(2)}) collective-permute-start(bf16[128,1024]{1,0:T(8,128)(2,1)S(1)} %shard_map.105.own.refs_0_), channel_id=1, source_target_pairs={{0,5},{1,4},{2,7},{3,6},{4,1},{5,0},{6,3},{7,2},{8,13},{9,12},{10,... | collective-permute-start | bytes 786440 | tf_op jit(solution)/shard_map/ppermute | solution.py:426
  40.5 0.3 collective-permute-start.14
  40.9 0.0 copy-start.4
  40.9 1.8 %collective-permute-start.10 = (bf16[6,128,128]{2,1,0:T(8,128)(2,1)S(1)}, bf16[6,128,128]{2,1,0:T(8,128)(2,1)S(1)}, u32[]{:S(2)}, u32[]{:S(2)}) collective-permute-start(bf16[6,128,128]{2,1,0:T(8,128)(2,1)S(1)} %slice.3), channel_id=1, source_target_pairs={{0,4},{2,6},{4,0},{6,2},{8,12},{10,14},{12,8},{14,10},{16,20},{18,... | collective-permute-start | bytes 589832 | tf_op jit(solution)/shard_map/ppermute | solution.py:419
  42.7 13.3 %collective-permute-done.10.relayed = bf16[6,128,128]{2,1,0:T(8,128)(2,1)S(1)} collective-permute-done((bf16[6,128,128]{2,1,0:T(8,128)(2,1)S(1)}, bf16[6,128,128]{2,1,0:T(8,128)(2,1)S(1)}, u32[]{:S(2)}, u32[]{:S(2)}) %collective-permute-start.10) | collective-permute-done | bytes 196640 | tf_op jit(solution)/shard_map/ppermute | solution.py:419
  56.0 0.0 collective-permute-start.12
  56.0 0.0 collective-permute-done.11.over_x.refs_1_
  56.0 0.5 collective-permute-start.13
  56.5 0.0 collective-permute-done.9.theirs
  56.5 3.2 %shard_map.106 = (bf16[2,1024,1024]{2,1,0:T(8,128)(2,1)S(1)}, bf16[1024,1024]{1,0:T(8,128)(2,1)S(1)}, bf16[1024,1024]{1,0:T(8,128)(2,1)S(1)}, f32[1024,1024]{1,0:T(8,128)S(1)}) custom-call(s32[4]{0:T(128)S(1)} %pad_add_fusion.where, f32[512,1024]{1,0:T(8,128)S(1)} %copy-done, f32[512,1024]{1,0:T(8,128)S(1)} %copy-done.1, ...), custom_call_target="tpu_custom_call" | custom-call | bytes 16777216 | tf_op jit(solution)/shard_map/pallas_call | solution.py:43
  59.7 0.0 collective-permute-done.15.refs_5_
  59.7 0.0 collective-permute-done.14.refs_4_
  59.8 0.0 copy-start.5
  59.8 0.1 collective-permute-start.16
  59.8 0.5 collective-permute-start.17
  60.4 1.9 %shard_map.107 = (bf16[512,256]{1,0:T(8,128)(2,1)S(1)}, bf16[512,256]{1,0:T(8,128)(2,1)S(1)}) custom-call(s32[4]{0:T(128)S(1)} %pad_add_fusion.where, f32[512,1024]{1,0:T(8,128)S(1)} %copy-done.4, bf16[2,1024,1024]{2,1,0:T(8,128)(2,1)S(1)} %get-tuple-element.57.bases, bf16[128,1024]{1,0:T(8,128)(2,1)S(1)} %shard_map.105.own.refs_0_, ...), custom_call_target="tpu_custom_call" | custom-call | flops 536870912 | bytes 4194304 | tf_op jit(solution)/shard_map/pallas_call | solution.py:43
  62.2 1.8 %collective-permute-start.18 = (bf16[512,256]{1,0:T(8,128)(2,1)S(1)}, bf16[512,256]{1,0:T(8,128)(2,1)S(1)}, u32[]{:S(2)}, u32[]{:S(2)}) collective-permute-start(bf16[512,256]{1,0:T(8,128)(2,1)S(1)} %get-tuple-element.65), channel_id=1, source_target_pairs={{0,1},{1,0},{2,3},{3,2},{4,5},{5,4},{6,7},{7,6},{8,9},{9,8},{10,11... | collective-permute-start | bytes 786440 | tf_op jit(solution)/shard_map/ppermute | solution.py:422
  64.0 0.0 collective-permute-done.16.refs_6_
  64.0 0.0 collective-permute-done.17.refs_7_
  64.0 7.5 %shard_map.108 = (bf16[1024,1024]{1,0:T(8,128)(2,1)S(1)}, bf16[1024,1024]{1,0:T(8,128)(2,1)S(1)}, f32[1024,256]{1,0:T(8,128)S(1)}) custom-call(s32[4]{0:T(128)S(1)} %pad_add_fusion.where, bf16[2,1024,1024]{2,1,0:T(8,128)(2,1)S(1)} %get-tuple-element.57.bases, bf16[1024,1024]{1,0:T(8,128)(2,1)S(1)} %get-tuple-element.58.turned, ...), custom_call_target="tpu_custom_call" | custom-call | flops 3221225472 | bytes 8388608 | tf_op jit(solution)/shard_map/pallas_call | solution.py:43
  71.5 0.0 collective-permute-done.18.came
  71.5 0.1 collective-permute-start.21
  71.6 2.8 %shard_map.109 = (bf16[512,256]{1,0:T(8,128)(2,1)S(1)}, bf16[512,256]{1,0:T(8,128)(2,1)S(1)}) custom-call(s32[4]{0:T(128)S(1)} %pad_add_fusion.where, bf16[2,1024,1024]{2,1,0:T(8,128)(2,1)S(1)} %get-tuple-element.57.bases, bf16[1024,1024]{1,0:T(8,128)(2,1)S(1)} %get-tuple-element.58.turned, bf16[512,256]{1,0:T(8,128)(2,1)S(1)} %get-tuple-element.60.mine, ...), custom_call_target="tpu_custom_call" | custom-call | flops 1073741824 | bytes 4194304 | tf_op jit(solution)/shard_map/pallas_call | solution.py:43
  74.4 0.8 collective-permute-start.19
  75.2 0.2 collective-permute-start.20
  75.4 6.5 %shard_map.110 = (bf16[1024,1024]{1,0:T(8,128)(2,1)S(1)}, bf16[1024,1024]{1,0:T(8,128)(2,1)S(1)}, f32[256,1024]{1,0:T(8,128)S(1)}, f32[1024,512]{1,0:T(8,128)}) custom-call(s32[4]{0:T(128)S(1)} %pad_add_fusion.where, bf16[1024,1024]{1,0:T(8,128)(2,1)S(1)} %get-tuple-element.71.start, bf16[1024,1024]{1,0:T(8,128)(2,1)S(1)} %get-tuple-element.72.start_turned, ...), custom_call_target="tpu_custom_call" | custom-call | flops 12884901888 | bytes 8388608 | tf_op jit(solution)/shard_map/pallas_call | solution.py:536
  81.9 1.3 %collective-permute-done.19.came = bf16[512,256]{1,0:T(8,128)(2,1)S(1)} collective-permute-done((bf16[512,256]{1,0:T(8,128)(2,1)S(1)}, bf16[512,256]{1,0:T(8,128)(2,1)S(1)}, u32[]{:S(2)}, u32[]{:S(2)}) %collective-permute-start.19) | collective-permute-done | bytes 262176 | tf_op jit(solution)/shard_map/ppermute | solution.py:422
  83.2 0.0 collective-permute-done.20.kept_next
  83.2 0.0 collective-permute-done.21.new_next
  83.2 0.0 collective-permute-start.22
  83.2 0.5 collective-permute-start.23
  83.7 2.9 %shard_map.111 = (f32[256,1024]{1,0:T(8,128)S(1)}, f32[512,1024]{1,0:T(8,128)}, f32[512,1024]{1,0:T(8,128)}, f32[1024,512]{1,0:T(8,128)}) custom-call(s32[4]{0:T(128)S(1)} %pad_add_fusion.where, bf16[1024,1024]{1,0:T(8,128)(2,1)S(1)} %get-tuple-element.77.current, bf16[1024,1024]{1,0:T(8,128)(2,1)S(1)} %get-tuple-element.78.turned, ...), custom_call_target="tpu_custom_call", output_to_operand_aliasing={{3}: (5, {})} | custom-call | flops 1073741824 | bytes 4194304 | tf_op jit(solution)/shard_map/pallas_call | solution.py:555
  86.6 0.0 collective-permute-done.22.came_next
  86.7 0.1 collective-permute-start.24
  86.8 0.0 collective-permute-done.23.top_next
  86.8 2.8 %shard_map.112 = (bf16[512,1024]{1,0:T(8,128)(2,1)}, f32[512,1024]{1,0:T(8,128)}, f32[512,1024]{1,0:T(8,128)}) custom-call(s32[4]{0:T(128)S(1)} %pad_add_fusion.where, bf16[512,256]{1,0:T(8,128)(2,1)S(1)} %get-tuple-element.68.kept, bf16[512,256]{1,0:T(8,128)(2,1)S(1)} %collective-permute-done.19.came, ...), custom_call_target="tpu_custom_call", output_to_operand_aliasing={{1}: (8, {}), {2}: (9, {})} | custom-call | flops 1073741824 | bytes 4194304 | tf_op jit(solution)/shard_map/pallas_call | solution.py:567
  89.6 0.0 collective-permute-done.24.low
  89.6 1.5 %shard_map.113 = (f32[512,1024]{1,0:T(8,128)}, f32[512,1024]{1,0:T(8,128)}) custom-call(s32[4]{0:T(128)S(1)} %pad_add_fusion.where, f32[256,1024]{1,0:T(8,128)S(1)} %collective-permute-done.24.low, f32[512,1024]{1,0:T(8,128)} %get-tuple-element.90.left_in, f32[512,1024]{1,0:T(8,128)} %get-tuple-element.91.right_in), custom_call_target="tpu_custom_call", output_to_operand_aliasing={{0}: (2, {}), {1}: (3, {})} | custom-call | bytes 2097152 | tf_op jit(solution)/shard_map/pallas_call | solution.py:43
  (13 shorter events, 0.1 us)
Async XLA Ops:
  1.9 2.1 %collective-permute-start = (bf16[256,1024]{1,0:T(8,128)(2,1)S(1)}, bf16[256,1024]{1,0:T(8,128)(2,1)S(1)}, u32[]{:S(2)}, u32[]{:S(2)}) collective-permute-start(bf16[256,1024]{1,0:T(8,128)(2,1)S(1)} %get-tuple-element.94), channel_id=1, source_target_pairs={{0,2},{2,0},{4,6},{6,4},{8,10},{10,8},{12,14},{14,12},{16,18},{18,... | collective-permute-start | bytes 1572872 | tf_op jit(solution)/shard_map/ppermute | solution.py:419
  4.0 52.5 %copy-start.1 = (f32[512,1024]{1,0:T(8,128)S(1)}, f32[512,1024]{1,0:T(8,128)}, u32[]{:S(2)}) copy-start(f32[512,1024]{1,0:T(8,128)} %right.3) | copy-start | bytes 6291460
  4.0 52.5 %copy-start.2 = (f32[512,1024]{1,0:T(8,128)S(1)}, f32[512,1024]{1,0:T(8,128)}, u32[]{:S(2)}) copy-start(f32[512,1024]{1,0:T(8,128)} %stat_left.3) | copy-start | bytes 6291460
  4.0 52.5 %copy-start.3 = (f32[512,1024]{1,0:T(8,128)S(1)}, f32[512,1024]{1,0:T(8,128)}, u32[]{:S(2)}) copy-start(f32[512,1024]{1,0:T(8,128)} %stat_right.3) | copy-start | bytes 6291460
  6.7 49.8 %copy-start = (f32[512,1024]{1,0:T(8,128)S(1)}, f32[512,1024]{1,0:T(8,128)}, u32[]{:S(2)}) copy-start(f32[512,1024]{1,0:T(8,128)} %left.3) | copy-start | bytes 6291460
  6.7 30.6 %collective-permute-start.8 = (bf16[38,128,128]{2,1,0:T(8,128)(2,1)S(1)}, bf16[38,128,128]{2,1,0:T(8,128)(2,1)S(1)}, u32[]{:S(2)}, u32[]{:S(2)}) collective-permute-start(bf16[38,128,128]{2,1,0:T(8,128)(2,1)S(1)} %get-tuple-element.55), channel_id=1, source_target_pairs={{0,1},{1,0},{2,3},{3,2},{4,5},{5,4},{6,7},{7,6},{8,9},{9,8},{10,11... | collective-permute-start | bytes 3735560 | tf_op jit(solution)/shard_map/ppermute | solution.py:422
  9.7 8.1 %collective-permute-start.1 = (bf16[128,1024]{1,0:T(8,128)(2,1)S(1)}, bf16[128,1024]{1,0:T(8,128)(2,1)S(1)}, u32[]{:S(2)}, u32[]{:S(2)}) collective-permute-start(bf16[128,1024]{1,0:T(8,128)(2,1)S(1)} %get-tuple-element.50), channel_id=1, source_target_pairs={{0,4},{2,6},{4,0},{6,2},{8,12},{10,14},{12,8},{14,10},{16,20},{18,... | collective-permute-start | bytes 786440 | tf_op jit(solution)/shard_map/ppermute | solution.py:419
  18.3 5.0 %collective-permute-start.2 = (bf16[32,1024]{1,0:T(8,128)(2,1)S(1)}, bf16[32,1024]{1,0:T(8,128)(2,1)S(1)}, u32[]{:S(2)}, u32[]{:S(2)}) collective-permute-start(bf16[32,1024]{1,0:T(8,128)(2,1)S(1)} %get-tuple-element.52), channel_id=1, source_target_pairs={{0,8},{2,10},{4,12},{6,14},{8,0},{10,2},{12,4},{14,6},{16,24},{18,... | collective-permute-start | bytes 196616 | tf_op jit(solution)/shard_map/ppermute | solution.py:419
  20.0 6.6 %collective-permute-start.3 = (bf16[32,1024]{1,0:T(8,128)(2,1)S(1)}, bf16[32,1024]{1,0:T(8,128)(2,1)S(1)}, u32[]{:S(2)}, u32[]{:S(2)}) collective-permute-start(bf16[32,1024]{1,0:T(8,128)(2,1)S(1)} %get-tuple-element.53), channel_id=1, source_target_pairs={{0,16},{2,18},{4,20},{6,22},{8,24},{10,26},{12,28},{14,30},{16,0},... | collective-permute-start | bytes 196616 | tf_op jit(solution)/shard_map/ppermute | solution.py:419
  22.6 6.1 %collective-permute-start.4 = (bf16[32,1024]{1,0:T(8,128)(2,1)S(1)}, bf16[32,1024]{1,0:T(8,128)(2,1)S(1)}, u32[]{:S(2)}, u32[]{:S(2)}) collective-permute-start(bf16[32,1024]{1,0:T(8,128)(2,1)S(1)} %get-tuple-element.54), channel_id=1, source_target_pairs={{0,24},{2,26},{4,28},{6,30},{8,16},{10,18},{12,20},{14,22},{16,8},... | collective-permute-start | bytes 196616 | tf_op jit(solution)/shard_map/ppermute | solution.py:419
  28.7 6.2 %collective-permute-start.7 = (bf16[32,1024]{1,0:T(8,128)(2,1)S(1)}, bf16[32,1024]{1,0:T(8,128)(2,1)S(1)}, u32[]{:S(2)}, u32[]{:S(2)}) collective-permute-start(bf16[32,1024]{1,0:T(8,128)(2,1)S(1)} %shard_map.104.refs_0_), channel_id=1, source_target_pairs={{0,24},{2,26},{4,28},{6,30},{8,16},{10,18},{12,20},{14,22},{16,8},... | collective-permute-start | bytes 196616 | tf_op jit(solution)/shard_map/ppermute | solution.py:419
  29.8 6.4 %collective-permute-start.6 = (bf16[32,1024]{1,0:T(8,128)(2,1)S(1)}, bf16[32,1024]{1,0:T(8,128)(2,1)S(1)}, u32[]{:S(2)}, u32[]{:S(2)}) collective-permute-start(bf16[32,1024]{1,0:T(8,128)(2,1)S(1)} %shard_map.104.refs_0_), channel_id=1, source_target_pairs={{0,16},{2,18},{4,20},{6,22},{8,24},{10,26},{12,28},{14,30},{16,0},... | collective-permute-start | bytes 196616 | tf_op jit(solution)/shard_map/ppermute | solution.py:419
  30.3 6.0 %collective-permute-start.5 = (bf16[32,1024]{1,0:T(8,128)(2,1)S(1)}, bf16[32,1024]{1,0:T(8,128)(2,1)S(1)}, u32[]{:S(2)}, u32[]{:S(2)}) collective-permute-start(bf16[32,1024]{1,0:T(8,128)(2,1)S(1)} %shard_map.104.refs_0_), channel_id=1, source_target_pairs={{0,8},{2,10},{4,12},{6,14},{8,0},{10,2},{12,4},{14,6},{16,24},{18,... | collective-permute-start | bytes 196616 | tf_op jit(solution)/shard_map/ppermute | solution.py:419
  37.3 19.1 %collective-permute-start.9 = (bf16[38,128,128]{2,1,0:T(8,128)(2,1)S(1)}, bf16[38,128,128]{2,1,0:T(8,128)(2,1)S(1)}, u32[]{:S(2)}, u32[]{:S(2)}) collective-permute-start(bf16[38,128,128]{2,1,0:T(8,128)(2,1)S(1)} %collective-permute-done.8.mine), channel_id=1, source_target_pairs={{0,2},{2,0},{4,6},{6,4},{8,10},{10,8},{12,14},{14,12},{16,18},{18,... | collective-permute-start | bytes 3735560 | tf_op jit(solution)/shard_map/ppermute | solution.py:419
  37.3 18.6 %collective-permute-start.11 = (bf16[128,1024]{1,0:T(8,128)(2,1)S(1)}, bf16[128,1024]{1,0:T(8,128)(2,1)S(1)}, u32[]{:S(2)}, u32[]{:S(2)}) collective-permute-start(bf16[128,1024]{1,0:T(8,128)(2,1)S(1)} %shard_map.105.own.refs_0_), channel_id=1, source_target_pairs={{0,4},{2,6},{4,0},{6,2},{8,12},{10,14},{12,8},{14,10},{16,20},{18,... | collective-permute-start | bytes 786440 | tf_op jit(solution)/shard_map/ppermute | solution.py:419
  39.1 20.6 %collective-permute-start.15 = (bf16[128,1024]{1,0:T(8,128)(2,1)S(1)}, bf16[128,1024]{1,0:T(8,128)(2,1)S(1)}, u32[]{:S(2)}, u32[]{:S(2)}) collective-permute-start(bf16[128,1024]{1,0:T(8,128)(2,1)S(1)} %shard_map.105.own.refs_0_), channel_id=1, source_target_pairs={{0,5},{1,4},{2,7},{3,6},{4,1},{5,0},{6,3},{7,2},{8,13},{9,12},{10,... | collective-permute-start | bytes 786440 | tf_op jit(solution)/shard_map/ppermute | solution.py:426
  40.5 19.2 %collective-permute-start.14 = (bf16[128,1024]{1,0:T(8,128)(2,1)S(1)}, bf16[128,1024]{1,0:T(8,128)(2,1)S(1)}, u32[]{:S(2)}, u32[]{:S(2)}) collective-permute-start(bf16[128,1024]{1,0:T(8,128)(2,1)S(1)} %shard_map.105.own.refs_0_), channel_id=1, source_target_pairs={{0,1},{1,0},{2,3},{3,2},{4,5},{5,4},{6,7},{7,6},{8,9},{9,8},{10,11... | collective-permute-start | bytes 786440 | tf_op jit(solution)/shard_map/ppermute | solution.py:422
  40.9 19.5 %copy-start.4 = (f32[512,1024]{1,0:T(8,128)S(1)}, f32[512,1024]{1,0:T(8,128)}, u32[]{:S(2)}) copy-start(f32[512,1024]{1,0:T(8,128)} %moment.1) | copy-start | bytes 6291460
  40.9 15.1 %collective-permute-start.10 = (bf16[6,128,128]{2,1,0:T(8,128)(2,1)S(1)}, bf16[6,128,128]{2,1,0:T(8,128)(2,1)S(1)}, u32[]{:S(2)}, u32[]{:S(2)}) collective-permute-start(bf16[6,128,128]{2,1,0:T(8,128)(2,1)S(1)} %slice.3), channel_id=1, source_target_pairs={{0,4},{2,6},{4,0},{6,2},{8,12},{10,14},{12,8},{14,10},{16,20},{18,... | collective-permute-start | bytes 589832 | tf_op jit(solution)/shard_map/ppermute | solution.py:419
  56.0 4.4 %collective-permute-start.12 = (bf16[128,1024]{1,0:T(8,128)(2,1)S(1)}, bf16[128,1024]{1,0:T(8,128)(2,1)S(1)}, u32[]{:S(2)}, u32[]{:S(2)}) collective-permute-start(bf16[128,1024]{1,0:T(8,128)(2,1)S(1)} %shard_map.105.own.refs_0_), channel_id=1, source_target_pairs={{0,2},{2,0},{4,6},{6,4},{8,10},{10,8},{12,14},{14,12},{16,18},{18,... | collective-permute-start | bytes 786440 | tf_op jit(solution)/shard_map/ppermute | solution.py:419
  56.0 4.4 %collective-permute-start.13 = (bf16[128,1024]{1,0:T(8,128)(2,1)S(1)}, bf16[128,1024]{1,0:T(8,128)(2,1)S(1)}, u32[]{:S(2)}, u32[]{:S(2)}) collective-permute-start(bf16[128,1024]{1,0:T(8,128)(2,1)S(1)} %collective-permute-done.11.over_x.refs_1_), channel_id=1, source_target_pairs={{0,2},{2,0},{4,6},{6,4},{8,10},{10,8},{12,14},{14,12},{16,18},{18,... | collective-permute-start | bytes 786440 | tf_op jit(solution)/shard_map/ppermute | solution.py:419
  59.8 4.3 %copy-start.5 = (f32[1024,512]{1,0:T(8,128)S(1)}, f32[1024,512]{1,0:T(8,128)}, u32[]{:S(2)}) copy-start(f32[1024,512]{1,0:T(8,128)} %second.1) | copy-start | bytes 6291460
  59.8 4.2 %collective-permute-start.16 = (bf16[128,1024]{1,0:T(8,128)(2,1)S(1)}, bf16[128,1024]{1,0:T(8,128)(2,1)S(1)}, u32[]{:S(2)}, u32[]{:S(2)}) collective-permute-start(bf16[128,1024]{1,0:T(8,128)(2,1)S(1)} %collective-permute-done.14.refs_4_), channel_id=1, source_target_pairs={{0,2},{2,0},{4,6},{6,4},{8,10},{10,8},{12,14},{14,12},{16,18},{18,... | collective-permute-start | bytes 786440 | tf_op jit(solution)/shard_map/ppermute | solution.py:419
  59.8 4.2 %collective-permute-start.17 = (bf16[128,1024]{1,0:T(8,128)(2,1)S(1)}, bf16[128,1024]{1,0:T(8,128)(2,1)S(1)}, u32[]{:S(2)}, u32[]{:S(2)}) collective-permute-start(bf16[128,1024]{1,0:T(8,128)(2,1)S(1)} %collective-permute-done.15.refs_5_), channel_id=1, source_target_pairs={{0,2},{2,0},{4,6},{6,4},{8,10},{10,8},{12,14},{14,12},{16,18},{18,... | collective-permute-start | bytes 786440 | tf_op jit(solution)/shard_map/ppermute | solution.py:419
  62.2 9.3 %collective-permute-start.18 = (bf16[512,256]{1,0:T(8,128)(2,1)S(1)}, bf16[512,256]{1,0:T(8,128)(2,1)S(1)}, u32[]{:S(2)}, u32[]{:S(2)}) collective-permute-start(bf16[512,256]{1,0:T(8,128)(2,1)S(1)} %get-tuple-element.65), channel_id=1, source_target_pairs={{0,1},{1,0},{2,3},{3,2},{4,5},{5,4},{6,7},{7,6},{8,9},{9,8},{10,11... | collective-permute-start | bytes 786440 | tf_op jit(solution)/shard_map/ppermute | solution.py:422
  71.5 11.7 %collective-permute-start.21 = (f32[1024,256]{1,0:T(8,128)S(1)}, f32[1024,256]{1,0:T(8,128)S(1)}, u32[]{:S(2)}, u32[]{:S(2)}) collective-permute-start(f32[1024,256]{1,0:T(8,128)S(1)} %get-tuple-element.67.new), channel_id=1, source_target_pairs={{0,2},{2,0},{4,6},{6,4},{8,10},{10,8},{12,14},{14,12},{16,18},{18,... | collective-permute-start | bytes 3145736 | tf_op jit(solution)/shard_map/ppermute | solution.py:419
  74.4 8.8 %collective-permute-start.19 = (bf16[512,256]{1,0:T(8,128)(2,1)S(1)}, bf16[512,256]{1,0:T(8,128)(2,1)S(1)}, u32[]{:S(2)}, u32[]{:S(2)}) collective-permute-start(bf16[512,256]{1,0:T(8,128)(2,1)S(1)} %get-tuple-element.74), channel_id=1, source_target_pairs={{0,1},{1,0},{2,3},{3,2},{4,5},{5,4},{6,7},{7,6},{8,9},{9,8},{10,11... | collective-permute-start | bytes 786440 | tf_op jit(solution)/shard_map/ppermute | solution.py:422
  75.2 8.0 %collective-permute-start.20 = (bf16[512,256]{1,0:T(8,128)(2,1)S(1)}, bf16[512,256]{1,0:T(8,128)(2,1)S(1)}, u32[]{:S(2)}, u32[]{:S(2)}) collective-permute-start(bf16[512,256]{1,0:T(8,128)(2,1)S(1)} %get-tuple-element.68.kept), channel_id=1, source_target_pairs={{0,2},{2,0},{4,6},{6,4},{8,10},{10,8},{12,14},{14,12},{16,18},{18,... | collective-permute-start | bytes 786440 | tf_op jit(solution)/shard_map/ppermute | solution.py:419
  83.2 3.4 %collective-permute-start.22 = (bf16[512,256]{1,0:T(8,128)(2,1)S(1)}, bf16[512,256]{1,0:T(8,128)(2,1)S(1)}, u32[]{:S(2)}, u32[]{:S(2)}) collective-permute-start(bf16[512,256]{1,0:T(8,128)(2,1)S(1)} %collective-permute-done.19.came), channel_id=1, source_target_pairs={{0,2},{2,0},{4,6},{6,4},{8,10},{10,8},{12,14},{14,12},{16,18},{18,... | collective-permute-start | bytes 786440 | tf_op jit(solution)/shard_map/ppermute | solution.py:419
  83.2 3.6 %collective-permute-start.23 = (f32[256,1024]{1,0:T(8,128)S(1)}, f32[256,1024]{1,0:T(8,128)S(1)}, u32[]{:S(2)}, u32[]{:S(2)}) collective-permute-start(f32[256,1024]{1,0:T(8,128)S(1)} %get-tuple-element.79.top), channel_id=1, source_target_pairs={{0,2},{2,0},{4,6},{6,4},{8,10},{10,8},{12,14},{14,12},{16,18},{18,... | collective-permute-start | bytes 3145736 | tf_op jit(solution)/shard_map/ppermute | solution.py:419
  86.7 3.0 %collective-permute-start.24 = (f32[256,1024]{1,0:T(8,128)S(1)}, f32[256,1024]{1,0:T(8,128)S(1)}, u32[]{:S(2)}, u32[]{:S(2)}) collective-permute-start(f32[256,1024]{1,0:T(8,128)S(1)} %get-tuple-element.85.low), channel_id=1, source_target_pairs={{0,2},{2,0},{4,6},{6,4},{8,10},{10,8},{12,14},{14,12},{16,18},{18,... | collective-permute-start | bytes 3145736 | tf_op jit(solution)/shard_map/ppermute | solution.py:419

commit v12 on v11

--- a/solution.py
+++ b/solution.py
@@ -94,7 +94,7 @@
     stat_in,
     sem,
 ):
-    position, core, x = where[0], where[1], where[2]
+    position, core, x, z = where[0], where[1], where[2], where[3]
     half, width = basis_in.shape[1:]
     size = state.shape[1]
     copies = [
@@ -123,12 +123,12 @@
     def tile_of(i, j):
         return stat_in[i * size : (i + 1) * size, j * size : (j + 1) * size]
 
-    @pl.when(x == 0)
+    @pl.when(z % 2 == 0)
     def _():
         for place in range(SPLIT + 1):
             state[base + place] = tile_of(*UPPER[place]).astype(HALF)
 
-    @pl.when(x == 1)
+    @pl.when(z % 2 == 1)
     def _():
         for place in range(SPLIT, len(UPPER)):
             state[base + place - SPLIT] = tile_of(*UPPER[place]).astype(HALF)
@@ -199,7 +199,7 @@
     base = (1 - position) * TILES
     first = rows * width // size**2
     same = diagonal(size)
-    near_x = where[2] == 0
+    even = where[3] % 2 == 0
     for number, (i, j) in enumerate(UPPER):
         if number < SPLIT:
             pair = mine[first + number], relayed[number]
@@ -207,11 +207,11 @@
             pair = mine[first + SPLIT], mine[first]
         else:
             pair = relayed[number - SPLIT], mine[first + number - SPLIT]
-        value = jnp.where(near_x, pair[0].astype(FULL), pair[1].astype(FULL))
+        value = jnp.where(even, pair[0].astype(FULL), pair[1].astype(FULL))
         if i == j:
             lines = slice(i * 16, (i + 1) * 16)
             line = jnp.where(
-                near_x,
+                even,
                 relayed[SPLIT, lines].astype(FULL),
                 mine[first + SPLIT, lines].astype(FULL),
             )[:1]
@@ -475,7 +475,7 @@
     part, state_mine = lax.optimization_barrier((part, state_mine))
     parts = [part, dp_swap(part, 2), shard_swap(part), cross_swap(part)]
     state_theirs = dp_swap(state_mine, 1)
-    state_relayed = dp_swap(state_mine[tiles:], 2)
+    state_relayed = dp_swap(state_mine[tiles:], 4)
     square = shaped((width, width), HALF)
     bases, left_turned, right_turned, stat = call(
         state_kernel,

time: 91.4 us -> 84.9 us (0.929)
  waiting for transfers between devices: 32 us -> 26.4 us
    ppermute x20, waiting for transfers between devices: 30.2 us -> 21.8 us  [dp_swap(): return lax.ppermute(value, 'dp', [(i, i ^ distance) for i in range(16)])]
    ppermute x1, waiting for transfers between devices: 0.01 us -> 1.69 us  [cross_swap(): return lax.ppermute(value, ('dp', 'shard'), pairs)]
    ppermute x4, waiting for transfers between devices: 1.81 us -> 2.89 us  [shard_swap(): return lax.ppermute(value, 'shard', [(0, 1), (1, 0)])]
  transfers between devices with their start and end apart: 25 -> 25, of which waited for: 10 -> 13; matrix products, arithmetic and copies ran while one was open for 0% -> 0% of each run, Pallas kernels for 32% -> 34%
where the time goes in v12:
time: 84.9 us; the launch traced here: 84.7 us
  Pallas kernels  33 us (39%)
  waiting for transfers between devices  26.4 us (31%)
  starting transfers between devices  23 us (27%)
  local copies, waits for them, and re-layouts  1.31 us (2%)
  between operations  0.98 us (1%)
    ppermute x20, waiting for transfers between devices, dp_swap(): return lax.ppermute(value, 'dp', [(i, i ^ distance) for i in range(16)])  21.8 us
    pallas_call x9, Pallas kernels, call(): pl.pallas_call(kernel, out_shape=outs, in_specs=specs, out_specs=[space]...  20.8 us
    ppermute x20, starting transfers between devices, dp_swap(): return lax.ppermute(value, 'dp', [(i, i ^ distance) for i in range(16)])  16.4 us
    pallas_call x1, Pallas kernels, fast_body(): pl.pallas_call(refresh_kernel, out_shape=[square, square, shaped((half, w...  6.49 us
    ppermute x4, starting transfers between devices, shard_swap(): return lax.ppermute(value, 'shard', [(0, 1), (1, 0)])  5.07 us
    pallas_call x1, Pallas kernels, fast_body(): pl.pallas_call(last_kernel, out_shape=[shaped((half, width), FULL), side,...  2.91 us
    ppermute x4, waiting for transfers between devices, shard_swap(): return lax.ppermute(value, 'shard', [(0, 1), (1, 0)])  2.89 us
    pallas_call x1, Pallas kernels, fast_body(): pl.pallas_call(update_kernel, out_shape=[shaped((rows, width), HALF), sid...  2.79 us
  transfers between devices with their start and end apart: 25, of which 13 were waited for; matrix products, arithmetic and copies ran while one was open for 0% of the time, Pallas kernels for 34%

profile of v12, /device:TPU:0, one launch (start us, length us, event | category | flops | bytes accessed | tf_op | source)
XLA Modules:
  0.0 84.7 jit_solution(6285054100141680554)
XLA Ops:
  0.6 1.3 %dynamic-slice_bitcast_fusion = (bf16[256,1024]{1,0:T(8,128)(2,1)S(1)}, bf16[256,1024]{1,0:T(8,128)(2,1)S(1)}) fusion(bf16[1,512,1024]{2,1,0:T(8,128)(2,1)} %param.7, s32[]{:T(128)S(6)} %select_n.7, s32[]{:T(128)S(6)} %select_n.6), kind=kLoop, calls=%fused_computation | loop fusion | bytes 2097160 | tf_op jit(solution)/shard_map/dynamic_slice | solution.py:428
  1.9 0.5 collective-permute-start
  2.4 0.1 pad_add_fusion.where
  2.5 1.5 %collective-permute-done.came = bf16[256,1024]{1,0:T(8,128)(2,1)S(1)} collective-permute-done((bf16[256,1024]{1,0:T(8,128)(2,1)S(1)}, bf16[256,1024]{1,0:T(8,128)(2,1)S(1)}, u32[]{:S(2)}, u32[]{:S(2)}) %collective-permute-start) | collective-permute-done | bytes 524320 | tf_op jit(solution)/shard_map/ppermute | solution.py:419
  4.0 2.7 %shard_map.102 = (bf16[38,128,128]{2,1,0:T(8,128)(2,1)S(1)}, f32[128,1024]{1,0:T(8,128)S(1)}, bf16[128,1024]{1,0:T(8,128)(2,1)S(1)}) custom-call(s32[4]{0:T(128)S(1)} %pad_add_fusion.where, bf16[256,1024]{1,0:T(8,128)(2,1)S(1)} %get-tuple-element.95.raw, bf16[256,1024]{1,0:T(8,128)(2,1)S(1)} %collective-permute-done.came, f32[512,1024]{1,0:T(8,128)} %left.3, ...), custom_call_target="tpu_custom_call" | custom-call | bytes 4194304 | tf_op jit(solution)/shard_map/pallas_call | solution.py:43
  6.7 0.0 copy-start
  6.7 3.0 %collective-permute-start.8 = (bf16[38,128,128]{2,1,0:T(8,128)(2,1)S(1)}, bf16[38,128,128]{2,1,0:T(8,128)(2,1)S(1)}, u32[]{:S(2)}, u32[]{:S(2)}) collective-permute-start(bf16[38,128,128]{2,1,0:T(8,128)(2,1)S(1)} %get-tuple-element.55), channel_id=1, source_target_pairs={{0,1},{1,0},{2,3},{3,2},{4,5},{5,4},{6,7},{7,6},{8,9},{9,8},{10,11... | collective-permute-start | bytes 3735560 | tf_op jit(solution)/shard_map/ppermute | solution.py:422
  9.7 1.5 %collective-permute-start.1 = (bf16[128,1024]{1,0:T(8,128)(2,1)S(1)}, bf16[128,1024]{1,0:T(8,128)(2,1)S(1)}, u32[]{:S(2)}, u32[]{:S(2)}) collective-permute-start(bf16[128,1024]{1,0:T(8,128)(2,1)S(1)} %get-tuple-element.50), channel_id=1, source_target_pairs={{0,4},{2,6},{4,0},{6,2},{8,12},{10,14},{12,8},{14,10},{16,20},{18,... | collective-permute-start | bytes 786440 | tf_op jit(solution)/shard_map/ppermute | solution.py:419
  11.2 6.6 %collective-permute-done.1.came = bf16[128,1024]{1,0:T(8,128)(2,1)S(1)} collective-permute-done((bf16[128,1024]{1,0:T(8,128)(2,1)S(1)}, bf16[128,1024]{1,0:T(8,128)(2,1)S(1)}, u32[]{:S(2)}, u32[]{:S(2)}) %collective-permute-start.1) | collective-permute-done | bytes 262176 | tf_op jit(solution)/shard_map/ppermute | solution.py:419
  17.7 0.6 shard_map.103
  18.3 1.7 %collective-permute-start.2 = (bf16[32,1024]{1,0:T(8,128)(2,1)S(1)}, bf16[32,1024]{1,0:T(8,128)(2,1)S(1)}, u32[]{:S(2)}, u32[]{:S(2)}) collective-permute-start(bf16[32,1024]{1,0:T(8,128)(2,1)S(1)} %get-tuple-element.52), channel_id=1, source_target_pairs={{0,8},{2,10},{4,12},{6,14},{8,0},{10,2},{12,4},{14,6},{16,24},{18,... | collective-permute-start | bytes 196616 | tf_op jit(solution)/shard_map/ppermute | solution.py:419
  20.0 2.6 %collective-permute-start.3 = (bf16[32,1024]{1,0:T(8,128)(2,1)S(1)}, bf16[32,1024]{1,0:T(8,128)(2,1)S(1)}, u32[]{:S(2)}, u32[]{:S(2)}) collective-permute-start(bf16[32,1024]{1,0:T(8,128)(2,1)S(1)} %get-tuple-element.53), channel_id=1, source_target_pairs={{0,16},{2,18},{4,20},{6,22},{8,24},{10,26},{12,28},{14,30},{16,0},... | collective-permute-start | bytes 196616 | tf_op jit(solution)/shard_map/ppermute | solution.py:419
  22.6 0.2 collective-permute-start.4
  22.8 0.5 collective-permute-done.2.one
  23.2 3.4 %collective-permute-done.3.two = bf16[32,1024]{1,0:T(8,128)(2,1)S(1)} collective-permute-done((bf16[32,1024]{1,0:T(8,128)(2,1)S(1)}, bf16[32,1024]{1,0:T(8,128)(2,1)S(1)}, u32[]{:S(2)}, u32[]{:S(2)}) %collective-permute-start.3) | collective-permute-done | bytes 65568 | tf_op jit(solution)/shard_map/ppermute | solution.py:419
  26.6 2.1 %collective-permute-done.4.three = bf16[32,1024]{1,0:T(8,128)(2,1)S(1)} collective-permute-done((bf16[32,1024]{1,0:T(8,128)(2,1)S(1)}, bf16[32,1024]{1,0:T(8,128)(2,1)S(1)}, u32[]{:S(2)}, u32[]{:S(2)}) %collective-permute-start.4) | collective-permute-done | bytes 65568 | tf_op jit(solution)/shard_map/ppermute | solution.py:419
  28.7 1.1 %collective-permute-start.7 = (bf16[32,1024]{1,0:T(8,128)(2,1)S(1)}, bf16[32,1024]{1,0:T(8,128)(2,1)S(1)}, u32[]{:S(2)}, u32[]{:S(2)}) collective-permute-start(bf16[32,1024]{1,0:T(8,128)(2,1)S(1)} %shard_map.104.refs_0_), channel_id=1, source_target_pairs={{0,24},{2,26},{4,28},{6,30},{8,16},{10,18},{12,20},{14,22},{16,8},... | collective-permute-start | bytes 196616 | tf_op jit(solution)/shard_map/ppermute | solution.py:419
  29.9 0.4 collective-permute-start.6
  30.3 2.9 %collective-permute-start.5 = (bf16[32,1024]{1,0:T(8,128)(2,1)S(1)}, bf16[32,1024]{1,0:T(8,128)(2,1)S(1)}, u32[]{:S(2)}, u32[]{:S(2)}) collective-permute-start(bf16[32,1024]{1,0:T(8,128)(2,1)S(1)} %shard_map.104.refs_0_), channel_id=1, source_target_pairs={{0,8},{2,10},{4,12},{6,14},{8,0},{10,2},{12,4},{14,6},{16,24},{18,... | collective-permute-start | bytes 196616 | tf_op jit(solution)/shard_map/ppermute | solution.py:419
  33.2 1.7 %collective-permute-done.7.refs_3_ = bf16[32,1024]{1,0:T(8,128)(2,1)S(1)} collective-permute-done((bf16[32,1024]{1,0:T(8,128)(2,1)S(1)}, bf16[32,1024]{1,0:T(8,128)(2,1)S(1)}, u32[]{:S(2)}, u32[]{:S(2)}) %collective-permute-start.7) | collective-permute-done | bytes 65568 | tf_op jit(solution)/shard_map/ppermute | solution.py:419
  34.9 1.3 %collective-permute-done.6.refs_2_ = bf16[32,1024]{1,0:T(8,128)(2,1)S(1)} collective-permute-done((bf16[32,1024]{1,0:T(8,128)(2,1)S(1)}, bf16[32,1024]{1,0:T(8,128)(2,1)S(1)}, u32[]{:S(2)}, u32[]{:S(2)}) %collective-permute-start.6) | collective-permute-done | bytes 65568 | tf_op jit(solution)/shard_map/ppermute | solution.py:419
  36.3 0.0 collective-permute-done.5.refs_1_
  36.3 0.6 shard_map.105.own.refs_0_
  36.9 0.5 collective-permute-done.8.mine
  37.3 0.0 collective-permute-start.9
  37.3 1.7 %collective-permute-start.11 = (bf16[128,1024]{1,0:T(8,128)(2,1)S(1)}, bf16[128,1024]{1,0:T(8,128)(2,1)S(1)}, u32[]{:S(2)}, u32[]{:S(2)}) collective-permute-start(bf16[128,1024]{1,0:T(8,128)(2,1)S(1)} %shard_map.105.own.refs_0_), channel_id=1, source_target_pairs={{0,4},{2,6},{4,0},{6,2},{8,12},{10,14},{12,8},{14,10},{16,20},{18,... | collective-permute-start | bytes 786440 | tf_op jit(solution)/shard_map/ppermute | solution.py:419
  39.1 1.5 %collective-permute-start.15 = (bf16[128,1024]{1,0:T(8,128)(2,1)S(1)}, bf16[128,1024]{1,0:T(8,128)(2,1)S(1)}, u32[]{:S(2)}, u32[]{:S(2)}) collective-permute-start(bf16[128,1024]{1,0:T(8,128)(2,1)S(1)} %shard_map.105.own.refs_0_), channel_id=1, source_target_pairs={{0,5},{1,4},{2,7},{3,6},{4,1},{5,0},{6,3},{7,2},{8,13},{9,12},{10,... | collective-permute-start | bytes 786440 | tf_op jit(solution)/shard_map/ppermute | solution.py:426
  40.6 0.3 collective-permute-start.14
  40.9 0.0 copy-start.4
  40.9 1.9 %collective-permute-start.10 = (bf16[6,128,128]{2,1,0:T(8,128)(2,1)S(1)}, bf16[6,128,128]{2,1,0:T(8,128)(2,1)S(1)}, u32[]{:S(2)}, u32[]{:S(2)}) collective-permute-start(bf16[6,128,128]{2,1,0:T(8,128)(2,1)S(1)} %slice.3), channel_id=1, source_target_pairs={{0,8},{2,10},{4,12},{6,14},{8,0},{10,2},{12,4},{14,6},{16,24},{18,... | collective-permute-start | bytes 589832 | tf_op jit(solution)/shard_map/ppermute | solution.py:419
  42.8 4.7 %collective-permute-done.10.relayed = bf16[6,128,128]{2,1,0:T(8,128)(2,1)S(1)} collective-permute-done((bf16[6,128,128]{2,1,0:T(8,128)(2,1)S(1)}, bf16[6,128,128]{2,1,0:T(8,128)(2,1)S(1)}, u32[]{:S(2)}, u32[]{:S(2)}) %collective-permute-start.10) | collective-permute-done | bytes 196640 | tf_op jit(solution)/shard_map/ppermute | solution.py:419
  47.5 0.0 collective-permute-start.12
  47.5 0.0 collective-permute-done.11.over_x.refs_1_
  47.5 0.5 collective-permute-start.13
  48.0 0.0 collective-permute-done.9.theirs
  48.1 3.2 %shard_map.106 = (bf16[2,1024,1024]{2,1,0:T(8,128)(2,1)S(1)}, bf16[1024,1024]{1,0:T(8,128)(2,1)S(1)}, bf16[1024,1024]{1,0:T(8,128)(2,1)S(1)}, f32[1024,1024]{1,0:T(8,128)S(1)}) custom-call(s32[4]{0:T(128)S(1)} %pad_add_fusion.where, f32[512,1024]{1,0:T(8,128)S(1)} %copy-done, f32[512,1024]{1,0:T(8,128)S(1)} %copy-done.1, ...), custom_call_target="tpu_custom_call" | custom-call | bytes 16777216 | tf_op jit(solution)/shard_map/pallas_call | solution.py:43
  51.3 1.7 %collective-permute-done.15.refs_5_ = bf16[128,1024]{1,0:T(8,128)(2,1)S(1)} collective-permute-done((bf16[128,1024]{1,0:T(8,128)(2,1)S(1)}, bf16[128,1024]{1,0:T(8,128)(2,1)S(1)}, u32[]{:S(2)}, u32[]{:S(2)}) %collective-permute-start.15) | collective-permute-done | bytes 262176 | tf_op jit(solution)/shard_map/ppermute | solution.py:426
  53.0 1.4 %collective-permute-done.14.refs_4_ = bf16[128,1024]{1,0:T(8,128)(2,1)S(1)} collective-permute-done((bf16[128,1024]{1,0:T(8,128)(2,1)S(1)}, bf16[128,1024]{1,0:T(8,128)(2,1)S(1)}, u32[]{:S(2)}, u32[]{:S(2)}) %collective-permute-start.14) | collective-permute-done | bytes 262176 | tf_op jit(solution)/shard_map/ppermute | solution.py:422
  54.3 0.0 collective-permute-start.16
  54.3 0.5 collective-permute-start.17
  54.8 0.0 collective-permute-done.12.next_own.refs_2_
  54.8 0.0 collective-permute-done.13.next_over_x.refs_3_
  54.9 1.9 %shard_map.107 = (bf16[512,256]{1,0:T(8,128)(2,1)S(1)}, bf16[512,256]{1,0:T(8,128)(2,1)S(1)}) custom-call(s32[4]{0:T(128)S(1)} %pad_add_fusion.where, f32[512,1024]{1,0:T(8,128)S(1)} %copy-done.4, bf16[2,1024,1024]{2,1,0:T(8,128)(2,1)S(1)} %get-tuple-element.57.bases, bf16[128,1024]{1,0:T(8,128)(2,1)S(1)} %shard_map.105.own.refs_0_, ...), custom_call_target="tpu_custom_call" | custom-call | flops 536870912 | bytes 4194304 | tf_op jit(solution)/shard_map/pallas_call | solution.py:43
  56.7 0.4 collective-permute-start.18
  57.1 0.0 collective-permute-done.16.refs_6_
  57.1 0.0 collective-permute-done.17.refs_7_
  57.1 7.5 %shard_map.108 = (bf16[1024,1024]{1,0:T(8,128)(2,1)S(1)}, bf16[1024,1024]{1,0:T(8,128)(2,1)S(1)}, f32[1024,256]{1,0:T(8,128)S(1)}) custom-call(s32[4]{0:T(128)S(1)} %pad_add_fusion.where, bf16[2,1024,1024]{2,1,0:T(8,128)(2,1)S(1)} %get-tuple-element.57.bases, bf16[1024,1024]{1,0:T(8,128)(2,1)S(1)} %get-tuple-element.58.turned, ...), custom_call_target="tpu_custom_call" | custom-call | flops 3221225472 | bytes 8388608 | tf_op jit(solution)/shard_map/pallas_call | solution.py:43
  64.6 0.4 collective-permute-done.18.came
  65.0 0.0 collective-permute-start.21
  65.0 2.8 %shard_map.109 = (bf16[512,256]{1,0:T(8,128)(2,1)S(1)}, bf16[512,256]{1,0:T(8,128)(2,1)S(1)}) custom-call(s32[4]{0:T(128)S(1)} %pad_add_fusion.where, bf16[2,1024,1024]{2,1,0:T(8,128)(2,1)S(1)} %get-tuple-element.57.bases, bf16[1024,1024]{1,0:T(8,128)(2,1)S(1)} %get-tuple-element.58.turned, bf16[512,256]{1,0:T(8,128)(2,1)S(1)} %get-tuple-element.60.mine, ...), custom_call_target="tpu_custom_call" | custom-call | flops 1073741824 | bytes 4194304 | tf_op jit(solution)/shard_map/pallas_call | solution.py:43
  67.9 1.5 %collective-permute-start.19 = (bf16[512,256]{1,0:T(8,128)(2,1)S(1)}, bf16[512,256]{1,0:T(8,128)(2,1)S(1)}, u32[]{:S(2)}, u32[]{:S(2)}) collective-permute-start(bf16[512,256]{1,0:T(8,128)(2,1)S(1)} %get-tuple-element.74), channel_id=1, source_target_pairs={{0,1},{1,0},{2,3},{3,2},{4,5},{5,4},{6,7},{7,6},{8,9},{9,8},{10,11... | collective-permute-start | bytes 786440 | tf_op jit(solution)/shard_map/ppermute | solution.py:422
  69.3 0.2 collective-permute-start.20
  69.5 6.5 %shard_map.110 = (bf16[1024,1024]{1,0:T(8,128)(2,1)S(1)}, bf16[1024,1024]{1,0:T(8,128)(2,1)S(1)}, f32[256,1024]{1,0:T(8,128)S(1)}, f32[1024,512]{1,0:T(8,128)}) custom-call(s32[4]{0:T(128)S(1)} %pad_add_fusion.where, bf16[1024,1024]{1,0:T(8,128)(2,1)S(1)} %get-tuple-element.71.start, bf16[1024,1024]{1,0:T(8,128)(2,1)S(1)} %get-tuple-element.72.start_turned, ...), custom_call_target="tpu_custom_call" | custom-call | flops 12884901888 | bytes 8388608 | tf_op jit(solution)/shard_map/pallas_call | solution.py:536
  76.0 0.6 collective-permute-done.19.came
  76.7 0.0 collective-permute-done.20.kept_next
  76.7 0.0 collective-permute-done.21.new_next
  76.7 0.0 collective-permute-start.22
  76.7 0.5 collective-permute-start.23
  77.2 2.9 %shard_map.111 = (f32[256,1024]{1,0:T(8,128)S(1)}, f32[512,1024]{1,0:T(8,128)}, f32[512,1024]{1,0:T(8,128)}, f32[1024,512]{1,0:T(8,128)}) custom-call(s32[4]{0:T(128)S(1)} %pad_add_fusion.where, bf16[1024,1024]{1,0:T(8,128)(2,1)S(1)} %get-tuple-element.77.current, bf16[1024,1024]{1,0:T(8,128)(2,1)S(1)} %get-tuple-element.78.turned, ...), custom_call_target="tpu_custom_call", output_to_operand_aliasing={{3}: (5, {})} | custom-call | flops 1073741824 | bytes 4194304 | tf_op jit(solution)/shard_map/pallas_call | solution.py:555
  80.1 0.0 collective-permute-done.22.came_next
  80.1 0.1 collective-permute-start.24
  80.2 0.0 collective-permute-done.23.top_next
  80.2 2.8 %shard_map.112 = (bf16[512,1024]{1,0:T(8,128)(2,1)}, f32[512,1024]{1,0:T(8,128)}, f32[512,1024]{1,0:T(8,128)}) custom-call(s32[4]{0:T(128)S(1)} %pad_add_fusion.where, bf16[512,256]{1,0:T(8,128)(2,1)S(1)} %get-tuple-element.68.kept, bf16[512,256]{1,0:T(8,128)(2,1)S(1)} %collective-permute-done.19.came, ...), custom_call_target="tpu_custom_call", output_to_operand_aliasing={{1}: (8, {}), {2}: (9, {})} | custom-call | flops 1073741824 | bytes 4194304 | tf_op jit(solution)/shard_map/pallas_call | solution.py:567
  83.1 1.5 %shard_map.113 = (f32[512,1024]{1,0:T(8,128)}, f32[512,1024]{1,0:T(8,128)}) custom-call(s32[4]{0:T(128)S(1)} %pad_add_fusion.where, f32[256,1024]{1,0:T(8,128)S(1)} %collective-permute-done.24.low, f32[512,1024]{1,0:T(8,128)} %get-tuple-element.90.left_in, f32[512,1024]{1,0:T(8,128)} %get-tuple-element.91.right_in), custom_call_target="tpu_custom_call", output_to_operand_aliasing={{0}: (2, {}), {1}: (3, {})} | custom-call | bytes 2097152 | tf_op jit(solution)/shard_map/pallas_call | solution.py:43
  (13 shorter events, 0.1 us)
Async XLA Ops:
  1.9 2.1 %collective-permute-start = (bf16[256,1024]{1,0:T(8,128)(2,1)S(1)}, bf16[256,1024]{1,0:T(8,128)(2,1)S(1)}, u32[]{:S(2)}, u32[]{:S(2)}) collective-permute-start(bf16[256,1024]{1,0:T(8,128)(2,1)S(1)} %get-tuple-element.94), channel_id=1, source_target_pairs={{0,2},{2,0},{4,6},{6,4},{8,10},{10,8},{12,14},{14,12},{16,18},{18,... | collective-permute-start | bytes 1572872 | tf_op jit(solution)/shard_map/ppermute | solution.py:419
  4.0 44.1 %copy-start.1 = (f32[512,1024]{1,0:T(8,128)S(1)}, f32[512,1024]{1,0:T(8,128)}, u32[]{:S(2)}) copy-start(f32[512,1024]{1,0:T(8,128)} %right.3) | copy-start | bytes 6291460
  4.0 44.1 %copy-start.2 = (f32[512,1024]{1,0:T(8,128)S(1)}, f32[512,1024]{1,0:T(8,128)}, u32[]{:S(2)}) copy-start(f32[512,1024]{1,0:T(8,128)} %stat_left.3) | copy-start | bytes 6291460
  4.0 44.1 %copy-start.3 = (f32[512,1024]{1,0:T(8,128)S(1)}, f32[512,1024]{1,0:T(8,128)}, u32[]{:S(2)}) copy-start(f32[512,1024]{1,0:T(8,128)} %stat_right.3) | copy-start | bytes 6291460
  6.7 41.4 %copy-start = (f32[512,1024]{1,0:T(8,128)S(1)}, f32[512,1024]{1,0:T(8,128)}, u32[]{:S(2)}) copy-start(f32[512,1024]{1,0:T(8,128)} %left.3) | copy-start | bytes 6291460
  6.7 30.6 %collective-permute-start.8 = (bf16[38,128,128]{2,1,0:T(8,128)(2,1)S(1)}, bf16[38,128,128]{2,1,0:T(8,128)(2,1)S(1)}, u32[]{:S(2)}, u32[]{:S(2)}) collective-permute-start(bf16[38,128,128]{2,1,0:T(8,128)(2,1)S(1)} %get-tuple-element.55), channel_id=1, source_target_pairs={{0,1},{1,0},{2,3},{3,2},{4,5},{5,4},{6,7},{7,6},{8,9},{9,8},{10,11... | collective-permute-start | bytes 3735560 | tf_op jit(solution)/shard_map/ppermute | solution.py:422
  9.7 8.1 %collective-permute-start.1 = (bf16[128,1024]{1,0:T(8,128)(2,1)S(1)}, bf16[128,1024]{1,0:T(8,128)(2,1)S(1)}, u32[]{:S(2)}, u32[]{:S(2)}) collective-permute-start(bf16[128,1024]{1,0:T(8,128)(2,1)S(1)} %get-tuple-element.50), channel_id=1, source_target_pairs={{0,4},{2,6},{4,0},{6,2},{8,12},{10,14},{12,8},{14,10},{16,20},{18,... | collective-permute-start | bytes 786440 | tf_op jit(solution)/shard_map/ppermute | solution.py:419
  18.3 4.9 %collective-permute-start.2 = (bf16[32,1024]{1,0:T(8,128)(2,1)S(1)}, bf16[32,1024]{1,0:T(8,128)(2,1)S(1)}, u32[]{:S(2)}, u32[]{:S(2)}) collective-permute-start(bf16[32,1024]{1,0:T(8,128)(2,1)S(1)} %get-tuple-element.52), channel_id=1, source_target_pairs={{0,8},{2,10},{4,12},{6,14},{8,0},{10,2},{12,4},{14,6},{16,24},{18,... | collective-permute-start | bytes 196616 | tf_op jit(solution)/shard_map/ppermute | solution.py:419
  20.0 6.6 %collective-permute-start.3 = (bf16[32,1024]{1,0:T(8,128)(2,1)S(1)}, bf16[32,1024]{1,0:T(8,128)(2,1)S(1)}, u32[]{:S(2)}, u32[]{:S(2)}) collective-permute-start(bf16[32,1024]{1,0:T(8,128)(2,1)S(1)} %get-tuple-element.53), channel_id=1, source_target_pairs={{0,16},{2,18},{4,20},{6,22},{8,24},{10,26},{12,28},{14,30},{16,0},... | collective-permute-start | bytes 196616 | tf_op jit(solution)/shard_map/ppermute | solution.py:419
  22.6 6.1 %collective-permute-start.4 = (bf16[32,1024]{1,0:T(8,128)(2,1)S(1)}, bf16[32,1024]{1,0:T(8,128)(2,1)S(1)}, u32[]{:S(2)}, u32[]{:S(2)}) collective-permute-start(bf16[32,1024]{1,0:T(8,128)(2,1)S(1)} %get-tuple-element.54), channel_id=1, source_target_pairs={{0,24},{2,26},{4,28},{6,30},{8,16},{10,18},{12,20},{14,22},{16,8},... | collective-permute-start | bytes 196616 | tf_op jit(solution)/shard_map/ppermute | solution.py:419
  28.7 6.2 %collective-permute-start.7 = (bf16[32,1024]{1,0:T(8,128)(2,1)S(1)}, bf16[32,1024]{1,0:T(8,128)(2,1)S(1)}, u32[]{:S(2)}, u32[]{:S(2)}) collective-permute-start(bf16[32,1024]{1,0:T(8,128)(2,1)S(1)} %shard_map.104.refs_0_), channel_id=1, source_target_pairs={{0,24},{2,26},{4,28},{6,30},{8,16},{10,18},{12,20},{14,22},{16,8},... | collective-permute-start | bytes 196616 | tf_op jit(solution)/shard_map/ppermute | solution.py:419
  29.9 6.4 %collective-permute-start.6 = (bf16[32,1024]{1,0:T(8,128)(2,1)S(1)}, bf16[32,1024]{1,0:T(8,128)(2,1)S(1)}, u32[]{:S(2)}, u32[]{:S(2)}) collective-permute-start(bf16[32,1024]{1,0:T(8,128)(2,1)S(1)} %shard_map.104.refs_0_), channel_id=1, source_target_pairs={{0,16},{2,18},{4,20},{6,22},{8,24},{10,26},{12,28},{14,30},{16,0},... | collective-permute-start | bytes 196616 | tf_op jit(solution)/shard_map/ppermute | solution.py:419
  30.3 6.0 %collective-permute-start.5 = (bf16[32,1024]{1,0:T(8,128)(2,1)S(1)}, bf16[32,1024]{1,0:T(8,128)(2,1)S(1)}, u32[]{:S(2)}, u32[]{:S(2)}) collective-permute-start(bf16[32,1024]{1,0:T(8,128)(2,1)S(1)} %shard_map.104.refs_0_), channel_id=1, source_target_pairs={{0,8},{2,10},{4,12},{6,14},{8,0},{10,2},{12,4},{14,6},{16,24},{18,... | collective-permute-start | bytes 196616 | tf_op jit(solution)/shard_map/ppermute | solution.py:419
  37.3 10.7 %collective-permute-start.9 = (bf16[38,128,128]{2,1,0:T(8,128)(2,1)S(1)}, bf16[38,128,128]{2,1,0:T(8,128)(2,1)S(1)}, u32[]{:S(2)}, u32[]{:S(2)}) collective-permute-start(bf16[38,128,128]{2,1,0:T(8,128)(2,1)S(1)} %collective-permute-done.8.mine), channel_id=1, source_target_pairs={{0,2},{2,0},{4,6},{6,4},{8,10},{10,8},{12,14},{14,12},{16,18},{18,... | collective-permute-start | bytes 3735560 | tf_op jit(solution)/shard_map/ppermute | solution.py:419
  37.3 10.2 %collective-permute-start.11 = (bf16[128,1024]{1,0:T(8,128)(2,1)S(1)}, bf16[128,1024]{1,0:T(8,128)(2,1)S(1)}, u32[]{:S(2)}, u32[]{:S(2)}) collective-permute-start(bf16[128,1024]{1,0:T(8,128)(2,1)S(1)} %shard_map.105.own.refs_0_), channel_id=1, source_target_pairs={{0,4},{2,6},{4,0},{6,2},{8,12},{10,14},{12,8},{14,10},{16,20},{18,... | collective-permute-start | bytes 786440 | tf_op jit(solution)/shard_map/ppermute | solution.py:419
  39.1 13.9 %collective-permute-start.15 = (bf16[128,1024]{1,0:T(8,128)(2,1)S(1)}, bf16[128,1024]{1,0:T(8,128)(2,1)S(1)}, u32[]{:S(2)}, u32[]{:S(2)}) collective-permute-start(bf16[128,1024]{1,0:T(8,128)(2,1)S(1)} %shard_map.105.own.refs_0_), channel_id=1, source_target_pairs={{0,5},{1,4},{2,7},{3,6},{4,1},{5,0},{6,3},{7,2},{8,13},{9,12},{10,... | collective-permute-start | bytes 786440 | tf_op jit(solution)/shard_map/ppermute | solution.py:426
  40.6 13.8 %collective-permute-start.14 = (bf16[128,1024]{1,0:T(8,128)(2,1)S(1)}, bf16[128,1024]{1,0:T(8,128)(2,1)S(1)}, u32[]{:S(2)}, u32[]{:S(2)}) collective-permute-start(bf16[128,1024]{1,0:T(8,128)(2,1)S(1)} %shard_map.105.own.refs_0_), channel_id=1, source_target_pairs={{0,1},{1,0},{2,3},{3,2},{4,5},{5,4},{6,7},{7,6},{8,9},{9,8},{10,11... | collective-permute-start | bytes 786440 | tf_op jit(solution)/shard_map/ppermute | solution.py:422
  40.9 14.0 %copy-start.4 = (f32[512,1024]{1,0:T(8,128)S(1)}, f32[512,1024]{1,0:T(8,128)}, u32[]{:S(2)}) copy-start(f32[512,1024]{1,0:T(8,128)} %moment.1) | copy-start | bytes 6291460
  40.9 6.7 %collective-permute-start.10 = (bf16[6,128,128]{2,1,0:T(8,128)(2,1)S(1)}, bf16[6,128,128]{2,1,0:T(8,128)(2,1)S(1)}, u32[]{:S(2)}, u32[]{:S(2)}) collective-permute-start(bf16[6,128,128]{2,1,0:T(8,128)(2,1)S(1)} %slice.3), channel_id=1, source_target_pairs={{0,8},{2,10},{4,12},{6,14},{8,0},{10,2},{12,4},{14,6},{16,24},{18,... | collective-permute-start | bytes 589832 | tf_op jit(solution)/shard_map/ppermute | solution.py:419
  47.5 7.3 %collective-permute-start.12 = (bf16[128,1024]{1,0:T(8,128)(2,1)S(1)}, bf16[128,1024]{1,0:T(8,128)(2,1)S(1)}, u32[]{:S(2)}, u32[]{:S(2)}) collective-permute-start(bf16[128,1024]{1,0:T(8,128)(2,1)S(1)} %shard_map.105.own.refs_0_), channel_id=1, source_target_pairs={{0,2},{2,0},{4,6},{6,4},{8,10},{10,8},{12,14},{14,12},{16,18},{18,... | collective-permute-start | bytes 786440 | tf_op jit(solution)/shard_map/ppermute | solution.py:419
  47.5 7.3 %collective-permute-start.13 = (bf16[128,1024]{1,0:T(8,128)(2,1)S(1)}, bf16[128,1024]{1,0:T(8,128)(2,1)S(1)}, u32[]{:S(2)}, u32[]{:S(2)}) collective-permute-start(bf16[128,1024]{1,0:T(8,128)(2,1)S(1)} %collective-permute-done.11.over_x.refs_1_), channel_id=1, source_target_pairs={{0,2},{2,0},{4,6},{6,4},{8,10},{10,8},{12,14},{14,12},{16,18},{18,... | collective-permute-start | bytes 786440 | tf_op jit(solution)/shard_map/ppermute | solution.py:419
  54.3 2.8 %copy-start.5 = (f32[1024,512]{1,0:T(8,128)S(1)}, f32[1024,512]{1,0:T(8,128)}, u32[]{:S(2)}) copy-start(f32[1024,512]{1,0:T(8,128)} %second.1) | copy-start | bytes 6291460
  54.3 2.8 %collective-permute-start.16 = (bf16[128,1024]{1,0:T(8,128)(2,1)S(1)}, bf16[128,1024]{1,0:T(8,128)(2,1)S(1)}, u32[]{:S(2)}, u32[]{:S(2)}) collective-permute-start(bf16[128,1024]{1,0:T(8,128)(2,1)S(1)} %collective-permute-done.14.refs_4_), channel_id=1, source_target_pairs={{0,2},{2,0},{4,6},{6,4},{8,10},{10,8},{12,14},{14,12},{16,18},{18,... | collective-permute-start | bytes 786440 | tf_op jit(solution)/shard_map/ppermute | solution.py:419
  54.3 2.8 %collective-permute-start.17 = (bf16[128,1024]{1,0:T(8,128)(2,1)S(1)}, bf16[128,1024]{1,0:T(8,128)(2,1)S(1)}, u32[]{:S(2)}, u32[]{:S(2)}) collective-permute-start(bf16[128,1024]{1,0:T(8,128)(2,1)S(1)} %collective-permute-done.15.refs_5_), channel_id=1, source_target_pairs={{0,2},{2,0},{4,6},{6,4},{8,10},{10,8},{12,14},{14,12},{16,18},{18,... | collective-permute-start | bytes 786440 | tf_op jit(solution)/shard_map/ppermute | solution.py:419
  56.7 8.3 %collective-permute-start.18 = (bf16[512,256]{1,0:T(8,128)(2,1)S(1)}, bf16[512,256]{1,0:T(8,128)(2,1)S(1)}, u32[]{:S(2)}, u32[]{:S(2)}) collective-permute-start(bf16[512,256]{1,0:T(8,128)(2,1)S(1)} %get-tuple-element.65), channel_id=1, source_target_pairs={{0,1},{1,0},{2,3},{3,2},{4,5},{5,4},{6,7},{7,6},{8,9},{9,8},{10,11... | collective-permute-start | bytes 786440 | tf_op jit(solution)/shard_map/ppermute | solution.py:422
  65.0 11.6 %collective-permute-start.21 = (f32[1024,256]{1,0:T(8,128)S(1)}, f32[1024,256]{1,0:T(8,128)S(1)}, u32[]{:S(2)}, u32[]{:S(2)}) collective-permute-start(f32[1024,256]{1,0:T(8,128)S(1)} %get-tuple-element.67.new), channel_id=1, source_target_pairs={{0,2},{2,0},{4,6},{6,4},{8,10},{10,8},{12,14},{14,12},{16,18},{18,... | collective-permute-start | bytes 3145736 | tf_op jit(solution)/shard_map/ppermute | solution.py:419
  67.9 8.8 %collective-permute-start.19 = (bf16[512,256]{1,0:T(8,128)(2,1)S(1)}, bf16[512,256]{1,0:T(8,128)(2,1)S(1)}, u32[]{:S(2)}, u32[]{:S(2)}) collective-permute-start(bf16[512,256]{1,0:T(8,128)(2,1)S(1)} %get-tuple-element.74), channel_id=1, source_target_pairs={{0,1},{1,0},{2,3},{3,2},{4,5},{5,4},{6,7},{7,6},{8,9},{9,8},{10,11... | collective-permute-start | bytes 786440 | tf_op jit(solution)/shard_map/ppermute | solution.py:422
  69.3 7.3 %collective-permute-start.20 = (bf16[512,256]{1,0:T(8,128)(2,1)S(1)}, bf16[512,256]{1,0:T(8,128)(2,1)S(1)}, u32[]{:S(2)}, u32[]{:S(2)}) collective-permute-start(bf16[512,256]{1,0:T(8,128)(2,1)S(1)} %get-tuple-element.68.kept), channel_id=1, source_target_pairs={{0,2},{2,0},{4,6},{6,4},{8,10},{10,8},{12,14},{14,12},{16,18},{18,... | collective-permute-start | bytes 786440 | tf_op jit(solution)/shard_map/ppermute | solution.py:419
  76.7 3.4 %collective-permute-start.22 = (bf16[512,256]{1,0:T(8,128)(2,1)S(1)}, bf16[512,256]{1,0:T(8,128)(2,1)S(1)}, u32[]{:S(2)}, u32[]{:S(2)}) collective-permute-start(bf16[512,256]{1,0:T(8,128)(2,1)S(1)} %collective-permute-done.19.came), channel_id=1, source_target_pairs={{0,2},{2,0},{4,6},{6,4},{8,10},{10,8},{12,14},{14,12},{16,18},{18,... | collective-permute-start | bytes 786440 | tf_op jit(solution)/shard_map/ppermute | solution.py:419
  76.7 3.6 %collective-permute-start.23 = (f32[256,1024]{1,0:T(8,128)S(1)}, f32[256,1024]{1,0:T(8,128)S(1)}, u32[]{:S(2)}, u32[]{:S(2)}) collective-permute-start(f32[256,1024]{1,0:T(8,128)S(1)} %get-tuple-element.79.top), channel_id=1, source_target_pairs={{0,2},{2,0},{4,6},{6,4},{8,10},{10,8},{12,14},{14,12},{16,18},{18,... | collective-permute-start | bytes 3145736 | tf_op jit(solution)/shard_map/ppermute | solution.py:419
  80.1 2.9 %collective-permute-start.24 = (f32[256,1024]{1,0:T(8,128)S(1)}, f32[256,1024]{1,0:T(8,128)S(1)}, u32[]{:S(2)}, u32[]{:S(2)}) collective-permute-start(f32[256,1024]{1,0:T(8,128)S(1)} %get-tuple-element.85.low), channel_id=1, source_target_pairs={{0,2},{2,0},{4,6},{6,4},{8,10},{10,8},{12,14},{14,12},{16,18},{18,... | collective-permute-start | bytes 3145736 | tf_op jit(solution)/shard_map/ppermute | solution.py:419

commit v13 on v12

--- a/solution.py
+++ b/solution.py
@@ -456,7 +456,7 @@
         [SMEM] + [VMEM] * 2,
         moved=2**20,
     )
-    pieces = [dp_swap(value, 4 * (k + 1)) for k, value in enumerate(sent)]
+    pieces = [dp_swap(sent[k], 4 * (k + 1)) for k in reversed(range(3))]
     (piece,) = call(
         third_sum_kernel,
         [shaped((chunk, width), HALF)],

time: 84.9 us -> 84.9 us (level)
    ppermute x20, waiting for transfers between devices: 21.8 us -> 20.7 us  [dp_swap(): return lax.ppermute(value, 'dp', [(i, i ^ distance) for i in range(16)])]
    ppermute x4, waiting for transfers between devices: 2.89 us -> 3.95 us  [shard_swap(): return lax.ppermute(value, 'shard', [(0, 1), (1, 0)])]
  transfers between devices with their start and end apart: 25 -> 25, of which waited for: 13 -> 12; matrix products, arithmetic and copies ran while one was open for 0% -> 0% of each run, Pallas kernels for 34% -> 34%
where the time goes in v13:
time: 84.9 us; the launch traced here: 84.7 us
  Pallas kernels  33 us (39%)
  waiting for transfers between devices  26.4 us (31%)
  starting transfers between devices  23 us (27%)
  local copies, waits for them, and re-layouts  1.31 us (2%)
  between operations  0.98 us (1%)
    pallas_call x9, Pallas kernels, call(): pl.pallas_call(kernel, out_shape=outs, in_specs=specs, out_specs=[space]...  20.8 us
    ppermute x20, waiting for transfers between devices, dp_swap(): return lax.ppermute(value, 'dp', [(i, i ^ distance) for i in range(16)])  20.7 us
    ppermute x20, starting transfers between devices, dp_swap(): return lax.ppermute(value, 'dp', [(i, i ^ distance) for i in range(16)])  16.4 us
    pallas_call x1, Pallas kernels, fast_body(): pl.pallas_call(refresh_kernel, out_shape=[square, square, shaped((half, w...  6.49 us
    ppermute x4, starting transfers between devices, shard_swap(): return lax.ppermute(value, 'shard', [(0, 1), (1, 0)])  5.07 us
    ppermute x4, waiting for transfers between devices, shard_swap(): return lax.ppermute(value, 'shard', [(0, 1), (1, 0)])  3.95 us
    pallas_call x1, Pallas kernels, fast_body(): pl.pallas_call(last_kernel, out_shape=[shaped((half, width), FULL), side,...  2.91 us
    pallas_call x1, Pallas kernels, fast_body(): pl.pallas_call(update_kernel, out_shape=[shaped((rows, width), HALF), sid...  2.79 us
  transfers between devices with their start and end apart: 25, of which 12 were waited for; matrix products, arithmetic and copies ran while one was open for 0% of the time, Pallas kernels for 34%

profile of v13, /device:TPU:0, one launch (start us, length us, event | category | flops | bytes accessed | tf_op | source)
XLA Modules:
  0.0 84.7 jit_solution(10997399954224606689)
XLA Ops:
  0.6 1.3 %dynamic-slice_bitcast_fusion = (bf16[256,1024]{1,0:T(8,128)(2,1)S(1)}, bf16[256,1024]{1,0:T(8,128)(2,1)S(1)}) fusion(bf16[1,512,1024]{2,1,0:T(8,128)(2,1)} %param.7, s32[]{:T(128)S(6)} %select_n.7, s32[]{:T(128)S(6)} %select_n.6), kind=kLoop, calls=%fused_computation | loop fusion | bytes 2097160 | tf_op jit(solution)/shard_map/dynamic_slice | solution.py:428
  1.9 0.5 collective-permute-start
  2.4 0.1 pad_add_fusion.where
  2.5 1.5 %collective-permute-done.came = bf16[256,1024]{1,0:T(8,128)(2,1)S(1)} collective-permute-done((bf16[256,1024]{1,0:T(8,128)(2,1)S(1)}, bf16[256,1024]{1,0:T(8,128)(2,1)S(1)}, u32[]{:S(2)}, u32[]{:S(2)}) %collective-permute-start) | collective-permute-done | bytes 524320 | tf_op jit(solution)/shard_map/ppermute | solution.py:419
  4.0 2.7 %shard_map.102 = (bf16[38,128,128]{2,1,0:T(8,128)(2,1)S(1)}, f32[128,1024]{1,0:T(8,128)S(1)}, bf16[128,1024]{1,0:T(8,128)(2,1)S(1)}) custom-call(s32[4]{0:T(128)S(1)} %pad_add_fusion.where, bf16[256,1024]{1,0:T(8,128)(2,1)S(1)} %get-tuple-element.95.raw, bf16[256,1024]{1,0:T(8,128)(2,1)S(1)} %collective-permute-done.came, f32[512,1024]{1,0:T(8,128)} %left.3, ...), custom_call_target="tpu_custom_call" | custom-call | bytes 4194304 | tf_op jit(solution)/shard_map/pallas_call | solution.py:43
  6.7 0.0 copy-start
  6.7 3.0 %collective-permute-start.8 = (bf16[38,128,128]{2,1,0:T(8,128)(2,1)S(1)}, bf16[38,128,128]{2,1,0:T(8,128)(2,1)S(1)}, u32[]{:S(2)}, u32[]{:S(2)}) collective-permute-start(bf16[38,128,128]{2,1,0:T(8,128)(2,1)S(1)} %get-tuple-element.55), channel_id=1, source_target_pairs={{0,1},{1,0},{2,3},{3,2},{4,5},{5,4},{6,7},{7,6},{8,9},{9,8},{10,11... | collective-permute-start | bytes 3735560 | tf_op jit(solution)/shard_map/ppermute | solution.py:422
  9.7 1.5 %collective-permute-start.1 = (bf16[128,1024]{1,0:T(8,128)(2,1)S(1)}, bf16[128,1024]{1,0:T(8,128)(2,1)S(1)}, u32[]{:S(2)}, u32[]{:S(2)}) collective-permute-start(bf16[128,1024]{1,0:T(8,128)(2,1)S(1)} %get-tuple-element.50), channel_id=1, source_target_pairs={{0,4},{2,6},{4,0},{6,2},{8,12},{10,14},{12,8},{14,10},{16,20},{18,... | collective-permute-start | bytes 786440 | tf_op jit(solution)/shard_map/ppermute | solution.py:419
  11.2 6.6 %collective-permute-done.1.came = bf16[128,1024]{1,0:T(8,128)(2,1)S(1)} collective-permute-done((bf16[128,1024]{1,0:T(8,128)(2,1)S(1)}, bf16[128,1024]{1,0:T(8,128)(2,1)S(1)}, u32[]{:S(2)}, u32[]{:S(2)}) %collective-permute-start.1) | collective-permute-done | bytes 262176 | tf_op jit(solution)/shard_map/ppermute | solution.py:419
  17.7 0.6 shard_map.103
  18.3 3.7 %collective-permute-start.2 = (bf16[32,1024]{1,0:T(8,128)(2,1)S(1)}, bf16[32,1024]{1,0:T(8,128)(2,1)S(1)}, u32[]{:S(2)}, u32[]{:S(2)}) collective-permute-start(bf16[32,1024]{1,0:T(8,128)(2,1)S(1)} %get-tuple-element.52), channel_id=1, source_target_pairs={{0,24},{2,26},{4,28},{6,30},{8,16},{10,18},{12,20},{14,22},{16,8},... | collective-permute-start | bytes 196616 | tf_op jit(solution)/shard_map/ppermute | solution.py:419
  22.1 0.0 collective-permute-start.3
  22.1 0.7 collective-permute-start.4
  22.8 2.0 %collective-permute-done.2.one = bf16[32,1024]{1,0:T(8,128)(2,1)S(1)} collective-permute-done((bf16[32,1024]{1,0:T(8,128)(2,1)S(1)}, bf16[32,1024]{1,0:T(8,128)(2,1)S(1)}, u32[]{:S(2)}, u32[]{:S(2)}) %collective-permute-start.2) | collective-permute-done | bytes 65568 | tf_op jit(solution)/shard_map/ppermute | solution.py:419
  24.8 2.6 %collective-permute-done.3.two = bf16[32,1024]{1,0:T(8,128)(2,1)S(1)} collective-permute-done((bf16[32,1024]{1,0:T(8,128)(2,1)S(1)}, bf16[32,1024]{1,0:T(8,128)(2,1)S(1)}, u32[]{:S(2)}, u32[]{:S(2)}) %collective-permute-start.3) | collective-permute-done | bytes 65568 | tf_op jit(solution)/shard_map/ppermute | solution.py:419
  27.4 0.0 collective-permute-done.4.three
  27.4 2.3 %collective-permute-start.7 = (bf16[32,1024]{1,0:T(8,128)(2,1)S(1)}, bf16[32,1024]{1,0:T(8,128)(2,1)S(1)}, u32[]{:S(2)}, u32[]{:S(2)}) collective-permute-start(bf16[32,1024]{1,0:T(8,128)(2,1)S(1)} %shard_map.104.refs_0_), channel_id=1, source_target_pairs={{0,24},{2,26},{4,28},{6,30},{8,16},{10,18},{12,20},{14,22},{16,8},... | collective-permute-start | bytes 196616 | tf_op jit(solution)/shard_map/ppermute | solution.py:419
  29.8 0.0 collective-permute-start.6
  29.8 2.1 %collective-permute-start.5 = (bf16[32,1024]{1,0:T(8,128)(2,1)S(1)}, bf16[32,1024]{1,0:T(8,128)(2,1)S(1)}, u32[]{:S(2)}, u32[]{:S(2)}) collective-permute-start(bf16[32,1024]{1,0:T(8,128)(2,1)S(1)} %shard_map.104.refs_0_), channel_id=1, source_target_pairs={{0,8},{2,10},{4,12},{6,14},{8,0},{10,2},{12,4},{14,6},{16,24},{18,... | collective-permute-start | bytes 196616 | tf_op jit(solution)/shard_map/ppermute | solution.py:419
  31.9 1.8 %collective-permute-done.7.refs_3_ = bf16[32,1024]{1,0:T(8,128)(2,1)S(1)} collective-permute-done((bf16[32,1024]{1,0:T(8,128)(2,1)S(1)}, bf16[32,1024]{1,0:T(8,128)(2,1)S(1)}, u32[]{:S(2)}, u32[]{:S(2)}) %collective-permute-start.7) | collective-permute-done | bytes 65568 | tf_op jit(solution)/shard_map/ppermute | solution.py:419
  33.7 1.5 %collective-permute-done.6.refs_2_ = bf16[32,1024]{1,0:T(8,128)(2,1)S(1)} collective-permute-done((bf16[32,1024]{1,0:T(8,128)(2,1)S(1)}, bf16[32,1024]{1,0:T(8,128)(2,1)S(1)}, u32[]{:S(2)}, u32[]{:S(2)}) %collective-permute-start.6) | collective-permute-done | bytes 65568 | tf_op jit(solution)/shard_map/ppermute | solution.py:419
  35.2 0.0 collective-permute-done.5.refs_1_
  35.2 0.6 shard_map.105.own.refs_0_
  35.8 1.5 %collective-permute-done.8.mine = bf16[38,128,128]{2,1,0:T(8,128)(2,1)S(1)} collective-permute-done((bf16[38,128,128]{2,1,0:T(8,128)(2,1)S(1)}, bf16[38,128,128]{2,1,0:T(8,128)(2,1)S(1)}, u32[]{:S(2)}, u32[]{:S(2)}) %collective-permute-start.8) | collective-permute-done | bytes 1245216 | tf_op jit(solution)/shard_map/ppermute | solution.py:422
  37.3 0.0 collective-permute-start.9
  37.3 1.7 %collective-permute-start.11 = (bf16[128,1024]{1,0:T(8,128)(2,1)S(1)}, bf16[128,1024]{1,0:T(8,128)(2,1)S(1)}, u32[]{:S(2)}, u32[]{:S(2)}) collective-permute-start(bf16[128,1024]{1,0:T(8,128)(2,1)S(1)} %shard_map.105.own.refs_0_), channel_id=1, source_target_pairs={{0,4},{2,6},{4,0},{6,2},{8,12},{10,14},{12,8},{14,10},{16,20},{18,... | collective-permute-start | bytes 786440 | tf_op jit(solution)/shard_map/ppermute | solution.py:419
  39.1 1.5 %collective-permute-start.15 = (bf16[128,1024]{1,0:T(8,128)(2,1)S(1)}, bf16[128,1024]{1,0:T(8,128)(2,1)S(1)}, u32[]{:S(2)}, u32[]{:S(2)}) collective-permute-start(bf16[128,1024]{1,0:T(8,128)(2,1)S(1)} %shard_map.105.own.refs_0_), channel_id=1, source_target_pairs={{0,5},{1,4},{2,7},{3,6},{4,1},{5,0},{6,3},{7,2},{8,13},{9,12},{10,... | collective-permute-start | bytes 786440 | tf_op jit(solution)/shard_map/ppermute | solution.py:426
  40.6 0.3 collective-permute-start.14
  40.9 0.0 copy-start.4
  40.9 1.9 %collective-permute-start.10 = (bf16[6,128,128]{2,1,0:T(8,128)(2,1)S(1)}, bf16[6,128,128]{2,1,0:T(8,128)(2,1)S(1)}, u32[]{:S(2)}, u32[]{:S(2)}) collective-permute-start(bf16[6,128,128]{2,1,0:T(8,128)(2,1)S(1)} %slice.3), channel_id=1, source_target_pairs={{0,8},{2,10},{4,12},{6,14},{8,0},{10,2},{12,4},{14,6},{16,24},{18,... | collective-permute-start | bytes 589832 | tf_op jit(solution)/shard_map/ppermute | solution.py:419
  42.8 4.7 %collective-permute-done.10.relayed = bf16[6,128,128]{2,1,0:T(8,128)(2,1)S(1)} collective-permute-done((bf16[6,128,128]{2,1,0:T(8,128)(2,1)S(1)}, bf16[6,128,128]{2,1,0:T(8,128)(2,1)S(1)}, u32[]{:S(2)}, u32[]{:S(2)}) %collective-permute-start.10) | collective-permute-done | bytes 196640 | tf_op jit(solution)/shard_map/ppermute | solution.py:419
  47.5 0.0 collective-permute-start.12
  47.5 0.0 collective-permute-done.11.over_x.refs_1_
  47.5 0.5 collective-permute-start.13
  48.0 0.0 collective-permute-done.9.theirs
  48.1 3.2 %shard_map.106 = (bf16[2,1024,1024]{2,1,0:T(8,128)(2,1)S(1)}, bf16[1024,1024]{1,0:T(8,128)(2,1)S(1)}, bf16[1024,1024]{1,0:T(8,128)(2,1)S(1)}, f32[1024,1024]{1,0:T(8,128)S(1)}) custom-call(s32[4]{0:T(128)S(1)} %pad_add_fusion.where, f32[512,1024]{1,0:T(8,128)S(1)} %copy-done, f32[512,1024]{1,0:T(8,128)S(1)} %copy-done.1, ...), custom_call_target="tpu_custom_call" | custom-call | bytes 16777216 | tf_op jit(solution)/shard_map/pallas_call | solution.py:43
  51.3 1.7 %collective-permute-done.15.refs_5_ = bf16[128,1024]{1,0:T(8,128)(2,1)S(1)} collective-permute-done((bf16[128,1024]{1,0:T(8,128)(2,1)S(1)}, bf16[128,1024]{1,0:T(8,128)(2,1)S(1)}, u32[]{:S(2)}, u32[]{:S(2)}) %collective-permute-start.15) | collective-permute-done | bytes 262176 | tf_op jit(solution)/shard_map/ppermute | solution.py:426
  53.0 1.4 %collective-permute-done.14.refs_4_ = bf16[128,1024]{1,0:T(8,128)(2,1)S(1)} collective-permute-done((bf16[128,1024]{1,0:T(8,128)(2,1)S(1)}, bf16[128,1024]{1,0:T(8,128)(2,1)S(1)}, u32[]{:S(2)}, u32[]{:S(2)}) %collective-permute-start.14) | collective-permute-done | bytes 262176 | tf_op jit(solution)/shard_map/ppermute | solution.py:422
  54.3 0.0 collective-permute-start.16
  54.3 0.5 collective-permute-start.17
  54.8 0.0 collective-permute-done.12.next_own.refs_2_
  54.8 0.0 collective-permute-done.13.next_over_x.refs_3_
  54.9 1.9 %shard_map.107 = (bf16[512,256]{1,0:T(8,128)(2,1)S(1)}, bf16[512,256]{1,0:T(8,128)(2,1)S(1)}) custom-call(s32[4]{0:T(128)S(1)} %pad_add_fusion.where, f32[512,1024]{1,0:T(8,128)S(1)} %copy-done.4, bf16[2,1024,1024]{2,1,0:T(8,128)(2,1)S(1)} %get-tuple-element.57.bases, bf16[128,1024]{1,0:T(8,128)(2,1)S(1)} %shard_map.105.own.refs_0_, ...), custom_call_target="tpu_custom_call" | custom-call | flops 536870912 | bytes 4194304 | tf_op jit(solution)/shard_map/pallas_call | solution.py:43
  56.7 0.4 collective-permute-start.18
  57.1 0.0 collective-permute-done.16.refs_6_
  57.1 0.0 collective-permute-done.17.refs_7_
  57.1 7.5 %shard_map.108 = (bf16[1024,1024]{1,0:T(8,128)(2,1)S(1)}, bf16[1024,1024]{1,0:T(8,128)(2,1)S(1)}, f32[1024,256]{1,0:T(8,128)S(1)}) custom-call(s32[4]{0:T(128)S(1)} %pad_add_fusion.where, bf16[2,1024,1024]{2,1,0:T(8,128)(2,1)S(1)} %get-tuple-element.57.bases, bf16[1024,1024]{1,0:T(8,128)(2,1)S(1)} %get-tuple-element.58.turned, ...), custom_call_target="tpu_custom_call" | custom-call | flops 3221225472 | bytes 8388608 | tf_op jit(solution)/shard_map/pallas_call | solution.py:43
  64.6 0.4 collective-permute-done.18.came
  65.0 0.0 collective-permute-start.21
  65.0 2.8 %shard_map.109 = (bf16[512,256]{1,0:T(8,128)(2,1)S(1)}, bf16[512,256]{1,0:T(8,128)(2,1)S(1)}) custom-call(s32[4]{0:T(128)S(1)} %pad_add_fusion.where, bf16[2,1024,1024]{2,1,0:T(8,128)(2,1)S(1)} %get-tuple-element.57.bases, bf16[1024,1024]{1,0:T(8,128)(2,1)S(1)} %get-tuple-element.58.turned, bf16[512,256]{1,0:T(8,128)(2,1)S(1)} %get-tuple-element.60.mine, ...), custom_call_target="tpu_custom_call" | custom-call | flops 1073741824 | bytes 4194304 | tf_op jit(solution)/shard_map/pallas_call | solution.py:43
  67.9 1.5 %collective-permute-start.19 = (bf16[512,256]{1,0:T(8,128)(2,1)S(1)}, bf16[512,256]{1,0:T(8,128)(2,1)S(1)}, u32[]{:S(2)}, u32[]{:S(2)}) collective-permute-start(bf16[512,256]{1,0:T(8,128)(2,1)S(1)} %get-tuple-element.74), channel_id=1, source_target_pairs={{0,1},{1,0},{2,3},{3,2},{4,5},{5,4},{6,7},{7,6},{8,9},{9,8},{10,11... | collective-permute-start | bytes 786440 | tf_op jit(solution)/shard_map/ppermute | solution.py:422
  69.3 0.2 collective-permute-start.20
  69.5 6.5 %shard_map.110 = (bf16[1024,1024]{1,0:T(8,128)(2,1)S(1)}, bf16[1024,1024]{1,0:T(8,128)(2,1)S(1)}, f32[256,1024]{1,0:T(8,128)S(1)}, f32[1024,512]{1,0:T(8,128)}) custom-call(s32[4]{0:T(128)S(1)} %pad_add_fusion.where, bf16[1024,1024]{1,0:T(8,128)(2,1)S(1)} %get-tuple-element.71.start, bf16[1024,1024]{1,0:T(8,128)(2,1)S(1)} %get-tuple-element.72.start_turned, ...), custom_call_target="tpu_custom_call" | custom-call | flops 12884901888 | bytes 8388608 | tf_op jit(solution)/shard_map/pallas_call | solution.py:536
  76.0 0.6 collective-permute-done.19.came
  76.7 0.0 collective-permute-done.20.kept_next
  76.7 0.0 collective-permute-done.21.new_next
  76.7 0.0 collective-permute-start.22
  76.7 0.5 collective-permute-start.23
  77.2 2.9 %shard_map.111 = (f32[256,1024]{1,0:T(8,128)S(1)}, f32[512,1024]{1,0:T(8,128)}, f32[512,1024]{1,0:T(8,128)}, f32[1024,512]{1,0:T(8,128)}) custom-call(s32[4]{0:T(128)S(1)} %pad_add_fusion.where, bf16[1024,1024]{1,0:T(8,128)(2,1)S(1)} %get-tuple-element.77.current, bf16[1024,1024]{1,0:T(8,128)(2,1)S(1)} %get-tuple-element.78.turned, ...), custom_call_target="tpu_custom_call", output_to_operand_aliasing={{3}: (5, {})} | custom-call | flops 1073741824 | bytes 4194304 | tf_op jit(solution)/shard_map/pallas_call | solution.py:555
  80.1 0.0 collective-permute-done.22.came_next
  80.1 0.1 collective-permute-start.24
  80.2 0.0 collective-permute-done.23.top_next
  80.2 2.8 %shard_map.112 = (bf16[512,1024]{1,0:T(8,128)(2,1)}, f32[512,1024]{1,0:T(8,128)}, f32[512,1024]{1,0:T(8,128)}) custom-call(s32[4]{0:T(128)S(1)} %pad_add_fusion.where, bf16[512,256]{1,0:T(8,128)(2,1)S(1)} %get-tuple-element.68.kept, bf16[512,256]{1,0:T(8,128)(2,1)S(1)} %collective-permute-done.19.came, ...), custom_call_target="tpu_custom_call", output_to_operand_aliasing={{1}: (8, {}), {2}: (9, {})} | custom-call | flops 1073741824 | bytes 4194304 | tf_op jit(solution)/shard_map/pallas_call | solution.py:567
  83.1 1.5 %shard_map.113 = (f32[512,1024]{1,0:T(8,128)}, f32[512,1024]{1,0:T(8,128)}) custom-call(s32[4]{0:T(128)S(1)} %pad_add_fusion.where, f32[256,1024]{1,0:T(8,128)S(1)} %collective-permute-done.24.low, f32[512,1024]{1,0:T(8,128)} %get-tuple-element.90.left_in, f32[512,1024]{1,0:T(8,128)} %get-tuple-element.91.right_in), custom_call_target="tpu_custom_call", output_to_operand_aliasing={{0}: (2, {}), {1}: (3, {})} | custom-call | bytes 2097152 | tf_op jit(solution)/shard_map/pallas_call | solution.py:43
  (13 shorter events, 0.1 us)
Async XLA Ops:
  1.9 2.1 %collective-permute-start = (bf16[256,1024]{1,0:T(8,128)(2,1)S(1)}, bf16[256,1024]{1,0:T(8,128)(2,1)S(1)}, u32[]{:S(2)}, u32[]{:S(2)}) collective-permute-start(bf16[256,1024]{1,0:T(8,128)(2,1)S(1)} %get-tuple-element.94), channel_id=1, source_target_pairs={{0,2},{2,0},{4,6},{6,4},{8,10},{10,8},{12,14},{14,12},{16,18},{18,... | collective-permute-start | bytes 1572872 | tf_op jit(solution)/shard_map/ppermute | solution.py:419
  4.0 44.1 %copy-start.1 = (f32[512,1024]{1,0:T(8,128)S(1)}, f32[512,1024]{1,0:T(8,128)}, u32[]{:S(2)}) copy-start(f32[512,1024]{1,0:T(8,128)} %right.3) | copy-start | bytes 6291460
  4.0 44.1 %copy-start.2 = (f32[512,1024]{1,0:T(8,128)S(1)}, f32[512,1024]{1,0:T(8,128)}, u32[]{:S(2)}) copy-start(f32[512,1024]{1,0:T(8,128)} %stat_left.3) | copy-start | bytes 6291460
  4.0 44.1 %copy-start.3 = (f32[512,1024]{1,0:T(8,128)S(1)}, f32[512,1024]{1,0:T(8,128)}, u32[]{:S(2)}) copy-start(f32[512,1024]{1,0:T(8,128)} %stat_right.3) | copy-start | bytes 6291460
  6.7 41.4 %copy-start = (f32[512,1024]{1,0:T(8,128)S(1)}, f32[512,1024]{1,0:T(8,128)}, u32[]{:S(2)}) copy-start(f32[512,1024]{1,0:T(8,128)} %left.3) | copy-start | bytes 6291460
  6.7 30.6 %collective-permute-start.8 = (bf16[38,128,128]{2,1,0:T(8,128)(2,1)S(1)}, bf16[38,128,128]{2,1,0:T(8,128)(2,1)S(1)}, u32[]{:S(2)}, u32[]{:S(2)}) collective-permute-start(bf16[38,128,128]{2,1,0:T(8,128)(2,1)S(1)} %get-tuple-element.55), channel_id=1, source_target_pairs={{0,1},{1,0},{2,3},{3,2},{4,5},{5,4},{6,7},{7,6},{8,9},{9,8},{10,11... | collective-permute-start | bytes 3735560 | tf_op jit(solution)/shard_map/ppermute | solution.py:422
  9.7 8.1 %collective-permute-start.1 = (bf16[128,1024]{1,0:T(8,128)(2,1)S(1)}, bf16[128,1024]{1,0:T(8,128)(2,1)S(1)}, u32[]{:S(2)}, u32[]{:S(2)}) collective-permute-start(bf16[128,1024]{1,0:T(8,128)(2,1)S(1)} %get-tuple-element.50), channel_id=1, source_target_pairs={{0,4},{2,6},{4,0},{6,2},{8,12},{10,14},{12,8},{14,10},{16,20},{18,... | collective-permute-start | bytes 786440 | tf_op jit(solution)/shard_map/ppermute | solution.py:419
  18.3 6.4 %collective-permute-start.2 = (bf16[32,1024]{1,0:T(8,128)(2,1)S(1)}, bf16[32,1024]{1,0:T(8,128)(2,1)S(1)}, u32[]{:S(2)}, u32[]{:S(2)}) collective-permute-start(bf16[32,1024]{1,0:T(8,128)(2,1)S(1)} %get-tuple-element.52), channel_id=1, source_target_pairs={{0,24},{2,26},{4,28},{6,30},{8,16},{10,18},{12,20},{14,22},{16,8},... | collective-permute-start | bytes 196616 | tf_op jit(solution)/shard_map/ppermute | solution.py:419
  22.1 5.3 %collective-permute-start.3 = (bf16[32,1024]{1,0:T(8,128)(2,1)S(1)}, bf16[32,1024]{1,0:T(8,128)(2,1)S(1)}, u32[]{:S(2)}, u32[]{:S(2)}) collective-permute-start(bf16[32,1024]{1,0:T(8,128)(2,1)S(1)} %get-tuple-element.53), channel_id=1, source_target_pairs={{0,16},{2,18},{4,20},{6,22},{8,24},{10,26},{12,28},{14,30},{16,0},... | collective-permute-start | bytes 196616 | tf_op jit(solution)/shard_map/ppermute | solution.py:419
  22.1 5.3 %collective-permute-start.4 = (bf16[32,1024]{1,0:T(8,128)(2,1)S(1)}, bf16[32,1024]{1,0:T(8,128)(2,1)S(1)}, u32[]{:S(2)}, u32[]{:S(2)}) collective-permute-start(bf16[32,1024]{1,0:T(8,128)(2,1)S(1)} %get-tuple-element.54), channel_id=1, source_target_pairs={{0,8},{2,10},{4,12},{6,14},{8,0},{10,2},{12,4},{14,6},{16,24},{18,... | collective-permute-start | bytes 196616 | tf_op jit(solution)/shard_map/ppermute | solution.py:419
  27.4 6.3 %collective-permute-start.7 = (bf16[32,1024]{1,0:T(8,128)(2,1)S(1)}, bf16[32,1024]{1,0:T(8,128)(2,1)S(1)}, u32[]{:S(2)}, u32[]{:S(2)}) collective-permute-start(bf16[32,1024]{1,0:T(8,128)(2,1)S(1)} %shard_map.104.refs_0_), channel_id=1, source_target_pairs={{0,24},{2,26},{4,28},{6,30},{8,16},{10,18},{12,20},{14,22},{16,8},... | collective-permute-start | bytes 196616 | tf_op jit(solution)/shard_map/ppermute | solution.py:419
  29.8 5.5 %collective-permute-start.6 = (bf16[32,1024]{1,0:T(8,128)(2,1)S(1)}, bf16[32,1024]{1,0:T(8,128)(2,1)S(1)}, u32[]{:S(2)}, u32[]{:S(2)}) collective-permute-start(bf16[32,1024]{1,0:T(8,128)(2,1)S(1)} %shard_map.104.refs_0_), channel_id=1, source_target_pairs={{0,16},{2,18},{4,20},{6,22},{8,24},{10,26},{12,28},{14,30},{16,0},... | collective-permute-start | bytes 196616 | tf_op jit(solution)/shard_map/ppermute | solution.py:419
  29.8 5.5 %collective-permute-start.5 = (bf16[32,1024]{1,0:T(8,128)(2,1)S(1)}, bf16[32,1024]{1,0:T(8,128)(2,1)S(1)}, u32[]{:S(2)}, u32[]{:S(2)}) collective-permute-start(bf16[32,1024]{1,0:T(8,128)(2,1)S(1)} %shard_map.104.refs_0_), channel_id=1, source_target_pairs={{0,8},{2,10},{4,12},{6,14},{8,0},{10,2},{12,4},{14,6},{16,24},{18,... | collective-permute-start | bytes 196616 | tf_op jit(solution)/shard_map/ppermute | solution.py:419
  37.3 10.7 %collective-permute-start.9 = (bf16[38,128,128]{2,1,0:T(8,128)(2,1)S(1)}, bf16[38,128,128]{2,1,0:T(8,128)(2,1)S(1)}, u32[]{:S(2)}, u32[]{:S(2)}) collective-permute-start(bf16[38,128,128]{2,1,0:T(8,128)(2,1)S(1)} %collective-permute-done.8.mine), channel_id=1, source_target_pairs={{0,2},{2,0},{4,6},{6,4},{8,10},{10,8},{12,14},{14,12},{16,18},{18,... | collective-permute-start | bytes 3735560 | tf_op jit(solution)/shard_map/ppermute | solution.py:419
  37.3 10.2 %collective-permute-start.11 = (bf16[128,1024]{1,0:T(8,128)(2,1)S(1)}, bf16[128,1024]{1,0:T(8,128)(2,1)S(1)}, u32[]{:S(2)}, u32[]{:S(2)}) collective-permute-start(bf16[128,1024]{1,0:T(8,128)(2,1)S(1)} %shard_map.105.own.refs_0_), channel_id=1, source_target_pairs={{0,4},{2,6},{4,0},{6,2},{8,12},{10,14},{12,8},{14,10},{16,20},{18,... | collective-permute-start | bytes 786440 | tf_op jit(solution)/shard_map/ppermute | solution.py:419
  39.1 13.9 %collective-permute-start.15 = (bf16[128,1024]{1,0:T(8,128)(2,1)S(1)}, bf16[128,1024]{1,0:T(8,128)(2,1)S(1)}, u32[]{:S(2)}, u32[]{:S(2)}) collective-permute-start(bf16[128,1024]{1,0:T(8,128)(2,1)S(1)} %shard_map.105.own.refs_0_), channel_id=1, source_target_pairs={{0,5},{1,4},{2,7},{3,6},{4,1},{5,0},{6,3},{7,2},{8,13},{9,12},{10,... | collective-permute-start | bytes 786440 | tf_op jit(solution)/shard_map/ppermute | solution.py:426
  40.6 13.8 %collective-permute-start.14 = (bf16[128,1024]{1,0:T(8,128)(2,1)S(1)}, bf16[128,1024]{1,0:T(8,128)(2,1)S(1)}, u32[]{:S(2)}, u32[]{:S(2)}) collective-permute-start(bf16[128,1024]{1,0:T(8,128)(2,1)S(1)} %shard_map.105.own.refs_0_), channel_id=1, source_target_pairs={{0,1},{1,0},{2,3},{3,2},{4,5},{5,4},{6,7},{7,6},{8,9},{9,8},{10,11... | collective-permute-start | bytes 786440 | tf_op jit(solution)/shard_map/ppermute | solution.py:422
  40.9 14.0 %copy-start.4 = (f32[512,1024]{1,0:T(8,128)S(1)}, f32[512,1024]{1,0:T(8,128)}, u32[]{:S(2)}) copy-start(f32[512,1024]{1,0:T(8,128)} %moment.1) | copy-start | bytes 6291460
  40.9 6.7 %collective-permute-start.10 = (bf16[6,128,128]{2,1,0:T(8,128)(2,1)S(1)}, bf16[6,128,128]{2,1,0:T(8,128)(2,1)S(1)}, u32[]{:S(2)}, u32[]{:S(2)}) collective-permute-start(bf16[6,128,128]{2,1,0:T(8,128)(2,1)S(1)} %slice.3), channel_id=1, source_target_pairs={{0,8},{2,10},{4,12},{6,14},{8,0},{10,2},{12,4},{14,6},{16,24},{18,... | collective-permute-start | bytes 589832 | tf_op jit(solution)/shard_map/ppermute | solution.py:419
  47.5 7.3 %collective-permute-start.12 = (bf16[128,1024]{1,0:T(8,128)(2,1)S(1)}, bf16[128,1024]{1,0:T(8,128)(2,1)S(1)}, u32[]{:S(2)}, u32[]{:S(2)}) collective-permute-start(bf16[128,1024]{1,0:T(8,128)(2,1)S(1)} %shard_map.105.own.refs_0_), channel_id=1, source_target_pairs={{0,2},{2,0},{4,6},{6,4},{8,10},{10,8},{12,14},{14,12},{16,18},{18,... | collective-permute-start | bytes 786440 | tf_op jit(solution)/shard_map/ppermute | solution.py:419
  47.5 7.3 %collective-permute-start.13 = (bf16[128,1024]{1,0:T(8,128)(2,1)S(1)}, bf16[128,1024]{1,0:T(8,128)(2,1)S(1)}, u32[]{:S(2)}, u32[]{:S(2)}) collective-permute-start(bf16[128,1024]{1,0:T(8,128)(2,1)S(1)} %collective-permute-done.11.over_x.refs_1_), channel_id=1, source_target_pairs={{0,2},{2,0},{4,6},{6,4},{8,10},{10,8},{12,14},{14,12},{16,18},{18,... | collective-permute-start | bytes 786440 | tf_op jit(solution)/shard_map/ppermute | solution.py:419
  54.3 2.8 %copy-start.5 = (f32[1024,512]{1,0:T(8,128)S(1)}, f32[1024,512]{1,0:T(8,128)}, u32[]{:S(2)}) copy-start(f32[1024,512]{1,0:T(8,128)} %second.1) | copy-start | bytes 6291460
  54.3 2.8 %collective-permute-start.16 = (bf16[128,1024]{1,0:T(8,128)(2,1)S(1)}, bf16[128,1024]{1,0:T(8,128)(2,1)S(1)}, u32[]{:S(2)}, u32[]{:S(2)}) collective-permute-start(bf16[128,1024]{1,0:T(8,128)(2,1)S(1)} %collective-permute-done.14.refs_4_), channel_id=1, source_target_pairs={{0,2},{2,0},{4,6},{6,4},{8,10},{10,8},{12,14},{14,12},{16,18},{18,... | collective-permute-start | bytes 786440 | tf_op jit(solution)/shard_map/ppermute | solution.py:419
  54.3 2.8 %collective-permute-start.17 = (bf16[128,1024]{1,0:T(8,128)(2,1)S(1)}, bf16[128,1024]{1,0:T(8,128)(2,1)S(1)}, u32[]{:S(2)}, u32[]{:S(2)}) collective-permute-start(bf16[128,1024]{1,0:T(8,128)(2,1)S(1)} %collective-permute-done.15.refs_5_), channel_id=1, source_target_pairs={{0,2},{2,0},{4,6},{6,4},{8,10},{10,8},{12,14},{14,12},{16,18},{18,... | collective-permute-start | bytes 786440 | tf_op jit(solution)/shard_map/ppermute | solution.py:419
  56.7 8.3 %collective-permute-start.18 = (bf16[512,256]{1,0:T(8,128)(2,1)S(1)}, bf16[512,256]{1,0:T(8,128)(2,1)S(1)}, u32[]{:S(2)}, u32[]{:S(2)}) collective-permute-start(bf16[512,256]{1,0:T(8,128)(2,1)S(1)} %get-tuple-element.65), channel_id=1, source_target_pairs={{0,1},{1,0},{2,3},{3,2},{4,5},{5,4},{6,7},{7,6},{8,9},{9,8},{10,11... | collective-permute-start | bytes 786440 | tf_op jit(solution)/shard_map/ppermute | solution.py:422
  65.0 11.6 %collective-permute-start.21 = (f32[1024,256]{1,0:T(8,128)S(1)}, f32[1024,256]{1,0:T(8,128)S(1)}, u32[]{:S(2)}, u32[]{:S(2)}) collective-permute-start(f32[1024,256]{1,0:T(8,128)S(1)} %get-tuple-element.67.new), channel_id=1, source_target_pairs={{0,2},{2,0},{4,6},{6,4},{8,10},{10,8},{12,14},{14,12},{16,18},{18,... | collective-permute-start | bytes 3145736 | tf_op jit(solution)/shard_map/ppermute | solution.py:419
  67.9 8.8 %collective-permute-start.19 = (bf16[512,256]{1,0:T(8,128)(2,1)S(1)}, bf16[512,256]{1,0:T(8,128)(2,1)S(1)}, u32[]{:S(2)}, u32[]{:S(2)}) collective-permute-start(bf16[512,256]{1,0:T(8,128)(2,1)S(1)} %get-tuple-element.74), channel_id=1, source_target_pairs={{0,1},{1,0},{2,3},{3,2},{4,5},{5,4},{6,7},{7,6},{8,9},{9,8},{10,11... | collective-permute-start | bytes 786440 | tf_op jit(solution)/shard_map/ppermute | solution.py:422
  69.3 7.3 %collective-permute-start.20 = (bf16[512,256]{1,0:T(8,128)(2,1)S(1)}, bf16[512,256]{1,0:T(8,128)(2,1)S(1)}, u32[]{:S(2)}, u32[]{:S(2)}) collective-permute-start(bf16[512,256]{1,0:T(8,128)(2,1)S(1)} %get-tuple-element.68.kept), channel_id=1, source_target_pairs={{0,2},{2,0},{4,6},{6,4},{8,10},{10,8},{12,14},{14,12},{16,18},{18,... | collective-permute-start | bytes 786440 | tf_op jit(solution)/shard_map/ppermute | solution.py:419
  76.7 3.4 %collective-permute-start.22 = (bf16[512,256]{1,0:T(8,128)(2,1)S(1)}, bf16[512,256]{1,0:T(8,128)(2,1)S(1)}, u32[]{:S(2)}, u32[]{:S(2)}) collective-permute-start(bf16[512,256]{1,0:T(8,128)(2,1)S(1)} %collective-permute-done.19.came), channel_id=1, source_target_pairs={{0,2},{2,0},{4,6},{6,4},{8,10},{10,8},{12,14},{14,12},{16,18},{18,... | collective-permute-start | bytes 786440 | tf_op jit(solution)/shard_map/ppermute | solution.py:419
  76.7 3.6 %collective-permute-start.23 = (f32[256,1024]{1,0:T(8,128)S(1)}, f32[256,1024]{1,0:T(8,128)S(1)}, u32[]{:S(2)}, u32[]{:S(2)}) collective-permute-start(f32[256,1024]{1,0:T(8,128)S(1)} %get-tuple-element.79.top), channel_id=1, source_target_pairs={{0,2},{2,0},{4,6},{6,4},{8,10},{10,8},{12,14},{14,12},{16,18},{18,... | collective-permute-start | bytes 3145736 | tf_op jit(solution)/shard_map/ppermute | solution.py:419
  80.1 2.9 %collective-permute-start.24 = (f32[256,1024]{1,0:T(8,128)S(1)}, f32[256,1024]{1,0:T(8,128)S(1)}, u32[]{:S(2)}, u32[]{:S(2)}) collective-permute-start(f32[256,1024]{1,0:T(8,128)S(1)} %get-tuple-element.85.low), channel_id=1, source_target_pairs={{0,2},{2,0},{4,6},{6,4},{8,10},{10,8},{12,14},{14,12},{16,18},{18,... | collective-permute-start | bytes 3145736 | tf_op jit(solution)/shard_map/ppermute | solution.py:419

commit v14 on v12

--- a/solution.py
+++ b/solution.py
@@ -369,13 +369,17 @@
 
 
 def refresh_kernel(
-    where, start, start_turned, new, current, turned, out, second_new, gram, *scratch
+    where, start, start_turned, new, new_next, current, turned, out, second_new, gram, *scratch
 ):
     width = start.shape[0]
     rows = width // 2
     between, sem = scratch[:-1], scratch[-1]
-    copy = pltpu.make_async_copy(new, second_new.at[:, tile(where[1], new.shape[1])], sem)
-    copy.start()
+    copies = [
+        pltpu.make_async_copy(value, second_new.at[:, tile(place, new.shape[1])], sem.at[i])
+        for i, (value, place) in enumerate(((new, where[1]), (new_next, 1 - where[1])))
+    ]
+    for copy in copies:
+        copy.start()
     source, source_turned = start, start_turned
     for iteration in range(NS_ITERS - 1):
         if iteration + 2 == NS_ITERS:
@@ -385,23 +389,14 @@
         improved(source, source_turned, slice(0, width), gram, result, result_turned)
         source, source_turned = result, result_turned
     improved(current, turned, tile(where[0] * 2, rows // 2), gram, out, None)
-    copy.wait()
-
-
-def last_kernel(
-    where, current, turned, top, new_next, second_in, out, left, right, second_new, gram, sem
-):
-    core = where[1]
-    copies = [
-        write_part(core, 0, 0, top, left, right, sem.at[0]),
-        pltpu.make_async_copy(
-            new_next, second_new.at[:, tile(1 - core, new_next.shape[1])], sem.at[1]
-        ),
-    ]
-    copies[1].start()
-    improved(current, turned, tile(where[0] * 2 + 1, out.shape[0]), gram, out, None)
     for copy in copies:
         copy.wait()
+
+
+def last_kernel(where, current, turned, top, out, left, right, gram, sem):
+    copy = write_part(where[1], 0, 0, top, left, right, sem.at[0])
+    improved(current, turned, tile(where[0] * 2 + 1, out.shape[0]), gram, out, None)
+    copy.wait()
 
 
 def fast_body(group_grads, moment, second, stat_left, stat_right, basis_left, basis_right):
@@ -527,41 +522,40 @@
         [shaped((rows, half), HALF)] * 2,
         (where, bases, left_turned, moment_mine, moment_came, new),
         [SMEM] + [VMEM] * 5,
-        flops=unit // 2,
+        flops=6 * unit,
         moved=2**22,
     )
-    start, back_sent = lax.optimization_barrier((start, back_sent))
+    start, back_sent, new_next = lax.optimization_barrier((start, back_sent, new_next))
     back_came = shard_swap(back_sent)
     back_kept_next = dp_swap(back_kept, 1)
     current, current_turned, top, second_new = pl.pallas_call(
         refresh_kernel,
         out_shape=[square, square, shaped((half, width), FULL), shaped((width, rows), FULL)],
-        in_specs=[SMEM] + [VMEM] * 2 + [ANY],
+        in_specs=[SMEM] + [VMEM] * 2 + [ANY] * 2,
         out_specs=[VMEM] * 3 + [ANY],
         scratch_shapes=[pltpu.VMEM((width, width), HALF)]
         + [pltpu.VMEM((2, width, width), HALF)] * (2 if NS_ITERS > 2 else 0)
-        + [pltpu.SemaphoreType.DMA(())],
+        + [pltpu.SemaphoreType.DMA((2,))],
         compiler_params=pltpu.CompilerParams(vmem_limit_bytes=24 * 2**20),
         cost_estimate=pl.CostEstimate(
             flops=6 * unit, bytes_accessed=2**23, transcendentals=0
         ),
-    )(where, start, start_turned, new)
+    )(where, start, start_turned, new, new_next)
     top_next = dp_swap(top, 1)
-    current, back_came, back_kept_next, new_next = lax.optimization_barrier(
-        (current, back_came, back_kept_next, new_next)
+    current, back_came, back_kept_next = lax.optimization_barrier(
+        (current, back_came, back_kept_next)
     )
     back_came_next = dp_swap(back_came, 1)
     side = shaped((rows, width), FULL)
-    low, left_new, right_new, second_new = pl.pallas_call(
+    low, left_new, right_new = pl.pallas_call(
         last_kernel,
-        out_shape=[shaped((half, width), FULL), side, side, shaped((width, rows), FULL)],
-        in_specs=[SMEM] + [VMEM] * 2 + [ANY] * 3,
-        out_specs=[VMEM] + [ANY] * 3,
-        scratch_shapes=[pltpu.VMEM((half, width), HALF), pltpu.SemaphoreType.DMA((2,))],
-        input_output_aliases={5: 3},
+        out_shape=[shaped((half, width), FULL), side, side],
+        in_specs=[SMEM] + [VMEM] * 2 + [ANY],
+        out_specs=[VMEM] + [ANY] * 2,
+        scratch_shapes=[pltpu.VMEM((half, width), HALF), pltpu.SemaphoreType.DMA((1,))],
         compiler_params=pltpu.CompilerParams(vmem_limit_bytes=24 * 2**20),
         cost_estimate=pl.CostEstimate(flops=unit // 2, bytes_accessed=2**22, transcendentals=0),
-    )(where, current, current_turned, top, new_next, second_new)
+    )(where, current, current_turned, top)
     low, back_came_next = lax.optimization_barrier((low, back_came_next))
     low_next = dp_swap(low, 1)
     update, left_new, right_new = pl.pallas_call(

time: 84.9 us -> 84.6 us (level)
  no operation moved by 1% of the time
where the time goes in v14:
time: 84.6 us; the launch traced here: 84.5 us
  Pallas kernels  33 us (39%)
  waiting for transfers between devices  25.8 us (30%)
  starting transfers between devices  23.3 us (28%)
  local copies, waits for them, and re-layouts  1.31 us (2%)
  between operations  0.98 us (1%)
    ppermute x20, waiting for transfers between devices, dp_swap(): return lax.ppermute(value, 'dp', [(i, i ^ distance) for i in range(16)])  21.8 us
    pallas_call x9, Pallas kernels, call(): pl.pallas_call(kernel, out_shape=outs, in_specs=specs, out_specs=[space]...  20.8 us
    ppermute x20, starting transfers between devices, dp_swap(): return lax.ppermute(value, 'dp', [(i, i ^ distance) for i in range(16)])  16.8 us
    pallas_call x1, Pallas kernels, fast_body(): pl.pallas_call(refresh_kernel, out_shape=[square, square, shaped((half, w...  6.84 us
    ppermute x4, starting transfers between devices, shard_swap(): return lax.ppermute(value, 'shard', [(0, 1), (1, 0)])  4.99 us
    pallas_call x1, Pallas kernels, fast_body(): pl.pallas_call(update_kernel, out_shape=[shaped((rows, width), HALF), sid...  2.79 us
    pallas_call x1, Pallas kernels, fast_body(): pl.pallas_call(last_kernel, out_shape=[shaped((half, width), FULL), side,...  2.55 us
    ppermute x4, waiting for transfers between devices, shard_swap(): return lax.ppermute(value, 'shard', [(0, 1), (1, 0)])  2.34 us
  transfers between devices with their start and end apart: 25, of which 13 were waited for; matrix products, arithmetic and copies ran while one was open for 0% of the time, Pallas kernels for 34%

profile of v14, /device:TPU:0, one launch (start us, length us, event | category | flops | bytes accessed | tf_op | source)
XLA Modules:
  0.0 84.5 jit_solution(5598219490681460477)
XLA Ops:
  0.6 1.3 %dynamic-slice_bitcast_fusion = (bf16[256,1024]{1,0:T(8,128)(2,1)S(1)}, bf16[256,1024]{1,0:T(8,128)(2,1)S(1)}) fusion(bf16[1,512,1024]{2,1,0:T(8,128)(2,1)} %param.7, s32[]{:T(128)S(6)} %select_n.7, s32[]{:T(128)S(6)} %select_n.6), kind=kLoop, calls=%fused_computation | loop fusion | bytes 2097160 | tf_op jit(solution)/shard_map/dynamic_slice | solution.py:423
  1.9 0.5 collective-permute-start
  2.4 0.1 pad_add_fusion.where
  2.5 1.5 %collective-permute-done.came = bf16[256,1024]{1,0:T(8,128)(2,1)S(1)} collective-permute-done((bf16[256,1024]{1,0:T(8,128)(2,1)S(1)}, bf16[256,1024]{1,0:T(8,128)(2,1)S(1)}, u32[]{:S(2)}, u32[]{:S(2)}) %collective-permute-start) | collective-permute-done | bytes 524320 | tf_op jit(solution)/shard_map/ppermute | solution.py:414
  4.0 2.7 %shard_map.102 = (bf16[38,128,128]{2,1,0:T(8,128)(2,1)S(1)}, f32[128,1024]{1,0:T(8,128)S(1)}, bf16[128,1024]{1,0:T(8,128)(2,1)S(1)}) custom-call(s32[4]{0:T(128)S(1)} %pad_add_fusion.where, bf16[256,1024]{1,0:T(8,128)(2,1)S(1)} %get-tuple-element.93.raw, bf16[256,1024]{1,0:T(8,128)(2,1)S(1)} %collective-permute-done.came, f32[512,1024]{1,0:T(8,128)} %left.3, ...), custom_call_target="tpu_custom_call" | custom-call | bytes 4194304 | tf_op jit(solution)/shard_map/pallas_call | solution.py:43
  6.7 0.0 copy-start
  6.7 3.0 %collective-permute-start.8 = (bf16[38,128,128]{2,1,0:T(8,128)(2,1)S(1)}, bf16[38,128,128]{2,1,0:T(8,128)(2,1)S(1)}, u32[]{:S(2)}, u32[]{:S(2)}) collective-permute-start(bf16[38,128,128]{2,1,0:T(8,128)(2,1)S(1)} %get-tuple-element.54), channel_id=1, source_target_pairs={{0,1},{1,0},{2,3},{3,2},{4,5},{5,4},{6,7},{7,6},{8,9},{9,8},{10,11... | collective-permute-start | bytes 3735560 | tf_op jit(solution)/shard_map/ppermute | solution.py:417
  9.7 1.5 %collective-permute-start.1 = (bf16[128,1024]{1,0:T(8,128)(2,1)S(1)}, bf16[128,1024]{1,0:T(8,128)(2,1)S(1)}, u32[]{:S(2)}, u32[]{:S(2)}) collective-permute-start(bf16[128,1024]{1,0:T(8,128)(2,1)S(1)} %get-tuple-element.49), channel_id=1, source_target_pairs={{0,4},{2,6},{4,0},{6,2},{8,12},{10,14},{12,8},{14,10},{16,20},{18,... | collective-permute-start | bytes 786440 | tf_op jit(solution)/shard_map/ppermute | solution.py:414
  11.2 6.6 %collective-permute-done.1.came = bf16[128,1024]{1,0:T(8,128)(2,1)S(1)} collective-permute-done((bf16[128,1024]{1,0:T(8,128)(2,1)S(1)}, bf16[128,1024]{1,0:T(8,128)(2,1)S(1)}, u32[]{:S(2)}, u32[]{:S(2)}) %collective-permute-start.1) | collective-permute-done | bytes 262176 | tf_op jit(solution)/shard_map/ppermute | solution.py:414
  17.7 0.6 shard_map.103
  18.3 1.7 %collective-permute-start.2 = (bf16[32,1024]{1,0:T(8,128)(2,1)S(1)}, bf16[32,1024]{1,0:T(8,128)(2,1)S(1)}, u32[]{:S(2)}, u32[]{:S(2)}) collective-permute-start(bf16[32,1024]{1,0:T(8,128)(2,1)S(1)} %get-tuple-element.51), channel_id=1, source_target_pairs={{0,8},{2,10},{4,12},{6,14},{8,0},{10,2},{12,4},{14,6},{16,24},{18,... | collective-permute-start | bytes 196616 | tf_op jit(solution)/shard_map/ppermute | solution.py:414
  20.0 2.6 %collective-permute-start.3 = (bf16[32,1024]{1,0:T(8,128)(2,1)S(1)}, bf16[32,1024]{1,0:T(8,128)(2,1)S(1)}, u32[]{:S(2)}, u32[]{:S(2)}) collective-permute-start(bf16[32,1024]{1,0:T(8,128)(2,1)S(1)} %get-tuple-element.52), channel_id=1, source_target_pairs={{0,16},{2,18},{4,20},{6,22},{8,24},{10,26},{12,28},{14,30},{16,0},... | collective-permute-start | bytes 196616 | tf_op jit(solution)/shard_map/ppermute | solution.py:414
  22.6 0.2 collective-permute-start.4
  22.8 0.5 collective-permute-done.2.one
  23.2 3.4 %collective-permute-done.3.two = bf16[32,1024]{1,0:T(8,128)(2,1)S(1)} collective-permute-done((bf16[32,1024]{1,0:T(8,128)(2,1)S(1)}, bf16[32,1024]{1,0:T(8,128)(2,1)S(1)}, u32[]{:S(2)}, u32[]{:S(2)}) %collective-permute-start.3) | collective-permute-done | bytes 65568 | tf_op jit(solution)/shard_map/ppermute | solution.py:414
  26.6 2.1 %collective-permute-done.4.three = bf16[32,1024]{1,0:T(8,128)(2,1)S(1)} collective-permute-done((bf16[32,1024]{1,0:T(8,128)(2,1)S(1)}, bf16[32,1024]{1,0:T(8,128)(2,1)S(1)}, u32[]{:S(2)}, u32[]{:S(2)}) %collective-permute-start.4) | collective-permute-done | bytes 65568 | tf_op jit(solution)/shard_map/ppermute | solution.py:414
  28.7 1.1 %collective-permute-start.7 = (bf16[32,1024]{1,0:T(8,128)(2,1)S(1)}, bf16[32,1024]{1,0:T(8,128)(2,1)S(1)}, u32[]{:S(2)}, u32[]{:S(2)}) collective-permute-start(bf16[32,1024]{1,0:T(8,128)(2,1)S(1)} %shard_map.104.refs_0_), channel_id=1, source_target_pairs={{0,24},{2,26},{4,28},{6,30},{8,16},{10,18},{12,20},{14,22},{16,8},... | collective-permute-start | bytes 196616 | tf_op jit(solution)/shard_map/ppermute | solution.py:414
  29.9 0.4 collective-permute-start.6
  30.3 2.9 %collective-permute-start.5 = (bf16[32,1024]{1,0:T(8,128)(2,1)S(1)}, bf16[32,1024]{1,0:T(8,128)(2,1)S(1)}, u32[]{:S(2)}, u32[]{:S(2)}) collective-permute-start(bf16[32,1024]{1,0:T(8,128)(2,1)S(1)} %shard_map.104.refs_0_), channel_id=1, source_target_pairs={{0,8},{2,10},{4,12},{6,14},{8,0},{10,2},{12,4},{14,6},{16,24},{18,... | collective-permute-start | bytes 196616 | tf_op jit(solution)/shard_map/ppermute | solution.py:414
  33.2 1.7 %collective-permute-done.7.refs_3_ = bf16[32,1024]{1,0:T(8,128)(2,1)S(1)} collective-permute-done((bf16[32,1024]{1,0:T(8,128)(2,1)S(1)}, bf16[32,1024]{1,0:T(8,128)(2,1)S(1)}, u32[]{:S(2)}, u32[]{:S(2)}) %collective-permute-start.7) | collective-permute-done | bytes 65568 | tf_op jit(solution)/shard_map/ppermute | solution.py:414
  34.9 1.3 %collective-permute-done.6.refs_2_ = bf16[32,1024]{1,0:T(8,128)(2,1)S(1)} collective-permute-done((bf16[32,1024]{1,0:T(8,128)(2,1)S(1)}, bf16[32,1024]{1,0:T(8,128)(2,1)S(1)}, u32[]{:S(2)}, u32[]{:S(2)}) %collective-permute-start.6) | collective-permute-done | bytes 65568 | tf_op jit(solution)/shard_map/ppermute | solution.py:414
  36.3 0.0 collective-permute-done.5.refs_1_
  36.3 0.6 shard_map.105.own.refs_0_
  36.9 0.5 collective-permute-done.8.mine
  37.3 0.0 collective-permute-start.9
  37.3 1.7 %collective-permute-start.11 = (bf16[128,1024]{1,0:T(8,128)(2,1)S(1)}, bf16[128,1024]{1,0:T(8,128)(2,1)S(1)}, u32[]{:S(2)}, u32[]{:S(2)}) collective-permute-start(bf16[128,1024]{1,0:T(8,128)(2,1)S(1)} %shard_map.105.own.refs_0_), channel_id=1, source_target_pairs={{0,4},{2,6},{4,0},{6,2},{8,12},{10,14},{12,8},{14,10},{16,20},{18,... | collective-permute-start | bytes 786440 | tf_op jit(solution)/shard_map/ppermute | solution.py:414
  39.1 1.5 %collective-permute-start.15 = (bf16[128,1024]{1,0:T(8,128)(2,1)S(1)}, bf16[128,1024]{1,0:T(8,128)(2,1)S(1)}, u32[]{:S(2)}, u32[]{:S(2)}) collective-permute-start(bf16[128,1024]{1,0:T(8,128)(2,1)S(1)} %shard_map.105.own.refs_0_), channel_id=1, source_target_pairs={{0,5},{1,4},{2,7},{3,6},{4,1},{5,0},{6,3},{7,2},{8,13},{9,12},{10,... | collective-permute-start | bytes 786440 | tf_op jit(solution)/shard_map/ppermute | solution.py:421
  40.6 0.3 collective-permute-start.14
  40.9 0.0 copy-start.4
  40.9 1.9 %collective-permute-start.10 = (bf16[6,128,128]{2,1,0:T(8,128)(2,1)S(1)}, bf16[6,128,128]{2,1,0:T(8,128)(2,1)S(1)}, u32[]{:S(2)}, u32[]{:S(2)}) collective-permute-start(bf16[6,128,128]{2,1,0:T(8,128)(2,1)S(1)} %slice.3), channel_id=1, source_target_pairs={{0,8},{2,10},{4,12},{6,14},{8,0},{10,2},{12,4},{14,6},{16,24},{18,... | collective-permute-start | bytes 589832 | tf_op jit(solution)/shard_map/ppermute | solution.py:414
  42.8 4.7 %collective-permute-done.10.relayed = bf16[6,128,128]{2,1,0:T(8,128)(2,1)S(1)} collective-permute-done((bf16[6,128,128]{2,1,0:T(8,128)(2,1)S(1)}, bf16[6,128,128]{2,1,0:T(8,128)(2,1)S(1)}, u32[]{:S(2)}, u32[]{:S(2)}) %collective-permute-start.10) | collective-permute-done | bytes 196640 | tf_op jit(solution)/shard_map/ppermute | solution.py:414
  47.5 0.0 collective-permute-start.12
  47.5 0.0 collective-permute-done.11.over_x.refs_1_
  47.5 0.5 collective-permute-start.13
  48.0 0.0 collective-permute-done.9.theirs
  48.1 3.2 %shard_map.106 = (bf16[2,1024,1024]{2,1,0:T(8,128)(2,1)S(1)}, bf16[1024,1024]{1,0:T(8,128)(2,1)S(1)}, bf16[1024,1024]{1,0:T(8,128)(2,1)S(1)}, f32[1024,1024]{1,0:T(8,128)S(1)}) custom-call(s32[4]{0:T(128)S(1)} %pad_add_fusion.where, f32[512,1024]{1,0:T(8,128)S(1)} %copy-done, f32[512,1024]{1,0:T(8,128)S(1)} %copy-done.1, ...), custom_call_target="tpu_custom_call" | custom-call | bytes 16777216 | tf_op jit(solution)/shard_map/pallas_call | solution.py:43
  51.3 1.7 %collective-permute-done.15.refs_5_ = bf16[128,1024]{1,0:T(8,128)(2,1)S(1)} collective-permute-done((bf16[128,1024]{1,0:T(8,128)(2,1)S(1)}, bf16[128,1024]{1,0:T(8,128)(2,1)S(1)}, u32[]{:S(2)}, u32[]{:S(2)}) %collective-permute-start.15) | collective-permute-done | bytes 262176 | tf_op jit(solution)/shard_map/ppermute | solution.py:421
  53.0 1.4 %collective-permute-done.14.refs_4_ = bf16[128,1024]{1,0:T(8,128)(2,1)S(1)} collective-permute-done((bf16[128,1024]{1,0:T(8,128)(2,1)S(1)}, bf16[128,1024]{1,0:T(8,128)(2,1)S(1)}, u32[]{:S(2)}, u32[]{:S(2)}) %collective-permute-start.14) | collective-permute-done | bytes 262176 | tf_op jit(solution)/shard_map/ppermute | solution.py:417
  54.3 0.0 collective-permute-start.16
  54.3 0.5 collective-permute-start.17
  54.8 0.0 collective-permute-done.12.next_own.refs_2_
  54.8 0.0 collective-permute-done.13.next_over_x.refs_3_
  54.9 1.9 %shard_map.107 = (bf16[512,256]{1,0:T(8,128)(2,1)S(1)}, bf16[512,256]{1,0:T(8,128)(2,1)S(1)}) custom-call(s32[4]{0:T(128)S(1)} %pad_add_fusion.where, f32[512,1024]{1,0:T(8,128)S(1)} %copy-done.4, bf16[2,1024,1024]{2,1,0:T(8,128)(2,1)S(1)} %get-tuple-element.56.bases, bf16[128,1024]{1,0:T(8,128)(2,1)S(1)} %shard_map.105.own.refs_0_, ...), custom_call_target="tpu_custom_call" | custom-call | flops 536870912 | bytes 4194304 | tf_op jit(solution)/shard_map/pallas_call | solution.py:43
  56.7 0.4 collective-permute-start.18
  57.1 0.0 collective-permute-done.16.refs_6_
  57.1 7.5 %shard_map.108 = (bf16[1024,1024]{1,0:T(8,128)(2,1)S(1)}, bf16[1024,1024]{1,0:T(8,128)(2,1)S(1)}, f32[1024,256]{1,0:T(8,128)S(1)}) custom-call(s32[4]{0:T(128)S(1)} %pad_add_fusion.where, bf16[2,1024,1024]{2,1,0:T(8,128)(2,1)S(1)} %get-tuple-element.56.bases, bf16[1024,1024]{1,0:T(8,128)(2,1)S(1)} %get-tuple-element.57.turned, ...), custom_call_target="tpu_custom_call" | custom-call | flops 3221225472 | bytes 8388608 | tf_op jit(solution)/shard_map/pallas_call | solution.py:43
  64.6 0.4 collective-permute-done.18.came
  65.0 0.0 collective-permute-start.19
  65.0 2.8 %shard_map.109 = (bf16[512,256]{1,0:T(8,128)(2,1)S(1)}, bf16[512,256]{1,0:T(8,128)(2,1)S(1)}) custom-call(s32[4]{0:T(128)S(1)} %pad_add_fusion.where, bf16[2,1024,1024]{2,1,0:T(8,128)(2,1)S(1)} %get-tuple-element.56.bases, bf16[1024,1024]{1,0:T(8,128)(2,1)S(1)} %get-tuple-element.57.turned, bf16[512,256]{1,0:T(8,128)(2,1)S(1)} %get-tuple-element.59.mine, ...), custom_call_target="tpu_custom_call" | custom-call | flops 12884901888 | bytes 4194304 | tf_op jit(solution)/shard_map/pallas_call | solution.py:43
  67.9 0.6 collective-permute-start.21
  68.4 0.0 collective-permute-done.19.new_next
  68.4 1.4 %collective-permute-start.20 = (bf16[512,256]{1,0:T(8,128)(2,1)S(1)}, bf16[512,256]{1,0:T(8,128)(2,1)S(1)}, u32[]{:S(2)}, u32[]{:S(2)}) collective-permute-start(bf16[512,256]{1,0:T(8,128)(2,1)S(1)} %get-tuple-element.74), channel_id=1, source_target_pairs={{0,1},{1,0},{2,3},{3,2},{4,5},{5,4},{6,7},{7,6},{8,9},{9,8},{10,11... | collective-permute-start | bytes 786440 | tf_op jit(solution)/shard_map/ppermute | solution.py:417
  69.8 6.8 %shard_map.110 = (bf16[1024,1024]{1,0:T(8,128)(2,1)S(1)}, bf16[1024,1024]{1,0:T(8,128)(2,1)S(1)}, f32[256,1024]{1,0:T(8,128)S(1)}, f32[1024,512]{1,0:T(8,128)}) custom-call(s32[4]{0:T(128)S(1)} %pad_add_fusion.where, bf16[1024,1024]{1,0:T(8,128)(2,1)S(1)} %get-tuple-element.70.start, bf16[1024,1024]{1,0:T(8,128)(2,1)S(1)} %get-tuple-element.71.start_turned, ...), custom_call_target="tpu_custom_call" | custom-call | flops 12884901888 | bytes 8388608 | tf_op jit(solution)/shard_map/pallas_call | solution.py:531
  76.7 0.0 collective-permute-done.21.kept_next
  76.7 0.1 collective-permute-done.20.came
  76.7 0.0 collective-permute-start.22
  76.8 0.5 collective-permute-start.23
  77.3 2.6 %shard_map.111 = (f32[256,1024]{1,0:T(8,128)S(1)}, f32[512,1024]{1,0:T(8,128)}, f32[512,1024]{1,0:T(8,128)}) custom-call(s32[4]{0:T(128)S(1)} %pad_add_fusion.where, bf16[1024,1024]{1,0:T(8,128)(2,1)S(1)} %get-tuple-element.77.current, bf16[1024,1024]{1,0:T(8,128)(2,1)S(1)} %get-tuple-element.78.turned, f32[256,1024]{1,0:T(8,128)S(1)} %get-tuple-element.79.top), custom_call_target="tpu_custom_call" | custom-call | flops 1073741824 | bytes 4194304 | tf_op jit(solution)/shard_map/pallas_call | solution.py:550
  79.8 0.0 collective-permute-done.22.came_next
  79.8 0.1 collective-permute-start.24
  80.0 0.0 collective-permute-done.23.top_next
  80.0 2.8 %shard_map.112 = (bf16[512,1024]{1,0:T(8,128)(2,1)}, f32[512,1024]{1,0:T(8,128)}, f32[512,1024]{1,0:T(8,128)}) custom-call(s32[4]{0:T(128)S(1)} %pad_add_fusion.where, bf16[512,256]{1,0:T(8,128)(2,1)S(1)} %get-tuple-element.67.kept, bf16[512,256]{1,0:T(8,128)(2,1)S(1)} %collective-permute-done.20.came, ...), custom_call_target="tpu_custom_call", output_to_operand_aliasing={{1}: (8, {}), {2}: (9, {})} | custom-call | flops 1073741824 | bytes 4194304 | tf_op jit(solution)/shard_map/pallas_call | solution.py:561
  82.8 0.0 collective-permute-done.24.low
  82.8 1.5 %shard_map.113 = (f32[512,1024]{1,0:T(8,128)}, f32[512,1024]{1,0:T(8,128)}) custom-call(s32[4]{0:T(128)S(1)} %pad_add_fusion.where, f32[256,1024]{1,0:T(8,128)S(1)} %collective-permute-done.24.low, f32[512,1024]{1,0:T(8,128)} %get-tuple-element.88.left_in, f32[512,1024]{1,0:T(8,128)} %get-tuple-element.89.right_in), custom_call_target="tpu_custom_call", output_to_operand_aliasing={{0}: (2, {}), {1}: (3, {})} | custom-call | bytes 2097152 | tf_op jit(solution)/shard_map/pallas_call | solution.py:43
  (13 shorter events, 0.1 us)
Async XLA Ops:
  1.9 2.1 %collective-permute-start = (bf16[256,1024]{1,0:T(8,128)(2,1)S(1)}, bf16[256,1024]{1,0:T(8,128)(2,1)S(1)}, u32[]{:S(2)}, u32[]{:S(2)}) collective-permute-start(bf16[256,1024]{1,0:T(8,128)(2,1)S(1)} %get-tuple-element.92), channel_id=1, source_target_pairs={{0,2},{2,0},{4,6},{6,4},{8,10},{10,8},{12,14},{14,12},{16,18},{18,... | collective-permute-start | bytes 1572872 | tf_op jit(solution)/shard_map/ppermute | solution.py:414
  4.0 44.1 %copy-start.1 = (f32[512,1024]{1,0:T(8,128)S(1)}, f32[512,1024]{1,0:T(8,128)}, u32[]{:S(2)}) copy-start(f32[512,1024]{1,0:T(8,128)} %right.3) | copy-start | bytes 6291460
  4.0 44.1 %copy-start.2 = (f32[512,1024]{1,0:T(8,128)S(1)}, f32[512,1024]{1,0:T(8,128)}, u32[]{:S(2)}) copy-start(f32[512,1024]{1,0:T(8,128)} %stat_left.3) | copy-start | bytes 6291460
  4.0 44.1 %copy-start.3 = (f32[512,1024]{1,0:T(8,128)S(1)}, f32[512,1024]{1,0:T(8,128)}, u32[]{:S(2)}) copy-start(f32[512,1024]{1,0:T(8,128)} %stat_right.3) | copy-start | bytes 6291460
  6.7 41.4 %copy-start = (f32[512,1024]{1,0:T(8,128)S(1)}, f32[512,1024]{1,0:T(8,128)}, u32[]{:S(2)}) copy-start(f32[512,1024]{1,0:T(8,128)} %left.3) | copy-start | bytes 6291460
  6.7 30.6 %collective-permute-start.8 = (bf16[38,128,128]{2,1,0:T(8,128)(2,1)S(1)}, bf16[38,128,128]{2,1,0:T(8,128)(2,1)S(1)}, u32[]{:S(2)}, u32[]{:S(2)}) collective-permute-start(bf16[38,128,128]{2,1,0:T(8,128)(2,1)S(1)} %get-tuple-element.54), channel_id=1, source_target_pairs={{0,1},{1,0},{2,3},{3,2},{4,5},{5,4},{6,7},{7,6},{8,9},{9,8},{10,11... | collective-permute-start | bytes 3735560 | tf_op jit(solution)/shard_map/ppermute | solution.py:417
  9.7 8.1 %collective-permute-start.1 = (bf16[128,1024]{1,0:T(8,128)(2,1)S(1)}, bf16[128,1024]{1,0:T(8,128)(2,1)S(1)}, u32[]{:S(2)}, u32[]{:S(2)}) collective-permute-start(bf16[128,1024]{1,0:T(8,128)(2,1)S(1)} %get-tuple-element.49), channel_id=1, source_target_pairs={{0,4},{2,6},{4,0},{6,2},{8,12},{10,14},{12,8},{14,10},{16,20},{18,... | collective-permute-start | bytes 786440 | tf_op jit(solution)/shard_map/ppermute | solution.py:414
  18.3 4.9 %collective-permute-start.2 = (bf16[32,1024]{1,0:T(8,128)(2,1)S(1)}, bf16[32,1024]{1,0:T(8,128)(2,1)S(1)}, u32[]{:S(2)}, u32[]{:S(2)}) collective-permute-start(bf16[32,1024]{1,0:T(8,128)(2,1)S(1)} %get-tuple-element.51), channel_id=1, source_target_pairs={{0,8},{2,10},{4,12},{6,14},{8,0},{10,2},{12,4},{14,6},{16,24},{18,... | collective-permute-start | bytes 196616 | tf_op jit(solution)/shard_map/ppermute | solution.py:414
  20.0 6.6 %collective-permute-start.3 = (bf16[32,1024]{1,0:T(8,128)(2,1)S(1)}, bf16[32,1024]{1,0:T(8,128)(2,1)S(1)}, u32[]{:S(2)}, u32[]{:S(2)}) collective-permute-start(bf16[32,1024]{1,0:T(8,128)(2,1)S(1)} %get-tuple-element.52), channel_id=1, source_target_pairs={{0,16},{2,18},{4,20},{6,22},{8,24},{10,26},{12,28},{14,30},{16,0},... | collective-permute-start | bytes 196616 | tf_op jit(solution)/shard_map/ppermute | solution.py:414
  22.6 6.1 %collective-permute-start.4 = (bf16[32,1024]{1,0:T(8,128)(2,1)S(1)}, bf16[32,1024]{1,0:T(8,128)(2,1)S(1)}, u32[]{:S(2)}, u32[]{:S(2)}) collective-permute-start(bf16[32,1024]{1,0:T(8,128)(2,1)S(1)} %get-tuple-element.53), channel_id=1, source_target_pairs={{0,24},{2,26},{4,28},{6,30},{8,16},{10,18},{12,20},{14,22},{16,8},... | collective-permute-start | bytes 196616 | tf_op jit(solution)/shard_map/ppermute | solution.py:414
  28.7 6.2 %collective-permute-start.7 = (bf16[32,1024]{1,0:T(8,128)(2,1)S(1)}, bf16[32,1024]{1,0:T(8,128)(2,1)S(1)}, u32[]{:S(2)}, u32[]{:S(2)}) collective-permute-start(bf16[32,1024]{1,0:T(8,128)(2,1)S(1)} %shard_map.104.refs_0_), channel_id=1, source_target_pairs={{0,24},{2,26},{4,28},{6,30},{8,16},{10,18},{12,20},{14,22},{16,8},... | collective-permute-start | bytes 196616 | tf_op jit(solution)/shard_map/ppermute | solution.py:414
  29.9 6.4 %collective-permute-start.6 = (bf16[32,1024]{1,0:T(8,128)(2,1)S(1)}, bf16[32,1024]{1,0:T(8,128)(2,1)S(1)}, u32[]{:S(2)}, u32[]{:S(2)}) collective-permute-start(bf16[32,1024]{1,0:T(8,128)(2,1)S(1)} %shard_map.104.refs_0_), channel_id=1, source_target_pairs={{0,16},{2,18},{4,20},{6,22},{8,24},{10,26},{12,28},{14,30},{16,0},... | collective-permute-start | bytes 196616 | tf_op jit(solution)/shard_map/ppermute | solution.py:414
  30.3 6.0 %collective-permute-start.5 = (bf16[32,1024]{1,0:T(8,128)(2,1)S(1)}, bf16[32,1024]{1,0:T(8,128)(2,1)S(1)}, u32[]{:S(2)}, u32[]{:S(2)}) collective-permute-start(bf16[32,1024]{1,0:T(8,128)(2,1)S(1)} %shard_map.104.refs_0_), channel_id=1, source_target_pairs={{0,8},{2,10},{4,12},{6,14},{8,0},{10,2},{12,4},{14,6},{16,24},{18,... | collective-permute-start | bytes 196616 | tf_op jit(solution)/shard_map/ppermute | solution.py:414
  37.3 10.7 %collective-permute-start.9 = (bf16[38,128,128]{2,1,0:T(8,128)(2,1)S(1)}, bf16[38,128,128]{2,1,0:T(8,128)(2,1)S(1)}, u32[]{:S(2)}, u32[]{:S(2)}) collective-permute-start(bf16[38,128,128]{2,1,0:T(8,128)(2,1)S(1)} %collective-permute-done.8.mine), channel_id=1, source_target_pairs={{0,2},{2,0},{4,6},{6,4},{8,10},{10,8},{12,14},{14,12},{16,18},{18,... | collective-permute-start | bytes 3735560 | tf_op jit(solution)/shard_map/ppermute | solution.py:414
  37.3 10.2 %collective-permute-start.11 = (bf16[128,1024]{1,0:T(8,128)(2,1)S(1)}, bf16[128,1024]{1,0:T(8,128)(2,1)S(1)}, u32[]{:S(2)}, u32[]{:S(2)}) collective-permute-start(bf16[128,1024]{1,0:T(8,128)(2,1)S(1)} %shard_map.105.own.refs_0_), channel_id=1, source_target_pairs={{0,4},{2,6},{4,0},{6,2},{8,12},{10,14},{12,8},{14,10},{16,20},{18,... | collective-permute-start | bytes 786440 | tf_op jit(solution)/shard_map/ppermute | solution.py:414
  39.1 13.9 %collective-permute-start.15 = (bf16[128,1024]{1,0:T(8,128)(2,1)S(1)}, bf16[128,1024]{1,0:T(8,128)(2,1)S(1)}, u32[]{:S(2)}, u32[]{:S(2)}) collective-permute-start(bf16[128,1024]{1,0:T(8,128)(2,1)S(1)} %shard_map.105.own.refs_0_), channel_id=1, source_target_pairs={{0,5},{1,4},{2,7},{3,6},{4,1},{5,0},{6,3},{7,2},{8,13},{9,12},{10,... | collective-permute-start | bytes 786440 | tf_op jit(solution)/shard_map/ppermute | solution.py:421
  40.6 13.8 %collective-permute-start.14 = (bf16[128,1024]{1,0:T(8,128)(2,1)S(1)}, bf16[128,1024]{1,0:T(8,128)(2,1)S(1)}, u32[]{:S(2)}, u32[]{:S(2)}) collective-permute-start(bf16[128,1024]{1,0:T(8,128)(2,1)S(1)} %shard_map.105.own.refs_0_), channel_id=1, source_target_pairs={{0,1},{1,0},{2,3},{3,2},{4,5},{5,4},{6,7},{7,6},{8,9},{9,8},{10,11... | collective-permute-start | bytes 786440 | tf_op jit(solution)/shard_map/ppermute | solution.py:417
  40.9 14.0 %copy-start.4 = (f32[512,1024]{1,0:T(8,128)S(1)}, f32[512,1024]{1,0:T(8,128)}, u32[]{:S(2)}) copy-start(f32[512,1024]{1,0:T(8,128)} %moment.1) | copy-start | bytes 6291460
  40.9 6.7 %collective-permute-start.10 = (bf16[6,128,128]{2,1,0:T(8,128)(2,1)S(1)}, bf16[6,128,128]{2,1,0:T(8,128)(2,1)S(1)}, u32[]{:S(2)}, u32[]{:S(2)}) collective-permute-start(bf16[6,128,128]{2,1,0:T(8,128)(2,1)S(1)} %slice.3), channel_id=1, source_target_pairs={{0,8},{2,10},{4,12},{6,14},{8,0},{10,2},{12,4},{14,6},{16,24},{18,... | collective-permute-start | bytes 589832 | tf_op jit(solution)/shard_map/ppermute | solution.py:414
  47.5 7.3 %collective-permute-start.12 = (bf16[128,1024]{1,0:T(8,128)(2,1)S(1)}, bf16[128,1024]{1,0:T(8,128)(2,1)S(1)}, u32[]{:S(2)}, u32[]{:S(2)}) collective-permute-start(bf16[128,1024]{1,0:T(8,128)(2,1)S(1)} %shard_map.105.own.refs_0_), channel_id=1, source_target_pairs={{0,2},{2,0},{4,6},{6,4},{8,10},{10,8},{12,14},{14,12},{16,18},{18,... | collective-permute-start | bytes 786440 | tf_op jit(solution)/shard_map/ppermute | solution.py:414
  47.5 7.3 %collective-permute-start.13 = (bf16[128,1024]{1,0:T(8,128)(2,1)S(1)}, bf16[128,1024]{1,0:T(8,128)(2,1)S(1)}, u32[]{:S(2)}, u32[]{:S(2)}) collective-permute-start(bf16[128,1024]{1,0:T(8,128)(2,1)S(1)} %collective-permute-done.11.over_x.refs_1_), channel_id=1, source_target_pairs={{0,2},{2,0},{4,6},{6,4},{8,10},{10,8},{12,14},{14,12},{16,18},{18,... | collective-permute-start | bytes 786440 | tf_op jit(solution)/shard_map/ppermute | solution.py:414
  54.3 2.8 %copy-start.5 = (f32[1024,512]{1,0:T(8,128)S(1)}, f32[1024,512]{1,0:T(8,128)}, u32[]{:S(2)}) copy-start(f32[1024,512]{1,0:T(8,128)} %second.1) | copy-start | bytes 6291460
  54.3 2.8 %collective-permute-start.16 = (bf16[128,1024]{1,0:T(8,128)(2,1)S(1)}, bf16[128,1024]{1,0:T(8,128)(2,1)S(1)}, u32[]{:S(2)}, u32[]{:S(2)}) collective-permute-start(bf16[128,1024]{1,0:T(8,128)(2,1)S(1)} %collective-permute-done.14.refs_4_), channel_id=1, source_target_pairs={{0,2},{2,0},{4,6},{6,4},{8,10},{10,8},{12,14},{14,12},{16,18},{18,... | collective-permute-start | bytes 786440 | tf_op jit(solution)/shard_map/ppermute | solution.py:414
  54.3 2.8 %collective-permute-start.17 = (bf16[128,1024]{1,0:T(8,128)(2,1)S(1)}, bf16[128,1024]{1,0:T(8,128)(2,1)S(1)}, u32[]{:S(2)}, u32[]{:S(2)}) collective-permute-start(bf16[128,1024]{1,0:T(8,128)(2,1)S(1)} %collective-permute-done.15.refs_5_), channel_id=1, source_target_pairs={{0,2},{2,0},{4,6},{6,4},{8,10},{10,8},{12,14},{14,12},{16,18},{18,... | collective-permute-start | bytes 786440 | tf_op jit(solution)/shard_map/ppermute | solution.py:414
  56.7 8.3 %collective-permute-start.18 = (bf16[512,256]{1,0:T(8,128)(2,1)S(1)}, bf16[512,256]{1,0:T(8,128)(2,1)S(1)}, u32[]{:S(2)}, u32[]{:S(2)}) collective-permute-start(bf16[512,256]{1,0:T(8,128)(2,1)S(1)} %get-tuple-element.64), channel_id=1, source_target_pairs={{0,1},{1,0},{2,3},{3,2},{4,5},{5,4},{6,7},{7,6},{8,9},{9,8},{10,11... | collective-permute-start | bytes 786440 | tf_op jit(solution)/shard_map/ppermute | solution.py:417
  65.0 3.4 %collective-permute-start.19 = (f32[1024,256]{1,0:T(8,128)S(1)}, f32[1024,256]{1,0:T(8,128)S(1)}, u32[]{:S(2)}, u32[]{:S(2)}) collective-permute-start(f32[1024,256]{1,0:T(8,128)S(1)} %get-tuple-element.66.new), channel_id=1, source_target_pairs={{0,2},{2,0},{4,6},{6,4},{8,10},{10,8},{12,14},{14,12},{16,18},{18,... | collective-permute-start | bytes 3145736 | tf_op jit(solution)/shard_map/ppermute | solution.py:414
  67.9 8.8 %collective-permute-start.21 = (bf16[512,256]{1,0:T(8,128)(2,1)S(1)}, bf16[512,256]{1,0:T(8,128)(2,1)S(1)}, u32[]{:S(2)}, u32[]{:S(2)}) collective-permute-start(bf16[512,256]{1,0:T(8,128)(2,1)S(1)} %get-tuple-element.67.kept), channel_id=1, source_target_pairs={{0,2},{2,0},{4,6},{6,4},{8,10},{10,8},{12,14},{14,12},{16,18},{18,... | collective-permute-start | bytes 786440 | tf_op jit(solution)/shard_map/ppermute | solution.py:414
  68.4 8.3 %collective-permute-start.20 = (bf16[512,256]{1,0:T(8,128)(2,1)S(1)}, bf16[512,256]{1,0:T(8,128)(2,1)S(1)}, u32[]{:S(2)}, u32[]{:S(2)}) collective-permute-start(bf16[512,256]{1,0:T(8,128)(2,1)S(1)} %get-tuple-element.74), channel_id=1, source_target_pairs={{0,1},{1,0},{2,3},{3,2},{4,5},{5,4},{6,7},{7,6},{8,9},{9,8},{10,11... | collective-permute-start | bytes 786440 | tf_op jit(solution)/shard_map/ppermute | solution.py:417
  76.7 3.1 %collective-permute-start.22 = (bf16[512,256]{1,0:T(8,128)(2,1)S(1)}, bf16[512,256]{1,0:T(8,128)(2,1)S(1)}, u32[]{:S(2)}, u32[]{:S(2)}) collective-permute-start(bf16[512,256]{1,0:T(8,128)(2,1)S(1)} %collective-permute-done.20.came), channel_id=1, source_target_pairs={{0,2},{2,0},{4,6},{6,4},{8,10},{10,8},{12,14},{14,12},{16,18},{18,... | collective-permute-start | bytes 786440 | tf_op jit(solution)/shard_map/ppermute | solution.py:414
  76.8 3.2 %collective-permute-start.23 = (f32[256,1024]{1,0:T(8,128)S(1)}, f32[256,1024]{1,0:T(8,128)S(1)}, u32[]{:S(2)}, u32[]{:S(2)}) collective-permute-start(f32[256,1024]{1,0:T(8,128)S(1)} %get-tuple-element.79.top), channel_id=1, source_target_pairs={{0,2},{2,0},{4,6},{6,4},{8,10},{10,8},{12,14},{14,12},{16,18},{18,... | collective-permute-start | bytes 3145736 | tf_op jit(solution)/shard_map/ppermute | solution.py:414
  79.8 3.0 %collective-permute-start.24 = (f32[256,1024]{1,0:T(8,128)S(1)}, f32[256,1024]{1,0:T(8,128)S(1)}, u32[]{:S(2)}, u32[]{:S(2)}) collective-permute-start(f32[256,1024]{1,0:T(8,128)S(1)} %get-tuple-element.83.low), channel_id=1, source_target_pairs={{0,2},{2,0},{4,6},{6,4},{8,10},{10,8},{12,14},{14,12},{16,18},{18,... | collective-permute-start | bytes 3145736 | tf_op jit(solution)/shard_map/ppermute | solution.py:414
